TPU v7x, 32 devices: a whole 2x2x4 slice. The times are simulated.
32 devices in a mesh: pair: 16 (over z, y, core), proj: 2 (over x).
Axes of the slice: x: 2, y: 2, z: 4, core: 2. Of those that a mesh axis runs over, the one named last changes fastest.
Arguments:
- val_orbitals: bfloat16 [128, 24576], P(('pair', 'proj')), may hold values from -6 to 6
- cond_orbitals: bfloat16 [512, 24576], P(('pair', 'proj')), may hold values from -6 to 6
- val_energy: float32 [128], P(('pair', 'proj')), may hold values from -1 to -0.25
- cond_energy: float32 [512], P(('pair', 'proj')), may hold values from 0.25 to 16
- val_slot: int32 [2048], P(('pair', 'proj')), may hold values from 0 to 3
- cond_slot: int32 [2048], P(('pair', 'proj')), may hold values from 0 to 15
- eigenvectors: bfloat16 [24576, 2048], P('proj', 'pair'), may hold values from -0.0390625 to 0.0390625
- frequencies: float32 [4], replicated, may hold values from 0.5 to 16
Outputs:
- chi_sub: float32 [2048, 4, 2048], P('pair', None, 'proj')
All inputs are finite; a program needn't handle non-finite values.
Results may differ from a plain program's by a relative error of at most 0.0045.
Values may be sent and summed in bfloat16 or wider, within the bound.
No kernel may reach another device: no remote copies, remote signals or barrier semaphores. Data moves between devices by JAX's collectives and lax.ppermute only.
A program may use at most 192 MiB of HBM per device.

v0:
```python
import math

import jax
import jax.numpy as jnp
from jax import lax
from jax.sharding import PartitionSpec as P


def weigh_rows(block, wrows):
    weighted = (
        block.astype(jnp.float32)[:, None, :] * wrows.astype(jnp.float32)[:, :, None]
    ).astype(jnp.bfloat16)
    return weighted.reshape(block.shape[0], wrows.shape[1] * block.shape[1])


def form_density(val_index, cond_index, val_source, cond_source):
    val_pick = val_index[:, None] == jnp.arange(val_source.shape[0], dtype=jnp.int32)[None, :]
    cond_pick = cond_index[:, None] == jnp.arange(cond_source.shape[0], dtype=jnp.int32)[None, :]
    val_rows = jnp.dot(
        val_pick.astype(jnp.bfloat16), val_source, preferred_element_type=jnp.float32
    )
    cond_rows = jnp.dot(
        cond_pick.astype(jnp.bfloat16), cond_source, preferred_element_type=jnp.float32
    )
    return (val_rows * cond_rows).astype(jnp.bfloat16)


def local(
    val_orbitals,
    cond_orbitals,
    val_energy,
    cond_energy,
    val_slot,
    cond_slot,
    eigenvectors,
    frequencies,
):
    val_count = val_orbitals.shape[0]
    cond_count = cond_orbitals.shape[0]
    per_dev = val_slot.shape[0]
    n_freq = frequencies.shape[0]
    n_proj = lax.axis_size("proj")
    n_pair = lax.axis_size("pair")
    proj_place = lax.axis_index("proj")
    val_pick = val_slot[:, None] == jnp.arange(val_count, dtype=jnp.int32)[None, :]
    cond_pick = cond_slot[:, None] == jnp.arange(cond_count, dtype=jnp.int32)[None, :]
    cond_level = jnp.sum(jnp.where(cond_pick, cond_energy[None, :], 0.0), axis=1)
    val_level = jnp.sum(jnp.where(val_pick, val_energy[None, :], 0.0), axis=1)
    energy_difference = cond_level - val_level
    weights = (
        4.0
        * energy_difference[:, None]
        / (energy_difference[:, None] ** 2 + frequencies[None, :] ** 2)
    ).astype(jnp.bfloat16)
    density = form_density(val_slot, cond_slot, val_orbitals, cond_orbitals)
    rows_mine = lax.all_to_all(density, "proj", split_axis=1, concat_axis=0, tiled=True)
    part_sums = jnp.dot(
        rows_mine,
        lax.all_gather(eigenvectors, "pair", axis=1, tiled=True),
        preferred_element_type=jnp.float32,
    )
    group_rows = part_sums.shape[0]
    n_sub = part_sums.shape[1]
    sblock = n_sub // n_proj
    padded = lax.dynamic_update_slice(
        jnp.zeros((group_rows, n_freq), jnp.float32),
        weights.astype(jnp.float32),
        (proj_place * per_dev, 0),
    )
    summed, weight_sum = lax.psum((part_sums, padded), "proj")
    coeffs = summed.astype(jnp.bfloat16)
    group_weights = weight_sum.astype(jnp.bfloat16)
    own_block = lax.dynamic_slice_in_dim(coeffs, proj_place * sblock, sblock, 1)
    tile_rows = n_sub // n_pair
    factor = -1.0 / math.sqrt(group_rows * n_pair)
    weighted = weigh_rows(own_block, group_weights)
    chi_tile = lax.psum_scatter(
        lax.dot_general(
            coeffs, weighted, (((0,), (0,)), ((), ())), preferred_element_type=jnp.float32
        ),
        "pair",
        scatter_dimension=0,
        tiled=True,
    )
    return (chi_tile * factor).reshape(tile_rows, n_freq, sblock)


def solution(mesh):
    return jax.shard_map(
        local,
        mesh=mesh,
        in_specs=(
            P(("pair", "proj"), None),
            P(("pair", "proj"), None),
            P(("pair", "proj")),
            P(("pair", "proj")),
            P(("pair", "proj")),
            P(("pair", "proj")),
            P("proj", "pair"),
            P(),
        ),
        out_specs=P("pair", None, "proj"),
        check_vma=False,
    )
```

profile of v0, /device:TPU:0, one launch (start us, length us, event | category | flops | bytes accessed | tf_op | source)
XLA Modules:
  0.0 674.9 jit_solution(15909613141914604024)
XLA Ops:
  6.5 0.0 copy-start
  6.5 0.0 copy-start.2
  6.5 0.0 copy-start.4
  6.5 0.0 all-gather.2.cloned.1.call-start
  6.5 0.7 all-gather.2.cloned.1.call-update
  7.3 0.3 copy-done.2
  7.5 0.0 copy-done.4
  7.5 0.0 copy-start.3
  7.5 1.0 fusion.3
  8.6 0.0 copy-done
  8.6 0.0 copy-done.3
  8.6 1.0 fusion
  9.6 1.9 copy.16
  11.5 0.0 copy-start.5
  11.5 0.0 copy-start.6
  11.5 0.0 copy-start.7
  11.5 5.3 all-to-all-start
  16.9 0.0 reduce-scatter.2.cloned.1.call-start
  16.9 0.0 copy-done.5
  16.9 0.0 copy-done.6
  17.0 0.1 select_reduce_fusion
  17.0 0.0 copy-done.7
  17.0 0.1 select_reduce_fusion.1
  17.1 0.1 fusion.4
  17.2 0.1 dynamic_update_slice.3
  17.3 37.2 %all-to-all-done = bf16[64,2,12288]{2,0,1:T(8,128)(2,1)} async-done(((bf16[64,2,12288]{2,0,1:T(8,128)(2,1)}), bf16[64,2,12288]{2,0,1:T(8,128)(2,1)}, u32[]{:S(2)}, u32[]{:S(2)}) %all-to-all-start) | async-done | bytes 3145760 | tf_op jit(solution)/shard_map/all_to_all | solution.py:56
  54.5 214.2 %all-gather.2.cloned.1.call-done = bf16[12288,2048]{1,0:T(8,128)(2,1)} async-done(((bf16[12288,128]{1,0:T(8,128)(2,1)}), bf16[12288,2048]{1,0:T(8,128)(2,1)}) %all-gather.2.cloned.1.call-update) | async-done | bytes 50331664 | tf_op jit(solution)/shard_map/all_gather | solution.py:59
  268.7 19.8 %fusion.6 = f32[128,2048]{1,0:T(8,128)S(1)} fusion(bf16[128,12288]{1,0:T(8,128)(2,1)} %bitcast.1, bf16[12288,2048]{1,0:T(8,128)(2,1)} %all-gather.2.cloned.1.call-done), kind=kOutput, calls=%fused_computation.19 | convolution fusion | flops 6442450944 | bytes 54525952 | tf_op jit(solution)/shard_map/dot_general | solution.py:57
  288.5 30.4 %all-reduce.2 = (bf16[128,2048]{1,0:T(8,128)(2,1)S(1)}, bf16[128,4]{0,1:T(4,128)(2,1)S(1)}) all-reduce(f32[128,2048]{1,0:T(8,128)S(1)} %fusion.6, f32[128,4]{0,1:T(4,128)S(1)} %dynamic_update_slice.3), channel_id=1, replica_groups=mesh['pair'=16,'proj'=2] {'proj'}, use_global_device_ids=true, to_apply=%region_0.1 | all-reduce | flops 262656 | bytes 1575936 | tf_op jit(solution)/shard_map/psum | solution.py:70
  318.9 0.1 copy.12
  319.1 0.4 multiply_convert_fusion
  319.6 0.4 copy.14
  319.9 13.2 %fusion.7 = f32[2048,4096]{1,0:T(8,128)} fusion(bf16[128,2048]{1,0:T(8,128)(2,1)S(1)} %get-tuple-element.5, bf16[128,4096]{1,0:T(8,128)(2,1)S(1)} %bitcast.17), kind=kOutput, calls=%fused_computation.20 | convolution fusion | flops 2147483648 | bytes 35127296 | tf_op jit(solution)/shard_map/dot_general | solution.py:78
  333.1 0.0 reduce-scatter.2.cloned.1.call-update
  333.1 330.7 %reduce-scatter.2.cloned.1.call-done = f32[128,4096]{1,0:T(8,128)} async-done(((f32[2048,4096]{1,0:T(8,128)}), f32[128,4096]{1,0:T(8,128)}) %reduce-scatter.2.cloned.1.call-update) | async-done | bytes 2097168 | tf_op jit(solution)/shard_map/reduce_scatter | solution.py:77
  663.8 0.0 copy-start.1
  663.8 1.8 broadcast_multiply_fusion
  665.7 2.4 reshape.32
  668.1 0.0 copy-done.1
  (4 shorter events, 0.1 us)
Async XLA Ops:
  6.5 2.0 copy-start
  6.5 1.0 copy-start.2
  6.5 1.0 copy-start.4
  6.5 262.2 %all-gather.2.cloned.1.call-start = ((), (), s32[]{:S(2)}) async-start(), calls=%async_computation.2 | async-start | bytes 53477376 | tf_op jit(solution)/shard_map/all_gather | solution.py:59
  7.5 1.1 copy-start.3
  11.5 5.4 copy-start.5
  11.5 5.4 copy-start.6
  11.5 5.5 copy-start.7
  11.5 43.0 %all-to-all-start = ((bf16[64,2,12288]{2,0,1:T(8,128)(2,1)}), bf16[64,2,12288]{2,0,1:T(8,128)(2,1)}, u32[]{:S(2)}, u32[]{:S(2)}) async-start(bf16[64,2,12288]{2,0,1:T(8,128)(2,1)} %bitcast.15), calls=%async_computation | async-start | bytes 6291456 | tf_op jit(solution)/shard_map/all_to_all | solution.py:56
  16.9 647.0 %reduce-scatter.2.cloned.1.call-start = ((), (), s32[]{:S(2)}) async-start(), calls=%async_computation.3 | async-start | bytes 35651584 | tf_op jit(solution)/shard_map/reduce_scatter | solution.py:77
  663.8 4.3 copy-start.1
Sparse Core Ops, SparseCore 0:
  8.9 259.8 all-gather.1
  333.2 330.5 reduce-scatter.1
where the time goes:
time: 675 us
  waiting for transfers between devices  583 us (86%)
  matrix products  35 us (5%)
  blocking collectives  30.4 us (5%)
  between operations  13.5 us (2%)
    reduce_scatter x1, waiting for transfers between devices, local(): lax.psum_scatter(lax.dot_general(coeffs, weighted, (((0,), (0,)), ((), ()...  331 us
    all_gather x1, waiting for transfers between devices, local(): lax.all_gather(eigenvectors, 'pair', axis=1, tiled=True)  214 us
    all_to_all x1, waiting for transfers between devices, local(): lax.all_to_all(density, 'proj', split_axis=1, concat_axis=0, tiled=True)  37.2 us
    psum x1, blocking collectives, local(): summed, weight_sum = lax.psum((part_sums, padded), 'proj')  30.4 us
    dot_general x1, matrix products, local(): jnp.dot(rows_mine, lax.all_gather(eigenvectors, 'pair', axis=1, tiled=Tru...  19.8 us
  transfers between devices with their start and end apart: 3, of which 3 were waited for; matrix products, arithmetic and copies ran while one was open for 1% of the time, Pallas kernels for 0%

commit v1 on v0

v1 whole, which is shorter than its diff:
```python
import math

import jax
import jax.numpy as jnp
from jax import lax
from jax.sharding import PartitionSpec as P

LANES = 128


def local(
    val_orbitals,
    cond_orbitals,
    val_energy,
    cond_energy,
    val_slot,
    cond_slot,
    eigenvectors,
    frequencies,
):
    val_count, n_grid = val_orbitals.shape
    cond_count = cond_orbitals.shape[0]
    per_dev = val_slot.shape[0]
    n_freq = frequencies.shape[0]
    n_proj = lax.axis_size("proj")
    n_pair = lax.axis_size("pair")
    x = lax.axis_index("proj")
    part = n_grid // n_proj
    segs = cond_count // val_count
    seg = part // segs
    combos = val_count * cond_count
    columns = eigenvectors.shape[1]
    fold = n_pair // n_proj

    gap = cond_energy[:, None] - val_energy[None, :]
    weights = (
        4.0 * gap[:, :, None] / (gap[:, :, None] ** 2 + frequencies[None, None, :] ** 2)
    ).astype(jnp.bfloat16)
    chosen = (cond_slot[:, None, None] == jnp.arange(cond_count, dtype=jnp.int32)[None, :, None]) & (
        val_slot[:, None, None] == jnp.arange(val_count, dtype=jnp.int32)[None, None, :]
    )
    counts = jnp.sum(chosen.astype(jnp.float32), axis=0).astype(jnp.bfloat16)
    extra = jnp.concatenate([weights, counts[:, :, None]], axis=2).reshape(
        cond_count, val_count * (n_freq + 1)
    )
    extra = jnp.pad(extra, ((0, 0), (0, LANES - extra.shape[1])))

    def packed(place):
        cond_part = lax.dynamic_slice_in_dim(cond_orbitals, place * part, part, 1)
        val_part = lax.dynamic_slice_in_dim(val_orbitals, place * part, part, 1)
        val_part = val_part.reshape(val_count, segs, seg).transpose(1, 0, 2)
        return jnp.concatenate([cond_part, val_part.reshape(cond_count, seg), extra], axis=1)

    pieces = [packed(x)]
    for k in range(1, n_proj):
        to_send = packed((x + k) % n_proj)
        pieces.append(
            lax.ppermute(to_send, "proj", [(s, (s + k) % n_proj) for s in range(n_proj)])
        )
    eig = eigenvectors.reshape(segs, seg, columns)
    running = None
    scales = []
    for k in range(n_proj):
        got = lax.all_gather(pieces[k], "pair", axis=0, tiled=True)
        got = got.reshape(n_pair, cond_count, part + seg + LANES)
        cond_rows = got[:, :, :part].reshape(n_pair, cond_count, segs, seg)
        val_rows = got[:, :, part : part + seg].reshape(n_pair, segs, val_count, seg)
        density = (
            cond_rows.astype(jnp.float32)[:, None]
            * val_rows.transpose(0, 2, 1, 3).astype(jnp.float32)[:, :, None]
        ).astype(jnp.bfloat16)
        sums = lax.dot_general(
            density.reshape(n_pair * combos, part),
            eigenvectors,
            (((1,), (0,)), ((), ())),
            preferred_element_type=jnp.float32,
        )
        if running is not None:
            sums = sums + running
        if k < n_proj - 1:
            running = lax.ppermute(
                sums, "proj", [(s, (s + 1) % n_proj) for s in range(n_proj)]
            )
        scales.append(got[:, :, part + seg : part + seg + val_count * (n_freq + 1)])
    coeffs = sums.astype(jnp.bfloat16)

    perm = []
    for j in range(n_pair):
        for s in range(n_proj):
            source = j * n_proj + s
            perm.append((source, (j % fold + fold * s) * n_proj + j // fold))
    share = lax.ppermute(coeffs, ("pair", "proj"), perm)
    right = lax.all_gather(share, "pair", axis=0, tiled=True)
    right = right.reshape(n_proj, fold, n_pair * combos, columns)

    own = [coeffs]
    for k in range(1, n_proj):
        own.append(
            lax.ppermute(coeffs, "proj", [(s, (s + k) % n_proj) for s in range(n_proj)])
        )
    factor = -1.0 / math.sqrt(per_dev * n_pair * n_proj)
    total = None
    left, rights = [], []
    for k in range(n_proj):
        place = (x - k + n_proj) % n_proj
        rows = own[k].astype(jnp.float32).reshape(n_pair, val_count, cond_count, columns)
        scale = scales[(k - 1) % n_proj].astype(jnp.float32)
        scale = scale.reshape(n_pair, cond_count, val_count, n_freq + 1).transpose(0, 2, 1, 3)
        scale = scale[..., :n_freq] * scale[..., n_freq:]
        weighted = (rows[..., None] * scale[:, :, :, None, :]).astype(jnp.bfloat16)
        left.append(weighted.reshape(n_pair * combos, columns * n_freq))
        rights.append(lax.dynamic_index_in_dim(right, place, 0, keepdims=False))
    left = jnp.concatenate(left, axis=0)
    rights = jnp.concatenate(rights, axis=1)
    chi = lax.dot_general(
        left, rights, (((0,), (1,)), ((), ())), preferred_element_type=jnp.float32
    )
    return (chi * factor).reshape(columns, n_freq, fold * columns)


def solution(mesh):
    return jax.shard_map(
        local,
        mesh=mesh,
        in_specs=(
            P(("pair", "proj"), None),
            P(("pair", "proj"), None),
            P(("pair", "proj")),
            P(("pair", "proj")),
            P(("pair", "proj")),
            P(("pair", "proj")),
            P("proj", "pair"),
            P(),
        ),
        out_specs=P("pair", None, "proj"),
        check_vma=False,
    )
```

time: 675 us -> 356 us (0.53)
  waiting for transfers between devices: 583 us -> 71.8 us
  local copies, waits for them, and re-layouts: 5.21 us -> 150 us
  other arithmetic: 2.59 us -> 70 us
  blocking collectives: 30.4 us -> 0 us
  starting transfers between devices: 5.36 us -> 22.5 us
  matrix products: 35 us -> 26.7 us
    reduce_scatter x1 -> x0, waiting for transfers between devices: 331 us -> none  [local(): lax.psum_scatter(lax.dot_general(coeffs, weighted, (((0,), (0,)), ((), ()...]
    all_gather x1 -> x3, waiting for transfers between devices: 214 us -> 60.1 us  [the longest x2 60.1 us: local(): got = lax.all_gather(pieces[k], 'pair', axis=0, tiled=True)]
    convert_element_type x1 -> x9, local copies, waits for them, and re-layouts: 0.12 us -> 73.4 us  [the longest x2 31.6 us: local(): weighted = (rows[..., None] * scale[:, :, :, None, :]).astype(jnp.bfloat16)]
    convert_element_type x3 -> x9, other arithmetic: 0.56 us -> 62.3 us  [the longest x2 30 us: local(): density = (cond_rows.astype(jnp.float32)[:, None] * val_rows.transpose(0,...]
    unnamed x17, local copies, waits for them, and re-layouts: 0.68 us -> 52.1 us
    all_to_all x1 -> x0, waiting for transfers between devices: 37.2 us -> none  [local(): lax.all_to_all(density, 'proj', split_axis=1, concat_axis=0, tiled=True)]
    psum x1 -> x0, blocking collectives: 30.4 us -> none  [local(): summed, weight_sum = lax.psum((part_sums, padded), 'proj')]
    ppermute x0 -> x4, starting transfers between devices: none -> 22.5 us  [the longest x1 17.3 us: local(): lax.ppermute(coeffs, 'proj', [(s, (s + k) % n_proj) for s in range(n_proj)])]
  transfers between devices with their start and end apart: 3 -> 7, of which waited for: 3 -> 2; matrix products, arithmetic and copies ran while one was open for 1% -> 60% of each run, Pallas kernels for 0% -> 0%
where the time goes in v1:
time: 356 us; the launch traced here: 354 us
  local copies, waits for them, and re-layouts  150 us (42%)
  waiting for transfers between devices  71.8 us (20%)
  other arithmetic  70 us (20%)
  matrix products  26.7 us (8%)
  starting transfers between devices  22.5 us (6%)
  between operations  13.3 us (4%)
    all_gather x2, waiting for transfers between devices, local(): got = lax.all_gather(pieces[k], 'pair', axis=0, tiled=True)  60.1 us
    unnamed x17, local copies, waits for them, and re-layouts  52.1 us
    convert_element_type x2, local copies, waits for them, and re-layouts, local(): weighted = (rows[..., None] * scale[:, :, :, None, :]).astype(jnp.bfloat16)  31.6 us
    convert_element_type x2, local copies, waits for them, and re-layouts, local(): cond_rows.astype(jnp.float32)[:, None]  30.8 us
    convert_element_type x2, other arithmetic, local(): density = (cond_rows.astype(jnp.float32)[:, None] * val_rows.transpose(0,...  30 us
    dot_general x2, matrix products, local(): lax.dot_general(density.reshape(n_pair * combos, part), eigenvectors, (((...  24.4 us
    ppermute x1, starting transfers between devices, local(): lax.ppermute(coeffs, 'proj', [(s, (s + k) % n_proj) for s in range(n_proj)])  17.3 us
    convert_element_type x2, other arithmetic, local(): cond_rows.astype(jnp.float32)[:, None]  14.8 us
  transfers between devices with their start and end apart: 7, of which 2 were waited for; matrix products, arithmetic and copies ran while one was open for 60% of the time, Pallas kernels for 0%

profile of v1, /device:TPU:0, one launch (start us, length us, event | category | flops | bytes accessed | tf_op | source)
XLA Modules:
  0.0 353.9 jit_solution(17777697312918749183)
XLA Ops:
  6.5 0.8 iota_compare_fusion.2
  7.4 0.8 iota_compare_fusion.1
  8.2 0.1 convert_reduce_fusion
  8.3 0.7 integer_pow.13
  9.0 0.7 subtract_multiply_fusion.1
  10.0 1.7 constant_dynamic-slice_fusion.2
  11.6 0.7 reshape.193
  12.3 1.9 constant_dynamic-slice_fusion.3
  14.2 1.6 reshape.197
  15.7 2.1 fusion.10
  17.9 3.0 collective-permute-start
  20.9 11.6 %collective-permute-done = bf16[16,15488]{1,0:T(8,128)(2,1)} collective-permute-done((bf16[16,15488]{1,0:T(8,128)(2,1)}, bf16[16,15488]{1,0:T(8,128)(2,1)}, u32[]{:S(2)}, u32[]{:S(2)}) %collective-permute-start) | collective-permute-done | bytes 495648 | tf_op jit(solution)/shard_map/ppermute | solution.py:58
  32.6 60.1 %all-gather.6.cloned.1.call-done = bf16[256,15488]{1,0:T(8,128)(2,1)} async-done(((bf16[16,15488]{1,0:T(8,128)(2,1)}), bf16[256,15488]{1,0:T(8,128)(2,1)}) %all-gather.6.cloned.1.call-update) | async-done | bytes 7929872 | tf_op jit(solution)/shard_map/all_gather | solution.py:64
  92.7 1.9 slice_convert_fusion.2
  94.7 1.8 copy.49
  96.5 3.6 %copy.50 = f32[16,4,4,3072]{3,2,1,0:T(4,128)} copy(f32[16,4,4,3072]{3,0,1,2:T(8,128)S(1)} %bitcast.61) | data formatting | bytes 6291456 | tf_op jit(solution)/shard_map/convert_element_type | solution.py:70
  100.1 6.0 %slice_convert_fusion = f32[16,16,12288]{2,1,0:T(8,128)} fusion(bf16[16,16,15488]{2,1,0:T(8,128)(2,1)S(1)} %bitcast.67), kind=kLoop, calls=%fused_computation.4 | loop fusion | flops 3145728 | bytes 18874368 | tf_op jit(solution)/shard_map/convert_element_type | solution.py:69
  106.1 15.4 %reshape.204 = f32[16,16,4,3072]{3,2,1,0:T(4,128)} reshape(f32[16,16,12288]{2,1,0:T(8,128)} %slice_convert_fusion) | data formatting | bytes 25165824 | tf_op jit(solution)/shard_map/convert_element_type | solution.py:69
  121.6 15.0 %multiply_convert_fusion = bf16[16,4,16,4,3072]{4,3,2,1,0:T(4,128)(2,1)} fusion(f32[16,4,4,3072]{3,2,1,0:T(4,128)} %copy.50, f32[16,16,4,3072]{3,2,1,0:T(4,128)} %reshape.204), kind=kLoop, calls=%fused_computation | loop fusion | flops 25165824 | bytes 40894464 | tf_op jit(solution)/shard_map/convert_element_type | solution.py:71
  136.6 25.3 %copy.60 = bf16[128,8,4,3072]{3,1,2,0:T(8,128)(2,1)} copy(bf16[128,8,4,3072]{3,2,1,0:T(4,128)(2,1)} %bitcast.57) | data formatting | bytes 50331648
  161.8 12.6 %fusion.14 = f32[1024,128]{1,0:T(8,128)} fusion(bf16[1024,12288]{1,0:T(8,128)(2,1)} %bitcast.60, bf16[12288,128]{1,0:T(8,128)(2,1)S(1)} %copy-done), kind=kOutput, calls=%fused_computation.44 | convolution fusion | flops 3221225472 | bytes 28835840 | tf_op jit(solution)/shard_map/dot_general | solution.py:72
  174.4 1.5 collective-permute-start.1
  175.9 1.8 slice_convert_fusion.3
  177.7 8.8 %slice_convert_fusion.1 = f32[16,16,12288]{2,1,0:T(8,128)} fusion(bf16[16,16,15488]{2,1,0:T(8,128)(2,1)} %bitcast.69), kind=kLoop, calls=%fused_computation.5 | loop fusion | flops 3145728 | bytes 18874368 | tf_op jit(solution)/shard_map/convert_element_type | solution.py:69
  186.5 1.8 copy.46
  188.3 3.6 %copy.47 = f32[16,4,4,3072]{3,2,1,0:T(4,128)} copy(f32[16,4,4,3072]{3,0,1,2:T(8,128)S(1)} %bitcast.62) | data formatting | bytes 6291456 | tf_op jit(solution)/shard_map/convert_element_type | solution.py:70
  191.9 15.4 %reshape.203 = f32[16,16,4,3072]{3,2,1,0:T(4,128)} reshape(f32[16,16,12288]{2,1,0:T(8,128)} %slice_convert_fusion.1) | data formatting | bytes 25165824 | tf_op jit(solution)/shard_map/convert_element_type | solution.py:69
  207.3 15.0 %multiply_convert_fusion.1 = bf16[16,4,16,4,3072]{4,3,2,1,0:T(4,128)(2,1)} fusion(f32[16,4,4,3072]{3,2,1,0:T(4,128)} %copy.47, f32[16,16,4,3072]{3,2,1,0:T(4,128)} %reshape.203), kind=kLoop, calls=%fused_computation.1 | loop fusion | flops 25165824 | bytes 40894464 | tf_op jit(solution)/shard_map/convert_element_type | solution.py:71
  222.3 25.2 %copy.59 = bf16[128,8,4,3072]{3,1,2,0:T(8,128)(2,1)} copy(bf16[128,8,4,3072]{3,2,1,0:T(4,128)(2,1)} %bitcast.58) | data formatting | bytes 50331648
  247.5 11.8 %fusion.6 = bf16[1024,128]{1,0:T(8,128)(2,1)S(1)} fusion(f32[1024,128]{1,0:T(8,128)} %collective-permute-done.1, bf16[1024,12288]{1,0:T(8,128)(2,1)} %bitcast.59, bf16[12288,128]{1,0:T(8,128)(2,1)S(1)} %copy-done), kind=kOutput, calls=%fused_computation.18 | convolution fusion | flops 3221487616 | bytes 29097984 | tf_op jit(solution)/shard_map/dot_general | solution.py:72
  259.3 0.7 copy-done.3
  260.0 0.7 collective-permute-start.3
  260.7 0.7 copy-done.4
  261.4 0.9 slice_convert_fusion.4
  262.3 0.2 copy.55
  262.6 1.5 slice_convert_fusion.5
  264.1 1.1 copy.52
  265.3 17.3 %collective-permute-start.2 = (bf16[1024,128]{1,0:T(8,128)(2,1)}, bf16[1024,128]{1,0:T(8,128)(2,1)}, u32[]{:S(2)}, u32[]{:S(2)}) collective-permute-start(bf16[1024,128]{1,0:T(8,128)(2,1)} %copy-done.3), channel_id=1, source_target_pairs={{0,1},{1,0},{2,3},{3,2},{4,5},{5,4},{6,7},{7,6},{8,9},{9,8},{10,11... | collective-permute-start | bytes 786440 | tf_op jit(solution)/shard_map/ppermute | solution.py:99
  282.6 4.4 %copy.51 = f32[16,4,16,128]{2,1,0,3:T(4,128)} copy(bf16[16,4,16,128]{3,2,1,0:T(8,128)(2,1)} %bitcast.78) | data formatting | bytes 786432 | tf_op jit(solution)/shard_map/mul | solution.py:110
  287.0 6.8 %multiply_convert_fusion.3 = bf16[16,4,16,128,4]{2,1,0,4,3:T(4,128)(2,1)} fusion(f32[16,4,16,4]{2,1,0,3:T(4,128)S(1)} %copy.53, f32[16,4,16,128]{2,1,0,3:T(4,128)} %copy.51), kind=kLoop, calls=%fused_computation.3 | loop fusion | flops 1048576 | bytes 1589248 | tf_op jit(solution)/shard_map/convert_element_type | solution.py:110
  293.9 15.8 %convert_element_type.114 = bf16[1024,512]{0,1:T(8,128)(2,1)} reshape(bf16[16,4,16,128,4]{2,1,0,4,3:T(4,128)(2,1)} %multiply_convert_fusion.3) | data formatting | bytes 2097152 | tf_op jit(solution)/shard_map/convert_element_type | solution.py:110
  309.7 4.4 %copy.54 = f32[16,4,16,128]{2,1,0,3:T(4,128)} copy(bf16[16,4,16,128]{3,2,1,0:T(8,128)(2,1)} %bitcast.30) | data formatting | bytes 786432 | tf_op jit(solution)/shard_map/mul | solution.py:110
  314.1 6.9 %multiply_convert_fusion.2 = bf16[16,4,16,128,4]{2,1,0,4,3:T(4,128)(2,1)} fusion(f32[16,4,16,4]{2,1,0,3:T(4,128)S(1)} %copy.56, f32[16,4,16,128]{2,1,0,3:T(4,128)} %copy.54), kind=kLoop, calls=%fused_computation.2 | loop fusion | flops 1048576 | bytes 1589248 | tf_op jit(solution)/shard_map/convert_element_type | solution.py:110
  321.0 15.8 %convert_element_type.116 = bf16[1024,512]{0,1:T(8,128)(2,1)} reshape(bf16[16,4,16,128,4]{2,1,0,4,3:T(4,128)(2,1)} %multiply_convert_fusion.2) | data formatting | bytes 2097152 | tf_op jit(solution)/shard_map/convert_element_type | solution.py:110
  336.8 2.7 dynamic-slice_bitcast_fusion.1
  339.6 2.3 broadcast_multiply_fusion
  342.0 2.6 copy.57
  344.5 2.9 reshape.202
  (35 shorter events, 0.7 us)
Async XLA Ops:
  6.5 155.3 %copy-start = (bf16[12288,128]{1,0:T(8,128)(2,1)S(1)}, bf16[12288,128]{1,0:T(8,128)(2,1)}, u32[]{:S(2)}) copy-start(bf16[12288,128]{1,0:T(8,128)(2,1)} %param.14) | copy-start | bytes 9437188
  6.5 86.2 %all-gather.6.cloned.1.call-start = ((), (), s32[]{:S(2)}) async-start(), calls=%async_computation.1 | async-start | bytes 8425472 | tf_op jit(solution)/shard_map/all_gather | solution.py:64
  17.9 158.0 %all-gather.4.cloned.1.call-start = ((), (), s32[]{:S(2)}) async-start(), calls=%async_computation | async-start | bytes 8425472 | tf_op jit(solution)/shard_map/all_gather | solution.py:64
  17.9 14.6 %collective-permute-start = (bf16[16,15488]{1,0:T(8,128)(2,1)}, bf16[16,15488]{1,0:T(8,128)(2,1)}, u32[]{:S(2)}, u32[]{:S(2)}) collective-permute-start(bf16[16,15488]{1,0:T(8,128)(2,1)} %get-tuple-element.11), channel_id=1, source_target_pairs={{0,1},{1,0},{2,3},{3,2},{4,5},{5,4},{6,7},{7,6},{8,9},{9,8},{10,11... | collective-permute-start | bytes 1486856 | tf_op jit(solution)/shard_map/ppermute | solution.py:58
  32.6 304.2 %all-gather.8.cloned.1.call-start = ((), (), s32[]{:S(2)}) async-start(), calls=%async_computation.2 | async-start | bytes 4456448 | tf_op jit(solution)/shard_map/all_gather | solution.py:93
  92.7 7.4 %slice-start = ((s8[7929856]{0:T(1024)(128)(4,1)}), s8[4194304]{0:T(1024)(128)(4,1)S(1)}, s32[]{:S(2)}) async-start(s8[7929856]{0:T(1024)(128)(4,1)} %bitcast.65), calls=%async_computation.3 | async-start | bytes 8388608
  94.7 5.5 %slice-start.1 = ((s8[7929856]{0:T(1024)(128)(4,1)}), s8[3735552]{0:T(1024)(128)(4,1)S(1)}, s32[]{:S(2)}) async-start(s8[7929856]{0:T(1024)(128)(4,1)} %bitcast.65), calls=%async_computation.4 | async-start | bytes 7471104
  174.4 73.1 %collective-permute-start.1 = (f32[1024,128]{1,0:T(8,128)}, f32[1024,128]{1,0:T(8,128)}, u32[]{:S(2)}, u32[]{:S(2)}) collective-permute-start(f32[1024,128]{1,0:T(8,128)} %fusion.14), channel_id=1, source_target_pairs={{0,1},{1,0},{2,3},{3,2},{4,5},{5,4},{6,7},{7,6},{8,9},{9,8},{10,11... | collective-permute-start | bytes 1572872 | tf_op jit(solution)/shard_map/ppermute | solution.py:81
  259.3 0.7 copy-start.3
  260.0 0.7 collective-permute-start.3
  260.7 0.7 copy-start.4
  265.3 44.4 %collective-permute-start.2 = (bf16[1024,128]{1,0:T(8,128)(2,1)}, bf16[1024,128]{1,0:T(8,128)(2,1)}, u32[]{:S(2)}, u32[]{:S(2)}) collective-permute-start(bf16[1024,128]{1,0:T(8,128)(2,1)} %copy-done.3), channel_id=1, source_target_pairs={{0,1},{1,0},{2,3},{3,2},{4,5},{5,4},{6,7},{7,6},{8,9},{9,8},{10,11... | collective-permute-start | bytes 786440 | tf_op jit(solution)/shard_map/ppermute | solution.py:99
  336.8 2.7 copy-start.1
  336.8 2.8 copy-start.2
Sparse Core Ops, SparseCore 0:
  18.0 74.6 all-gather.5
  94.9 70.2 all-gather.3
  261.5 65.0 all-gather.7

commit v2 on v1

--- a/solution.py
+++ b/solution.py
@@ -1,11 +1,160 @@
+import functools
 import math
 
 import jax
 import jax.numpy as jnp
 from jax import lax
+from jax.experimental import pallas as pl
+from jax.experimental.pallas import tpu as pltpu
 from jax.sharding import PartitionSpec as P
 
 LANES = 128
+
+def project_kernel(segs, val_count, cond_count, with_running, *refs):
+    conds = refs[:segs]
+    val = refs[segs]
+    eigs = refs[segs + 1 : 2 * segs + 1]
+    rest = refs[2 * segs + 1 :]
+    running = rest[0] if with_running else None
+    out, density, total = rest[-3:]
+    blocks = val.shape[0] // cond_count
+    combos = val_count * cond_count
+
+    @pl.when(pl.program_id(0) == 0)
+    def _():
+        if with_running:
+            total[...] = running[...]
+        else:
+            total[...] = jnp.zeros_like(total)
+
+    for k in range(segs):
+
+        @pl.loop(0, blocks)
+        def _(j):
+            rows = pl.ds(pl.multiple_of(j * cond_count, cond_count), cond_count)
+            c = conds[k][rows, :].astype(jnp.float32)
+            vals = val[rows, :].astype(jnp.float32)
+            for v in range(val_count):
+                at = k * val_count + v
+                product = (c * vals[at : at + 1, :]).astype(jnp.bfloat16)
+                start = pl.multiple_of(j * combos + v * cond_count, cond_count)
+                density[pl.ds(start, cond_count), :] = product
+
+        total[...] += jnp.dot(density[...], eigs[k][...], preferred_element_type=jnp.float32)
+
+    @pl.when(pl.program_id(0) == pl.num_programs(0) - 1)
+    def _():
+        out[...] = total[...].astype(out.dtype)
+
+
+def project(packed_rows, eigenvectors, running, val_count, cond_count, out_type):
+    part, columns = eigenvectors.shape
+    segs = cond_count // val_count
+    seg = part // segs
+    rows = packed_rows.shape[0]
+    width = math.gcd(seg, 768)
+    steps = seg // width
+    out_rows = rows * val_count
+    in_specs = (
+        [pl.BlockSpec((rows, width), functools.partial(lambda k, i: (0, k * steps + i), k)) for k in range(segs)]
+        + [pl.BlockSpec((rows, width), lambda i: (0, segs * steps + i))]
+        + [pl.BlockSpec((width, columns), functools.partial(lambda k, i: (k * steps + i, 0), k)) for k in range(segs)]
+    )
+    operands = [packed_rows] * (segs + 1) + [eigenvectors] * segs
+    if running is not None:
+        in_specs.append(pl.BlockSpec((out_rows, columns), lambda i: (0, 0)))
+        operands.append(running)
+    return pl.pallas_call(
+        functools.partial(project_kernel, segs, val_count, cond_count, running is not None),
+        out_shape=jax.ShapeDtypeStruct((out_rows, columns), out_type),
+        grid=(steps,),
+        in_specs=in_specs,
+        out_specs=pl.BlockSpec((out_rows, columns), lambda i: (0, 0)),
+        scratch_shapes=[
+            pltpu.VMEM((out_rows, width), jnp.bfloat16),
+            pltpu.VMEM((out_rows, columns), jnp.float32),
+        ],
+        compiler_params=pltpu.CompilerParams(vmem_limit_bytes=40 * 1024 * 1024),
+        cost_estimate=pl.CostEstimate(
+            flops=2 * out_rows * part * columns,
+            bytes_accessed=2 * (packed_rows.size + eigenvectors.size),
+            transcendentals=0,
+        ),
+        name="project",
+    )(*operands)
+
+
+def chi_kernel(count, val_count, cond_count, n_freq, factor, order, *refs):
+    lefts = refs[:count]
+    scales = refs[count : 2 * count]
+    rights = refs[2 * count : 4 * count]
+    out, weighted = refs[4 * count :]
+    rows, columns = lefts[0].shape
+    combos = val_count * cond_count
+    stride = n_freq + 1
+
+    @pl.when(pl.program_id(0) == 0)
+    def _():
+        for k in range(count):
+
+            @pl.loop(0, rows // combos)
+            def _(j):
+                at = pl.multiple_of(j * cond_count, cond_count)
+                scale = scales[k][pl.ds(at, cond_count), :].astype(jnp.float32)
+                for v in range(val_count):
+                    start = pl.multiple_of(j * combos + v * cond_count, cond_count)
+                    coeffs = lefts[k][pl.ds(start, cond_count), :].astype(jnp.float32)
+                    number = scale[:, v * stride + n_freq : v * stride + n_freq + 1]
+                    for f in range(n_freq):
+                        factor_f = scale[:, v * stride + f : v * stride + f + 1] * number
+                        weighted[pl.ds(k * rows + start, cond_count), f * columns : (f + 1) * columns] = (
+                            coeffs * factor_f
+                        ).astype(jnp.bfloat16)
+
+    right = jnp.concatenate(
+        [jnp.concatenate([rights[2 * k][0], rights[2 * k + 1][0]], axis=1) for k in range(count)], axis=0
+    )
+    for f in range(n_freq):
+        chi = lax.dot_general(
+            weighted[:, f * columns : (f + 1) * columns],
+            right,
+            (((0,), (0,)), ((), ())),
+            preferred_element_type=jnp.float32,
+        )
+        out[:, f, :] = chi * factor
+
+
+def make_chi(lefts, scales, right, order, fold, val_count, cond_count, n_freq, factor):
+    count = len(lefts)
+    rows, columns = lefts[0].shape
+    whole = lambda shape: pl.BlockSpec(shape, lambda i, order: tuple(0 for _ in shape))
+    right_specs = []
+    for k in range(count):
+        for half in range(2):
+            right_specs.append(
+                pl.BlockSpec(
+                    (1, rows, columns),
+                    functools.partial(lambda k, half, i, order: (order[k] * fold + 2 * i + half, 0, 0), k, half),
+                )
+            )
+    return pl.pallas_call(
+        functools.partial(chi_kernel, count, val_count, cond_count, n_freq, factor),
+        out_shape=jax.ShapeDtypeStruct((columns, n_freq, fold * columns), jnp.float32),
+        grid_spec=pltpu.PrefetchScalarGridSpec(
+            num_scalar_prefetch=1,
+            grid=(fold // 2,),
+            in_specs=[whole(a.shape) for a in lefts] + [whole(a.shape) for a in scales] + right_specs,
+            out_specs=pl.BlockSpec((columns, n_freq, 2 * columns), lambda i, order: (0, 0, i)),
+            scratch_shapes=[pltpu.VMEM((count * rows, n_freq * columns), jnp.bfloat16)],
+        ),
+        compiler_params=pltpu.CompilerParams(vmem_limit_bytes=40 * 1024 * 1024),
+        cost_estimate=pl.CostEstimate(
+            flops=2 * count * rows * columns * n_freq * fold * columns,
+            bytes_accessed=2 * right.size + 4 * columns * n_freq * fold * columns,
+            transcendentals=0,
+        ),
+        name="chi",
+    )(order, *lefts, *scales, *([right] * (2 * count)))
 
 
 def local(
@@ -57,32 +206,25 @@
         pieces.append(
             lax.ppermute(to_send, "proj", [(s, (s + k) % n_proj) for s in range(n_proj)])
         )
-    eig = eigenvectors.reshape(segs, seg, columns)
     running = None
     scales = []
     for k in range(n_proj):
         got = lax.all_gather(pieces[k], "pair", axis=0, tiled=True)
-        got = got.reshape(n_pair, cond_count, part + seg + LANES)
-        cond_rows = got[:, :, :part].reshape(n_pair, cond_count, segs, seg)
-        val_rows = got[:, :, part : part + seg].reshape(n_pair, segs, val_count, seg)
-        density = (
-            cond_rows.astype(jnp.float32)[:, None]
-            * val_rows.transpose(0, 2, 1, 3).astype(jnp.float32)[:, :, None]
-        ).astype(jnp.bfloat16)
-        sums = lax.dot_general(
-            density.reshape(n_pair * combos, part),
+        last = k == n_proj - 1
+        sums = project(
+            got,
             eigenvectors,
-            (((1,), (0,)), ((), ())),
-            preferred_element_type=jnp.float32,
-        )
-        if running is not None:
-            sums = sums + running
+            running,
+            val_count,
+            cond_count,
+            jnp.bfloat16 if last else jnp.float32,
+        )
         if k < n_proj - 1:
             running = lax.ppermute(
                 sums, "proj", [(s, (s + 1) % n_proj) for s in range(n_proj)]
             )
-        scales.append(got[:, :, part + seg : part + seg + val_count * (n_freq + 1)])
-    coeffs = sums.astype(jnp.bfloat16)
+        scales.append(got[:, part + seg :])
+    coeffs = sums
 
     perm = []
     for j in range(n_pair):
@@ -91,7 +233,7 @@
             perm.append((source, (j % fold + fold * s) * n_proj + j // fold))
     share = lax.ppermute(coeffs, ("pair", "proj"), perm)
     right = lax.all_gather(share, "pair", axis=0, tiled=True)
-    right = right.reshape(n_proj, fold, n_pair * combos, columns)
+    right = right.reshape(n_pair, n_pair * combos, columns)
 
     own = [coeffs]
     for k in range(1, n_proj):
@@ -99,21 +241,23 @@
             lax.ppermute(coeffs, "proj", [(s, (s + k) % n_proj) for s in range(n_proj)])
         )
     factor = -1.0 / math.sqrt(per_dev * n_pair * n_proj)
-    total = None
-    left, rights = [], []
+    order = (x - jnp.arange(n_proj, dtype=jnp.int32)) % n_proj
+    scales = [scales[(k - 1) % n_proj] for k in range(n_proj)]
+    if columns % LANES == 0:
+        return make_chi(own, scales, right, order, fold, val_count, cond_count, n_freq, factor)
+    left = []
     for k in range(n_proj):
-        place = (x - k + n_proj) % n_proj
         rows = own[k].astype(jnp.float32).reshape(n_pair, val_count, cond_count, columns)
-        scale = scales[(k - 1) % n_proj].astype(jnp.float32)
+        scale = scales[k][:, : val_count * (n_freq + 1)].astype(jnp.float32)
         scale = scale.reshape(n_pair, cond_count, val_count, n_freq + 1).transpose(0, 2, 1, 3)
         scale = scale[..., :n_freq] * scale[..., n_freq:]
         weighted = (rows[..., None] * scale[:, :, :, None, :]).astype(jnp.bfloat16)
         left.append(weighted.reshape(n_pair * combos, columns * n_freq))
-        rights.append(lax.dynamic_index_in_dim(right, place, 0, keepdims=False))
     left = jnp.concatenate(left, axis=0)
-    rights = jnp.concatenate(rights, axis=1)
+    right = jnp.take(right.reshape(n_proj, fold, n_pair * combos, columns), order, axis=0)
+    right = right.transpose(1, 0, 2, 3).reshape(fold, n_proj * n_pair * combos, columns)
     chi = lax.dot_general(
-        left, rights, (((0,), (1,)), ((), ())), preferred_element_type=jnp.float32
+        left, right, (((0,), (1,)), ((), ())), preferred_element_type=jnp.float32
     )
     return (chi * factor).reshape(columns, n_freq, fold * columns)
 

time: 356 us -> 273 us (0.77)
  local copies, waits for them, and re-layouts: 150 us -> 13.4 us
  waiting for transfers between devices: 71.8 us -> 162 us
  other arithmetic: 70 us -> 4.29 us
  Pallas kernels: 0 us -> 55.7 us
  matrix products: 26.7 us -> 0 us
    convert_element_type x8 -> x0, local copies, waits for them, and re-layouts: 73.4 us -> none  [the longest x2 31.6 us: local(): weighted = (rows[..., None] * scale[:, :, :, None, :]).astype(jnp.bfloat16)]
    convert_element_type x8 -> x0, other arithmetic: 62.2 us -> none  [the longest x2 30 us: local(): density = (cond_rows.astype(jnp.float32)[:, None] * val_rows.transpose(0,...]
    pallas_call x0 -> x3, Pallas kernels: none -> 55.7 us  [the longest x2 44.5 us: project(): pl.pallas_call(functools.partial(project_kernel, segs, val_count, cond_co...]
    all_gather x2, waiting for transfers between devices: 60.1 us -> 106 us  [local(): got = lax.all_gather(pieces[k], 'pair', axis=0, tiled=True)]
    unnamed x17 -> x10, local copies, waits for them, and re-layouts: 52.1 us -> 9.39 us
    all_gather x1, waiting for transfers between devices: 0.01 us -> 40.6 us  [local(): right = lax.all_gather(share, 'pair', axis=0, tiled=True)]
    dot_general x3 -> x0, matrix products: 26.7 us -> none  [the longest x2 24.4 us: local(): lax.dot_general(density.reshape(n_pair * combos, part), eigenvectors, (((...]
    mul x7 -> x0, local copies, waits for them, and re-layouts: 11.5 us -> none  [the longest x2 8.79 us: local(): weighted = (rows[..., None] * scale[:, :, :, None, :]).astype(jnp.bfloat16)]
  transfers between devices with their start and end apart: 7 -> 7, of which waited for: 2 -> 5; matrix products, arithmetic and copies ran while one was open for 60% -> 1% of each run, Pallas kernels for 0% -> 8%
where the time goes in v2:
time: 273 us
  waiting for transfers between devices  162 us (59%)
  Pallas kernels  55.7 us (20%)
  starting transfers between devices  23.8 us (9%)
  local copies, waits for them, and re-layouts  13.4 us (5%)
  between operations  13.2 us (5%)
  other arithmetic  4.29 us (2%)
    all_gather x2, waiting for transfers between devices, local(): got = lax.all_gather(pieces[k], 'pair', axis=0, tiled=True)  106 us
    pallas_call x2, Pallas kernels, project(): pl.pallas_call(functools.partial(project_kernel, segs, val_count, cond_co...  44.5 us
    all_gather x1, waiting for transfers between devices, local(): right = lax.all_gather(share, 'pair', axis=0, tiled=True)  40.6 us
    ppermute x1, starting transfers between devices, local(): lax.ppermute(coeffs, 'proj', [(s, (s + k) % n_proj) for s in range(n_proj)])  18.6 us
    ppermute x1, waiting for transfers between devices, local(): lax.ppermute(to_send, 'proj', [(s, (s + k) % n_proj) for s in range(n_pro...  11.6 us
    pallas_call x1, Pallas kernels, make_chi(): pl.pallas_call(functools.partial(chi_kernel, count, val_count, cond_count...  11.2 us
    unnamed x10, local copies, waits for them, and re-layouts  9.39 us
  transfers between devices with their start and end apart: 7, of which 5 were waited for; matrix products, arithmetic and copies ran while one was open for 1% of the time, Pallas kernels for 8%

profile of v2, /device:TPU:0, one launch (start us, length us, event | category | flops | bytes accessed | tf_op | source)
XLA Modules:
  0.0 272.7 jit_solution(183599831348123077)
XLA Ops:
  6.5 0.0 copy-start
  6.5 0.0 all-gather.6.cloned.1.call-start
  6.5 0.8 iota_compare_fusion.2
  7.4 0.8 integer_pow.13
  8.2 0.7 iota_compare_fusion.1
  8.8 0.1 convert_reduce_fusion
  8.9 0.7 subtract_multiply_fusion.1
  9.7 0.1 fusion.3
  9.8 0.1 copy.13
  9.9 1.0 constant_dynamic-slice_fusion
  11.0 1.2 constant_dynamic-slice_fusion.1
  12.1 1.1 fusion.2
  13.2 0.0 all-gather.6.cloned.1.call-update
  13.2 0.0 all-gather.4.cloned.1.call-start
  13.3 3.0 %collective-permute-start = (bf16[16,15488]{1,0:T(8,128)(2,1)}, bf16[16,15488]{1,0:T(8,128)(2,1)}, u32[]{:S(2)}, u32[]{:S(2)}) collective-permute-start(bf16[16,15488]{1,0:T(8,128)(2,1)} %get-tuple-element.10), channel_id=1, source_target_pairs={{0,1},{1,0},{2,3},{3,2},{4,5},{5,4},{6,7},{7,6},{8,9},{9,8},{10,11... | collective-permute-start | bytes 1486856 | tf_op jit(solution)/shard_map/ppermute | solution.py:207
  16.3 11.6 %collective-permute-done = bf16[16,15488]{1,0:T(8,128)(2,1)} collective-permute-done((bf16[16,15488]{1,0:T(8,128)(2,1)}, bf16[16,15488]{1,0:T(8,128)(2,1)}, u32[]{:S(2)}, u32[]{:S(2)}) %collective-permute-start) | collective-permute-done | bytes 495648 | tf_op jit(solution)/shard_map/ppermute | solution.py:207
  27.9 0.0 all-gather.4.cloned.1.call-update
  27.9 0.0 all-gather.8.cloned.1.call-start
  28.0 60.1 %all-gather.6.cloned.1.call-done.refs_0_.refs_1_.refs_2_.refs_3_.refs_4_ = bf16[256,15488]{1,0:T(8,128)(2,1)} async-done(((bf16[16,15488]{1,0:T(8,128)(2,1)}), bf16[256,15488]{1,0:T(8,128)(2,1)}) %all-gather.6.cloned.1.call-update) | async-done | bytes 7929872 | tf_op jit(solution)/shard_map/all_gather | solution.py:212
  88.1 0.0 copy-done
  88.1 0.0 copy-start.1
  88.1 3.2 %copy-done.1 = bf16[256,15488]{1,0:T(8,128)(2,1)S(1)} copy-done((bf16[256,15488]{1,0:T(8,128)(2,1)S(1)}, bf16[256,15488]{1,0:T(8,128)(2,1)}, u32[]{:S(2)}) %copy-start.1) | copy-done | bytes 7929880
  91.3 22.3 %project.2 = f32[1024,128]{1,0:T(8,128)} custom-call(bf16[256,15488]{1,0:T(8,128)(2,1)S(1)} %copy-done.1, bf16[256,15488]{1,0:T(8,128)(2,1)S(1)} %copy-done.1, bf16[256,15488]{1,0:T(8,128)(2,1)S(1)} %copy-done.1, bf16[256,15488]{1,0:T(8,128)(2,1)S(1)} %copy-done.1, bf16[256,15488]{1,0:T(8,128)(2,1)S(1)} %copy-done.1, bf16[12288,128]{1,0:T(8,128)(2,1)S(1)} %copy-done, ...), custom_call_target="tpu_custom_call" | custom-call | flops 3221225472 | bytes 11075584 | tf_op jit(solution)/shard_map/project/pallas_call | solution.py:67
  113.6 1.5 collective-permute-start.1
  115.1 45.5 %all-gather.4.cloned.1.call-done.refs_0_.refs_1_.refs_2_.refs_3_.refs_4_ = bf16[256,15488]{1,0:T(8,128)(2,1)} async-done(((bf16[16,15488]{1,0:T(8,128)(2,1)}), bf16[256,15488]{1,0:T(8,128)(2,1)}) %all-gather.4.cloned.1.call-update) | async-done | bytes 7929872 | tf_op jit(solution)/shard_map/all_gather | solution.py:212
  160.6 0.0 collective-permute-done.1.refs_9_
  160.6 0.0 copy-start.2
  160.6 3.2 %copy-done.2 = bf16[256,15488]{1,0:T(8,128)(2,1)S(1)} copy-done((bf16[256,15488]{1,0:T(8,128)(2,1)S(1)}, bf16[256,15488]{1,0:T(8,128)(2,1)}, u32[]{:S(2)}) %copy-start.2) | copy-done | bytes 7929880
  163.9 22.2 %project.3.refs_0_ = bf16[1024,128]{1,0:T(8,128)(2,1)S(1)} custom-call(bf16[256,15488]{1,0:T(8,128)(2,1)S(1)} %copy-done.2, bf16[256,15488]{1,0:T(8,128)(2,1)S(1)} %copy-done.2, bf16[256,15488]{1,0:T(8,128)(2,1)S(1)} %copy-done.2, bf16[256,15488]{1,0:T(8,128)(2,1)S(1)} %copy-done.2, bf16[256,15488]{1,0:T(8,128)(2,1)S(1)} %copy-done.2, ...), custom_call_target="tpu_custom_call" | custom-call | flops 3221225472 | bytes 11075584 | tf_op jit(solution)/shard_map/project/pallas_call | solution.py:67
  186.1 0.7 collective-permute-start.3
  186.8 0.0 collective-permute-done.3
  186.8 0.0 copy-start.4
  186.8 0.7 copy-done.4
  187.5 0.0 all-gather.8.cloned.1.call-update
  187.5 18.6 %collective-permute-start.2 = (bf16[1024,128]{1,0:T(8,128)(2,1)S(1)}, bf16[1024,128]{1,0:T(8,128)(2,1)S(1)}, u32[]{:S(2)}, u32[]{:S(2)}) collective-permute-start(bf16[1024,128]{1,0:T(8,128)(2,1)S(1)} %project.3.refs_0_), channel_id=1, source_target_pairs={{0,1},{1,0},{2,3},{3,2},{4,5},{5,4},{6,7},{7,6},{8,9},{9,8},{10,11... | collective-permute-start | bytes 786440 | tf_op jit(solution)/shard_map/ppermute | solution.py:241
  206.2 0.8 slice.9.refs_3_
  207.0 0.8 slice.8.refs_2_
  207.8 4.3 %collective-permute-done.2.refs_1_ = bf16[1024,128]{1,0:T(8,128)(2,1)S(1)} collective-permute-done((bf16[1024,128]{1,0:T(8,128)(2,1)S(1)}, bf16[1024,128]{1,0:T(8,128)(2,1)S(1)}, u32[]{:S(2)}, u32[]{:S(2)}) %collective-permute-start.2) | collective-permute-done | bytes 262176 | tf_op jit(solution)/shard_map/ppermute | solution.py:241
  212.2 40.6 %all-gather.8.cloned.1.call-done = bf16[16384,128]{1,0:T(8,128)(2,1)} async-done(((bf16[1024,128]{1,0:T(8,128)(2,1)}), bf16[16384,128]{1,0:T(8,128)(2,1)}) %all-gather.8.cloned.1.call-update) | async-done | bytes 4194320 | tf_op jit(solution)/shard_map/all_gather | solution.py:235
  252.8 0.0 copy-start.3
  252.8 2.2 copy-done.3
  255.0 11.2 %chi.1 = f32[128,4,1024]{2,1,0:T(4,128)} custom-call(s32[2]{0:T(128)S(1)} %and_select_fusion.order, bf16[1024,128]{1,0:T(8,128)(2,1)S(1)} %project.3.refs_0_, bf16[1024,128]{1,0:T(8,128)(2,1)S(1)} %collective-permute-done.2.refs_1_, bf16[256,128]{1,0:T(8,128)(2,1)S(1)} %slice.8.refs_2_, bf16[256,128]{1,0:T(8,128)(2,1)S(1)} %slice.9.refs_3_, ...), custom_call_target="tpu_custom_call" | custom-call | flops 2147483648 | bytes 6291456 | tf_op jit(solution)/shard_map/chi/pallas_call | solution.py:140
  (6 shorter events, 0.1 us)
Async XLA Ops:
  6.5 81.5 %copy-start = (bf16[12288,128]{1,0:T(8,128)(2,1)S(1)}, bf16[12288,128]{1,0:T(8,128)(2,1)}, u32[]{:S(2)}) copy-start(bf16[12288,128]{1,0:T(8,128)(2,1)} %refs_8_.3) | copy-start | bytes 9437188
  6.5 81.5 %all-gather.6.cloned.1.call-start = ((), (), s32[]{:S(2)}) async-start(), calls=%async_computation.1 | async-start | bytes 8425472 | tf_op jit(solution)/shard_map/all_gather | solution.py:212
  13.2 147.4 %all-gather.4.cloned.1.call-start = ((), (), s32[]{:S(2)}) async-start(), calls=%async_computation | async-start | bytes 8425472 | tf_op jit(solution)/shard_map/all_gather | solution.py:212
  13.3 14.6 %collective-permute-start = (bf16[16,15488]{1,0:T(8,128)(2,1)}, bf16[16,15488]{1,0:T(8,128)(2,1)}, u32[]{:S(2)}, u32[]{:S(2)}) collective-permute-start(bf16[16,15488]{1,0:T(8,128)(2,1)} %get-tuple-element.10), channel_id=1, source_target_pairs={{0,1},{1,0},{2,3},{3,2},{4,5},{5,4},{6,7},{7,6},{8,9},{9,8},{10,11... | collective-permute-start | bytes 1486856 | tf_op jit(solution)/shard_map/ppermute | solution.py:207
  27.9 224.9 %all-gather.8.cloned.1.call-start = ((), (), s32[]{:S(2)}) async-start(), calls=%async_computation.2 | async-start | bytes 4456448 | tf_op jit(solution)/shard_map/all_gather | solution.py:235
  88.1 3.3 %copy-start.1 = (bf16[256,15488]{1,0:T(8,128)(2,1)S(1)}, bf16[256,15488]{1,0:T(8,128)(2,1)}, u32[]{:S(2)}) copy-start(bf16[256,15488]{1,0:T(8,128)(2,1)} %all-gather.6.cloned.1.call-done.refs_0_.refs_1_.refs_2_.refs_3_.refs_4_) | copy-start | bytes 23789572
  113.6 47.0 %collective-permute-start.1 = (f32[1024,128]{1,0:T(8,128)}, f32[1024,128]{1,0:T(8,128)}, u32[]{:S(2)}, u32[]{:S(2)}) collective-permute-start(f32[1024,128]{1,0:T(8,128)} %project.2), channel_id=1, source_target_pairs={{0,1},{1,0},{2,3},{3,2},{4,5},{5,4},{6,7},{7,6},{8,9},{9,8},{10,11... | collective-permute-start | bytes 1572872 | tf_op jit(solution)/shard_map/ppermute | solution.py:223
  160.6 3.3 %copy-start.2 = (bf16[256,15488]{1,0:T(8,128)(2,1)S(1)}, bf16[256,15488]{1,0:T(8,128)(2,1)}, u32[]{:S(2)}) copy-start(bf16[256,15488]{1,0:T(8,128)(2,1)} %all-gather.4.cloned.1.call-done.refs_0_.refs_1_.refs_2_.refs_3_.refs_4_) | copy-start | bytes 23789572
  186.1 0.7 collective-permute-start.3
  186.8 0.7 copy-start.4
  187.5 24.6 %collective-permute-start.2 = (bf16[1024,128]{1,0:T(8,128)(2,1)S(1)}, bf16[1024,128]{1,0:T(8,128)(2,1)S(1)}, u32[]{:S(2)}, u32[]{:S(2)}) collective-permute-start(bf16[1024,128]{1,0:T(8,128)(2,1)S(1)} %project.3.refs_0_), channel_id=1, source_target_pairs={{0,1},{1,0},{2,3},{3,2},{4,5},{5,4},{6,7},{7,6},{8,9},{9,8},{10,11... | collective-permute-start | bytes 786440 | tf_op jit(solution)/shard_map/ppermute | solution.py:241
  252.8 2.2 copy-start.3
Sparse Core Ops, SparseCore 0:
  13.3 74.6 all-gather.5
  90.3 70.3 all-gather.3
  187.6 65.1 all-gather.7

commit v3 on v0

v3 whole, which is shorter than its diff:
```python
import functools
import math

import jax
import jax.numpy as jnp
from jax import lax
from jax.experimental import pallas as pl
from jax.experimental.pallas import tpu as pltpu
from jax.sharding import Mesh
from jax.sharding import PartitionSpec as P

LANES = 128
AXES = ("z", "y", "c", "x")


def project_kernel(segs, val_count, cond_count, *refs):
    conds = refs[:segs]
    val = refs[segs]
    eigs = refs[segs + 1 : 2 * segs + 1]
    out, density, total = refs[2 * segs + 1 :]
    blocks = val.shape[0] // cond_count
    combos = val_count * cond_count
    groups, _, columns = out.shape

    for k in range(segs):

        @pl.loop(0, blocks)
        def _(j):
            rows = pl.ds(pl.multiple_of(j * cond_count, cond_count), cond_count)
            c = conds[k][rows, :].astype(jnp.float32)
            vals = val[rows, :].astype(jnp.float32)
            for v in range(val_count):
                at = k * val_count + v
                product = (c * vals[at : at + 1, :]).astype(jnp.bfloat16)
                start = pl.multiple_of(j * combos + v * cond_count, cond_count)
                density[pl.ds(start, cond_count), :] = product

        eig = jnp.concatenate([eigs[k][q] for q in range(groups)], axis=1)
        sums = jnp.dot(density[...], eig, preferred_element_type=jnp.float32)
        if k == 0:

            @pl.when(pl.program_id(0) == 0)
            def _():
                total[...] = sums

            @pl.when(pl.program_id(0) > 0)
            def _():
                total[...] += sums
        else:
            total[...] += sums

    @pl.when(pl.program_id(0) == pl.num_programs(0) - 1)
    def _():
        for q in range(groups):
            out[q] = total[:, q * columns : (q + 1) * columns].astype(out.dtype)


def project(unit, eigs, val_count, cond_count):
    groups, part, columns = eigs.shape
    segs = cond_count // val_count
    seg = part // segs
    rows = unit.shape[0]
    out_rows = rows * val_count
    if seg % LANES or columns % LANES:
        blocks = rows // cond_count
        cond = unit[:, :part].reshape(blocks, 1, cond_count, segs, seg)
        val = unit[:, part : part + seg].reshape(blocks, segs, val_count, seg)
        val = val.transpose(0, 2, 1, 3)[:, :, None]
        density = (cond.astype(jnp.float32) * val.astype(jnp.float32)).astype(jnp.bfloat16)
        sums = jnp.einsum(
            "pg,qgs->qps", density.reshape(out_rows, part), eigs, preferred_element_type=jnp.float32
        )
        return sums.astype(jnp.bfloat16)
    width = math.gcd(seg, 384)
    steps = seg // width
    in_specs = (
        [
            pl.BlockSpec((rows, width), functools.partial(lambda k, i: (0, k * steps + i), k))
            for k in range(segs)
        ]
        + [pl.BlockSpec((rows, width), lambda i: (0, segs * steps + i))]
        + [
            pl.BlockSpec(
                (groups, width, columns), functools.partial(lambda k, i: (0, k * steps + i, 0), k)
            )
            for k in range(segs)
        ]
    )
    return pl.pallas_call(
        functools.partial(project_kernel, segs, val_count, cond_count),
        out_shape=jax.ShapeDtypeStruct((groups, out_rows, columns), jnp.bfloat16),
        grid=(steps,),
        in_specs=in_specs,
        out_specs=pl.BlockSpec((groups, out_rows, columns), lambda i: (0, 0, 0)),
        scratch_shapes=[
            pltpu.VMEM((out_rows, width), jnp.bfloat16),
            pltpu.VMEM((out_rows, groups * columns), jnp.float32),
        ],
        compiler_params=pltpu.CompilerParams(vmem_limit_bytes=32 * 1024 * 1024),
        cost_estimate=pl.CostEstimate(
            flops=2 * out_rows * part * groups * columns,
            bytes_accessed=2 * (unit.size + eigs.size),
            transcendentals=0,
        ),
        name="project",
    )(*([unit] * (segs + 1)), *([eigs] * segs))


def chi_kernel(slots, parts, val_count, cond_count, n_freq, factor, place, *refs):
    lefts = refs[0]
    scales = refs[1 : 1 + slots]
    rights = refs[1 + slots : 1 + slots + 2 * parts]
    out, weighted = refs[1 + slots + 2 * parts :]
    rows, columns = lefts.shape[2:]
    combos = val_count * cond_count
    blocks = rows // combos
    stride = n_freq + 1

    @pl.when(pl.program_id(0) == 0)
    def _():
        for k in range(slots):
            for h in range(parts):
                base = (k * parts + h) * rows

                @pl.loop(0, blocks)
                def _(j):
                    at = pl.multiple_of((h * blocks + j) * cond_count, cond_count)
                    scale = scales[k][pl.ds(at, cond_count), :].astype(jnp.float32)
                    for v in range(val_count):
                        start = pl.multiple_of(j * combos + v * cond_count, cond_count)
                        coeffs = lefts[h, k, pl.ds(start, cond_count), :].astype(jnp.float32)
                        number = scale[:, v * stride + n_freq : v * stride + n_freq + 1]
                        for f in range(n_freq):
                            one = scale[:, v * stride + f : v * stride + f + 1] * number
                            weighted[
                                pl.ds(base + start, cond_count), f * columns : (f + 1) * columns
                            ] = (coeffs * one).astype(jnp.bfloat16)

    shift = place[pl.program_id(0)]
    pieces = []
    for k in range(slots):
        for h in range(parts):
            at = lax.bitwise_xor(shift, k)
            pieces.append(
                jnp.concatenate([rights[2 * h][0, at], rights[2 * h + 1][0, at]], axis=1)
            )
    right = jnp.concatenate(pieces, axis=0)
    for f in range(n_freq):
        chi = lax.dot_general(
            weighted[:, f * columns : (f + 1) * columns],
            right,
            (((0,), (0,)), ((), ())),
            preferred_element_type=jnp.float32,
        )
        out[:, f, :] = chi * factor


def make_chi(lefts, units, right, place, val_count, cond_count, n_freq, factor):
    parts, slots, rows, columns = lefts.shape
    members = right.shape[0]
    tiles = members // (2 * parts)
    unit_rows, unit_width = units[0].shape
    last = unit_width // LANES - 1
    right_specs = [
        pl.BlockSpec(
            (1, slots, rows, columns),
            functools.partial(lambda h, c, i, place: (h * tiles * 2 + i * 2 + c, 0, 0, 0), h, c),
        )
        for h in range(parts)
        for c in range(2)
    ]
    return pl.pallas_call(
        functools.partial(chi_kernel, slots, parts, val_count, cond_count, n_freq, factor),
        out_shape=jax.ShapeDtypeStruct((columns, n_freq, tiles * 2 * columns), jnp.float32),
        grid_spec=pltpu.PrefetchScalarGridSpec(
            num_scalar_prefetch=1,
            grid=(tiles,),
            in_specs=[pl.BlockSpec(lefts.shape, lambda i, place: (0, 0, 0, 0))]
            + [pl.BlockSpec((unit_rows, LANES), lambda i, place: (0, last))] * slots
            + right_specs,
            out_specs=pl.BlockSpec((columns, n_freq, 2 * columns), lambda i, place: (0, 0, i)),
            scratch_shapes=[pltpu.VMEM((slots * parts * rows, n_freq * columns), jnp.bfloat16)],
        ),
        compiler_params=pltpu.CompilerParams(vmem_limit_bytes=32 * 1024 * 1024),
        cost_estimate=pl.CostEstimate(
            flops=2 * slots * parts * rows * columns * n_freq * tiles * 2 * columns,
            bytes_accessed=2 * right.size + 4 * columns * n_freq * tiles * 2 * columns,
            transcendentals=0,
        ),
        name="chi",
    )(place, lefts, *units, *([right] * (2 * parts)))


def local(
    shape,
    val_orbitals,
    cond_orbitals,
    val_energy,
    cond_energy,
    val_slot,
    cond_slot,
    eigenvectors,
    frequencies,
):
    nz, ny, nc, nx = shape
    val_count, n_grid = val_orbitals.shape
    cond_count = cond_orbitals.shape[0]
    per_dev = val_slot.shape[0]
    n_freq = frequencies.shape[0]
    z = lax.axis_index("z")
    x = lax.axis_index("x")
    group = ny * nc
    n_parts = group * nx
    part = n_grid // n_parts
    segs = cond_count // val_count
    seg = part // segs
    combos = val_count * cond_count
    columns = eigenvectors.shape[1]
    zfold = nz // nx

    def along_z(array, pairs):
        return lax.ppermute(array, "z", pairs)

    gap = cond_energy[:, None] - val_energy[None, :]
    weights = (
        4.0 * gap[:, :, None] / (gap[:, :, None] ** 2 + frequencies[None, None, :] ** 2)
    ).astype(jnp.bfloat16)
    chosen = (cond_slot[:, None, None] == jnp.arange(cond_count, dtype=jnp.int32)[None, :, None]) & (
        val_slot[:, None, None] == jnp.arange(val_count, dtype=jnp.int32)[None, None, :]
    )
    counts = jnp.sum(chosen.astype(jnp.float32), axis=0).astype(jnp.bfloat16)
    extra = jnp.concatenate([weights, counts[:, :, None]], axis=2).reshape(
        cond_count, val_count * (n_freq + 1)
    )
    extra = jnp.pad(extra, ((0, 0), (0, LANES - extra.shape[1])))

    cond_parts = cond_orbitals.reshape(cond_count, nx, group, part).transpose(2, 1, 0, 3)
    val_parts = val_orbitals.reshape(val_count, nx, group, segs, seg).transpose(2, 1, 3, 0, 4)
    packed = jnp.concatenate(
        [
            cond_parts.reshape(n_parts, cond_count, part),
            val_parts.reshape(n_parts, cond_count, seg),
            jnp.broadcast_to(extra, (n_parts,) + extra.shape),
        ],
        axis=2,
    )
    unit = lax.all_to_all(packed, ("y", "c", "x"), 0, 0, tiled=True)
    unit = unit.reshape(n_parts * cond_count, part + seg + LANES)
    eigs = lax.all_to_all(
        eigenvectors.reshape(group, part, columns), ("y", "c"), 0, 0, tiled=True
    )

    if nz == 4:
        inner = (z == 1) | (z == 2)
        near = along_z(unit, [(0, 1), (1, 0), (2, 3), (3, 2)])
        middle = along_z(unit, [(1, 2), (2, 1)])
        across = along_z(near, [(1, 2), (2, 1)])
        outward = along_z(middle, [(1, 0), (2, 3)])
        far = along_z(across, [(1, 0), (2, 3)])
        units = [unit, near, jnp.where(inner, across, outward), jnp.where(inner, middle, far)]
    else:
        every = lax.all_gather(unit, "z", axis=0)
        units = [
            lax.dynamic_index_in_dim(every, lax.bitwise_xor(z, k), 0, keepdims=False)
            for k in range(nz)
        ]

    own = []
    for k in range(nz):
        sums = project(units[k], eigs, val_count, cond_count)
        sums = sums.reshape(n_parts, -1, columns)
        sums = lax.all_to_all(sums, ("y", "c", "x"), 0, 0, tiled=True)
        own.append(jnp.sum(sums.astype(jnp.float32), axis=0).astype(jnp.bfloat16))
    own = jnp.stack(own)

    lefts = lax.all_gather(own, "x", axis=0)
    perm = []
    for s in range(nz):
        for q in range(group):
            for t in range(nx):
                perm.append(
                    (
                        (s * group + q) * nx + t,
                        ((s % zfold + zfold * t) * group + q) * nx + s // zfold,
                    )
                )
    share = lax.ppermute(own, AXES, perm)
    right = lax.all_gather(share, ("z", "y", "c"), axis=0)
    source = x * zfold + jnp.arange(zfold, dtype=jnp.int32)
    place = lax.bitwise_xor(jnp.broadcast_to(z, source.shape).astype(jnp.int32), source)
    factor = -1.0 / math.sqrt(per_dev * nz * n_parts)
    if columns % LANES == 0:
        return make_chi(
            lefts, units, right, jnp.repeat(place, ny), val_count, cond_count, n_freq, factor
        )
    rows = own.shape[1]
    total = 0.0
    for k in range(nz):
        scale = units[k][:, part + seg : part + seg + val_count * (n_freq + 1)].astype(jnp.float32)
        scale = scale.reshape(n_parts, cond_count, val_count, n_freq + 1).transpose(0, 2, 1, 3)
        scale = scale.reshape(nx, rows, n_freq + 1)
        scale = scale[..., :n_freq] * scale[..., n_freq:]
        weighted = (lefts[:, k, :, :, None].astype(jnp.float32) * scale[:, :, None, :]).astype(
            jnp.bfloat16
        )
        weighted = weighted.reshape(nx * rows, columns * n_freq)
        for low in range(zfold):
            at = lax.bitwise_xor(place[low], k)
            piece = lax.dynamic_index_in_dim(right, at, 1, keepdims=False)
            piece = piece.reshape(nx, zfold, group, rows, columns)[:, low]
            piece = piece.transpose(0, 2, 1, 3).reshape(nx * rows, group * columns)
            chi = lax.dot_general(
                weighted, piece, (((0,), (0,)), ((), ())), preferred_element_type=jnp.float32
            )
            chi = jnp.pad(chi, ((0, 0), (low * group * columns, (zfold - 1 - low) * group * columns)))
            total = total + chi
    return (total * factor).reshape(columns, n_freq, zfold * group * columns)


def solution(mesh):
    n_pair = mesh.shape["pair"]
    n_proj = mesh.shape["proj"]
    shape = (n_pair // 4, 2, 2, n_proj)
    grid = Mesh(mesh.devices.reshape(shape), AXES)
    return jax.shard_map(
        functools.partial(local, shape),
        mesh=grid,
        in_specs=(
            P(AXES, None),
            P(AXES, None),
            P(AXES),
            P(AXES),
            P(AXES),
            P(AXES),
            P("x", ("z", "y", "c")),
            P(),
        ),
        out_specs=P(("z", "y", "c"), None, "x"),
        check_vma=False,
    )
```

time: 675 us -> 232 us (0.34)
  waiting for transfers between devices: 583 us -> 87.5 us
  matrix products: 35 us -> 0 us
  Pallas kernels: 0 us -> 32.3 us
  starting transfers between devices: 5.36 us -> 29.1 us
  blocking collectives: 30.4 us -> 43.2 us
  other arithmetic: 2.59 us -> 11.8 us
  local copies, waits for them, and re-layouts: 5.21 us -> 13.3 us
    reduce_scatter x1 -> x0, waiting for transfers between devices: 331 us -> none  [local(): lax.psum_scatter(lax.dot_general(coeffs, weighted, (((0,), (0,)), ((), ()...]
    all_gather x1, waiting for transfers between devices: 214 us -> 41.8 us  [local(): right = lax.all_gather(share, ('z', 'y', 'c'), axis=0)]
    dot_general x4 -> x0, matrix products: 35 us -> none  [the longest x1 19.8 us: local(): jnp.dot(rows_mine, lax.all_gather(eigenvectors, 'pair', axis=1, tiled=Tru...]
    pallas_call x0 -> x5, Pallas kernels: none -> 32.3 us  [the longest x4 20.3 us: project(): pl.pallas_call(functools.partial(project_kernel, segs, val_count, cond_co...]
    psum x1 -> x0, blocking collectives: 30.4 us -> none  [local(): summed, weight_sum = lax.psum((part_sums, padded), 'proj')]
    ppermute x0 -> x6, waiting for transfers between devices: none -> 28.2 us  [the longest x5 28.2 us: along_z(): return lax.ppermute(array, 'z', pairs)]
    all_gather x0 -> x1, blocking collectives: none -> 23.6 us  [local(): lefts = lax.all_gather(own, 'x', axis=0)]
    all_to_all x1 -> x5, waiting for transfers between devices: 37.2 us -> 17.4 us  [the longest x1 8.82 us: local(): lax.all_to_all(eigenvectors.reshape(group, part, columns), ('y', 'c'), 0,...]
  transfers between devices with their start and end apart: 3 -> 12, of which waited for: 3 -> 7; matrix products, arithmetic and copies ran while one was open for 1% -> 3% of each run, Pallas kernels for 0% -> 9%
where the time goes in v3:
time: 232 us; the launch traced here: 231 us
  waiting for transfers between devices  87.5 us (38%)
  blocking collectives  43.2 us (19%)
  Pallas kernels  32.3 us (14%)
  starting transfers between devices  29.1 us (13%)
  between operations  13.7 us (6%)
  local copies, waits for them, and re-layouts  13.3 us (6%)
  other arithmetic  11.8 us (5%)
    all_gather x1, waiting for transfers between devices, local(): right = lax.all_gather(share, ('z', 'y', 'c'), axis=0)  41.8 us
    ppermute x5, waiting for transfers between devices, along_z(): return lax.ppermute(array, 'z', pairs)  28.2 us
    all_gather x1, blocking collectives, local(): lefts = lax.all_gather(own, 'x', axis=0)  23.6 us
    pallas_call x4, Pallas kernels, project(): pl.pallas_call(functools.partial(project_kernel, segs, val_count, cond_co...  20.3 us
    all_to_all x1, blocking collectives, local(): unit = lax.all_to_all(packed, ('y', 'c', 'x'), 0, 0, tiled=True)  19.6 us
    all_to_all x4, starting transfers between devices, local(): sums = lax.all_to_all(sums, ('y', 'c', 'x'), 0, 0, tiled=True)  16.6 us
    pallas_call x1, Pallas kernels, make_chi(): pl.pallas_call(functools.partial(chi_kernel, slots, parts, val_count, con...  12 us
    unnamed x25, local copies, waits for them, and re-layouts  9.64 us
  transfers between devices with their start and end apart: 12, of which 7 were waited for; matrix products, arithmetic and copies ran while one was open for 3% of the time, Pallas kernels for 9%

profile of v3, /device:TPU:0, one launch (start us, length us, event | category | flops | bytes accessed | tf_op | source)
XLA Modules:
  0.0 230.9 jit_solution(14741525754700175220)
XLA Ops:
  6.5 0.7 iota_compare_fusion.1
  7.2 0.7 integer_pow.13
  7.9 0.7 iota_compare_fusion
  8.7 0.7 subtract_multiply_fusion.1
  9.7 1.1 reshape.148
  11.0 1.7 reshape.146
  12.7 0.4 copy.20
  13.2 19.6 %all_to_all.30 = bf16[8,16,3968]{2,1,0:T(8,128)(2,1)} all-to-all(bf16[8,16,3968]{2,1,0:T(8,128)(2,1)S(1)} %pad_maximum_fusion), channel_id=1, replica_groups=mesh['z'=4,'y'=2,'c'=2,'x'=2] {'y','c','x'}, dimensions={0} | all-to-all | bytes 2031616 | tf_op jit(solution)/shard_map/all_to_all | solution.py:247
  32.8 3.7 %all-to-all-start.1 = ((bf16[4,3072,128]{2,1,0:T(8,128)(2,1)}), bf16[4,3072,128]{2,1,0:T(8,128)(2,1)S(1)}, u32[]{:S(2)}, u32[]{:S(2)}) async-start(bf16[4,3072,128]{2,1,0:T(8,128)(2,1)} %bitcast.37), calls=%async_computation.1 | async-start | bytes 6291456 | tf_op jit(solution)/shard_map/all_to_all | solution.py:249
  36.6 1.6 collective-permute-start
  38.2 1.6 collective-permute-start.2
  39.8 21.9 %collective-permute-done.refs_0_.refs_1_.refs_2_.refs_3_.refs_4_ = bf16[128,3968]{1,0:T(8,128)(2,1)} collective-permute-done((bf16[128,3968]{1,0:T(8,128)(2,1)}, bf16[128,3968]{1,0:T(8,128)(2,1)}, u32[]{:S(2)}, u32[]{:S(2)}) %collective-permute-start) | collective-permute-done | bytes 1015840 | tf_op jit(solution)/shard_map/ppermute | solution.py:222
  61.7 1.6 collective-permute-start.1
  63.3 1.3 collective-permute-start.3
  64.6 8.8 %all-to-all-done.1.refs_5_.refs_6_.refs_7_.refs_8_ = bf16[4,3072,128]{2,1,0:T(8,128)(2,1)S(1)} async-done(((bf16[4,3072,128]{2,1,0:T(8,128)(2,1)}), bf16[4,3072,128]{2,1,0:T(8,128)(2,1)S(1)}, u32[]{:S(2)}, u32[]{:S(2)}) %all-to-all-start.1) | async-done | bytes 3145760 | tf_op jit(solution)/shard_map/all_to_all | solution.py:249
  73.5 1.2 copy-done.1
  74.7 4.9 %project.4 = bf16[4,512,128]{2,1,0:T(8,128)(2,1)S(1)} custom-call(bf16[128,3968]{1,0:T(8,128)(2,1)S(1)} %bitcast.26, bf16[128,3968]{1,0:T(8,128)(2,1)S(1)} %bitcast.27, bf16[128,3968]{1,0:T(8,128)(2,1)S(1)} %bitcast.28, bf16[128,3968]{1,0:T(8,128)(2,1)S(1)} %bitcast.29, bf16[128,3968]{1,0:T(8,128)(2,1)S(1)} %bitcast.30, ...), custom_call_target="tpu_custom_call" | custom-call | flops 1610612736 | bytes 4161536 | tf_op jit(solution)/shard_map/project/pallas_call | solution.py:89
  79.6 0.8 copy-done.7
  80.4 4.1 %all-to-all-start.2 = ((bf16[8,256,128]{2,1,0:T(8,128)(2,1)}), bf16[8,256,128]{2,1,0:T(8,128)(2,1)}, u32[]{:S(2)}, u32[]{:S(2)}) async-start(bf16[8,256,128]{2,1,0:T(8,128)(2,1)} %bitcast.32), calls=%async_computation.2 | async-start | bytes 1048576 | tf_op jit(solution)/shard_map/all_to_all | solution.py:272
  84.6 5.4 %project.5 = bf16[4,512,128]{2,1,0:T(8,128)(2,1)S(1)} custom-call(bf16[128,3968]{1,0:T(8,128)(2,1)} %collective-permute-done.refs_0_.refs_1_.refs_2_.refs_3_.refs_4_, bf16[128,3968]{1,0:T(8,128)(2,1)} %collective-permute-done.refs_0_.refs_1_.refs_2_.refs_3_.refs_4_, bf16[128,3968]{1,0:T(8,128)(2,1)} %collective-permute-done.refs_0_.refs_1_.refs_2_.refs_3_.refs_4_, ...), custom_call_target="tpu_custom_call" | custom-call | flops 1610612736 | bytes 4161536 | tf_op jit(solution)/shard_map/project/pallas_call | solution.py:89
  90.0 0.8 copy-done.8
  90.8 1.3 collective-permute-start.4
  92.1 1.7 all-to-all-done.2
  93.8 4.1 %all-to-all-start.3 = ((bf16[8,256,128]{2,1,0:T(8,128)(2,1)}), bf16[8,256,128]{2,1,0:T(8,128)(2,1)}, u32[]{:S(2)}, u32[]{:S(2)}) async-start(bf16[8,256,128]{2,1,0:T(8,128)(2,1)} %bitcast.33), calls=%async_computation.3 | async-start | bytes 1048576 | tf_op jit(solution)/shard_map/all_to_all | solution.py:272
  98.0 1.3 broadcast_select_fusion.1.refs_0_.refs_1_.refs_2_.refs_3_.refs_4_
  99.3 5.0 %project.6 = bf16[4,512,128]{2,1,0:T(8,128)(2,1)S(1)} custom-call(bf16[128,3968]{1,0:T(8,128)(2,1)S(1)} %broadcast_select_fusion.1.refs_0_.refs_1_.refs_2_.refs_3_.refs_4_, bf16[128,3968]{1,0:T(8,128)(2,1)S(1)} %broadcast_select_fusion.1.refs_0_.refs_1_.refs_2_.refs_3_.refs_4_, ...), custom_call_target="tpu_custom_call" | custom-call | flops 1610612736 | bytes 4161536 | tf_op jit(solution)/shard_map/project/pallas_call | solution.py:89
  104.3 0.9 copy-done.3
  105.3 0.8 copy-done.9
  106.1 1.2 all-to-all-done.3
  107.2 4.1 %all-to-all-start.4 = ((bf16[8,256,128]{2,1,0:T(8,128)(2,1)}), bf16[8,256,128]{2,1,0:T(8,128)(2,1)}, u32[]{:S(2)}, u32[]{:S(2)}) async-start(bf16[8,256,128]{2,1,0:T(8,128)(2,1)} %bitcast.34), calls=%async_computation.4 | async-start | bytes 1048576 | tf_op jit(solution)/shard_map/all_to_all | solution.py:272
  111.4 6.3 %collective-permute-done.4 = bf16[128,3968]{1,0:T(8,128)(2,1)} collective-permute-done((bf16[128,3968]{1,0:T(8,128)(2,1)}, bf16[128,3968]{1,0:T(8,128)(2,1)}, u32[]{:S(2)}, u32[]{:S(2)}) %collective-permute-start.4) | collective-permute-done | bytes 1015840 | tf_op jit(solution)/shard_map/ppermute | solution.py:222
  117.7 1.3 broadcast_select_fusion.refs_0_.refs_1_.refs_2_.refs_3_.refs_4_
  119.0 5.0 %project.7 = bf16[4,512,128]{2,1,0:T(8,128)(2,1)S(1)} custom-call(bf16[128,3968]{1,0:T(8,128)(2,1)S(1)} %broadcast_select_fusion.refs_0_.refs_1_.refs_2_.refs_3_.refs_4_, bf16[128,3968]{1,0:T(8,128)(2,1)S(1)} %broadcast_select_fusion.refs_0_.refs_1_.refs_2_.refs_3_.refs_4_, ...), custom_call_target="tpu_custom_call" | custom-call | flops 1610612736 | bytes 4161536 | tf_op jit(solution)/shard_map/project/pallas_call | solution.py:89
  124.0 1.0 copy-done.5
  125.0 0.8 copy-done.10
  125.8 4.1 %all-to-all-start.5 = ((bf16[8,256,128]{2,1,0:T(8,128)(2,1)}), bf16[8,256,128]{2,1,0:T(8,128)(2,1)}, u32[]{:S(2)}, u32[]{:S(2)}) async-start(bf16[8,256,128]{2,1,0:T(8,128)(2,1)} %bitcast.35), calls=%async_computation.5 | async-start | bytes 1048576 | tf_op jit(solution)/shard_map/all_to_all | solution.py:272
  130.0 1.3 reduce_sum.58
  131.3 1.1 reduce_sum.59
  132.4 1.1 reduce_sum.60
  133.5 5.7 %all-to-all-done.5 = bf16[8,256,128]{2,1,0:T(8,128)(2,1)} async-done(((bf16[8,256,128]{2,1,0:T(8,128)(2,1)}), bf16[8,256,128]{2,1,0:T(8,128)(2,1)}, u32[]{:S(2)}, u32[]{:S(2)}) %all-to-all-start.5) | async-done | bytes 524320 | tf_op jit(solution)/shard_map/all_to_all | solution.py:272
  139.2 1.7 reduce_sum.61
  140.9 0.9 pad_maximum_fusion.1
  141.8 1.4 collective-permute-start.5
  143.4 23.6 %all-gather = bf16[8,256,128]{2,1,0:T(8,128)(2,1)} all-gather(bf16[4,256,128]{2,1,0:T(8,128)(2,1)S(1)} %pad_maximum_fusion.1), channel_id=2, replica_groups=mesh['z'=4,'y'=2,'c'=2,'x'=2] {'x'}, dimensions={0}, use_global_device_ids=true | all-gather | bytes 786432 | tf_op jit(solution)/shard_map/all_gather | solution.py:276
  167.0 41.8 %all-gather.4.cloned.1.call-done = bf16[64,256,128]{2,1,0:T(8,128)(2,1)} async-done(((bf16[4,256,128]{2,1,0:T(8,128)(2,1)}), bf16[64,256,128]{2,1,0:T(8,128)(2,1)}) %all-gather.4.cloned.1.call-update) | async-done | bytes 4194320 | tf_op jit(solution)/shard_map/all_gather | solution.py:288
  208.8 2.2 copy-done
  211.0 1.0 copy-done.11
  212.1 12.0 %chi.1 = f32[128,4,1024]{2,1,0:T(4,128)} custom-call(s32[4]{0:T(128)S(1)} %reshape.145.place, bf16[2,4,256,128]{3,2,1,0:T(8,128)(2,1)S(1)} %bitcast.36, bf16[128,3968]{1,0:T(8,128)(2,1)S(1)} %bitcast.31, bf16[128,3968]{1,0:T(8,128)(2,1)} %collective-permute-done.refs_0_.refs_1_.refs_2_.refs_3_.refs_4_, bf16[128,3968]{1,0:T(8,128)(2,1)S(1)} %copy-done.4, ...), custom_call_target="tpu_custom_call" | custom-call | flops 2147483648 | bytes 6291456 | tf_op jit(solution)/shard_map/chi/pallas_call | solution.py:172
  (36 shorter events, 0.9 us)
Async XLA Ops:
  32.8 40.6 %all-to-all-start.1 = ((bf16[4,3072,128]{2,1,0:T(8,128)(2,1)}), bf16[4,3072,128]{2,1,0:T(8,128)(2,1)S(1)}, u32[]{:S(2)}, u32[]{:S(2)}) async-start(bf16[4,3072,128]{2,1,0:T(8,128)(2,1)} %bitcast.37), calls=%async_computation.1 | async-start | bytes 6291456 | tf_op jit(solution)/shard_map/all_to_all | solution.py:249
  36.6 25.2 %collective-permute-start = (bf16[128,3968]{1,0:T(8,128)(2,1)}, bf16[128,3968]{1,0:T(8,128)(2,1)}, u32[]{:S(2)}, u32[]{:S(2)}) collective-permute-start(bf16[128,3968]{1,0:T(8,128)(2,1)} %bitcast.24), channel_id=1, source_target_pairs={{0,8},{8,0},{16,24},{24,16},{1,9},{9,1},{17,25},{25,17},{2,10},{10... | collective-permute-start | bytes 3047432 | tf_op jit(solution)/shard_map/ppermute | solution.py:222
  38.2 25.1 %collective-permute-start.2 = (bf16[128,3968]{1,0:T(8,128)(2,1)}, bf16[128,3968]{1,0:T(8,128)(2,1)}, u32[]{:S(2)}, u32[]{:S(2)}) collective-permute-start(bf16[128,3968]{1,0:T(8,128)(2,1)} %bitcast.25), channel_id=1, source_target_pairs={{8,16},{16,8},{9,17},{17,9},{10,18},{18,10},{11,19},{19,11},{12,20... | collective-permute-start | bytes 3047432 | tf_op jit(solution)/shard_map/ppermute | solution.py:222
  61.7 29.1 %collective-permute-start.1 = (bf16[128,3968]{1,0:T(8,128)(2,1)}, bf16[128,3968]{1,0:T(8,128)(2,1)}, u32[]{:S(2)}, u32[]{:S(2)}) collective-permute-start(bf16[128,3968]{1,0:T(8,128)(2,1)} %collective-permute-done.refs_0_.refs_1_.refs_2_.refs_3_.refs_4_), channel_id=1, source_target_pairs={{8,16},{16,8},{9,17},{17,9},{10,18},{18,10},{11,19},{19,11},{12,20... | collective-permute-start | bytes 3047432 | tf_op jit(solution)/shard_map/ppermute | solution.py:222
  63.3 34.6 %collective-permute-start.3 = (bf16[128,3968]{1,0:T(8,128)(2,1)}, bf16[128,3968]{1,0:T(8,128)(2,1)}, u32[]{:S(2)}, u32[]{:S(2)}) collective-permute-start(bf16[128,3968]{1,0:T(8,128)(2,1)} %collective-permute-done.2), channel_id=1, source_target_pairs={{8,0},{16,24},{9,1},{17,25},{10,2},{18,26},{11,3},{19,27},{12,4},{... | collective-permute-start | bytes 3047432 | tf_op jit(solution)/shard_map/ppermute | solution.py:222
  73.5 1.2 copy-start.1
  79.6 0.8 copy-start.7
  80.4 13.4 %all-to-all-start.2 = ((bf16[8,256,128]{2,1,0:T(8,128)(2,1)}), bf16[8,256,128]{2,1,0:T(8,128)(2,1)}, u32[]{:S(2)}, u32[]{:S(2)}) async-start(bf16[8,256,128]{2,1,0:T(8,128)(2,1)} %bitcast.32), calls=%async_computation.2 | async-start | bytes 1048576 | tf_op jit(solution)/shard_map/all_to_all | solution.py:272
  90.0 0.8 copy-start.8
  90.8 26.9 %collective-permute-start.4 = (bf16[128,3968]{1,0:T(8,128)(2,1)}, bf16[128,3968]{1,0:T(8,128)(2,1)}, u32[]{:S(2)}, u32[]{:S(2)}) collective-permute-start(bf16[128,3968]{1,0:T(8,128)(2,1)} %collective-permute-done.1), channel_id=1, source_target_pairs={{8,0},{16,24},{9,1},{17,25},{10,2},{18,26},{11,3},{19,27},{12,4},{... | collective-permute-start | bytes 3047432 | tf_op jit(solution)/shard_map/ppermute | solution.py:222
  93.8 13.4 %all-to-all-start.3 = ((bf16[8,256,128]{2,1,0:T(8,128)(2,1)}), bf16[8,256,128]{2,1,0:T(8,128)(2,1)}, u32[]{:S(2)}, u32[]{:S(2)}) async-start(bf16[8,256,128]{2,1,0:T(8,128)(2,1)} %bitcast.33), calls=%async_computation.3 | async-start | bytes 1048576 | tf_op jit(solution)/shard_map/all_to_all | solution.py:272
  104.3 1.0 copy-start.3
  105.3 0.8 copy-start.9
  107.2 18.5 %all-to-all-start.4 = ((bf16[8,256,128]{2,1,0:T(8,128)(2,1)}), bf16[8,256,128]{2,1,0:T(8,128)(2,1)}, u32[]{:S(2)}, u32[]{:S(2)}) async-start(bf16[8,256,128]{2,1,0:T(8,128)(2,1)} %bitcast.34), calls=%async_computation.4 | async-start | bytes 1048576 | tf_op jit(solution)/shard_map/all_to_all | solution.py:272
  124.0 1.0 copy-start.5
  125.0 0.8 copy-start.10
  125.8 13.4 %all-to-all-start.5 = ((bf16[8,256,128]{2,1,0:T(8,128)(2,1)}), bf16[8,256,128]{2,1,0:T(8,128)(2,1)}, u32[]{:S(2)}, u32[]{:S(2)}) async-start(bf16[8,256,128]{2,1,0:T(8,128)(2,1)} %bitcast.35), calls=%async_computation.5 | async-start | bytes 1048576 | tf_op jit(solution)/shard_map/all_to_all | solution.py:272
  129.9 78.9 %copy-start.2 = (bf16[8,16,3968]{2,1,0:T(8,128)(2,1)S(1)}, bf16[8,16,3968]{2,1,0:T(8,128)(2,1)}, u32[]{:S(2)}) copy-start(bf16[8,16,3968]{2,1,0:T(8,128)(2,1)} %all_to_all.30) | copy-start | bytes 3047428
  129.9 78.9 %copy-start.4 = (bf16[128,3968]{1,0:T(8,128)(2,1)S(1)}, bf16[128,3968]{1,0:T(8,128)(2,1)}, u32[]{:S(2)}) copy-start(bf16[128,3968]{1,0:T(8,128)(2,1)} %copy-done.3) | copy-start | bytes 3047428
  129.9 78.9 %copy-start.6 = (bf16[128,3968]{1,0:T(8,128)(2,1)S(1)}, bf16[128,3968]{1,0:T(8,128)(2,1)}, u32[]{:S(2)}) copy-start(bf16[128,3968]{1,0:T(8,128)(2,1)} %copy-done.5) | copy-start | bytes 3047428
  130.0 78.9 %all-gather.4.cloned.1.call-start = ((), (), s32[]{:S(2)}) async-start(), calls=%async_computation.6 | async-start | bytes 4456448 | tf_op jit(solution)/shard_map/all_gather | solution.py:288
  141.8 1.4 collective-permute-start.5
  208.8 2.2 copy-start
  211.0 1.0 copy-start.11
Sparse Core Ops, SparseCore 0:
  143.3 65.4 all-gather.3

commit v4 on v3

v4 whole, which is shorter than its diff:
```python
import functools
import math

import jax
import jax.numpy as jnp
from jax import lax
from jax.experimental import pallas as pl
from jax.experimental.pallas import tpu as pltpu
from jax.sharding import Mesh
from jax.sharding import PartitionSpec as P

LANES = 128
AXES = ("z", "y", "c", "x")


def project_kernel(segs, val_count, cond_count, *refs):
    conds = refs[:segs]
    val = refs[segs]
    eigs = refs[segs + 1 : 2 * segs + 1]
    out, density, total = refs[2 * segs + 1 :]
    blocks = val.shape[0] // cond_count
    groups, _, columns = out.shape

    for k in range(segs):

        @pl.loop(0, blocks)
        def _(j):
            rows = pl.ds(pl.multiple_of(j * cond_count, cond_count), cond_count)
            c = conds[k][rows, :].astype(jnp.float32)
            vals = val[rows, :].astype(jnp.float32)
            for v in range(val_count):
                at = k * val_count + v
                product = (c * vals[at : at + 1, :]).astype(jnp.bfloat16)
                start = pl.multiple_of(v * val.shape[0] + j * cond_count, cond_count)
                density[pl.ds(start, cond_count), :] = product

        eig = jnp.concatenate([eigs[k][q] for q in range(groups)], axis=1)
        sums = jnp.dot(density[...], eig, preferred_element_type=jnp.float32)
        if k == 0:

            @pl.when(pl.program_id(0) == 0)
            def _():
                total[...] = sums

            @pl.when(pl.program_id(0) > 0)
            def _():
                total[...] += sums
        else:
            total[...] += sums

    @pl.when(pl.program_id(0) == pl.num_programs(0) - 1)
    def _():
        for q in range(groups):
            out[q] = total[:, q * columns : (q + 1) * columns].astype(out.dtype)


def project(unit, eigs, val_count, cond_count, out_type):
    groups, part, columns = eigs.shape
    segs = cond_count // val_count
    seg = part // segs
    rows = unit.shape[0]
    out_rows = rows * val_count
    if seg % LANES or columns % LANES:
        blocks = rows // cond_count
        cond = unit[:, :part].reshape(1, blocks, cond_count, segs, seg)
        val = unit[:, part:].reshape(blocks, segs, val_count, seg)
        val = val.transpose(2, 0, 1, 3)[:, :, None]
        density = (cond.astype(jnp.float32) * val.astype(jnp.float32)).astype(jnp.bfloat16)
        sums = jnp.einsum(
            "pg,qgs->qps", density.reshape(out_rows, part), eigs, preferred_element_type=jnp.float32
        )
        return sums.astype(out_type)
    width = math.gcd(seg, 384)
    steps = seg // width
    in_specs = (
        [
            pl.BlockSpec((rows, width), functools.partial(lambda k, i: (0, k * steps + i), k))
            for k in range(segs)
        ]
        + [pl.BlockSpec((rows, width), lambda i: (0, segs * steps + i))]
        + [
            pl.BlockSpec(
                (groups, width, columns), functools.partial(lambda k, i: (0, k * steps + i, 0), k)
            )
            for k in range(segs)
        ]
    )
    return pl.pallas_call(
        functools.partial(project_kernel, segs, val_count, cond_count),
        out_shape=jax.ShapeDtypeStruct((groups, out_rows, columns), out_type),
        grid=(steps,),
        in_specs=in_specs,
        out_specs=pl.BlockSpec((groups, out_rows, columns), lambda i: (0, 0, 0)),
        scratch_shapes=[
            pltpu.VMEM((out_rows, width), jnp.bfloat16),
            pltpu.VMEM((out_rows, groups * columns), jnp.float32),
        ],
        compiler_params=pltpu.CompilerParams(vmem_limit_bytes=32 * 1024 * 1024),
        cost_estimate=pl.CostEstimate(
            flops=2 * out_rows * part * groups * columns,
            bytes_accessed=2 * (unit.size + eigs.size),
            transcendentals=0,
        ),
        name="project",
    )(*([unit] * (segs + 1)), *([eigs] * segs))


def weigh_kernel(early, late, n_freq, scalars, *refs):
    own_a, mate_a, own_b, mate_b = refs[:4]
    scales = refs[4 : 4 + early + late]
    out = refs[-1]
    rows, columns = own_b.shape[1:]
    stride = n_freq + 1
    width = scales[0].shape[0]
    mine = scalars[0]
    for k in range(early + late):
        scale = scales[k][...].astype(jnp.float32).T
        own = (own_a[k] if k < early else own_b[k - early]).astype(jnp.float32).T
        mate = (mate_a[k] if k < early else mate_b[k - early]).astype(jnp.float32).T
        for h in range(2):
            coeffs = jnp.where(mine == h, own, mate)
            for at in range(0, rows, width):
                v = (h * rows + at) // width
                number = scale[v * stride + n_freq : v * stride + n_freq + 1, :]
                for f in range(n_freq):
                    one = scale[v * stride + f : v * stride + f + 1, :] * number
                    out[k, f * columns : (f + 1) * columns, h * rows + at : h * rows + at + width] = (
                        coeffs[:, at : at + width] * one
                    ).astype(jnp.bfloat16)


def weigh(own_a, mate_a, own_b, mate_b, scales, scalars, n_freq):
    early, rows, columns = own_a.shape
    late = own_b.shape[0]
    width = scales.shape[1]
    whole = lambda shape: pl.BlockSpec(shape, lambda i, scalars: tuple(0 for _ in shape))
    shape = (early + late, n_freq * columns, 2 * rows)
    return pl.pallas_call(
        functools.partial(weigh_kernel, early, late, n_freq),
        out_shape=jax.ShapeDtypeStruct(shape, jnp.bfloat16),
        grid_spec=pltpu.PrefetchScalarGridSpec(
            num_scalar_prefetch=1,
            grid=(1,),
            in_specs=[whole(a.shape) for a in (own_a, mate_a, own_b, mate_b)]
            + [
                pl.BlockSpec(
                    (None, width, LANES),
                    functools.partial(lambda k, i, scalars: (scalars[1 + k], 0, 0), k),
                )
                for k in range(early + late)
            ],
            out_specs=whole(shape),
        ),
        compiler_params=pltpu.CompilerParams(vmem_limit_bytes=24 * 1024 * 1024),
        cost_estimate=pl.CostEstimate(
            flops=2 * math.prod(shape), bytes_accessed=3 * math.prod(shape), transcendentals=0
        ),
        name="weigh",
    )(scalars, own_a, mate_a, own_b, mate_b, *([scales] * (early + late)))


def chi_kernel(early, late, n_freq, factor, place, *refs):
    weighted = refs[0]
    rights_a = refs[1:5]
    rights_b = refs[5:9]
    out = refs[9]
    columns = out.shape[0]
    shift = place[pl.program_id(0)]
    left, right = [], []
    for r in range(early + late):
        left.append(weighted[lax.bitwise_xor(shift, r)])
        for h in range(2):
            pair = [
                rights_a[2 * h + c][0, r] if r < early else rights_b[2 * h + c][0, r - early] for c in range(2)
            ]
            right.append(jnp.concatenate(pair, axis=1))
    chi = jnp.dot(
        jnp.concatenate(left, axis=1),
        jnp.concatenate(right, axis=0),
        preferred_element_type=jnp.float32,
    )
    for f in range(n_freq):
        out[:, f, :] = chi[f * columns : (f + 1) * columns, :] * factor


def make_chi(weighted, right_a, right_b, place, n_freq, factor):
    members, early, rows, columns = right_a.shape
    tiles = members // 4
    late = right_b.shape[1]

    def right_specs(slots):
        return [
            pl.BlockSpec(
                (1, slots, rows, columns),
                functools.partial(lambda h, c, i, place: (h * tiles * 2 + i * 2 + c, 0, 0, 0), h, c),
            )
            for h in range(2)
            for c in range(2)
        ]

    return pl.pallas_call(
        functools.partial(chi_kernel, early, late, n_freq, factor),
        out_shape=jax.ShapeDtypeStruct((columns, n_freq, tiles * 2 * columns), jnp.float32),
        grid_spec=pltpu.PrefetchScalarGridSpec(
            num_scalar_prefetch=1,
            grid=(tiles,),
            in_specs=[pl.BlockSpec(weighted.shape, lambda i, place: (0, 0, 0))]
            + right_specs(early)
            + right_specs(late),
            out_specs=pl.BlockSpec((columns, n_freq, 2 * columns), lambda i, place: (0, 0, i)),
        ),
        compiler_params=pltpu.CompilerParams(vmem_limit_bytes=32 * 1024 * 1024),
        cost_estimate=pl.CostEstimate(
            flops=2 * weighted.size * tiles * 2 * columns,
            bytes_accessed=2 * (right_a.size + right_b.size) + 4 * columns * n_freq * tiles * 2 * columns,
            transcendentals=0,
        ),
        name="chi",
    )(place, weighted, *([right_a] * 4), *([right_b] * 4))


def local(
    shape,
    val_orbitals,
    cond_orbitals,
    val_energy,
    cond_energy,
    val_slot,
    cond_slot,
    eigenvectors,
    frequencies,
):
    nz, ny, nc, nx = shape
    val_count, n_grid = val_orbitals.shape
    cond_count = cond_orbitals.shape[0]
    per_dev = val_slot.shape[0]
    n_freq = frequencies.shape[0]
    z = lax.axis_index("z")
    x = lax.axis_index("x")
    group = ny * nc
    n_parts = group * nx
    part = n_grid // n_parts
    segs = cond_count // val_count
    seg = part // segs
    columns = eigenvectors.shape[1]
    zfold = nz // nx

    def along_z(array, pairs):
        return lax.ppermute(array, "z", pairs)

    gap = cond_energy[:, None] - val_energy[None, :]
    weights = (
        4.0 * gap[:, :, None] / (gap[:, :, None] ** 2 + frequencies[None, None, :] ** 2)
    ).astype(jnp.bfloat16)
    chosen = (cond_slot[:, None, None] == jnp.arange(cond_count, dtype=jnp.int32)[None, :, None]) & (
        val_slot[:, None, None] == jnp.arange(val_count, dtype=jnp.int32)[None, None, :]
    )
    counts = jnp.sum(chosen.astype(jnp.float32), axis=0).astype(jnp.bfloat16)
    extra = jnp.concatenate([weights, counts[:, :, None]], axis=2).reshape(
        cond_count, val_count * (n_freq + 1)
    )
    extra = jnp.pad(extra, ((0, 0), (0, LANES - extra.shape[1])))
    scales = lax.all_gather(extra, AXES, axis=0).reshape(nz, n_parts * cond_count, LANES)

    cond_parts = cond_orbitals.reshape(cond_count, nx, group, part).transpose(2, 1, 0, 3)
    val_parts = val_orbitals.reshape(val_count, nx, group, segs, seg).transpose(2, 1, 3, 0, 4)
    packed = jnp.concatenate(
        [cond_parts.reshape(n_parts, cond_count, part), val_parts.reshape(n_parts, cond_count, seg)],
        axis=2,
    )
    unit = lax.all_to_all(packed, ("y", "c", "x"), 0, 0, tiled=True)
    unit = unit.reshape(n_parts * cond_count, part + seg)
    eigs = lax.all_to_all(
        eigenvectors.reshape(group, part, columns), ("y", "c"), 0, 0, tiled=True
    )

    if nz == 4:
        inner = (z == 1) | (z == 2)
        near = along_z(unit, [(0, 1), (1, 0), (2, 3), (3, 2)])
        middle = along_z(unit, [(1, 2), (2, 1)])
        across = along_z(near, [(1, 2), (2, 1)])
        outward = along_z(middle, [(1, 0), (2, 3)])
        far = along_z(across, [(1, 0), (2, 3)])
        units = [unit, near, jnp.where(inner, across, outward), jnp.where(inner, middle, far)]
    else:
        every = lax.all_gather(unit, "z", axis=0)
        units = [
            lax.dynamic_index_in_dim(every, lax.bitwise_xor(z, k), 0, keepdims=False)
            for k in range(nz)
        ]

    planes = lax.bitwise_xor(z.astype(jnp.int32), jnp.arange(nz, dtype=jnp.int32))
    source = x.astype(jnp.int32) * zfold + jnp.arange(zfold, dtype=jnp.int32)
    place = lax.bitwise_xor(jnp.broadcast_to(z.astype(jnp.int32), source.shape), source)
    factor = -1.0 / math.sqrt(per_dev * nz * n_parts)
    perm = []
    for s in range(nz):
        for q in range(group):
            for t in range(nx):
                perm.append(
                    (
                        (s * group + q) * nx + t,
                        ((s % zfold + zfold * t) * group + q) * nx + s // zfold,
                    )
                )

    def coefficients(k, sent_type):
        sums = project(units[k], eigs, val_count, cond_count, sent_type)
        sums = sums.reshape(n_parts, -1, columns)
        sums = lax.all_to_all(sums, ("y", "c", "x"), 0, 0, tiled=True)
        return jnp.sum(sums.astype(jnp.float32), axis=0).astype(jnp.bfloat16)

    def swapped(own):
        return lax.ppermute(own, AXES, perm)

    def gathered(share):
        return lax.all_gather(share, ("z", "y", "c"), axis=0)

    if columns % LANES == 0 and nx == 2 and nz == 4:
        units[1], scales = lax.optimization_barrier((units[1], scales))
        own_a = jnp.stack([coefficients(k, jnp.float32) for k in range(2)])
        share_a = swapped(own_a)
        right_a = gathered(share_a)
        units[2], _ = lax.optimization_barrier((units[2], share_a))
        own_b = jnp.stack([coefficients(2, jnp.float32), coefficients(3, jnp.bfloat16)])
        share_b, _ = lax.optimization_barrier((swapped(own_b), right_a))
        right_b = gathered(share_b)
        mate_a = lax.ppermute(own_a, "x", [(0, 1), (1, 0)])
        mate_b = lax.ppermute(own_b, "x", [(0, 1), (1, 0)])
        scalars = jnp.concatenate([x.astype(jnp.int32)[None], planes])
        weighted = weigh(own_a, mate_a, own_b, mate_b, scales, scalars, n_freq)
        return make_chi(weighted, right_a, right_b, jnp.repeat(place, ny), n_freq, factor)
    own = jnp.stack([coefficients(k, jnp.float32) for k in range(nz)])
    right = gathered(swapped(own))
    lefts = lax.all_gather(own, "x", axis=0)
    rows = own.shape[1]
    total = 0.0
    for k in range(nz):
        scale = lax.dynamic_index_in_dim(scales, planes[k], 0, keepdims=False)
        scale = scale[:, : val_count * (n_freq + 1)].astype(jnp.float32)
        scale = scale.reshape(n_parts * cond_count, val_count, n_freq + 1).transpose(1, 0, 2)
        scale = scale.reshape(nx, rows, n_freq + 1)
        scale = scale[..., :n_freq] * scale[..., n_freq:]
        weighted = (lefts[:, k, :, :, None].astype(jnp.float32) * scale[:, :, None, :]).astype(
            jnp.bfloat16
        )
        weighted = weighted.reshape(nx * rows, columns * n_freq)
        for low in range(zfold):
            at = lax.bitwise_xor(place[low], k)
            piece = lax.dynamic_index_in_dim(right, at, 1, keepdims=False)
            piece = piece.reshape(nx, zfold, group, rows, columns)[:, low]
            piece = piece.transpose(0, 2, 1, 3).reshape(nx * rows, group * columns)
            chi = lax.dot_general(
                weighted, piece, (((0,), (0,)), ((), ())), preferred_element_type=jnp.float32
            )
            chi = jnp.pad(chi, ((0, 0), (low * group * columns, (zfold - 1 - low) * group * columns)))
            total = total + chi
    return (total * factor).reshape(columns, n_freq, zfold * group * columns)


def solution(mesh):
    n_pair = mesh.shape["pair"]
    n_proj = mesh.shape["proj"]
    shape = (n_pair // 4, 2, 2, n_proj)
    grid = Mesh(mesh.devices.reshape(shape), AXES)
    return jax.shard_map(
        functools.partial(local, shape),
        mesh=grid,
        in_specs=(
            P(AXES, None),
            P(AXES, None),
            P(AXES),
            P(AXES),
            P(AXES),
            P(AXES),
            P("x", ("z", "y", "c")),
            P(),
        ),
        out_specs=P(("z", "y", "c"), None, "x"),
        check_vma=False,
    )
```

time: 232 us -> 303 us (1.31)
  blocking collectives: 43.2 us -> 103 us
  waiting for transfers between devices: 87.5 us -> 101 us
  starting transfers between devices: 29.1 us -> 40 us
  Pallas kernels: 32.3 us -> 24.8 us
  other arithmetic: 11.8 us -> 6.81 us
    all_gather x1, blocking collectives: 23.6 us -> 83.9 us  [local(): lax.all_gather(extra, AXES, axis=0).reshape(nz, n_parts * cond_count, LANES)]
    all_to_all x4, waiting for transfers between devices: 8.56 us -> 30.8 us  [coefficients(): sums = lax.all_to_all(sums, ('y', 'c', 'x'), 0, 0, tiled=True)]
    all_gather x1 -> x2, waiting for transfers between devices: 41.8 us -> 29.9 us  [gathered(): return lax.all_gather(share, ('z', 'y', 'c'), axis=0)]
    ppermute x1 -> x4, starting transfers between devices: 1.35 us -> 12.4 us  [the longest x1 10.9 us: local(): mate_a = lax.ppermute(own_a, 'x', [(0, 1), (1, 0)])]
    all_to_all x1, waiting for transfers between devices: 8.82 us -> 0.01 us  [local(): lax.all_to_all(eigenvectors.reshape(group, part, columns), ('y', 'c'), 0,...]
    pallas_call x1 -> x2, Pallas kernels: 12 us -> 5.53 us  [the longest x1 4.48 us: make_chi(): pl.pallas_call(functools.partial(chi_kernel, early, late, n_freq, factor)...]
    ppermute x5, waiting for transfers between devices: 28.2 us -> 34.6 us  [along_z(): return lax.ppermute(array, 'z', pairs)]
    ppermute x1 -> x4, waiting for transfers between devices: 0.01 us -> 6.17 us  [the longest x1 3.98 us: local(): mate_a = lax.ppermute(own_a, 'x', [(0, 1), (1, 0)])]
  transfers between devices with their start and end apart: 12 -> 16, of which waited for: 7 -> 8; matrix products, arithmetic and copies ran while one was open for 3% -> 2% of each run, Pallas kernels for 9% -> 5%
where the time goes in v4:
time: 303 us; the launch traced here: 302 us
  blocking collectives  103 us (34%)
  waiting for transfers between devices  101 us (33%)
  starting transfers between devices  40 us (13%)
  Pallas kernels  24.8 us (8%)
  between operations  13.8 us (5%)
  local copies, waits for them, and re-layouts  12.2 us (4%)
  other arithmetic  6.81 us (2%)
    all_gather x1, blocking collectives, local(): lax.all_gather(extra, AXES, axis=0).reshape(nz, n_parts * cond_count, LANES)  83.9 us
    ppermute x5, waiting for transfers between devices, along_z(): return lax.ppermute(array, 'z', pairs)  34.6 us
    all_to_all x4, waiting for transfers between devices, coefficients(): sums = lax.all_to_all(sums, ('y', 'c', 'x'), 0, 0, tiled=True)  30.8 us
    all_gather x2, waiting for transfers between devices, gathered(): return lax.all_gather(share, ('z', 'y', 'c'), axis=0)  29.9 us
    pallas_call x4, Pallas kernels, project(): pl.pallas_call(functools.partial(project_kernel, segs, val_count, cond_co...  19.3 us
    all_to_all x1, blocking collectives, local(): unit = lax.all_to_all(packed, ('y', 'c', 'x'), 0, 0, tiled=True)  19.3 us
    all_to_all x4, starting transfers between devices, coefficients(): sums = lax.all_to_all(sums, ('y', 'c', 'x'), 0, 0, tiled=True)  16.2 us
    ppermute x1, starting transfers between devices, local(): mate_a = lax.ppermute(own_a, 'x', [(0, 1), (1, 0)])  10.9 us
  transfers between devices with their start and end apart: 16, of which 8 were waited for; matrix products, arithmetic and copies ran while one was open for 2% of the time, Pallas kernels for 5%

profile of v4, /device:TPU:0, one launch (start us, length us, event | category | flops | bytes accessed | tf_op | source)
XLA Modules:
  0.0 302.2 jit_solution(1844953136116676413)
XLA Ops:
  6.5 1.8 reshape.173
  8.3 0.4 copy.20
  8.8 0.2 reshape.175
  8.9 0.2 copy.21
  9.2 19.3 %all_to_all.30 = bf16[8,16,3840]{2,1,0:T(8,128)(2,1)} all-to-all(bf16[8,16,3840]{2,1,0:T(8,128)(2,1)S(1)} %pad_maximum_fusion), channel_id=1, replica_groups=mesh['z'=4,'y'=2,'c'=2,'x'=2] {'y','c','x'}, dimensions={0} | all-to-all | bytes 1966080 | tf_op jit(solution)/shard_map/all_to_all | solution.py:271
  28.5 3.8 %all-to-all-start.1 = ((bf16[4,3072,128]{2,1,0:T(8,128)(2,1)}), bf16[4,3072,128]{2,1,0:T(8,128)(2,1)S(1)}, u32[]{:S(2)}, u32[]{:S(2)}) async-start(bf16[4,3072,128]{2,1,0:T(8,128)(2,1)} %bitcast.51), calls=%async_computation.1 | async-start | bytes 6291456 | tf_op jit(solution)/shard_map/all_to_all | solution.py:273
  32.3 1.6 collective-permute-start
  34.3 0.1 copy.24
  34.5 83.9 %all-gather = bf16[512,128]{1,0:T(8,128)(2,1)S(1)} all-gather(bf16[16,128]{1,0:T(8,128)(2,1)S(1)} %pad.4.clone), channel_id=2, replica_groups=mesh['z'=4,'y'=2,'c'=2,'x'=2] {'z','y','c','x'}, dimensions={0}, use_global_device_ids=true | all-gather | bytes 135168 | tf_op jit(solution)/shard_map/all_gather | solution.py:263
  118.4 5.4 %project.5 = f32[4,512,128]{2,1,0:T(8,128)S(1)} custom-call(bf16[128,3840]{1,0:T(8,128)(2,1)} %collective-permute-done.refs_0_.refs_1_.refs_2_.refs_3_.refs_4_, bf16[128,3840]{1,0:T(8,128)(2,1)} %collective-permute-done.refs_0_.refs_1_.refs_2_.refs_3_.refs_4_, bf16[128,3840]{1,0:T(8,128)(2,1)} %collective-permute-done.refs_0_.refs_1_.refs_2_.refs_3_.refs_4_, ...), custom_call_target="tpu_custom_call" | custom-call | flops 1610612736 | bytes 4128768 | tf_op jit(solution)/shard_map/project/pallas_call | solution.py:88
  123.7 1.0 copy-done.5
  124.7 4.2 %all-to-all-start.3 = ((f32[8,256,128]{2,1,0:T(8,128)}), f32[8,256,128]{2,1,0:T(8,128)}, u32[]{:S(2)}, u32[]{:S(2)}) async-start(f32[8,256,128]{2,1,0:T(8,128)} %bitcast.45), calls=%async_computation.3 | async-start | bytes 2097152 | tf_op jit(solution)/shard_map/all_to_all | solution.py:310
  129.0 1.6 collective-permute-start.2
  130.6 1.2 copy-done
  131.8 4.6 %project.4 = f32[4,512,128]{2,1,0:T(8,128)S(1)} custom-call(bf16[128,3840]{1,0:T(8,128)(2,1)S(1)} %bitcast.30, bf16[128,3840]{1,0:T(8,128)(2,1)S(1)} %bitcast.31, bf16[128,3840]{1,0:T(8,128)(2,1)S(1)} %bitcast.32, bf16[128,3840]{1,0:T(8,128)(2,1)S(1)} %bitcast.33, bf16[128,3840]{1,0:T(8,128)(2,1)S(1)} %bitcast.34, ...), custom_call_target="tpu_custom_call" | custom-call | flops 1610612736 | bytes 4128768 | tf_op jit(solution)/shard_map/project/pallas_call | solution.py:88
  136.4 1.0 copy-done.3
  137.4 6.5 %all-to-all-done.3 = f32[8,256,128]{2,1,0:T(8,128)} async-done(((f32[8,256,128]{2,1,0:T(8,128)}), f32[8,256,128]{2,1,0:T(8,128)}, u32[]{:S(2)}, u32[]{:S(2)}) %all-to-all-start.3) | async-done | bytes 1048608 | tf_op jit(solution)/shard_map/all_to_all | solution.py:310
  143.9 4.2 %all-to-all-start.2 = ((f32[8,256,128]{2,1,0:T(8,128)}), f32[8,256,128]{2,1,0:T(8,128)}, u32[]{:S(2)}, u32[]{:S(2)}) async-start(f32[8,256,128]{2,1,0:T(8,128)} %bitcast.43), calls=%async_computation.2 | async-start | bytes 2097152 | tf_op jit(solution)/shard_map/all_to_all | solution.py:310
  148.2 1.7 collective-permute-start.3
  149.8 1.3 collective-permute-start.6
  151.1 1.3 reduce_sum.50
  152.4 10.6 %all-to-all-done.2 = f32[8,256,128]{2,1,0:T(8,128)} async-done(((f32[8,256,128]{2,1,0:T(8,128)}), f32[8,256,128]{2,1,0:T(8,128)}, u32[]{:S(2)}, u32[]{:S(2)}) %all-to-all-start.2) | async-done | bytes 1048608 | tf_op jit(solution)/shard_map/all_to_all | solution.py:310
  163.1 1.3 reduce_sum.48
  164.4 0.7 collective-permute-start.5
  165.1 0.6 copy-done.8
  165.8 1.3 collective-permute-start.4
  167.1 12.4 %collective-permute-done.6 = bf16[128,3840]{1,0:T(8,128)(2,1)} collective-permute-done((bf16[128,3840]{1,0:T(8,128)(2,1)}, bf16[128,3840]{1,0:T(8,128)(2,1)}, u32[]{:S(2)}, u32[]{:S(2)}) %collective-permute-start.6) | collective-permute-done | bytes 983072 | tf_op jit(solution)/shard_map/ppermute | solution.py:249
  179.4 1.3 broadcast_select_fusion.refs_0_.refs_1_.refs_2_.refs_3_.refs_4_
  180.7 4.7 %project.7 = bf16[4,512,128]{2,1,0:T(8,128)(2,1)S(1)} custom-call(bf16[128,3840]{1,0:T(8,128)(2,1)S(1)} %broadcast_select_fusion.refs_0_.refs_1_.refs_2_.refs_3_.refs_4_, bf16[128,3840]{1,0:T(8,128)(2,1)S(1)} %broadcast_select_fusion.refs_0_.refs_1_.refs_2_.refs_3_.refs_4_, ...), custom_call_target="tpu_custom_call" | custom-call | flops 1610612736 | bytes 4128768 | tf_op jit(solution)/shard_map/project/pallas_call | solution.py:88
  185.4 0.8 copy-done.6
  186.2 4.2 %all-to-all-start.5 = ((bf16[8,256,128]{2,1,0:T(8,128)(2,1)}), bf16[8,256,128]{2,1,0:T(8,128)(2,1)}, u32[]{:S(2)}, u32[]{:S(2)}) async-start(bf16[8,256,128]{2,1,0:T(8,128)(2,1)} %bitcast.50), calls=%async_computation.5 | async-start | bytes 1048576 | tf_op jit(solution)/shard_map/all_to_all | solution.py:310
  190.4 22.2 %collective-permute-done.4 = bf16[128,3840]{1,0:T(8,128)(2,1)} collective-permute-done((bf16[128,3840]{1,0:T(8,128)(2,1)}, bf16[128,3840]{1,0:T(8,128)(2,1)}, u32[]{:S(2)}, u32[]{:S(2)}) %collective-permute-start.4) | collective-permute-done | bytes 983072 | tf_op jit(solution)/shard_map/ppermute | solution.py:249
  212.5 1.3 broadcast_select_fusion.1.refs_0_.refs_1_.refs_2_.refs_3_.refs_4_
  213.9 4.7 %project.6 = f32[4,512,128]{2,1,0:T(8,128)S(1)} custom-call(bf16[128,3840]{1,0:T(8,128)(2,1)S(1)} %broadcast_select_fusion.1.refs_0_.refs_1_.refs_2_.refs_3_.refs_4_, bf16[128,3840]{1,0:T(8,128)(2,1)S(1)} %broadcast_select_fusion.1.refs_0_.refs_1_.refs_2_.refs_3_.refs_4_, ...), custom_call_target="tpu_custom_call" | custom-call | flops 1610612736 | bytes 4128768 | tf_op jit(solution)/shard_map/project/pallas_call | solution.py:88
  218.5 1.0 copy-done.4
  219.5 3.6 %all-to-all-start.4 = ((f32[8,256,128]{2,1,0:T(8,128)}), f32[8,256,128]{2,1,0:T(8,128)S(1)}, u32[]{:S(2)}, u32[]{:S(2)}) async-start(f32[8,256,128]{2,1,0:T(8,128)} %bitcast.44), calls=%async_computation.4 | async-start | bytes 2097152 | tf_op jit(solution)/shard_map/all_to_all | solution.py:310
  223.1 1.1 reduce_sum.52
  224.2 13.7 %all-to-all-done.4 = f32[8,256,128]{2,1,0:T(8,128)S(1)} async-done(((f32[8,256,128]{2,1,0:T(8,128)}), f32[8,256,128]{2,1,0:T(8,128)S(1)}, u32[]{:S(2)}, u32[]{:S(2)}) %all-to-all-start.4) | async-done | bytes 1048608 | tf_op jit(solution)/shard_map/all_to_all | solution.py:310
  238.0 0.7 collective-permute-start.8
  238.7 0.6 copy-done.9
  239.4 10.9 %collective-permute-start.1 = (bf16[2,256,128]{2,1,0:T(8,128)(2,1)S(1)}, bf16[2,256,128]{2,1,0:T(8,128)(2,1)S(1)}, u32[]{:S(2)}, u32[]{:S(2)}) collective-permute-start(bf16[2,256,128]{2,1,0:T(8,128)(2,1)S(1)} %pad_maximum_fusion.1.refs_0_), channel_id=1, source_target_pairs={{0,1},{1,0},{2,3},{3,2},{4,5},{5,4},{6,7},{7,6},{8,9},{9,8},{10,11... | collective-permute-start | bytes 393224 | tf_op jit(solution)/shard_map/ppermute | solution.py:328
  250.6 4.0 %collective-permute-done.1.refs_1_ = bf16[2,256,128]{2,1,0:T(8,128)(2,1)S(1)} collective-permute-done((bf16[2,256,128]{2,1,0:T(8,128)(2,1)S(1)}, bf16[2,256,128]{2,1,0:T(8,128)(2,1)S(1)}, u32[]{:S(2)}, u32[]{:S(2)}) %collective-permute-start.1) | collective-permute-done | bytes 131104 | tf_op jit(solution)/shard_map/ppermute | solution.py:328
  254.6 2.2 collective-permute-done.7.refs_3_
  256.8 1.1 weigh.1.refs_0_
  257.9 29.8 %all-gather.8.cloned.1.call-done = bf16[32,256,128]{2,1,0:T(8,128)(2,1)} async-done(((bf16[2,256,128]{2,1,0:T(8,128)(2,1)}), bf16[32,256,128]{2,1,0:T(8,128)(2,1)}) %all-gather.8.cloned.1.call-update) | async-done | bytes 2097168 | tf_op jit(solution)/shard_map/all_gather | solution.py:317
  287.7 1.6 copy-done.1
  289.3 1.6 copy-done.2
  290.9 4.5 %chi.1 = f32[128,4,1024]{2,1,0:T(4,128)} custom-call(s32[4]{0:T(128)S(1)} %reshape.172.place, bf16[4,512,512]{2,1,0:T(8,128)(2,1)S(1)} %weigh.1.refs_0_, bf16[16,2,256,128]{3,2,1,0:T(8,128)(2,1)S(1)} %bitcast.35, bf16[16,2,256,128]{3,2,1,0:T(8,128)(2,1)S(1)} %bitcast.36, bf16[16,2,256,128]{3,2,1,0:T(8,128)(2,1)S(1)} %bitcast.37, ...), custom_call_target="tpu_custom_call" | custom-call | flops 2147483648 | bytes 6291456 | tf_op jit(solution)/shard_map/chi/pallas_call | solution.py:201
  (54 shorter events, 1.0 us)
Async XLA Ops:
  6.5 2.2 copy-start.7
  28.5 5.5 %copy-start.13 = (s32[64]{0:T(128)S(1)}, s32[64]{0:T(128)}, u32[]{:S(2)}) copy-start(s32[64]{0:T(128)} %param.12) | copy-start | bytes 772
  28.5 5.5 %copy-start.14 = (f32[4]{0:T(128)S(1)}, f32[4]{0:T(128)}, u32[]{:S(2)}) copy-start(f32[4]{0:T(128)} %param.15) | copy-start | bytes 52
  28.5 5.5 %copy-start.10 = (s32[64]{0:T(128)S(1)}, s32[64]{0:T(128)}, u32[]{:S(2)}) copy-start(s32[64]{0:T(128)} %param.13) | copy-start | bytes 772
  28.5 5.7 %copy-start.11 = (f32[4]{0:T(128)S(1)}, f32[4]{0:T(128)}, u32[]{:S(2)}) copy-start(f32[4]{0:T(128)} %param.10) | copy-start | bytes 52
  28.5 5.7 %copy-start.12 = (f32[16]{0:T(128)S(1)}, f32[16]{0:T(128)}, u32[]{:S(2)}) copy-start(f32[16]{0:T(128)} %param.11) | copy-start | bytes 196
  28.5 89.9 %all-to-all-start.1 = ((bf16[4,3072,128]{2,1,0:T(8,128)(2,1)}), bf16[4,3072,128]{2,1,0:T(8,128)(2,1)S(1)}, u32[]{:S(2)}, u32[]{:S(2)}) async-start(bf16[4,3072,128]{2,1,0:T(8,128)(2,1)} %bitcast.51), calls=%async_computation.1 | async-start | bytes 6291456 | tf_op jit(solution)/shard_map/all_to_all | solution.py:273
  32.3 86.0 %collective-permute-start = (bf16[128,3840]{1,0:T(8,128)(2,1)}, bf16[128,3840]{1,0:T(8,128)(2,1)}, u32[]{:S(2)}, u32[]{:S(2)}) collective-permute-start(bf16[128,3840]{1,0:T(8,128)(2,1)} %bitcast.28), channel_id=1, source_target_pairs={{0,8},{8,0},{16,24},{24,16},{1,9},{9,1},{17,25},{25,17},{2,10},{10... | collective-permute-start | bytes 2949128 | tf_op jit(solution)/shard_map/ppermute | solution.py:249
  123.7 1.0 copy-start.5
  124.7 19.2 %all-to-all-start.3 = ((f32[8,256,128]{2,1,0:T(8,128)}), f32[8,256,128]{2,1,0:T(8,128)}, u32[]{:S(2)}, u32[]{:S(2)}) async-start(f32[8,256,128]{2,1,0:T(8,128)} %bitcast.45), calls=%async_computation.3 | async-start | bytes 2097152 | tf_op jit(solution)/shard_map/all_to_all | solution.py:310
  129.0 20.9 %collective-permute-start.2 = (bf16[128,3840]{1,0:T(8,128)(2,1)}, bf16[128,3840]{1,0:T(8,128)(2,1)}, u32[]{:S(2)}, u32[]{:S(2)}) collective-permute-start(bf16[128,3840]{1,0:T(8,128)(2,1)} %collective-permute-done.refs_0_.refs_1_.refs_2_.refs_3_.refs_4_), channel_id=1, source_target_pairs={{8,16},{16,8},{9,17},{17,9},{10,18},{18,10},{11,19},{19,11},{12,20... | collective-permute-start | bytes 2949128 | tf_op jit(solution)/shard_map/ppermute | solution.py:249
  130.6 1.2 copy-start
  136.4 1.0 copy-start.3
  143.9 19.2 %all-to-all-start.2 = ((f32[8,256,128]{2,1,0:T(8,128)}), f32[8,256,128]{2,1,0:T(8,128)}, u32[]{:S(2)}, u32[]{:S(2)}) async-start(f32[8,256,128]{2,1,0:T(8,128)} %bitcast.43), calls=%async_computation.2 | async-start | bytes 2097152 | tf_op jit(solution)/shard_map/all_to_all | solution.py:310
  148.1 90.6 %all-gather.6.cloned.1.call-start = ((), (), s32[]{:S(2)}) async-start(), calls=%async_computation.6 | async-start | bytes 2228224 | tf_op jit(solution)/shard_map/all_gather | solution.py:317
  148.2 17.6 %collective-permute-start.3 = (bf16[128,3840]{1,0:T(8,128)(2,1)}, bf16[128,3840]{1,0:T(8,128)(2,1)}, u32[]{:S(2)}, u32[]{:S(2)}) collective-permute-start(bf16[128,3840]{1,0:T(8,128)(2,1)} %bitcast.29), channel_id=1, source_target_pairs={{8,16},{16,8},{9,17},{17,9},{10,18},{18,10},{11,19},{19,11},{12,20... | collective-permute-start | bytes 2949128 | tf_op jit(solution)/shard_map/ppermute | solution.py:249
  149.8 29.6 %collective-permute-start.6 = (bf16[128,3840]{1,0:T(8,128)(2,1)}, bf16[128,3840]{1,0:T(8,128)(2,1)}, u32[]{:S(2)}, u32[]{:S(2)}) collective-permute-start(bf16[128,3840]{1,0:T(8,128)(2,1)} %collective-permute-done.2), channel_id=1, source_target_pairs={{8,0},{16,24},{9,1},{17,25},{10,2},{18,26},{11,3},{19,27},{12,4},{... | collective-permute-start | bytes 2949128 | tf_op jit(solution)/shard_map/ppermute | solution.py:249
  164.4 0.7 collective-permute-start.5
  165.1 0.7 copy-start.8
  165.8 46.8 %collective-permute-start.4 = (bf16[128,3840]{1,0:T(8,128)(2,1)}, bf16[128,3840]{1,0:T(8,128)(2,1)}, u32[]{:S(2)}, u32[]{:S(2)}) collective-permute-start(bf16[128,3840]{1,0:T(8,128)(2,1)} %collective-permute-done.3), channel_id=1, source_target_pairs={{8,0},{16,24},{9,1},{17,25},{10,2},{18,26},{11,3},{19,27},{12,4},{... | collective-permute-start | bytes 2949128 | tf_op jit(solution)/shard_map/ppermute | solution.py:249
  185.4 0.8 copy-start.6
  186.2 33.3 %all-to-all-start.5 = ((bf16[8,256,128]{2,1,0:T(8,128)(2,1)}), bf16[8,256,128]{2,1,0:T(8,128)(2,1)}, u32[]{:S(2)}, u32[]{:S(2)}) async-start(bf16[8,256,128]{2,1,0:T(8,128)(2,1)} %bitcast.50), calls=%async_computation.5 | async-start | bytes 1048576 | tf_op jit(solution)/shard_map/all_to_all | solution.py:310
  218.5 1.0 copy-start.4
  219.5 18.4 %all-to-all-start.4 = ((f32[8,256,128]{2,1,0:T(8,128)}), f32[8,256,128]{2,1,0:T(8,128)S(1)}, u32[]{:S(2)}, u32[]{:S(2)}) async-start(f32[8,256,128]{2,1,0:T(8,128)} %bitcast.44), calls=%async_computation.4 | async-start | bytes 2097152 | tf_op jit(solution)/shard_map/all_to_all | solution.py:310
  223.1 64.6 %all-gather.8.cloned.1.call-start = ((), (), s32[]{:S(2)}) async-start(), calls=%async_computation.7 | async-start | bytes 2228224 | tf_op jit(solution)/shard_map/all_gather | solution.py:317
  238.0 0.7 collective-permute-start.8
  238.7 0.7 copy-start.9
  239.4 15.2 %collective-permute-start.1 = (bf16[2,256,128]{2,1,0:T(8,128)(2,1)S(1)}, bf16[2,256,128]{2,1,0:T(8,128)(2,1)S(1)}, u32[]{:S(2)}, u32[]{:S(2)}) collective-permute-start(bf16[2,256,128]{2,1,0:T(8,128)(2,1)S(1)} %pad_maximum_fusion.1.refs_0_), channel_id=1, source_target_pairs={{0,1},{1,0},{2,3},{3,2},{4,5},{5,4},{6,7},{7,6},{8,9},{9,8},{10,11... | collective-permute-start | bytes 393224 | tf_op jit(solution)/shard_map/ppermute | solution.py:328
  250.3 6.5 %collective-permute-start.7 = (bf16[2,256,128]{2,1,0:T(8,128)(2,1)S(1)}, bf16[2,256,128]{2,1,0:T(8,128)(2,1)S(1)}, u32[]{:S(2)}, u32[]{:S(2)}) collective-permute-start(bf16[2,256,128]{2,1,0:T(8,128)(2,1)S(1)} %pad_maximum_fusion.2.refs_2_), channel_id=1, source_target_pairs={{0,1},{1,0},{2,3},{3,2},{4,5},{5,4},{6,7},{7,6},{8,9},{9,8},{10,11... | collective-permute-start | bytes 393224 | tf_op jit(solution)/shard_map/ppermute | solution.py:329
  287.7 1.6 copy-start.1
  289.3 1.6 copy-start.2
Sparse Core Ops, SparseCore 0:
  165.9 47.6 all-gather.5
  239.5 48.1 all-gather.7

commit v5 on v4

--- a/solution.py
+++ b/solution.py
@@ -11,6 +11,108 @@
 
 LANES = 128
 AXES = ("z", "y", "c", "x")
+
+
+def pack_kernel(nx, part, seg, val_energy, cond_energy, val_slot, cond_slot, frequencies, *refs):
+    conds = refs[:nx]
+    vals = refs[nx : 2 * nx]
+    out, extra = refs[2 * nx :]
+    val_count = val_energy.shape[0]
+    cond_count = cond_energy.shape[0]
+    n_freq = frequencies.shape[0]
+    stride = n_freq + 1
+
+    @pl.when(pl.program_id(0) == 0)
+    def _():
+        row = lax.broadcasted_iota(jnp.int32, (cond_count, LANES), 0)
+        lane = lax.broadcasted_iota(jnp.int32, (cond_count, LANES), 1)
+        cond_level = jnp.zeros((cond_count, LANES), jnp.float32)
+        for c in range(cond_count):
+            cond_level = jnp.where(row == c, cond_energy[c], cond_level)
+        val_level = jnp.zeros((cond_count, LANES), jnp.float32)
+        freq = jnp.zeros((cond_count, LANES), jnp.float32)
+        is_count = lane < 0
+        for v in range(val_count):
+            for f in range(stride):
+                here = lane == v * stride + f
+                val_level = jnp.where(here, val_energy[v], val_level)
+                if f < n_freq:
+                    freq = jnp.where(here, frequencies[f], freq)
+                else:
+                    is_count = is_count | here
+        gap = cond_level - val_level
+        weight = 4.0 * gap / (gap * gap + freq * freq)
+
+        def add(p, number):
+            here = (row == cond_slot[p]) & (lane == val_slot[p] * stride + n_freq)
+            return number + jnp.where(here, 1.0, 0.0)
+
+        number = lax.fori_loop(0, val_slot.shape[0], add, jnp.zeros((cond_count, LANES), jnp.float32))
+        used = lane < val_count * stride
+        extra[...] = jnp.where(used, jnp.where(is_count, number, weight), 0.0).astype(jnp.bfloat16)
+
+    for t in range(nx):
+        out[t, :, :part] = conds[t][...]
+        val = vals[t][...].astype(jnp.float32)
+        pieces = [val[:, k * seg : (k + 1) * seg] for k in range(part // seg)]
+        out[t, :, part : part + seg] = jnp.concatenate(pieces, axis=0).astype(jnp.bfloat16)
+        out[t, :, part + seg :] = extra[...]
+
+
+def pack(val_orbitals, cond_orbitals, val_energy, cond_energy, val_slot, cond_slot, frequencies, nx, group):
+    val_count, n_grid = val_orbitals.shape
+    cond_count = cond_orbitals.shape[0]
+    n_freq = frequencies.shape[0]
+    n_parts = group * nx
+    part = n_grid // n_parts
+    segs = cond_count // val_count
+    seg = part // segs
+    width = part + seg + LANES
+    if seg % LANES == 0:
+        smem = pl.BlockSpec(memory_space=pltpu.SMEM)
+        piece = lambda rows: [
+            pl.BlockSpec((rows, part), functools.partial(lambda t, i: (0, t * group + i), t))
+            for t in range(nx)
+        ]
+        return pl.pallas_call(
+            functools.partial(pack_kernel, nx, part, seg),
+            out_shape=jax.ShapeDtypeStruct((n_parts, cond_count, width), jnp.bfloat16),
+            grid=(group,),
+            in_specs=[smem] * 5 + piece(cond_count) + piece(val_count),
+            out_specs=pl.BlockSpec((nx, cond_count, width), lambda i: (i, 0, 0)),
+            scratch_shapes=[pltpu.VMEM((cond_count, LANES), jnp.bfloat16)],
+            name="pack",
+        )(
+            val_energy,
+            cond_energy,
+            val_slot,
+            cond_slot,
+            frequencies,
+            *([cond_orbitals] * nx),
+            *([val_orbitals] * nx),
+        )
+    gap = cond_energy[:, None] - val_energy[None, :]
+    weights = (
+        4.0 * gap[:, :, None] / (gap[:, :, None] ** 2 + frequencies[None, None, :] ** 2)
+    ).astype(jnp.bfloat16)
+    chosen = (cond_slot[:, None, None] == jnp.arange(cond_count, dtype=jnp.int32)[None, :, None]) & (
+        val_slot[:, None, None] == jnp.arange(val_count, dtype=jnp.int32)[None, None, :]
+    )
+    counts = jnp.sum(chosen.astype(jnp.float32), axis=0).astype(jnp.bfloat16)
+    extra = jnp.concatenate([weights, counts[:, :, None]], axis=2).reshape(
+        cond_count, val_count * (n_freq + 1)
+    )
+    extra = jnp.pad(extra, ((0, 0), (0, LANES - extra.shape[1])))
+    cond_parts = cond_orbitals.reshape(cond_count, nx, group, part).transpose(2, 1, 0, 3)
+    val_parts = val_orbitals.reshape(val_count, nx, group, segs, seg).transpose(2, 1, 3, 0, 4)
+    return jnp.concatenate(
+        [
+            cond_parts.reshape(n_parts, cond_count, part),
+            val_parts.reshape(n_parts, cond_count, seg),
+            jnp.broadcast_to(extra, (n_parts,) + extra.shape),
+        ],
+        axis=2,
+    )
 
 
 def project_kernel(segs, val_count, cond_count, *refs):
@@ -63,7 +165,7 @@
     if seg % LANES or columns % LANES:
         blocks = rows // cond_count
         cond = unit[:, :part].reshape(1, blocks, cond_count, segs, seg)
-        val = unit[:, part:].reshape(blocks, segs, val_count, seg)
+        val = unit[:, part : part + seg].reshape(blocks, segs, val_count, seg)
         val = val.transpose(2, 0, 1, 3)[:, :, None]
         density = (cond.astype(jnp.float32) * val.astype(jnp.float32)).astype(jnp.bfloat16)
         sums = jnp.einsum(
@@ -129,10 +231,11 @@
                     ).astype(jnp.bfloat16)
 
 
-def weigh(own_a, mate_a, own_b, mate_b, scales, scalars, n_freq):
+def weigh(own_a, mate_a, own_b, mate_b, units, scalars, n_freq):
     early, rows, columns = own_a.shape
     late = own_b.shape[0]
-    width = scales.shape[1]
+    width = units[0].shape[0]
+    last = units[0].shape[1] // LANES - 1
     whole = lambda shape: pl.BlockSpec(shape, lambda i, scalars: tuple(0 for _ in shape))
     shape = (early + late, n_freq * columns, 2 * rows)
     return pl.pallas_call(
@@ -142,13 +245,7 @@
             num_scalar_prefetch=1,
             grid=(1,),
             in_specs=[whole(a.shape) for a in (own_a, mate_a, own_b, mate_b)]
-            + [
-                pl.BlockSpec(
-                    (None, width, LANES),
-                    functools.partial(lambda k, i, scalars: (scalars[1 + k], 0, 0), k),
-                )
-                for k in range(early + late)
-            ],
+            + [pl.BlockSpec((width, LANES), lambda i, scalars: (0, last))] * (early + late),
             out_specs=whole(shape),
         ),
         compiler_params=pltpu.CompilerParams(vmem_limit_bytes=24 * 1024 * 1024),
@@ -156,23 +253,21 @@
             flops=2 * math.prod(shape), bytes_accessed=3 * math.prod(shape), transcendentals=0
         ),
         name="weigh",
-    )(scalars, own_a, mate_a, own_b, mate_b, *([scales] * (early + late)))
-
-
-def chi_kernel(early, late, n_freq, factor, place, *refs):
+    )(scalars, own_a, mate_a, own_b, mate_b, *units)
+
+
+def chi_kernel(early, n_freq, factor, scalars, *refs):
     weighted = refs[0]
     rights_a = refs[1:5]
     rights_b = refs[5:9]
     out = refs[9]
     columns = out.shape[0]
-    shift = place[pl.program_id(0)]
+    shift = lax.bitwise_xor(scalars[0], scalars[3] + pl.program_id(0) // 2)
     left, right = [], []
-    for r in range(early + late):
+    for r in range(early + 1):
         left.append(weighted[lax.bitwise_xor(shift, r)])
         for h in range(2):
-            pair = [
-                rights_a[2 * h + c][0, r] if r < early else rights_b[2 * h + c][0, r - early] for c in range(2)
-            ]
+            pair = [rights_a[2 * h + c][0, r] if r < early else rights_b[2 * h + c][0] for c in range(2)]
             right.append(jnp.concatenate(pair, axis=1))
     chi = jnp.dot(
         jnp.concatenate(left, axis=1),
@@ -183,31 +278,35 @@
         out[:, f, :] = chi[f * columns : (f + 1) * columns, :] * factor
 
 
-def make_chi(weighted, right_a, right_b, place, n_freq, factor):
+def make_chi(weighted, right_a, right_b, scalars, n_freq, factor):
     members, early, rows, columns = right_a.shape
     tiles = members // 4
-    late = right_b.shape[1]
-
-    def right_specs(slots):
-        return [
-            pl.BlockSpec(
-                (1, slots, rows, columns),
-                functools.partial(lambda h, c, i, place: (h * tiles * 2 + i * 2 + c, 0, 0, 0), h, c),
-            )
-            for h in range(2)
-            for c in range(2)
-        ]
-
+
+    def near(h, c, i, scalars):
+        z = lax.bitwise_xor(scalars[0], h * 2 + i // 2)
+        y = lax.bitwise_xor(scalars[1], lax.rem(i, 2))
+        core = lax.bitwise_xor(scalars[2], c)
+        return ((core * 2 + y) * 4 + z, 0, 0)
+
+    places = [(h, c) for h in range(2) for c in range(2)]
     return pl.pallas_call(
-        functools.partial(chi_kernel, early, late, n_freq, factor),
+        functools.partial(chi_kernel, early, n_freq, factor),
         out_shape=jax.ShapeDtypeStruct((columns, n_freq, tiles * 2 * columns), jnp.float32),
         grid_spec=pltpu.PrefetchScalarGridSpec(
             num_scalar_prefetch=1,
             grid=(tiles,),
-            in_specs=[pl.BlockSpec(weighted.shape, lambda i, place: (0, 0, 0))]
-            + right_specs(early)
-            + right_specs(late),
-            out_specs=pl.BlockSpec((columns, n_freq, 2 * columns), lambda i, place: (0, 0, i)),
+            in_specs=[pl.BlockSpec(weighted.shape, lambda i, scalars: (0, 0, 0))]
+            + [
+                pl.BlockSpec(
+                    (1, early, rows, columns),
+                    functools.partial(
+                        lambda h, c, i, scalars: (h * tiles * 2 + i * 2 + c, 0, 0, 0), h, c
+                    ),
+                )
+                for h, c in places
+            ]
+            + [pl.BlockSpec((1, rows, columns), functools.partial(near, h, c)) for h, c in places],
+            out_specs=pl.BlockSpec((columns, n_freq, 2 * columns), lambda i, scalars: (0, 0, i)),
         ),
         compiler_params=pltpu.CompilerParams(vmem_limit_bytes=32 * 1024 * 1024),
         cost_estimate=pl.CostEstimate(
@@ -216,7 +315,7 @@
             transcendentals=0,
         ),
         name="chi",
-    )(place, weighted, *([right_a] * 4), *([right_b] * 4))
+    )(scalars, weighted, *([right_a] * 4), *([right_b] * 4))
 
 
 def local(
@@ -248,28 +347,11 @@
     def along_z(array, pairs):
         return lax.ppermute(array, "z", pairs)
 
-    gap = cond_energy[:, None] - val_energy[None, :]
-    weights = (
-        4.0 * gap[:, :, None] / (gap[:, :, None] ** 2 + frequencies[None, None, :] ** 2)
-    ).astype(jnp.bfloat16)
-    chosen = (cond_slot[:, None, None] == jnp.arange(cond_count, dtype=jnp.int32)[None, :, None]) & (
-        val_slot[:, None, None] == jnp.arange(val_count, dtype=jnp.int32)[None, None, :]
-    )
-    counts = jnp.sum(chosen.astype(jnp.float32), axis=0).astype(jnp.bfloat16)
-    extra = jnp.concatenate([weights, counts[:, :, None]], axis=2).reshape(
-        cond_count, val_count * (n_freq + 1)
-    )
-    extra = jnp.pad(extra, ((0, 0), (0, LANES - extra.shape[1])))
-    scales = lax.all_gather(extra, AXES, axis=0).reshape(nz, n_parts * cond_count, LANES)
-
-    cond_parts = cond_orbitals.reshape(cond_count, nx, group, part).transpose(2, 1, 0, 3)
-    val_parts = val_orbitals.reshape(val_count, nx, group, segs, seg).transpose(2, 1, 3, 0, 4)
-    packed = jnp.concatenate(
-        [cond_parts.reshape(n_parts, cond_count, part), val_parts.reshape(n_parts, cond_count, seg)],
-        axis=2,
+    packed = pack(
+        val_orbitals, cond_orbitals, val_energy, cond_energy, val_slot, cond_slot, frequencies, nx, group
     )
     unit = lax.all_to_all(packed, ("y", "c", "x"), 0, 0, tiled=True)
-    unit = unit.reshape(n_parts * cond_count, part + seg)
+    unit = unit.reshape(n_parts * cond_count, part + seg + LANES)
     eigs = lax.all_to_all(
         eigenvectors.reshape(group, part, columns), ("y", "c"), 0, 0, tiled=True
     )
@@ -289,7 +371,6 @@
             for k in range(nz)
         ]
 
-    planes = lax.bitwise_xor(z.astype(jnp.int32), jnp.arange(nz, dtype=jnp.int32))
     source = x.astype(jnp.int32) * zfold + jnp.arange(zfold, dtype=jnp.int32)
     place = lax.bitwise_xor(jnp.broadcast_to(z.astype(jnp.int32), source.shape), source)
     factor = -1.0 / math.sqrt(per_dev * nz * n_parts)
@@ -316,28 +397,33 @@
     def gathered(share):
         return lax.all_gather(share, ("z", "y", "c"), axis=0)
 
-    if columns % LANES == 0 and nx == 2 and nz == 4:
-        units[1], scales = lax.optimization_barrier((units[1], scales))
-        own_a = jnp.stack([coefficients(k, jnp.float32) for k in range(2)])
+    if columns % LANES == 0 and seg % LANES == 0 and nx == 2 and nz == 4:
+        flip = [(0, 1), (1, 0)]
+        own_a = jnp.stack([coefficients(k, jnp.float32) for k in range(nz - 1)])
         share_a = swapped(own_a)
         right_a = gathered(share_a)
-        units[2], _ = lax.optimization_barrier((units[2], share_a))
-        own_b = jnp.stack([coefficients(2, jnp.float32), coefficients(3, jnp.bfloat16)])
-        share_b, _ = lax.optimization_barrier((swapped(own_b), right_a))
-        right_b = gathered(share_b)
-        mate_a = lax.ppermute(own_a, "x", [(0, 1), (1, 0)])
-        mate_b = lax.ppermute(own_b, "x", [(0, 1), (1, 0)])
-        scalars = jnp.concatenate([x.astype(jnp.int32)[None], planes])
-        weighted = weigh(own_a, mate_a, own_b, mate_b, scales, scalars, n_freq)
-        return make_chi(weighted, right_a, right_b, jnp.repeat(place, ny), n_freq, factor)
+        units[-1], _ = lax.optimization_barrier((units[-1], own_a))
+        own_b = coefficients(nz - 1, jnp.bfloat16)
+        share_b = swapped(own_b)
+        held = jnp.stack(
+            [share_b] + [along_z(share_b, [(t, t ^ k) for t in range(nz)]) for k in range(1, nz)]
+        )
+        held = jnp.concatenate([held, lax.ppermute(held, "y", flip)])
+        right_b = jnp.concatenate([held, lax.ppermute(held, "c", flip)])
+        mate_a = lax.ppermute(own_a, "x", flip)
+        mate_b = lax.ppermute(own_b, "x", flip)
+        weighted = weigh(
+            own_a, mate_a, own_b[None], mate_b[None], units, x.astype(jnp.int32)[None], n_freq
+        )
+        scalars = jnp.stack([z, lax.axis_index("y"), lax.axis_index("c"), x * zfold]).astype(jnp.int32)
+        return make_chi(weighted, right_a, right_b, scalars, n_freq, factor)
     own = jnp.stack([coefficients(k, jnp.float32) for k in range(nz)])
     right = gathered(swapped(own))
     lefts = lax.all_gather(own, "x", axis=0)
     rows = own.shape[1]
     total = 0.0
     for k in range(nz):
-        scale = lax.dynamic_index_in_dim(scales, planes[k], 0, keepdims=False)
-        scale = scale[:, : val_count * (n_freq + 1)].astype(jnp.float32)
+        scale = units[k][:, part + seg : part + seg + val_count * (n_freq + 1)].astype(jnp.float32)
         scale = scale.reshape(n_parts * cond_count, val_count, n_freq + 1).transpose(1, 0, 2)
         scale = scale.reshape(nx, rows, n_freq + 1)
         scale = scale[..., :n_freq] * scale[..., n_freq:]

time: 303 us -> 272 us (0.90)
  blocking collectives: 103 us -> 49.1 us
  starting transfers between devices: 40 us -> 49.1 us
  Pallas kernels: 24.8 us -> 31.2 us
  waiting for transfers between devices: 101 us -> 105 us
  local copies, waits for them, and re-layouts: 12.2 us -> 15.9 us
    all_gather x1 -> x0, blocking collectives: 83.9 us -> none  [local(): lax.all_gather(extra, AXES, axis=0).reshape(nz, n_parts * cond_count, LANES)]
    all_gather x2 -> x1, waiting for transfers between devices: 29.9 us -> 0.01 us  [gathered(): return lax.all_gather(share, ('z', 'y', 'c'), axis=0)]
    all_to_all x0 -> x1, blocking collectives: none -> 29.3 us  [coefficients(): sums = lax.all_to_all(sums, ('y', 'c', 'x'), 0, 0, tiled=True)]
    ppermute x5 -> x8, waiting for transfers between devices: 34.6 us -> 61.2 us  [along_z(): return lax.ppermute(array, 'z', pairs)]
    ppermute x5 -> x8, starting transfers between devices: 7.49 us -> 28.4 us  [along_z(): return lax.ppermute(array, 'z', pairs)]
    ppermute x2 -> x4, starting transfers between devices: 11 us -> 2.87 us  [the longest x1 2.02 us: local(): mate_b = lax.ppermute(own_b, 'x', flip)]
    all_to_all x1, waiting for transfers between devices: 0.01 us -> 6.54 us  [local(): lax.all_to_all(eigenvectors.reshape(group, part, columns), ('y', 'c'), 0,...]
    pallas_call x1 -> x2, Pallas kernels: 4.48 us -> 9.83 us  [the longest x1 5.86 us: make_chi(): pl.pallas_call(functools.partial(chi_kernel, early, n_freq, factor), out_...]
  transfers between devices with their start and end apart: 16 -> 19, of which waited for: 8 -> 12; matrix products, arithmetic and copies ran while one was open for 2% -> 4% of each run, Pallas kernels for 5% -> 8%
where the time goes in v5:
time: 272 us; the launch traced here: 271 us
  waiting for transfers between devices  105 us (39%)
  blocking collectives  49.1 us (18%)
  starting transfers between devices  49.1 us (18%)
  Pallas kernels  31.2 us (11%)
  local copies, waits for them, and re-layouts  15.9 us (6%)
  between operations  13.7 us (5%)
  other arithmetic  6.55 us (2%)
    ppermute x8, waiting for transfers between devices, along_z(): return lax.ppermute(array, 'z', pairs)  61.2 us
    all_to_all x1, blocking collectives, coefficients(): sums = lax.all_to_all(sums, ('y', 'c', 'x'), 0, 0, tiled=True)  29.3 us
    ppermute x8, starting transfers between devices, along_z(): return lax.ppermute(array, 'z', pairs)  28.4 us
    all_to_all x3, waiting for transfers between devices, coefficients(): sums = lax.all_to_all(sums, ('y', 'c', 'x'), 0, 0, tiled=True)  26.8 us
    pallas_call x4, Pallas kernels, project(): pl.pallas_call(functools.partial(project_kernel, segs, val_count, cond_co...  20.1 us
    all_to_all x1, blocking collectives, local(): unit = lax.all_to_all(packed, ('y', 'c', 'x'), 0, 0, tiled=True)  19.8 us
    unnamed x30, local copies, waits for them, and re-layouts  13.2 us
    all_to_all x3, starting transfers between devices, coefficients(): sums = lax.all_to_all(sums, ('y', 'c', 'x'), 0, 0, tiled=True)  12.7 us
  transfers between devices with their start and end apart: 19, of which 12 were waited for; matrix products, arithmetic and copies ran while one was open for 4% of the time, Pallas kernels for 8%

profile of v5, /device:TPU:0, one launch (start us, length us, event | category | flops | bytes accessed | tf_op | source)
XLA Modules:
  0.0 270.7 jit_solution(13676355648244253148)
XLA Ops:
  6.5 4.0 %pack.1 = bf16[8,16,3968]{2,1,0:T(8,128)(2,1)} custom-call(f32[4]{0:T(128)} %val_energy.1, f32[16]{0:T(128)} %cond_energy.1, s32[64]{0:T(128)} %val_slot.1, s32[64]{0:T(128)} %cond_slot.1, f32[4]{0:T(128)} %frequencies.1, bf16[16,24576]{1,0:T(8,128)(2,1)} %refs_1_.1, bf16[16,24576]{1,0:T(8,128)(2,1)} %refs_1_.1, bf16[4,24576]{1,0:T(4,128)(2,1)} %refs_3_.1, ...), custom_call_target="tpu_custom_call" | custom-call | tf_op jit(solution)/shard_map/pack/pallas_call | solution.py:77
  10.5 19.8 %all_to_all.30 = bf16[8,16,3968]{2,1,0:T(8,128)(2,1)} all-to-all(bf16[8,16,3968]{2,1,0:T(8,128)(2,1)} %pack.1), channel_id=1, replica_groups=mesh['z'=4,'y'=2,'c'=2,'x'=2] {'y','c','x'}, dimensions={0} | all-to-all | bytes 2031616 | tf_op jit(solution)/shard_map/all_to_all | solution.py:353
  30.3 3.7 %all-to-all-start.1 = ((bf16[4,3072,128]{2,1,0:T(8,128)(2,1)}), bf16[4,3072,128]{2,1,0:T(8,128)(2,1)S(1)}, u32[]{:S(2)}, u32[]{:S(2)}) async-start(bf16[4,3072,128]{2,1,0:T(8,128)(2,1)} %bitcast.53), calls=%async_computation.1 | async-start | bytes 6291456 | tf_op jit(solution)/shard_map/all_to_all | solution.py:355
  34.0 1.6 collective-permute-start.2
  35.6 3.9 %collective-permute-start = (bf16[128,3968]{1,0:T(8,128)(2,1)}, bf16[128,3968]{1,0:T(8,128)(2,1)}, u32[]{:S(2)}, u32[]{:S(2)}) collective-permute-start(bf16[128,3968]{1,0:T(8,128)(2,1)} %bitcast.40), channel_id=1, source_target_pairs={{0,8},{8,0},{16,24},{24,16},{1,9},{9,1},{17,25},{25,17},{2,10},{10... | collective-permute-start | bytes 3047432 | tf_op jit(solution)/shard_map/ppermute | solution.py:348
  39.6 1.3 collective-permute-start.3
  40.9 21.8 %collective-permute-done.refs_0_.refs_1_.refs_2_.refs_3_.refs_4_.refs_5_ = bf16[128,3968]{1,0:T(8,128)(2,1)} collective-permute-done((bf16[128,3968]{1,0:T(8,128)(2,1)}, bf16[128,3968]{1,0:T(8,128)(2,1)}, u32[]{:S(2)}, u32[]{:S(2)}) %collective-permute-start) | collective-permute-done | bytes 1015840 | tf_op jit(solution)/shard_map/ppermute | solution.py:348
  62.7 1.7 collective-permute-start.1
  64.4 6.5 %all-to-all-done.1.refs_5_.refs_6_.refs_7_.refs_8_ = bf16[4,3072,128]{2,1,0:T(8,128)(2,1)S(1)} async-done(((bf16[4,3072,128]{2,1,0:T(8,128)(2,1)}), bf16[4,3072,128]{2,1,0:T(8,128)(2,1)S(1)}, u32[]{:S(2)}, u32[]{:S(2)}) %all-to-all-start.1) | async-done | bytes 3145760 | tf_op jit(solution)/shard_map/all_to_all | solution.py:355
  70.9 5.3 %project.5 = f32[4,512,128]{2,1,0:T(8,128)S(1)} custom-call(bf16[128,3968]{1,0:T(8,128)(2,1)} %collective-permute-done.refs_0_.refs_1_.refs_2_.refs_3_.refs_4_.refs_5_, bf16[128,3968]{1,0:T(8,128)(2,1)} %collective-permute-done.refs_0_.refs_1_.refs_2_.refs_3_.refs_4_.refs_5_, ...), custom_call_target="tpu_custom_call" | custom-call | flops 1610612736 | bytes 4161536 | tf_op jit(solution)/shard_map/project/pallas_call | solution.py:190
  76.3 1.0 copy-done.9
  77.2 4.2 %all-to-all-start.3 = ((f32[8,256,128]{2,1,0:T(8,128)}), f32[8,256,128]{2,1,0:T(8,128)}, u32[]{:S(2)}, u32[]{:S(2)}) async-start(f32[8,256,128]{2,1,0:T(8,128)} %bitcast.47), calls=%async_computation.3 | async-start | bytes 2097152 | tf_op jit(solution)/shard_map/all_to_all | solution.py:391
  81.5 1.2 copy-done.1
  82.7 4.9 %project.4 = f32[4,512,128]{2,1,0:T(8,128)S(1)} custom-call(bf16[128,3968]{1,0:T(8,128)(2,1)S(1)} %bitcast.41, bf16[128,3968]{1,0:T(8,128)(2,1)S(1)} %bitcast.42, bf16[128,3968]{1,0:T(8,128)(2,1)S(1)} %bitcast.43, bf16[128,3968]{1,0:T(8,128)(2,1)S(1)} %bitcast.44, bf16[128,3968]{1,0:T(8,128)(2,1)S(1)} %bitcast.45, ...), custom_call_target="tpu_custom_call" | custom-call | flops 1610612736 | bytes 4161536 | tf_op jit(solution)/shard_map/project/pallas_call | solution.py:190
  87.6 1.0 copy-done.10
  88.6 7.8 %all-to-all-done.3 = f32[8,256,128]{2,1,0:T(8,128)} async-done(((f32[8,256,128]{2,1,0:T(8,128)}), f32[8,256,128]{2,1,0:T(8,128)}, u32[]{:S(2)}, u32[]{:S(2)}) %all-to-all-start.3) | async-done | bytes 1048608 | tf_op jit(solution)/shard_map/all_to_all | solution.py:391
  96.4 4.2 %all-to-all-start.2 = ((f32[8,256,128]{2,1,0:T(8,128)}), f32[8,256,128]{2,1,0:T(8,128)}, u32[]{:S(2)}, u32[]{:S(2)}) async-start(f32[8,256,128]{2,1,0:T(8,128)} %bitcast.48), calls=%async_computation.2 | async-start | bytes 2097152 | tf_op jit(solution)/shard_map/all_to_all | solution.py:391
  100.7 1.3 broadcast_select_fusion.1.refs_0_.refs_1_.refs_2_.refs_3_.refs_4_.refs_6_
  102.0 5.0 %project.6 = f32[4,512,128]{2,1,0:T(8,128)S(1)} custom-call(bf16[128,3968]{1,0:T(8,128)(2,1)S(1)} %broadcast_select_fusion.1.refs_0_.refs_1_.refs_2_.refs_3_.refs_4_.refs_6_, bf16[128,3968]{1,0:T(8,128)(2,1)S(1)} %broadcast_select_fusion.1.refs_0_.refs_1_.refs_2_.refs_3_.refs_4_.refs_6_, ...), custom_call_target="tpu_custom_call" | custom-call | flops 1610612736 | bytes 4161536 | tf_op jit(solution)/shard_map/project/pallas_call | solution.py:190
  107.0 0.9 copy-done.3
  107.9 1.0 copy-done.11
  108.9 6.7 %all-to-all-done.2 = f32[8,256,128]{2,1,0:T(8,128)} async-done(((f32[8,256,128]{2,1,0:T(8,128)}), f32[8,256,128]{2,1,0:T(8,128)}, u32[]{:S(2)}, u32[]{:S(2)}) %all-to-all-start.2) | async-done | bytes 1048608 | tf_op jit(solution)/shard_map/all_to_all | solution.py:391
  115.6 4.2 %all-to-all-start.4 = ((f32[8,256,128]{2,1,0:T(8,128)}), f32[8,256,128]{2,1,0:T(8,128)}, u32[]{:S(2)}, u32[]{:S(2)}) async-start(f32[8,256,128]{2,1,0:T(8,128)} %bitcast.49), calls=%async_computation.4 | async-start | bytes 2097152 | tf_op jit(solution)/shard_map/all_to_all | solution.py:391
  119.9 1.3 reduce_sum.40
  121.2 1.3 reduce_sum.39
  122.5 12.3 %all-to-all-done.4 = f32[8,256,128]{2,1,0:T(8,128)} async-done(((f32[8,256,128]{2,1,0:T(8,128)}), f32[8,256,128]{2,1,0:T(8,128)}, u32[]{:S(2)}, u32[]{:S(2)}) %all-to-all-start.4) | async-done | bytes 1048608 | tf_op jit(solution)/shard_map/all_to_all | solution.py:391
  134.8 1.3 reduce_sum.41
  137.5 1.3 collective-permute-start.5
  138.8 35.1 %collective-permute-done.5 = bf16[128,3968]{1,0:T(8,128)(2,1)S(1)} collective-permute-done((bf16[128,3968]{1,0:T(8,128)(2,1)}, bf16[128,3968]{1,0:T(8,128)(2,1)S(1)}, u32[]{:S(2)}, u32[]{:S(2)}) %collective-permute-start.5) | collective-permute-done | bytes 1015840 | tf_op jit(solution)/shard_map/ppermute | solution.py:348
  174.0 5.0 %project.7 = bf16[4,512,128]{2,1,0:T(8,128)(2,1)S(1)} custom-call(bf16[128,3968]{1,0:T(8,128)(2,1)S(1)} %broadcast_select_fusion.refs_0_.refs_1_.refs_2_.refs_3_.refs_4_.refs_7_, bf16[128,3968]{1,0:T(8,128)(2,1)S(1)} %broadcast_select_fusion.refs_0_.refs_1_.refs_2_.refs_3_.refs_4_.refs_7_, ...), custom_call_target="tpu_custom_call" | custom-call | flops 1610612736 | bytes 4161536 | tf_op jit(solution)/shard_map/project/pallas_call | solution.py:190
  179.0 29.3 %all_to_all.31 = bf16[8,256,128]{2,1,0:T(8,128)(2,1)} all-to-all(bf16[8,256,128]{2,1,0:T(8,128)(2,1)S(1)} %bitcast.50), channel_id=1, replica_groups=mesh['z'=4,'y'=2,'c'=2,'x'=2] {'y','c','x'}, dimensions={0} | all-to-all | bytes 1048576 | tf_op jit(solution)/shard_map/all_to_all | solution.py:391
  208.3 1.1 reduce_sum.42
  210.1 18.0 %collective-permute-start.11 = (bf16[256,128]{1,0:T(8,128)(2,1)S(1)}, bf16[256,128]{1,0:T(8,128)(2,1)S(1)}, u32[]{:S(2)}, u32[]{:S(2)}) collective-permute-start(bf16[256,128]{1,0:T(8,128)(2,1)S(1)} %collective-permute-done.8), channel_id=1, source_target_pairs={{0,24},{8,16},{16,8},{24,0},{1,25},{9,17},{17,9},{25,1},{2,26},{10... | collective-permute-start | bytes 196616 | tf_op jit(solution)/shard_map/ppermute | solution.py:348
  229.3 1.6 collective-permute-done.11
  230.9 2.4 collective-permute-done.10
  233.7 0.8 collective-permute-start.12
  235.2 0.7 constant_dynamic-update-slice_fusion.2
  236.5 3.9 %collective-permute-done.12 = bf16[4,256,128]{2,1,0:T(8,128)(2,1)S(1)} collective-permute-done((bf16[4,256,128]{2,1,0:T(8,128)(2,1)S(1)}, bf16[4,256,128]{2,1,0:T(8,128)(2,1)S(1)}, u32[]{:S(2)}, u32[]{:S(2)}) %collective-permute-start.12) | collective-permute-done | bytes 262176 | tf_op jit(solution)/shard_map/ppermute | solution.py:411
  240.4 0.9 constant_dynamic-update-slice_fusion
  241.3 2.0 collective-permute-start.6
  243.4 5.6 %collective-permute-done.4.refs_1_ = bf16[3,256,128]{2,1,0:T(8,128)(2,1)S(1)} collective-permute-done((bf16[3,256,128]{2,1,0:T(8,128)(2,1)S(1)}, bf16[3,256,128]{2,1,0:T(8,128)(2,1)S(1)}, u32[]{:S(2)}, u32[]{:S(2)}) %collective-permute-start.4) | collective-permute-done | bytes 196640 | tf_op jit(solution)/shard_map/ppermute | solution.py:413
  249.0 1.0 collective-permute-done.6
  250.0 1.3 weigh.1.refs_0_
  251.3 1.3 copy-done.7
  252.6 1.9 constant_dynamic-update-slice_fusion.5.refs_5_.refs_6_.refs_7_.refs_8_
  254.5 1.9 copy-done
  256.4 1.6 copy-done.8
  258.0 5.9 %chi.1 = f32[128,4,1024]{2,1,0:T(4,128)} custom-call(s32[4]{0:T(128)S(1)} %pad_add_fusion.scalars, bf16[4,512,512]{2,1,0:T(8,128)(2,1)S(1)} %copy-done.8, bf16[16,3,256,128]{3,2,1,0:T(8,128)(2,1)S(1)} %bitcast.35, bf16[16,3,256,128]{3,2,1,0:T(8,128)(2,1)S(1)} %bitcast.36, bf16[16,3,256,128]{3,2,1,0:T(8,128)(2,1)S(1)} %bitcast.37, ...), custom_call_target="tpu_custom_call" | custom-call | flops 2147483648 | bytes 6291456 | tf_op jit(solution)/shard_map/chi/pallas_call | solution.py:292
  (41 shorter events, 5.2 us)
Async XLA Ops:
  30.3 40.6 %all-to-all-start.1 = ((bf16[4,3072,128]{2,1,0:T(8,128)(2,1)}), bf16[4,3072,128]{2,1,0:T(8,128)(2,1)S(1)}, u32[]{:S(2)}, u32[]{:S(2)}) async-start(bf16[4,3072,128]{2,1,0:T(8,128)(2,1)} %bitcast.53), calls=%async_computation.1 | async-start | bytes 6291456 | tf_op jit(solution)/shard_map/all_to_all | solution.py:355
  34.0 5.5 %collective-permute-start.2 = (bf16[128,3968]{1,0:T(8,128)(2,1)}, bf16[128,3968]{1,0:T(8,128)(2,1)}, u32[]{:S(2)}, u32[]{:S(2)}) collective-permute-start(bf16[128,3968]{1,0:T(8,128)(2,1)} %bitcast.39), channel_id=1, source_target_pairs={{8,16},{16,8},{9,17},{17,9},{10,18},{18,10},{11,19},{19,11},{12,20... | collective-permute-start | bytes 3047432 | tf_op jit(solution)/shard_map/ppermute | solution.py:348
  35.6 27.0 %collective-permute-start = (bf16[128,3968]{1,0:T(8,128)(2,1)}, bf16[128,3968]{1,0:T(8,128)(2,1)}, u32[]{:S(2)}, u32[]{:S(2)}) collective-permute-start(bf16[128,3968]{1,0:T(8,128)(2,1)} %bitcast.40), channel_id=1, source_target_pairs={{0,8},{8,0},{16,24},{24,16},{1,9},{9,1},{17,25},{25,17},{2,10},{10... | collective-permute-start | bytes 3047432 | tf_op jit(solution)/shard_map/ppermute | solution.py:348
  39.6 61.1 %collective-permute-start.3 = (bf16[128,3968]{1,0:T(8,128)(2,1)}, bf16[128,3968]{1,0:T(8,128)(2,1)}, u32[]{:S(2)}, u32[]{:S(2)}) collective-permute-start(bf16[128,3968]{1,0:T(8,128)(2,1)} %collective-permute-done.2), channel_id=1, source_target_pairs={{8,0},{16,24},{9,1},{17,25},{10,2},{18,26},{11,3},{19,27},{12,4},{... | collective-permute-start | bytes 3047432 | tf_op jit(solution)/shard_map/ppermute | solution.py:348
  62.7 38.0 %collective-permute-start.1 = (bf16[128,3968]{1,0:T(8,128)(2,1)}, bf16[128,3968]{1,0:T(8,128)(2,1)}, u32[]{:S(2)}, u32[]{:S(2)}) collective-permute-start(bf16[128,3968]{1,0:T(8,128)(2,1)} %collective-permute-done.refs_0_.refs_1_.refs_2_.refs_3_.refs_4_.refs_5_), channel_id=1, source_target_pairs={{8,16},{16,8},{9,17},{17,9},{10,18},{18,10},{11,19},{19,11},{12,20... | collective-permute-start | bytes 3047432 | tf_op jit(solution)/shard_map/ppermute | solution.py:348
  76.3 1.0 copy-start.9
  77.2 19.2 %all-to-all-start.3 = ((f32[8,256,128]{2,1,0:T(8,128)}), f32[8,256,128]{2,1,0:T(8,128)}, u32[]{:S(2)}, u32[]{:S(2)}) async-start(f32[8,256,128]{2,1,0:T(8,128)} %bitcast.47), calls=%async_computation.3 | async-start | bytes 2097152 | tf_op jit(solution)/shard_map/all_to_all | solution.py:391
  81.5 1.2 copy-start.1
  87.6 1.0 copy-start.10
  96.4 19.2 %all-to-all-start.2 = ((f32[8,256,128]{2,1,0:T(8,128)}), f32[8,256,128]{2,1,0:T(8,128)}, u32[]{:S(2)}, u32[]{:S(2)}) async-start(f32[8,256,128]{2,1,0:T(8,128)} %bitcast.48), calls=%async_computation.2 | async-start | bytes 2097152 | tf_op jit(solution)/shard_map/all_to_all | solution.py:391
  107.0 1.0 copy-start.3
  107.9 1.0 copy-start.11
  115.6 19.2 %all-to-all-start.4 = ((f32[8,256,128]{2,1,0:T(8,128)}), f32[8,256,128]{2,1,0:T(8,128)}, u32[]{:S(2)}, u32[]{:S(2)}) async-start(f32[8,256,128]{2,1,0:T(8,128)} %bitcast.49), calls=%async_computation.4 | async-start | bytes 2097152 | tf_op jit(solution)/shard_map/all_to_all | solution.py:391
  119.8 134.6 %all-gather.3.cloned.1.call-start = ((), (), s32[]{:S(2)}) async-start(), calls=%async_computation.6 | async-start | bytes 3342336 | tf_op jit(solution)/shard_map/all_gather | solution.py:398
  136.1 0.7 collective-permute-start.7
  136.8 0.7 copy-start.12
  137.5 36.4 %collective-permute-start.5 = (bf16[128,3968]{1,0:T(8,128)(2,1)}, bf16[128,3968]{1,0:T(8,128)(2,1)S(1)}, u32[]{:S(2)}, u32[]{:S(2)}) collective-permute-start(bf16[128,3968]{1,0:T(8,128)(2,1)} %collective-permute-done.1), channel_id=1, source_target_pairs={{8,0},{16,24},{9,1},{17,25},{10,2},{18,26},{11,3},{19,27},{12,4},{... | collective-permute-start | bytes 3047432 | tf_op jit(solution)/shard_map/ppermute | solution.py:348
  174.0 5.0 %copy-start.5 = (bf16[128,3968]{1,0:T(8,128)(2,1)}, bf16[128,3968]{1,0:T(8,128)(2,1)S(1)}, u32[]{:S(2)}) copy-start(bf16[128,3968]{1,0:T(8,128)(2,1)S(1)} %broadcast_select_fusion.refs_0_.refs_1_.refs_2_.refs_3_.refs_4_.refs_7_) | copy-start | bytes 3047428
  179.0 71.0 %copy-start.2 = (bf16[8,16,3968]{2,1,0:T(8,128)(2,1)S(1)}, bf16[8,16,3968]{2,1,0:T(8,128)(2,1)}, u32[]{:S(2)}) copy-start(bf16[8,16,3968]{2,1,0:T(8,128)(2,1)} %all_to_all.30) | copy-start | bytes 3047428
  179.0 71.0 %copy-start.4 = (bf16[128,3968]{1,0:T(8,128)(2,1)S(1)}, bf16[128,3968]{1,0:T(8,128)(2,1)}, u32[]{:S(2)}) copy-start(bf16[128,3968]{1,0:T(8,128)(2,1)} %copy-done.3) | copy-start | bytes 3047428
  179.0 71.0 %copy-start.6 = (bf16[128,3968]{1,0:T(8,128)(2,1)S(1)}, bf16[128,3968]{1,0:T(8,128)(2,1)}, u32[]{:S(2)}) copy-start(bf16[128,3968]{1,0:T(8,128)(2,1)} %copy-done.5) | copy-start | bytes 3047428
  209.4 0.7 collective-permute-start.8
  210.1 20.8 %collective-permute-start.11 = (bf16[256,128]{1,0:T(8,128)(2,1)S(1)}, bf16[256,128]{1,0:T(8,128)(2,1)S(1)}, u32[]{:S(2)}, u32[]{:S(2)}) collective-permute-start(bf16[256,128]{1,0:T(8,128)(2,1)S(1)} %collective-permute-done.8), channel_id=1, source_target_pairs={{0,24},{8,16},{16,8},{24,0},{1,25},{9,17},{17,9},{25,1},{2,26},{10... | collective-permute-start | bytes 196616 | tf_op jit(solution)/shard_map/ppermute | solution.py:348
  228.1 5.2 %collective-permute-start.10 = (bf16[256,128]{1,0:T(8,128)(2,1)S(1)}, bf16[256,128]{1,0:T(8,128)(2,1)S(1)}, u32[]{:S(2)}, u32[]{:S(2)}) collective-permute-start(bf16[256,128]{1,0:T(8,128)(2,1)S(1)} %collective-permute-done.8), channel_id=1, source_target_pairs={{0,16},{8,24},{16,0},{24,8},{1,17},{9,25},{17,1},{25,9},{2,18},{10... | collective-permute-start | bytes 196616 | tf_op jit(solution)/shard_map/ppermute | solution.py:348
  228.1 5.5 %collective-permute-start.9 = (bf16[256,128]{1,0:T(8,128)(2,1)S(1)}, bf16[256,128]{1,0:T(8,128)(2,1)S(1)}, u32[]{:S(2)}, u32[]{:S(2)}) collective-permute-start(bf16[256,128]{1,0:T(8,128)(2,1)S(1)} %collective-permute-done.8), channel_id=1, source_target_pairs={{0,8},{8,0},{16,24},{24,16},{1,9},{9,1},{17,25},{25,17},{2,10},{10... | collective-permute-start | bytes 196616 | tf_op jit(solution)/shard_map/ppermute | solution.py:348
  233.7 6.8 %collective-permute-start.12 = (bf16[4,256,128]{2,1,0:T(8,128)(2,1)S(1)}, bf16[4,256,128]{2,1,0:T(8,128)(2,1)S(1)}, u32[]{:S(2)}, u32[]{:S(2)}) collective-permute-start(bf16[4,256,128]{2,1,0:T(8,128)(2,1)S(1)} %pad_maximum_fusion), channel_id=1, source_target_pairs={{0,4},{4,0},{1,5},{5,1},{2,6},{6,2},{3,7},{7,3},{8,12},{12,8},{9,1... | collective-permute-start | bytes 786440 | tf_op jit(solution)/shard_map/ppermute | solution.py:411
  241.3 11.3 %collective-permute-start.13 = (bf16[8,256,128]{2,1,0:T(8,128)(2,1)}, bf16[8,256,128]{2,1,0:T(8,128)(2,1)}, u32[]{:S(2)}, u32[]{:S(2)}) collective-permute-start(bf16[8,256,128]{2,1,0:T(8,128)(2,1)} %get-tuple-element.7), channel_id=1, source_target_pairs={{0,2},{2,0},{1,3},{3,1},{4,6},{6,4},{5,7},{7,5},{8,10},{10,8},{9,1... | collective-permute-start | bytes 1572872 | tf_op jit(solution)/shard_map/ppermute | solution.py:412
  241.3 7.7 %collective-permute-start.4 = (bf16[3,256,128]{2,1,0:T(8,128)(2,1)S(1)}, bf16[3,256,128]{2,1,0:T(8,128)(2,1)S(1)}, u32[]{:S(2)}, u32[]{:S(2)}) collective-permute-start(bf16[3,256,128]{2,1,0:T(8,128)(2,1)S(1)} %pad_maximum_fusion.1.refs_0_), channel_id=1, source_target_pairs={{0,1},{1,0},{2,3},{3,2},{4,5},{5,4},{6,7},{7,6},{8,9},{9,8},{10,11... | collective-permute-start | bytes 589832 | tf_op jit(solution)/shard_map/ppermute | solution.py:413
  241.3 8.7 %collective-permute-start.6 = (bf16[256,128]{1,0:T(8,128)(2,1)S(1)}, bf16[256,128]{1,0:T(8,128)(2,1)S(1)}, u32[]{:S(2)}, u32[]{:S(2)}) collective-permute-start(bf16[256,128]{1,0:T(8,128)(2,1)S(1)} %reduce_sum.42), channel_id=1, source_target_pairs={{0,1},{1,0},{2,3},{3,2},{4,5},{5,4},{6,7},{7,6},{8,9},{9,8},{10,11... | collective-permute-start | bytes 196616 | tf_op jit(solution)/shard_map/ppermute | solution.py:414
  251.3 1.3 copy-start.7
  254.5 1.9 copy-start
  256.4 1.6 copy-start.8
Sparse Core Ops, SparseCore 0:
  137.6 60.1 all-gather.2

commit v6 on v5

v6 whole, which is shorter than its diff:
```python
import functools
import math

import jax
import jax.numpy as jnp
from jax import lax
from jax.experimental import pallas as pl
from jax.experimental.pallas import tpu as pltpu
from jax.sharding import Mesh
from jax.sharding import PartitionSpec as P

LANES = 128
AXES = ("z", "y", "c", "x")


def pack_kernel(nx, part, seg, val_energy, cond_energy, val_slot, cond_slot, frequencies, *refs):
    conds = refs[:nx]
    vals = refs[nx : 2 * nx]
    out, extra = refs[2 * nx :]
    val_count = val_energy.shape[0]
    cond_count = cond_energy.shape[0]
    n_freq = frequencies.shape[0]
    stride = n_freq + 1

    @pl.when(pl.program_id(0) == 0)
    def _():
        row = lax.broadcasted_iota(jnp.int32, (cond_count, LANES), 0)
        lane = lax.broadcasted_iota(jnp.int32, (cond_count, LANES), 1)
        cond_level = jnp.zeros((cond_count, LANES), jnp.float32)
        for c in range(cond_count):
            cond_level = jnp.where(row == c, cond_energy[c], cond_level)
        val_level = jnp.zeros((cond_count, LANES), jnp.float32)
        freq = jnp.zeros((cond_count, LANES), jnp.float32)
        is_count = lane < 0
        for v in range(val_count):
            for f in range(stride):
                here = lane == v * stride + f
                val_level = jnp.where(here, val_energy[v], val_level)
                if f < n_freq:
                    freq = jnp.where(here, frequencies[f], freq)
                else:
                    is_count = is_count | here
        gap = cond_level - val_level
        weight = 4.0 * gap / (gap * gap + freq * freq)

        def add(p, number):
            here = (row == cond_slot[p]) & (lane == val_slot[p] * stride + n_freq)
            return number + jnp.where(here, 1.0, 0.0)

        number = lax.fori_loop(0, val_slot.shape[0], add, jnp.zeros((cond_count, LANES), jnp.float32))
        used = lane < val_count * stride
        extra[...] = jnp.where(used, jnp.where(is_count, number, weight), 0.0).astype(jnp.bfloat16)

    for t in range(nx):
        out[t, :, :part] = conds[t][...]
        val = vals[t][...].astype(jnp.float32)
        pieces = [val[:, k * seg : (k + 1) * seg] for k in range(part // seg)]
        out[t, :, part : part + seg] = jnp.concatenate(pieces, axis=0).astype(jnp.bfloat16)
        out[t, :, part + seg :] = extra[...]


def pack(val_orbitals, cond_orbitals, val_energy, cond_energy, val_slot, cond_slot, frequencies, nx, group):
    val_count, n_grid = val_orbitals.shape
    cond_count = cond_orbitals.shape[0]
    n_freq = frequencies.shape[0]
    n_parts = group * nx
    part = n_grid // n_parts
    segs = cond_count // val_count
    seg = part // segs
    width = part + seg + LANES
    if seg % LANES == 0:
        smem = pl.BlockSpec(memory_space=pltpu.SMEM)
        piece = lambda rows: [
            pl.BlockSpec((rows, part), functools.partial(lambda t, i: (0, t * group + i), t))
            for t in range(nx)
        ]
        return pl.pallas_call(
            functools.partial(pack_kernel, nx, part, seg),
            out_shape=jax.ShapeDtypeStruct((n_parts, cond_count, width), jnp.bfloat16),
            grid=(group,),
            in_specs=[smem] * 5 + piece(cond_count) + piece(val_count),
            out_specs=pl.BlockSpec((nx, cond_count, width), lambda i: (i, 0, 0)),
            scratch_shapes=[pltpu.VMEM((cond_count, LANES), jnp.bfloat16)],
            name="pack",
        )(
            val_energy,
            cond_energy,
            val_slot,
            cond_slot,
            frequencies,
            *([cond_orbitals] * nx),
            *([val_orbitals] * nx),
        )
    gap = cond_energy[:, None] - val_energy[None, :]
    weights = (
        4.0 * gap[:, :, None] / (gap[:, :, None] ** 2 + frequencies[None, None, :] ** 2)
    ).astype(jnp.bfloat16)
    chosen = (cond_slot[:, None, None] == jnp.arange(cond_count, dtype=jnp.int32)[None, :, None]) & (
        val_slot[:, None, None] == jnp.arange(val_count, dtype=jnp.int32)[None, None, :]
    )
    counts = jnp.sum(chosen.astype(jnp.float32), axis=0).astype(jnp.bfloat16)
    extra = jnp.concatenate([weights, counts[:, :, None]], axis=2).reshape(
        cond_count, val_count * (n_freq + 1)
    )
    extra = jnp.pad(extra, ((0, 0), (0, LANES - extra.shape[1])))
    cond_parts = cond_orbitals.reshape(cond_count, nx, group, part).transpose(2, 1, 0, 3)
    val_parts = val_orbitals.reshape(val_count, nx, group, segs, seg).transpose(2, 1, 3, 0, 4)
    return jnp.concatenate(
        [
            cond_parts.reshape(n_parts, cond_count, part),
            val_parts.reshape(n_parts, cond_count, seg),
            jnp.broadcast_to(extra, (n_parts,) + extra.shape),
        ],
        axis=2,
    )


def project_kernel(segs, val_count, cond_count, place, *refs):
    conds = refs[:segs]
    val = refs[segs]
    eigs = refs[segs + 1 : 5 * segs + 1]
    keep, send, density, total = refs[5 * segs + 1 :]
    rows = val.shape[0]
    blocks = rows // cond_count
    columns = keep.shape[-1]
    half = keep.shape[-2]
    turn = place[0] * 2

    for k in range(segs):

        @pl.loop(0, blocks)
        def _(j):
            at = pl.ds(pl.multiple_of(j * cond_count, cond_count), cond_count)
            c = conds[k][at, :].astype(jnp.float32)
            vals = val[at, :].astype(jnp.float32)
            for v in range(val_count):
                row = k * val_count + v
                product = (c * vals[row : row + 1, :]).astype(jnp.bfloat16)
                start = lax.bitwise_xor(v, turn) * rows + j * cond_count
                density[pl.ds(pl.multiple_of(start, cond_count), cond_count), :] = product

        eig = jnp.concatenate([eigs[4 * k + q][...] for q in range(4)], axis=1)
        sums = jnp.dot(density[...], eig, preferred_element_type=jnp.float32)
        if k == 0:

            @pl.when(pl.program_id(0) == 0)
            def _():
                total[...] = sums

            @pl.when(pl.program_id(0) > 0)
            def _():
                total[...] += sums
        else:
            total[...] += sums

    @pl.when(pl.program_id(0) == pl.num_programs(0) - 1)
    def _():
        for q in range(4):
            out = send if q % 2 else keep
            for h in range(2):
                out[q // 2, h] = total[h * half : (h + 1) * half, q * columns : (q + 1) * columns]


def project(unit, eigs, place, val_count, cond_count):
    part, columns = eigs[0].shape
    segs = cond_count // val_count
    seg = part // segs
    rows = unit.shape[0]
    half = rows * val_count // 2
    width = math.gcd(seg, 384)
    steps = seg // width
    in_specs = (
        [
            pl.BlockSpec((rows, width), functools.partial(lambda k, i, place: (0, k * steps + i), k))
            for k in range(segs)
        ]
        + [pl.BlockSpec((rows, width), lambda i, place: (0, segs * steps + i))]
        + [
            pl.BlockSpec((width, columns), functools.partial(lambda k, i, place: (k * steps + i, 0), k))
            for k in range(segs)
            for q in range(4)
        ]
    )
    shape = (2, 2, half, columns)
    out = jax.ShapeDtypeStruct(shape, jnp.float32)
    out_spec = pl.BlockSpec(shape, lambda i, place: (0, 0, 0, 0))
    return pl.pallas_call(
        functools.partial(project_kernel, segs, val_count, cond_count),
        out_shape=[out, out],
        grid_spec=pltpu.PrefetchScalarGridSpec(
            num_scalar_prefetch=1,
            grid=(steps,),
            in_specs=in_specs,
            out_specs=[out_spec, out_spec],
            scratch_shapes=[
                pltpu.VMEM((2 * half, width), jnp.bfloat16),
                pltpu.VMEM((2 * half, 4 * columns), jnp.float32),
            ],
        ),
        compiler_params=pltpu.CompilerParams(vmem_limit_bytes=32 * 1024 * 1024),
        cost_estimate=pl.CostEstimate(
            flops=16 * half * part * columns,
            bytes_accessed=2 * (unit.size + 4 * part * columns),
            transcendentals=0,
        ),
        name="project",
    )(place, *([unit] * (segs + 1)), *(list(eigs) * segs))


def weigh_kernel(slots, n_freq, place, *refs):
    owns = refs[:slots]
    mates = refs[slots : 2 * slots]
    scales = refs[2 * slots : 3 * slots]
    out = refs[-1]
    rows, columns = owns[0].shape
    stride = n_freq + 1
    width = scales[0].shape[0]
    mine = place[0]
    for k in range(slots):
        scale = scales[k][...].astype(jnp.float32).T
        own = owns[k][...].astype(jnp.float32).T
        mate = mates[k][...].astype(jnp.float32).T
        for h in range(2):
            coeffs = jnp.where(mine == h, own, mate)
            for at in range(0, rows, width):
                v = (h * rows + at) // width
                number = scale[v * stride + n_freq : v * stride + n_freq + 1, :]
                for f in range(n_freq):
                    one = scale[v * stride + f : v * stride + f + 1, :] * number
                    out[k, f * columns : (f + 1) * columns, h * rows + at : h * rows + at + width] = (
                        coeffs[:, at : at + width] * one
                    ).astype(jnp.bfloat16)


def weigh(owns, mates, units, place, n_freq):
    slots = len(owns)
    rows, columns = owns[0].shape
    width = units[0].shape[0]
    last = units[0].shape[1] // LANES - 1
    shape = (slots, n_freq * columns, 2 * rows)
    return pl.pallas_call(
        functools.partial(weigh_kernel, slots, n_freq),
        out_shape=jax.ShapeDtypeStruct(shape, jnp.bfloat16),
        grid_spec=pltpu.PrefetchScalarGridSpec(
            num_scalar_prefetch=1,
            grid=(1,),
            in_specs=[pl.BlockSpec((rows, columns), lambda i, place: (0, 0))] * (2 * slots)
            + [pl.BlockSpec((width, LANES), lambda i, place: (0, last))] * slots,
            out_specs=pl.BlockSpec(shape, lambda i, place: (0, 0, 0)),
        ),
        compiler_params=pltpu.CompilerParams(vmem_limit_bytes=24 * 1024 * 1024),
        cost_estimate=pl.CostEstimate(
            flops=2 * math.prod(shape), bytes_accessed=3 * math.prod(shape), transcendentals=0
        ),
        name="weigh",
    )(place, *owns, *mates, *units)


def chi_kernel(early, late, n_freq, factor, scalars, *refs):
    weighted = refs[0]
    rights_a = refs[1:5]
    rights_b = refs[5 : 5 + 4 * late]
    out = refs[5 + 4 * late]
    columns = out.shape[0]
    core = scalars[2]
    shift = lax.bitwise_xor(scalars[0], scalars[3] + pl.program_id(0) // 2)
    left, right = [], []
    for r in range(early + late):
        left.append(weighted[lax.bitwise_xor(shift, r)])
        for h in range(2):
            if r < early:
                pair = [rights_a[2 * h + c][0, r] for c in range(2)]
            else:
                at = 4 * (r - early) + 2 * h
                own, mate = rights_b[at][0], rights_b[at + 1][0]
                pair = [jnp.where(core == c, own, mate) for c in range(2)]
            right.append(jnp.concatenate(pair, axis=1))
    chi = jnp.dot(
        jnp.concatenate(left, axis=1),
        jnp.concatenate(right, axis=0),
        preferred_element_type=jnp.float32,
    )
    for f in range(n_freq):
        out[:, f, :] = chi[f * columns : (f + 1) * columns, :] * factor


def make_chi(weighted, right_a, rights_b, scalars, n_freq, factor):
    members, early, rows, columns = right_a.shape
    tiles = members // 4
    late = len(rights_b)

    def near(h, i, scalars):
        z = lax.bitwise_xor(scalars[0], h * 2 + i // 2)
        y = lax.bitwise_xor(scalars[1], lax.rem(i, 2))
        return (y * 4 + z, 0, 0)

    return pl.pallas_call(
        functools.partial(chi_kernel, early, late, n_freq, factor),
        out_shape=jax.ShapeDtypeStruct((columns, n_freq, tiles * 2 * columns), jnp.float32),
        grid_spec=pltpu.PrefetchScalarGridSpec(
            num_scalar_prefetch=1,
            grid=(tiles,),
            in_specs=[pl.BlockSpec(weighted.shape, lambda i, scalars: (0, 0, 0))]
            + [
                pl.BlockSpec(
                    (1, early, rows, columns),
                    functools.partial(
                        lambda h, c, i, scalars: (h * tiles * 2 + i * 2 + c, 0, 0, 0), h, c
                    ),
                )
                for h in range(2)
                for c in range(2)
            ]
            + [
                pl.BlockSpec((1, rows, columns), functools.partial(near, h))
                for r in range(late)
                for h in range(2)
                for c in range(2)
            ],
            out_specs=pl.BlockSpec((columns, n_freq, 2 * columns), lambda i, scalars: (0, 0, i)),
        ),
        compiler_params=pltpu.CompilerParams(vmem_limit_bytes=32 * 1024 * 1024),
        cost_estimate=pl.CostEstimate(
            flops=2 * weighted.size * tiles * 2 * columns,
            bytes_accessed=2 * (early + late) * members * rows * columns
            + 4 * columns * n_freq * tiles * 2 * columns,
            transcendentals=0,
        ),
        name="chi",
    )(scalars, weighted, *([right_a] * 4), *[a for pair in rights_b for a in pair * 2])


def fast(shape, unit, eigenvectors, part, val_count, cond_count, n_freq, factor):
    nz, ny, nc, nx = shape
    z, y, c, x = [lax.axis_index(name).astype(jnp.int32) for name in AXES]
    columns = eigenvectors.shape[1]
    places = [(i, j, k, t) for i in range(nz) for j in range(ny) for k in range(nc) for t in range(nx)]
    number = {place: at for at, place in enumerate(places)}

    def send(array, target):
        pairs = [(number[place], target(*place)) for place in places]
        return lax.ppermute(
            array, AXES, [(source, number[to]) for source, to in pairs if to is not None]
        )

    def along_z(array, moves):
        moves = dict(moves)
        return send(array, lambda i, j, k, t: (moves[i], j, k, t) if i in moves else None)

    here = y * nc + c
    eigs = []
    for k in range(ny * nc):
        at = lax.bitwise_xor(here, k) * part
        rows = lax.dynamic_slice_in_dim(eigenvectors, at, part, 0)
        eigs.append(
            send(rows, functools.partial(lambda q, i, j, k, t: (i, j ^ (q // 2), k ^ (q % 2), t), k))
            if k
            else rows
        )

    inner = (z == 1) | (z == 2)
    near = along_z(unit, [(0, 1), (1, 0), (2, 3), (3, 2)])
    middle = along_z(unit, [(1, 2), (2, 1)])
    across = along_z(near, [(1, 2), (2, 1)])
    outward = along_z(middle, [(1, 0), (2, 3)])
    far = along_z(across, [(1, 0), (2, 3)])
    units = [unit, near, jnp.where(inner, across, outward), jnp.where(inner, middle, far)]

    place = x[None]

    def coefficients(unit):
        keep, away = project(unit, eigs, place, val_count, cond_count)
        sums = keep + send(away, lambda i, j, k, t: (i, j, 1 - k, t))
        total = sums[0, 0] + send(sums[0, 1], lambda i, j, k, t: (i, j, k, 1 - t))
        total = total + send(sums[1, 0], lambda i, j, k, t: (i, 1 - j, k, t))
        total = total + send(sums[1, 1], lambda i, j, k, t: (i, 1 - j, k, 1 - t))
        return total.astype(jnp.bfloat16)

    def mate(own):
        return send(own, lambda i, j, k, t: (i, j, k, 1 - t))

    def share(own, m):
        return send(own, lambda i, j, k, t: ((2 * t + i % 2) ^ m, j, k, i // 2))

    def spread(own):
        held = jnp.stack([share(own, m) for m in range(nz)])
        held = jnp.concatenate([held, send(held, lambda i, j, k, t: (i, 1 - j, k, t))])
        return held, send(held, lambda i, j, k, t: (i, j, 1 - k, t))

    owns = [coefficients(units[k]) for k in range(2)]
    share_a = share(jnp.stack(owns), 0)
    right_a = lax.all_gather(share_a, ("z", "y", "c"), axis=0)
    mates = [mate(own) for own in owns]
    units[3], _ = lax.optimization_barrier((units[3], (share_a, mates)))
    rights_b = []
    for k in range(2, nz):
        own = coefficients(units[k])
        rights_b.append(spread(own))
        owns.append(own)
        mates.append(mate(own))
    weighted = weigh(owns, mates, units, place, n_freq)
    scalars = jnp.stack([z, y, c, 2 * x])
    return make_chi(weighted, right_a, rights_b, scalars, n_freq, factor)


def plain(shape, unit, eigenvectors, part, val_count, cond_count, n_freq, factor):
    nz, ny, nc, nx = shape
    z = lax.axis_index("z").astype(jnp.int32)
    x = lax.axis_index("x").astype(jnp.int32)
    group = ny * nc
    n_parts = group * nx
    segs = cond_count // val_count
    seg = part // segs
    columns = eigenvectors.shape[1]
    zfold = nz // nx
    eigs = lax.all_to_all(
        eigenvectors.reshape(group, part, columns), ("y", "c"), 0, 0, tiled=True
    )
    every = lax.all_gather(unit, "z", axis=0)

    def coefficients(unit):
        cond = unit[:, :part].reshape(1, n_parts, cond_count, segs, seg)
        val = unit[:, part : part + seg].reshape(n_parts, segs, val_count, seg)
        val = val.transpose(2, 0, 1, 3)[:, :, None]
        density = (cond.astype(jnp.float32) * val.astype(jnp.float32)).astype(jnp.bfloat16)
        sums = jnp.einsum(
            "pg,qgs->qps", density.reshape(-1, part), eigs, preferred_element_type=jnp.float32
        )
        sums = sums.reshape(n_parts, -1, columns)
        sums = lax.all_to_all(sums, ("y", "c", "x"), 0, 0, tiled=True)
        return jnp.sum(sums, axis=0).astype(jnp.bfloat16)

    own = jnp.stack([coefficients(every[k]) for k in range(nz)])
    lefts = lax.all_gather(own, "x", axis=0)
    perm = []
    for s in range(nz):
        for q in range(group):
            for t in range(nx):
                target = ((s % zfold + zfold * t) * group + q) * nx + s // zfold
                perm.append(((s * group + q) * nx + t, target))
    share = lax.ppermute(own, AXES, perm)
    right = lax.all_gather(share, ("z", "y", "c"), axis=0)
    rows = own.shape[1]
    total = 0.0
    for k in range(nz):
        scale = every[k][:, part + seg : part + seg + val_count * (n_freq + 1)].astype(jnp.float32)
        scale = scale.reshape(n_parts * cond_count, val_count, n_freq + 1).transpose(1, 0, 2)
        scale = scale.reshape(nx, rows, n_freq + 1)
        scale = scale[..., :n_freq] * scale[..., n_freq:]
        weighted = (lefts[:, k, :, :, None].astype(jnp.float32) * scale[:, :, None, :]).astype(
            jnp.bfloat16
        )
        weighted = weighted.reshape(nx * rows, columns * n_freq)
        piece = right[:, k].reshape(nx, zfold * group, rows, columns)
        piece = piece.transpose(0, 2, 1, 3).reshape(nx * rows, zfold * group * columns)
        total = total + lax.dot_general(
            weighted, piece, (((0,), (0,)), ((), ())), preferred_element_type=jnp.float32
        )
    return (total * factor).reshape(columns, n_freq, zfold * group * columns)


def local(
    shape,
    val_orbitals,
    cond_orbitals,
    val_energy,
    cond_energy,
    val_slot,
    cond_slot,
    eigenvectors,
    frequencies,
):
    nz, ny, nc, nx = shape
    val_count, n_grid = val_orbitals.shape
    cond_count = cond_orbitals.shape[0]
    n_parts = ny * nc * nx
    part = n_grid // n_parts
    seg = part * val_count // cond_count
    columns = eigenvectors.shape[1]
    factor = -1.0 / math.sqrt(val_slot.shape[0] * nz * n_parts)
    packed = pack(
        val_orbitals,
        cond_orbitals,
        val_energy,
        cond_energy,
        val_slot,
        cond_slot,
        frequencies,
        nx,
        ny * nc,
    )
    unit = lax.all_to_all(packed, ("y", "c", "x"), 0, 0, tiled=True)
    unit = unit.reshape(n_parts * cond_count, part + seg + LANES)
    on_tiles = columns % LANES == 0 and seg % LANES == 0
    run = fast if on_tiles and nx == 2 and nz == 4 and val_count == 4 else plain
    return run(
        shape, unit, eigenvectors, part, val_count, cond_count, frequencies.shape[0], factor
    )


def solution(mesh):
    n_pair = mesh.shape["pair"]
    n_proj = mesh.shape["proj"]
    shape = (n_pair // 4, 2, 2, n_proj)
    grid = Mesh(mesh.devices.reshape(shape), AXES)
    return jax.shard_map(
        functools.partial(local, shape),
        mesh=grid,
        in_specs=(
            P(AXES, None),
            P(AXES, None),
            P(AXES),
            P(AXES),
            P(AXES),
            P(AXES),
            P("x", ("z", "y", "c")),
            P(),
        ),
        out_specs=P(("z", "y", "c"), None, "x"),
        check_vma=False,
    )
```

time: 272 us -> 208 us (0.76)
  blocking collectives: 49.1 us -> 0 us
  waiting for transfers between devices: 105 us -> 88.9 us
  starting transfers between devices: 49.1 us -> 55.3 us
  local copies, waits for them, and re-layouts: 15.9 us -> 11.4 us
    all_to_all x2 -> x0, blocking collectives: 49.1 us -> none  [the longest x1 29.3 us: coefficients(): sums = lax.all_to_all(sums, ('y', 'c', 'x'), 0, 0, tiled=True)]
    all_to_all x4 -> x1, waiting for transfers between devices: 33.3 us -> 14.6 us  [local(): unit = lax.all_to_all(packed, ('y', 'c', 'x'), 0, 0, tiled=True)]
    ppermute x14 -> x41, starting transfers between devices: 32.6 us -> 50.1 us  [send(): lax.ppermute(array, AXES, [(source, number[to]) for source, to in pairs i...]
    all_to_all x4 -> x1, starting transfers between devices: 16.4 us -> 5.17 us  [local(): unit = lax.all_to_all(packed, ('y', 'c', 'x'), 0, 0, tiled=True)]
    unnamed x30 -> x26, local copies, waits for them, and re-layouts: 13.2 us -> 7.95 us
    reduce_sum x4 -> x0, other arithmetic: 4.96 us -> none  [coefficients(): return jnp.sum(sums.astype(jnp.float32), axis=0).astype(jnp.bfloat16)]
    dynamic_slice x0 -> x1, local copies, waits for them, and re-layouts: none -> 3.29 us  [fast(): rows = lax.dynamic_slice_in_dim(eigenvectors, at, part, 0)]
    ppermute x14 -> x41, waiting for transfers between devices: 71.7 us -> 74.3 us  [send(): lax.ppermute(array, AXES, [(source, number[to]) for source, to in pairs i...]
  transfers between devices with their start and end apart: 19 -> 43, of which waited for: 12 -> 18; matrix products, arithmetic and copies ran while one was open for 4% -> 6% of each run, Pallas kernels for 8% -> 11%
where the time goes in v6:
time: 208 us; the launch traced here: 207 us
  waiting for transfers between devices  88.9 us (43%)
  starting transfers between devices  55.3 us (27%)
  Pallas kernels  32.1 us (15%)
  between operations  13.8 us (7%)
  local copies, waits for them, and re-layouts  11.4 us (5%)
  other arithmetic  5.28 us (3%)
    ppermute x41, waiting for transfers between devices, send(): lax.ppermute(array, AXES, [(source, number[to]) for source, to in pairs i...  74.3 us
    ppermute x41, starting transfers between devices, send(): lax.ppermute(array, AXES, [(source, number[to]) for source, to in pairs i...  50.1 us
    pallas_call x4, Pallas kernels, project(): pl.pallas_call(functools.partial(project_kernel, segs, val_count, cond_co...  21 us
    all_to_all x1, waiting for transfers between devices, local(): unit = lax.all_to_all(packed, ('y', 'c', 'x'), 0, 0, tiled=True)  14.6 us
    unnamed x26, local copies, waits for them, and re-layouts  7.95 us
    pallas_call x1, Pallas kernels, make_chi(): pl.pallas_call(functools.partial(chi_kernel, early, late, n_freq, factor)...  5.88 us
    all_to_all x1, starting transfers between devices, local(): unit = lax.all_to_all(packed, ('y', 'c', 'x'), 0, 0, tiled=True)  5.17 us
  transfers between devices with their start and end apart: 43, of which 18 were waited for; matrix products, arithmetic and copies ran while one was open for 6% of the time, Pallas kernels for 11%

profile of v6, /device:TPU:0, one launch (start us, length us, event | category | flops | bytes accessed | tf_op | source)
XLA Modules:
  0.0 206.9 jit_solution(2632032794641842628)
XLA Ops:
  6.5 4.0 %pack.1 = bf16[8,16,3968]{2,1,0:T(8,128)(2,1)} custom-call(f32[4]{0:T(128)} %val_energy.1, f32[16]{0:T(128)} %cond_energy.1, s32[64]{0:T(128)} %val_slot.1, s32[64]{0:T(128)} %cond_slot.1, f32[4]{0:T(128)} %frequencies.1, bf16[16,24576]{1,0:T(8,128)(2,1)} %refs_1_.1, bf16[16,24576]{1,0:T(8,128)(2,1)} %refs_1_.1, bf16[4,24576]{1,0:T(4,128)(2,1)} %refs_3_.1, ...), custom_call_target="tpu_custom_call" | custom-call | tf_op jit(solution)/shard_map/pack/pallas_call | solution.py:77
  10.5 5.2 %all-to-all-start = ((bf16[8,16,3968]{2,1,0:T(8,128)(2,1)}), bf16[8,16,3968]{2,1,0:T(8,128)(2,1)}, u32[]{:S(2)}, u32[]{:S(2)}) async-start(bf16[8,16,3968]{2,1,0:T(8,128)(2,1)} %pack.1), calls=%async_computation | async-start | bytes 2031616 | tf_op jit(solution)/shard_map/all_to_all | solution.py:492
  15.8 14.6 %all-to-all-done = bf16[8,16,3968]{2,1,0:T(8,128)(2,1)} async-done(((bf16[8,16,3968]{2,1,0:T(8,128)(2,1)}), bf16[8,16,3968]{2,1,0:T(8,128)(2,1)}, u32[]{:S(2)}, u32[]{:S(2)}) %all-to-all-start) | async-done | bytes 1015840 | tf_op jit(solution)/shard_map/all_to_all | solution.py:492
  30.4 2.0 collective-permute-start.7
  32.4 1.6 collective-permute-start.13
  34.0 3.3 %constant_dynamic-slice_fusion = (bf16[3072,128]{1,0:T(8,128)(2,1)}, bf16[3072,128]{1,0:T(8,128)(2,1)}, bf16[3072,128]{1,0:T(8,128)(2,1)S(1)}, bf16[3072,128]{1,0:T(8,128)(2,1)}) fusion(bf16[12288,128]{1,0:T(8,128)(2,1)} %param.14, s32[]{:T(128)S(6)} %select_n.27, s32[]{:T(128)S(6)} %select_n.25, s32[]{:T(128)S(6)} %select_n.24, s32[]{:T(128)S(6)} %select_n.26), kind=kLoop, calls=%fused_computation.47 | loop fusion | bytes 6291472 | tf_op jit(solution)/shard_map/dynamic_slice | solution.py:354
  37.9 1.3 collective-permute-start.2
  39.1 15.8 %collective-permute-done.7.refs_0_.refs_1_.refs_2_.refs_3_.refs_4_.refs_9_ = bf16[128,3968]{1,0:T(8,128)(2,1)} collective-permute-done((bf16[128,3968]{1,0:T(8,128)(2,1)}, bf16[128,3968]{1,0:T(8,128)(2,1)}, u32[]{:S(2)}, u32[]{:S(2)}) %collective-permute-start.7) | collective-permute-done | bytes 1015840 | tf_op jit(solution)/shard_map/ppermute | solution.py:342
  55.0 1.6 collective-permute-start.12
  56.6 1.3 collective-permute-start.14
  57.9 16.0 %collective-permute-done.2.refs_8_.refs_12_.refs_16_.refs_20_ = bf16[3072,128]{1,0:T(8,128)(2,1)S(1)} collective-permute-done((bf16[3072,128]{1,0:T(8,128)(2,1)}, bf16[3072,128]{1,0:T(8,128)(2,1)S(1)}, u32[]{:S(2)}, u32[]{:S(2)}) %collective-permute-start.2) | collective-permute-done | bytes 786464 | tf_op jit(solution)/shard_map/ppermute | solution.py:342
  73.9 6.1 %project.4 = (f32[2,2,256,128]{3,2,1,0:T(8,128)S(1)}, f32[2,2,256,128]{3,2,1,0:T(8,128)}) custom-call(s32[1]{0:T(128)} %bitcast.4.place, bf16[128,3968]{1,0:T(8,128)(2,1)} %bitcast.5.refs_0_.refs_1_.refs_2_.refs_3_.refs_4_.refs_8_, bf16[128,3968]{1,0:T(8,128)(2,1)} %bitcast.5.refs_0_.refs_1_.refs_2_.refs_3_.refs_4_.refs_8_, ...), custom_call_target="tpu_custom_call" | custom-call | flops 1610612736 | bytes 4161536 | tf_op jit(solution)/shard_map/project/pallas_call | solution.py:187
  81.5 1.9 collective-permute-done.3
  85.7 1.5 collective-permute-start.5
  88.2 5.4 %project.5 = (f32[2,2,256,128]{3,2,1,0:T(8,128)S(1)}, f32[2,2,256,128]{3,2,1,0:T(8,128)S(1)}) custom-call(s32[1]{0:T(128)} %bitcast.4.place, bf16[128,3968]{1,0:T(8,128)(2,1)} %collective-permute-done.7.refs_0_.refs_1_.refs_2_.refs_3_.refs_4_.refs_9_, bf16[128,3968]{1,0:T(8,128)(2,1)} %collective-permute-done.7.refs_0_.refs_1_.refs_2_.refs_3_.refs_4_.refs_9_, ...), custom_call_target="tpu_custom_call" | custom-call | flops 1610612736 | bytes 4161536 | tf_op jit(solution)/shard_map/project/pallas_call | solution.py:187
  93.7 1.3 broadcast_select_fusion.1.refs_0_.refs_1_.refs_2_.refs_3_.refs_4_.refs_10_
  95.1 4.8 %project.6 = (f32[2,2,256,128]{3,2,1,0:T(8,128)S(1)}, f32[2,2,256,128]{3,2,1,0:T(8,128)S(1)}) custom-call(s32[1]{0:T(128)} %bitcast.4.place, bf16[128,3968]{1,0:T(8,128)(2,1)S(1)} %broadcast_select_fusion.1.refs_0_.refs_1_.refs_2_.refs_3_.refs_4_.refs_10_, bf16[128,3968]{1,0:T(8,128)(2,1)S(1)} %broadcast_select_fusion.1.refs_0_.refs_1_.refs_2_.refs_3_.refs_4_.refs_10_, ...), custom_call_target="tpu_custom_call" | custom-call | flops 1610612736 | bytes 4161536 | tf_op jit(solution)/shard_map/project/pallas_call | solution.py:187
  101.6 1.5 collective-permute-start.10
  104.1 1.3 collective-permute-start.19
  106.6 1.4 collective-permute-done.11
  108.4 2.4 %collective-permute-done.10 = f32[256,128]{1,0:T(8,128)S(1)} collective-permute-done((f32[256,128]{1,0:T(8,128)S(1)}, f32[256,128]{1,0:T(8,128)S(1)}, u32[]{:S(2)}, u32[]{:S(2)}) %collective-permute-start.10) | collective-permute-done | bytes 131104 | tf_op jit(solution)/shard_map/ppermute | solution.py:342
  112.7 2.5 %collective-permute-done.17 = f32[256,128]{1,0:T(8,128)S(1)} collective-permute-done((f32[256,128]{1,0:T(8,128)S(1)}, f32[256,128]{1,0:T(8,128)S(1)}, u32[]{:S(2)}, u32[]{:S(2)}) %collective-permute-start.17) | collective-permute-done | bytes 131104 | tf_op jit(solution)/shard_map/ppermute | solution.py:342
  115.8 1.3 collective-permute-start.29
  117.1 3.0 %collective-permute-start.30 = (bf16[256,128]{1,0:T(8,128)(2,1)S(1)}, bf16[256,128]{1,0:T(8,128)(2,1)}, u32[]{:S(2)}, u32[]{:S(2)}) collective-permute-start(bf16[256,128]{1,0:T(8,128)(2,1)S(1)} %fusion.7.refs_2_), channel_id=1, source_target_pairs={{0,8},{1,24},{2,10},{3,26},{4,12},{5,28},{6,14},{7,30},{8,0},{9,16... | collective-permute-start | bytes 196616 | tf_op jit(solution)/shard_map/ppermute | solution.py:342
  120.1 4.5 %collective-permute-start.31 = (bf16[256,128]{1,0:T(8,128)(2,1)S(1)}, bf16[256,128]{1,0:T(8,128)(2,1)}, u32[]{:S(2)}, u32[]{:S(2)}) collective-permute-start(bf16[256,128]{1,0:T(8,128)(2,1)S(1)} %fusion.7.refs_2_), channel_id=1, source_target_pairs={{0,16},{1,0},{2,18},{3,2},{4,20},{5,4},{6,22},{7,6},{8,24},{9,8},{... | collective-permute-start | bytes 196616 | tf_op jit(solution)/shard_map/ppermute | solution.py:342
  124.6 1.8 collective-permute-start.32
  126.4 2.6 %collective-permute-start.21 = (bf16[256,128]{1,0:T(8,128)(2,1)S(1)}, bf16[256,128]{1,0:T(8,128)(2,1)S(1)}, u32[]{:S(2)}, u32[]{:S(2)}) collective-permute-start(bf16[256,128]{1,0:T(8,128)(2,1)S(1)} %fusion.15.refs_0_), channel_id=1, source_target_pairs={{0,1},{1,0},{2,3},{3,2},{4,5},{5,4},{6,7},{7,6},{8,9},{9,8},{10,11... | collective-permute-start | bytes 196616 | tf_op jit(solution)/shard_map/ppermute | solution.py:342
  129.0 10.3 %collective-permute-done.30 = bf16[256,128]{1,0:T(8,128)(2,1)} collective-permute-done((bf16[256,128]{1,0:T(8,128)(2,1)S(1)}, bf16[256,128]{1,0:T(8,128)(2,1)}, u32[]{:S(2)}, u32[]{:S(2)}) %collective-permute-start.30) | collective-permute-done | bytes 65568 | tf_op jit(solution)/shard_map/ppermute | solution.py:342
  140.9 1.3 broadcast_select_fusion.refs_0_.refs_1_.refs_2_.refs_3_.refs_4_.refs_11_
  142.3 1.3 collective-permute-done.22.refs_5_
  143.6 4.7 %project.7 = (f32[2,2,256,128]{3,2,1,0:T(8,128)S(1)}, f32[2,2,256,128]{3,2,1,0:T(8,128)S(1)}) custom-call(s32[1]{0:T(128)} %bitcast.4.place, bf16[128,3968]{1,0:T(8,128)(2,1)S(1)} %broadcast_select_fusion.refs_0_.refs_1_.refs_2_.refs_3_.refs_4_.refs_11_, bf16[128,3968]{1,0:T(8,128)(2,1)S(1)} %broadcast_select_fusion.refs_0_.refs_1_.refs_2_.refs_3_.refs_4_.refs_11_, ...), custom_call_target="tpu_custom_call" | custom-call | flops 1610612736 | bytes 4161536 | tf_op jit(solution)/shard_map/project/pallas_call | solution.py:187
  151.1 1.7 collective-permute-start.26
  153.4 1.3 collective-permute-start.24
  154.7 3.7 %collective-permute-done.26 = f32[256,128]{1,0:T(8,128)S(1)} collective-permute-done((f32[256,128]{1,0:T(8,128)S(1)}, f32[256,128]{1,0:T(8,128)S(1)}, u32[]{:S(2)}, u32[]{:S(2)}) %collective-permute-start.26) | collective-permute-done | bytes 131104 | tf_op jit(solution)/shard_map/ppermute | solution.py:342
  158.4 4.8 %collective-permute-done.25 = f32[256,128]{1,0:T(8,128)S(1)} collective-permute-done((f32[256,128]{1,0:T(8,128)S(1)}, f32[256,128]{1,0:T(8,128)S(1)}, u32[]{:S(2)}, u32[]{:S(2)}) %collective-permute-start.25) | collective-permute-done | bytes 131104 | tf_op jit(solution)/shard_map/ppermute | solution.py:342
  164.0 4.9 %collective-permute-start.37 = (bf16[256,128]{1,0:T(8,128)(2,1)S(1)}, bf16[256,128]{1,0:T(8,128)(2,1)S(1)}, u32[]{:S(2)}, u32[]{:S(2)}) collective-permute-start(bf16[256,128]{1,0:T(8,128)(2,1)S(1)} %fusion.3.refs_3_), channel_id=1, source_target_pairs={{0,16},{1,0},{2,18},{3,2},{4,20},{5,4},{6,22},{7,6},{8,24},{9,8},{... | collective-permute-start | bytes 196616 | tf_op jit(solution)/shard_map/ppermute | solution.py:342
  169.9 1.3 collective-permute-done.37
  171.2 3.6 %collective-permute-done.38 = bf16[256,128]{1,0:T(8,128)(2,1)S(1)} collective-permute-done((bf16[256,128]{1,0:T(8,128)(2,1)S(1)}, bf16[256,128]{1,0:T(8,128)(2,1)S(1)}, u32[]{:S(2)}, u32[]{:S(2)}) %collective-permute-start.38) | collective-permute-done | bytes 65568 | tf_op jit(solution)/shard_map/ppermute | solution.py:342
  174.8 2.8 %collective-permute-start.39 = (bf16[4,256,128]{2,1,0:T(8,128)(2,1)S(1)}, bf16[4,256,128]{2,1,0:T(8,128)(2,1)S(1)}, u32[]{:S(2)}, u32[]{:S(2)}) collective-permute-start(bf16[4,256,128]{2,1,0:T(8,128)(2,1)S(1)} %pad_maximum_fusion.1), channel_id=1, source_target_pairs={{0,4},{1,5},{2,6},{3,7},{4,0},{5,1},{6,2},{7,3},{8,12},{9,13},{10,... | collective-permute-start | bytes 786440 | tf_op jit(solution)/shard_map/ppermute | solution.py:342
  177.7 4.3 %collective-permute-done.39 = bf16[4,256,128]{2,1,0:T(8,128)(2,1)S(1)} collective-permute-done((bf16[4,256,128]{2,1,0:T(8,128)(2,1)S(1)}, bf16[4,256,128]{2,1,0:T(8,128)(2,1)S(1)}, u32[]{:S(2)}, u32[]{:S(2)}) %collective-permute-start.39) | collective-permute-done | bytes 262176 | tf_op jit(solution)/shard_map/ppermute | solution.py:342
  182.1 2.0 collective-permute-start.27
  184.3 2.5 %collective-permute-done.27.refs_6_ = bf16[256,128]{1,0:T(8,128)(2,1)S(1)} collective-permute-done((bf16[256,128]{1,0:T(8,128)(2,1)S(1)}, bf16[256,128]{1,0:T(8,128)(2,1)S(1)}, u32[]{:S(2)}, u32[]{:S(2)}) %collective-permute-start.27) | collective-permute-done | bytes 65568 | tf_op jit(solution)/shard_map/ppermute | solution.py:342
  186.8 1.6 collective-permute-done.28.refs_7_
  188.4 1.3 weigh.1.refs_0_
  189.7 1.3 copy-done.5
  191.0 1.6 copy-done.4
  192.6 1.6 copy-done.6
  194.2 5.9 %chi.1 = f32[128,4,1024]{2,1,0:T(4,128)} custom-call(s32[4]{0:T(128)S(1)} %pad_add_fusion.scalars, bf16[4,512,512]{2,1,0:T(8,128)(2,1)S(1)} %copy-done.6, bf16[16,2,256,128]{3,2,1,0:T(8,128)(2,1)S(1)} %bitcast.89, bf16[16,2,256,128]{3,2,1,0:T(8,128)(2,1)S(1)} %bitcast.90, bf16[16,2,256,128]{3,2,1,0:T(8,128)(2,1)S(1)} %bitcast.91, ...), custom_call_target="tpu_custom_call" | custom-call | flops 2147483648 | bytes 6291456 | tf_op jit(solution)/shard_map/chi/pallas_call | solution.py:297
  (93 shorter events, 19.3 us)
Async XLA Ops:
  10.5 19.9 %all-to-all-start = ((bf16[8,16,3968]{2,1,0:T(8,128)(2,1)}), bf16[8,16,3968]{2,1,0:T(8,128)(2,1)}, u32[]{:S(2)}, u32[]{:S(2)}) async-start(bf16[8,16,3968]{2,1,0:T(8,128)(2,1)} %pack.1), calls=%async_computation | async-start | bytes 2031616 | tf_op jit(solution)/shard_map/all_to_all | solution.py:492
  15.7 175.3 %all-gather.3.cloned.1.call-start = ((), (), s32[]{:S(2)}) async-start(), calls=%async_computation.1 | async-start | bytes 2228224 | tf_op jit(solution)/shard_map/all_gather | solution.py:392
  30.4 24.6 %collective-permute-start.7 = (bf16[128,3968]{1,0:T(8,128)(2,1)}, bf16[128,3968]{1,0:T(8,128)(2,1)}, u32[]{:S(2)}, u32[]{:S(2)}) collective-permute-start(bf16[128,3968]{1,0:T(8,128)(2,1)} %bitcast.5.refs_0_.refs_1_.refs_2_.refs_3_.refs_4_.refs_8_), channel_id=1, source_target_pairs={{0,8},{1,9},{2,10},{3,11},{4,12},{5,13},{6,14},{7,15},{8,0},{9,1},... | collective-permute-start | bytes 3047432 | tf_op jit(solution)/shard_map/ppermute | solution.py:342
  32.4 24.2 %collective-permute-start.13 = (bf16[128,3968]{1,0:T(8,128)(2,1)}, bf16[128,3968]{1,0:T(8,128)(2,1)}, u32[]{:S(2)}, u32[]{:S(2)}) collective-permute-start(bf16[128,3968]{1,0:T(8,128)(2,1)} %bitcast.5.refs_0_.refs_1_.refs_2_.refs_3_.refs_4_.refs_8_), channel_id=1, source_target_pairs={{8,16},{9,17},{10,18},{11,19},{12,20},{13,21},{14,22},{15,23},{16,... | collective-permute-start | bytes 3047432 | tf_op jit(solution)/shard_map/ppermute | solution.py:342
  37.3 20.6 %collective-permute-start = (bf16[3072,128]{1,0:T(8,128)(2,1)}, bf16[3072,128]{1,0:T(8,128)(2,1)S(1)}, u32[]{:S(2)}, u32[]{:S(2)}) collective-permute-start(bf16[3072,128]{1,0:T(8,128)(2,1)} %get-tuple-element.24), channel_id=1, source_target_pairs={{0,2},{1,3},{2,0},{3,1},{4,6},{5,7},{6,4},{7,5},{8,10},{9,11},{10,... | collective-permute-start | bytes 2359304 | tf_op jit(solution)/shard_map/ppermute | solution.py:342
  37.3 20.6 %collective-permute-start.1 = (bf16[3072,128]{1,0:T(8,128)(2,1)}, bf16[3072,128]{1,0:T(8,128)(2,1)S(1)}, u32[]{:S(2)}, u32[]{:S(2)}) collective-permute-start(bf16[3072,128]{1,0:T(8,128)(2,1)} %get-tuple-element.26), channel_id=1, source_target_pairs={{0,4},{1,5},{2,6},{3,7},{4,0},{5,1},{6,2},{7,3},{8,12},{9,13},{10,... | collective-permute-start | bytes 2359304 | tf_op jit(solution)/shard_map/ppermute | solution.py:342
  37.9 36.0 %collective-permute-start.2 = (bf16[3072,128]{1,0:T(8,128)(2,1)}, bf16[3072,128]{1,0:T(8,128)(2,1)S(1)}, u32[]{:S(2)}, u32[]{:S(2)}) collective-permute-start(bf16[3072,128]{1,0:T(8,128)(2,1)} %get-tuple-element.23), channel_id=1, source_target_pairs={{0,6},{1,7},{2,4},{3,5},{4,2},{5,3},{6,0},{7,1},{8,14},{9,15},{10,... | collective-permute-start | bytes 2359304 | tf_op jit(solution)/shard_map/ppermute | solution.py:342
  55.0 38.6 %collective-permute-start.12 = (bf16[128,3968]{1,0:T(8,128)(2,1)}, bf16[128,3968]{1,0:T(8,128)(2,1)}, u32[]{:S(2)}, u32[]{:S(2)}) collective-permute-start(bf16[128,3968]{1,0:T(8,128)(2,1)} %collective-permute-done.7.refs_0_.refs_1_.refs_2_.refs_3_.refs_4_.refs_9_), channel_id=1, source_target_pairs={{8,16},{9,17},{10,18},{11,19},{12,20},{13,21},{14,22},{15,23},{16,... | collective-permute-start | bytes 3047432 | tf_op jit(solution)/shard_map/ppermute | solution.py:342
  56.6 37.1 %collective-permute-start.14 = (bf16[128,3968]{1,0:T(8,128)(2,1)}, bf16[128,3968]{1,0:T(8,128)(2,1)}, u32[]{:S(2)}, u32[]{:S(2)}) collective-permute-start(bf16[128,3968]{1,0:T(8,128)(2,1)} %collective-permute-done.13), channel_id=1, source_target_pairs={{8,0},{9,1},{10,2},{11,3},{12,4},{13,5},{14,6},{15,7},{16,24},{17,... | collective-permute-start | bytes 3047432 | tf_op jit(solution)/shard_map/ppermute | solution.py:342
  80.9 2.5 %collective-permute-start.3 = (f32[2,2,256,128]{3,2,1,0:T(8,128)}, f32[2,2,256,128]{3,2,1,0:T(8,128)}, u32[]{:S(2)}, u32[]{:S(2)}) collective-permute-start(f32[2,2,256,128]{3,2,1,0:T(8,128)} %get-tuple-element.15), channel_id=1, source_target_pairs={{0,2},{1,3},{2,0},{3,1},{4,6},{5,7},{6,4},{7,5},{8,10},{9,11},{10,... | collective-permute-start | bytes 1572872 | tf_op jit(solution)/shard_map/ppermute | solution.py:342
  84.6 15.8 %collective-permute-start.6 = (f32[256,128]{1,0:T(8,128)S(1)}, f32[256,128]{1,0:T(8,128)S(1)}, u32[]{:S(2)}, u32[]{:S(2)}) collective-permute-start(f32[256,128]{1,0:T(8,128)S(1)} %get-tuple-element.37), channel_id=1, source_target_pairs={{0,5},{1,4},{2,7},{3,6},{4,1},{5,0},{6,3},{7,2},{8,13},{9,12},{10,... | collective-permute-start | bytes 393224 | tf_op jit(solution)/shard_map/ppermute | solution.py:342
  85.7 14.7 %collective-permute-start.5 = (f32[256,128]{1,0:T(8,128)S(1)}, f32[256,128]{1,0:T(8,128)S(1)}, u32[]{:S(2)}, u32[]{:S(2)}) collective-permute-start(f32[256,128]{1,0:T(8,128)S(1)} %get-tuple-element.38), channel_id=1, source_target_pairs={{0,4},{1,5},{2,6},{3,7},{4,0},{5,1},{6,2},{7,3},{8,12},{9,13},{10,... | collective-permute-start | bytes 393224 | tf_op jit(solution)/shard_map/ppermute | solution.py:342
  87.2 13.2 %collective-permute-start.4 = (f32[256,128]{1,0:T(8,128)S(1)}, f32[256,128]{1,0:T(8,128)S(1)}, u32[]{:S(2)}, u32[]{:S(2)}) collective-permute-start(f32[256,128]{1,0:T(8,128)S(1)} %get-tuple-element.36), channel_id=1, source_target_pairs={{0,1},{1,0},{2,3},{3,2},{4,5},{5,4},{6,7},{7,6},{8,9},{9,8},{10,11... | collective-permute-start | bytes 393224 | tf_op jit(solution)/shard_map/ppermute | solution.py:342
  93.6 6.8 %collective-permute-start.8 = (f32[2,2,256,128]{3,2,1,0:T(8,128)S(1)}, f32[2,2,256,128]{3,2,1,0:T(8,128)S(1)}, u32[]{:S(2)}, u32[]{:S(2)}) collective-permute-start(f32[2,2,256,128]{3,2,1,0:T(8,128)S(1)} %get-tuple-element.17), channel_id=1, source_target_pairs={{0,2},{1,3},{2,0},{3,1},{4,6},{5,7},{6,4},{7,5},{8,10},{9,11},{10,... | collective-permute-start | bytes 1572872 | tf_op jit(solution)/shard_map/ppermute | solution.py:342
  95.0 4.8 %copy-start = (bf16[128,3968]{1,0:T(8,128)(2,1)}, bf16[128,3968]{1,0:T(8,128)(2,1)S(1)}, u32[]{:S(2)}) copy-start(bf16[128,3968]{1,0:T(8,128)(2,1)S(1)} %broadcast_select_fusion.1.refs_0_.refs_1_.refs_2_.refs_3_.refs_4_.refs_10_) | copy-start | bytes 3047428
  99.8 5.5 %collective-permute-start.15 = (f32[2,2,256,128]{3,2,1,0:T(8,128)S(1)}, f32[2,2,256,128]{3,2,1,0:T(8,128)S(1)}, u32[]{:S(2)}, u32[]{:S(2)}) collective-permute-start(f32[2,2,256,128]{3,2,1,0:T(8,128)S(1)} %get-tuple-element.19), channel_id=1, source_target_pairs={{0,2},{1,3},{2,0},{3,1},{4,6},{5,7},{6,4},{7,5},{8,10},{9,11},{10,... | collective-permute-start | bytes 1572872 | tf_op jit(solution)/shard_map/ppermute | solution.py:342
  100.6 7.4 %collective-permute-start.11 = (f32[256,128]{1,0:T(8,128)S(1)}, f32[256,128]{1,0:T(8,128)S(1)}, u32[]{:S(2)}, u32[]{:S(2)}) collective-permute-start(f32[256,128]{1,0:T(8,128)S(1)} %get-tuple-element.34), channel_id=1, source_target_pairs={{0,5},{1,4},{2,7},{3,6},{4,1},{5,0},{6,3},{7,2},{8,13},{9,12},{10,... | collective-permute-start | bytes 393224 | tf_op jit(solution)/shard_map/ppermute | solution.py:342
  101.6 9.2 %collective-permute-start.10 = (f32[256,128]{1,0:T(8,128)S(1)}, f32[256,128]{1,0:T(8,128)S(1)}, u32[]{:S(2)}, u32[]{:S(2)}) collective-permute-start(f32[256,128]{1,0:T(8,128)S(1)} %get-tuple-element.35), channel_id=1, source_target_pairs={{0,4},{1,5},{2,6},{3,7},{4,0},{5,1},{6,2},{7,3},{8,12},{9,13},{10,... | collective-permute-start | bytes 393224 | tf_op jit(solution)/shard_map/ppermute | solution.py:342
  103.1 8.7 %collective-permute-start.9 = (f32[256,128]{1,0:T(8,128)S(1)}, f32[256,128]{1,0:T(8,128)S(1)}, u32[]{:S(2)}, u32[]{:S(2)}) collective-permute-start(f32[256,128]{1,0:T(8,128)S(1)} %get-tuple-element.33), channel_id=1, source_target_pairs={{0,1},{1,0},{2,3},{3,2},{4,5},{5,4},{6,7},{7,6},{8,9},{9,8},{10,11... | collective-permute-start | bytes 393224 | tf_op jit(solution)/shard_map/ppermute | solution.py:342
  104.1 36.8 %collective-permute-start.19 = (bf16[128,3968]{1,0:T(8,128)(2,1)}, bf16[128,3968]{1,0:T(8,128)(2,1)}, u32[]{:S(2)}, u32[]{:S(2)}) collective-permute-start(bf16[128,3968]{1,0:T(8,128)(2,1)} %collective-permute-done.12), channel_id=1, source_target_pairs={{8,0},{9,1},{10,2},{11,3},{12,4},{13,5},{14,6},{15,7},{16,24},{17,... | collective-permute-start | bytes 3047432 | tf_op jit(solution)/shard_map/ppermute | solution.py:342
  105.5 7.2 %collective-permute-start.18 = (f32[256,128]{1,0:T(8,128)S(1)}, f32[256,128]{1,0:T(8,128)S(1)}, u32[]{:S(2)}, u32[]{:S(2)}) collective-permute-start(f32[256,128]{1,0:T(8,128)S(1)} %get-tuple-element.31), channel_id=1, source_target_pairs={{0,5},{1,4},{2,7},{3,6},{4,1},{5,0},{6,3},{7,2},{8,13},{9,12},{10,... | collective-permute-start | bytes 393224 | tf_op jit(solution)/shard_map/ppermute | solution.py:342
  107.9 7.3 %collective-permute-start.17 = (f32[256,128]{1,0:T(8,128)S(1)}, f32[256,128]{1,0:T(8,128)S(1)}, u32[]{:S(2)}, u32[]{:S(2)}) collective-permute-start(f32[256,128]{1,0:T(8,128)S(1)} %get-tuple-element.32), channel_id=1, source_target_pairs={{0,4},{1,5},{2,6},{3,7},{4,0},{5,1},{6,2},{7,3},{8,12},{9,13},{10,... | collective-permute-start | bytes 393224 | tf_op jit(solution)/shard_map/ppermute | solution.py:342
  110.8 5.0 %collective-permute-start.16 = (f32[256,128]{1,0:T(8,128)S(1)}, f32[256,128]{1,0:T(8,128)S(1)}, u32[]{:S(2)}, u32[]{:S(2)}) collective-permute-start(f32[256,128]{1,0:T(8,128)S(1)} %get-tuple-element.30), channel_id=1, source_target_pairs={{0,1},{1,0},{2,3},{3,2},{4,5},{5,4},{6,7},{7,6},{8,9},{9,8},{10,11... | collective-permute-start | bytes 393224 | tf_op jit(solution)/shard_map/ppermute | solution.py:342
  111.8 12.8 %collective-permute-start.20 = (bf16[2,256,128]{2,1,0:T(8,128)(2,1)S(1)}, bf16[2,256,128]{2,1,0:T(8,128)(2,1)S(1)}, u32[]{:S(2)}, u32[]{:S(2)}) collective-permute-start(bf16[2,256,128]{2,1,0:T(8,128)(2,1)S(1)} %pad_maximum_fusion.2), channel_id=1, source_target_pairs={{0,0},{1,16},{2,2},{3,18},{4,4},{5,20},{6,6},{7,22},{8,8},{9,24},{... | collective-permute-start | bytes 393224 | tf_op jit(solution)/shard_map/ppermute | solution.py:342
  115.8 10.6 %collective-permute-start.29 = (bf16[256,128]{1,0:T(8,128)(2,1)S(1)}, bf16[256,128]{1,0:T(8,128)(2,1)}, u32[]{:S(2)}, u32[]{:S(2)}) collective-permute-start(bf16[256,128]{1,0:T(8,128)(2,1)S(1)} %fusion.7.refs_2_), channel_id=1, source_target_pairs={{0,0},{1,16},{2,2},{3,18},{4,4},{5,20},{6,6},{7,22},{8,8},{9,24},{... | collective-permute-start | bytes 196616 | tf_op jit(solution)/shard_map/ppermute | solution.py:342
  117.1 22.3 %collective-permute-start.30 = (bf16[256,128]{1,0:T(8,128)(2,1)S(1)}, bf16[256,128]{1,0:T(8,128)(2,1)}, u32[]{:S(2)}, u32[]{:S(2)}) collective-permute-start(bf16[256,128]{1,0:T(8,128)(2,1)S(1)} %fusion.7.refs_2_), channel_id=1, source_target_pairs={{0,8},{1,24},{2,10},{3,26},{4,12},{5,28},{6,14},{7,30},{8,0},{9,16... | collective-permute-start | bytes 196616 | tf_op jit(solution)/shard_map/ppermute | solution.py:342
  120.1 19.3 %collective-permute-start.31 = (bf16[256,128]{1,0:T(8,128)(2,1)S(1)}, bf16[256,128]{1,0:T(8,128)(2,1)}, u32[]{:S(2)}, u32[]{:S(2)}) collective-permute-start(bf16[256,128]{1,0:T(8,128)(2,1)S(1)} %fusion.7.refs_2_), channel_id=1, source_target_pairs={{0,16},{1,0},{2,18},{3,2},{4,20},{5,4},{6,22},{7,6},{8,24},{9,8},{... | collective-permute-start | bytes 196616 | tf_op jit(solution)/shard_map/ppermute | solution.py:342
  124.6 1.8 copy-start.8
  124.6 14.8 %collective-permute-start.32 = (bf16[256,128]{1,0:T(8,128)(2,1)S(1)}, bf16[256,128]{1,0:T(8,128)(2,1)S(1)}, u32[]{:S(2)}, u32[]{:S(2)}) collective-permute-start(bf16[256,128]{1,0:T(8,128)(2,1)S(1)} %fusion.7.refs_2_), channel_id=1, source_target_pairs={{0,24},{1,8},{2,26},{3,10},{4,28},{5,12},{6,30},{7,14},{8,16},{9,0... | collective-permute-start | bytes 196616 | tf_op jit(solution)/shard_map/ppermute | solution.py:342
  126.4 15.8 %collective-permute-start.21 = (bf16[256,128]{1,0:T(8,128)(2,1)S(1)}, bf16[256,128]{1,0:T(8,128)(2,1)S(1)}, u32[]{:S(2)}, u32[]{:S(2)}) collective-permute-start(bf16[256,128]{1,0:T(8,128)(2,1)S(1)} %fusion.15.refs_0_), channel_id=1, source_target_pairs={{0,1},{1,0},{2,3},{3,2},{4,5},{5,4},{6,7},{7,6},{8,9},{9,8},{10,11... | collective-permute-start | bytes 196616 | tf_op jit(solution)/shard_map/ppermute | solution.py:342
  139.4 4.3 %collective-permute-start.22 = (bf16[256,128]{1,0:T(8,128)(2,1)S(1)}, bf16[256,128]{1,0:T(8,128)(2,1)S(1)}, u32[]{:S(2)}, u32[]{:S(2)}) collective-permute-start(bf16[256,128]{1,0:T(8,128)(2,1)S(1)} %fusion.11.refs_1_), channel_id=1, source_target_pairs={{0,1},{1,0},{2,3},{3,2},{4,5},{5,4},{6,7},{7,6},{8,9},{9,8},{10,11... | collective-permute-start | bytes 196616 | tf_op jit(solution)/shard_map/ppermute | solution.py:342
  140.3 29.4 %collective-permute-start.33 = (bf16[4,256,128]{2,1,0:T(8,128)(2,1)S(1)}, bf16[4,256,128]{2,1,0:T(8,128)(2,1)S(1)}, u32[]{:S(2)}, u32[]{:S(2)}) collective-permute-start(bf16[4,256,128]{2,1,0:T(8,128)(2,1)S(1)} %pad_maximum_fusion), channel_id=1, source_target_pairs={{0,4},{1,5},{2,6},{3,7},{4,0},{5,1},{6,2},{7,3},{8,12},{9,13},{10,... | collective-permute-start | bytes 786440 | tf_op jit(solution)/shard_map/ppermute | solution.py:342
  142.3 6.1 %copy-start.2 = (bf16[128,3968]{1,0:T(8,128)(2,1)}, bf16[128,3968]{1,0:T(8,128)(2,1)S(1)}, u32[]{:S(2)}) copy-start(bf16[128,3968]{1,0:T(8,128)(2,1)S(1)} %broadcast_select_fusion.refs_0_.refs_1_.refs_2_.refs_3_.refs_4_.refs_11_) | copy-start | bytes 3047428
  148.3 2.7 %collective-permute-start.23 = (f32[2,2,256,128]{3,2,1,0:T(8,128)S(1)}, f32[2,2,256,128]{3,2,1,0:T(8,128)S(1)}, u32[]{:S(2)}, u32[]{:S(2)}) collective-permute-start(f32[2,2,256,128]{3,2,1,0:T(8,128)S(1)} %get-tuple-element.22), channel_id=1, source_target_pairs={{0,2},{1,3},{2,0},{3,1},{4,6},{5,7},{6,4},{7,5},{8,10},{9,11},{10,... | collective-permute-start | bytes 1572872 | tf_op jit(solution)/shard_map/ppermute | solution.py:342
  151.1 37.3 %copy-start.1 = (bf16[128,3968]{1,0:T(8,128)(2,1)S(1)}, bf16[128,3968]{1,0:T(8,128)(2,1)}, u32[]{:S(2)}) copy-start(bf16[128,3968]{1,0:T(8,128)(2,1)} %copy-done) | copy-start | bytes 3047428
  151.1 37.3 %copy-start.3 = (bf16[128,3968]{1,0:T(8,128)(2,1)S(1)}, bf16[128,3968]{1,0:T(8,128)(2,1)}, u32[]{:S(2)}) copy-start(bf16[128,3968]{1,0:T(8,128)(2,1)} %copy-done.2) | copy-start | bytes 3047428
  151.1 7.3 %collective-permute-start.26 = (f32[256,128]{1,0:T(8,128)S(1)}, f32[256,128]{1,0:T(8,128)S(1)}, u32[]{:S(2)}, u32[]{:S(2)}) collective-permute-start(f32[256,128]{1,0:T(8,128)S(1)} %get-tuple-element.28), channel_id=1, source_target_pairs={{0,5},{1,4},{2,7},{3,6},{4,1},{5,0},{6,3},{7,2},{8,13},{9,12},{10,... | collective-permute-start | bytes 393224 | tf_op jit(solution)/shard_map/ppermute | solution.py:342
  152.8 10.4 %collective-permute-start.25 = (f32[256,128]{1,0:T(8,128)S(1)}, f32[256,128]{1,0:T(8,128)S(1)}, u32[]{:S(2)}, u32[]{:S(2)}) collective-permute-start(f32[256,128]{1,0:T(8,128)S(1)} %get-tuple-element.29), channel_id=1, source_target_pairs={{0,4},{1,5},{2,6},{3,7},{4,0},{5,1},{6,2},{7,3},{8,12},{9,13},{10,... | collective-permute-start | bytes 393224 | tf_op jit(solution)/shard_map/ppermute | solution.py:342
  153.4 9.8 %collective-permute-start.24 = (f32[256,128]{1,0:T(8,128)S(1)}, f32[256,128]{1,0:T(8,128)S(1)}, u32[]{:S(2)}, u32[]{:S(2)}) collective-permute-start(f32[256,128]{1,0:T(8,128)S(1)} %get-tuple-element.27), channel_id=1, source_target_pairs={{0,1},{1,0},{2,3},{3,2},{4,5},{5,4},{6,7},{7,6},{8,9},{9,8},{10,11... | collective-permute-start | bytes 393224 | tf_op jit(solution)/shard_map/ppermute | solution.py:342
  163.3 6.6 %collective-permute-start.35 = (bf16[256,128]{1,0:T(8,128)(2,1)S(1)}, bf16[256,128]{1,0:T(8,128)(2,1)S(1)}, u32[]{:S(2)}, u32[]{:S(2)}) collective-permute-start(bf16[256,128]{1,0:T(8,128)(2,1)S(1)} %fusion.3.refs_3_), channel_id=1, source_target_pairs={{0,0},{1,16},{2,2},{3,18},{4,4},{5,20},{6,6},{7,22},{8,8},{9,24},{... | collective-permute-start | bytes 196616 | tf_op jit(solution)/shard_map/ppermute | solution.py:342
  163.9 5.9 %collective-permute-start.36 = (bf16[256,128]{1,0:T(8,128)(2,1)S(1)}, bf16[256,128]{1,0:T(8,128)(2,1)S(1)}, u32[]{:S(2)}, u32[]{:S(2)}) collective-permute-start(bf16[256,128]{1,0:T(8,128)(2,1)S(1)} %fusion.3.refs_3_), channel_id=1, source_target_pairs={{0,8},{1,24},{2,10},{3,26},{4,12},{5,28},{6,14},{7,30},{8,0},{9,16... | collective-permute-start | bytes 196616 | tf_op jit(solution)/shard_map/ppermute | solution.py:342
  164.0 7.1 %collective-permute-start.37 = (bf16[256,128]{1,0:T(8,128)(2,1)S(1)}, bf16[256,128]{1,0:T(8,128)(2,1)S(1)}, u32[]{:S(2)}, u32[]{:S(2)}) collective-permute-start(bf16[256,128]{1,0:T(8,128)(2,1)S(1)} %fusion.3.refs_3_), channel_id=1, source_target_pairs={{0,16},{1,0},{2,18},{3,2},{4,20},{5,4},{6,22},{7,6},{8,24},{9,8},{... | collective-permute-start | bytes 196616 | tf_op jit(solution)/shard_map/ppermute | solution.py:342
  168.9 5.9 %collective-permute-start.38 = (bf16[256,128]{1,0:T(8,128)(2,1)S(1)}, bf16[256,128]{1,0:T(8,128)(2,1)S(1)}, u32[]{:S(2)}, u32[]{:S(2)}) collective-permute-start(bf16[256,128]{1,0:T(8,128)(2,1)S(1)} %fusion.3.refs_3_), channel_id=1, source_target_pairs={{0,24},{1,8},{2,26},{3,10},{4,28},{5,12},{6,30},{7,14},{8,16},{9,0... | collective-permute-start | bytes 196616 | tf_op jit(solution)/shard_map/ppermute | solution.py:342
  169.7 21.2 %collective-permute-start.34 = (bf16[8,256,128]{2,1,0:T(8,128)(2,1)S(1)}, bf16[8,256,128]{2,1,0:T(8,128)(2,1)}, u32[]{:S(2)}, u32[]{:S(2)}) collective-permute-start(bf16[8,256,128]{2,1,0:T(8,128)(2,1)S(1)} %constant_dynamic-update-slice_fusion.refs_5_.refs_7_), channel_id=1, source_target_pairs={{0,2},{1,3},{2,0},{3,1},{4,6},{5,7},{6,4},{7,5},{8,10},{9,11},{10,... | collective-permute-start | bytes 1572872 | tf_op jit(solution)/shard_map/ppermute | solution.py:342
  174.8 7.1 %collective-permute-start.39 = (bf16[4,256,128]{2,1,0:T(8,128)(2,1)S(1)}, bf16[4,256,128]{2,1,0:T(8,128)(2,1)S(1)}, u32[]{:S(2)}, u32[]{:S(2)}) collective-permute-start(bf16[4,256,128]{2,1,0:T(8,128)(2,1)S(1)} %pad_maximum_fusion.1), channel_id=1, source_target_pairs={{0,4},{1,5},{2,6},{3,7},{4,0},{5,1},{6,2},{7,3},{8,12},{9,13},{10,... | collective-permute-start | bytes 786440 | tf_op jit(solution)/shard_map/ppermute | solution.py:342
  182.0 9.0 %collective-permute-start.40 = (bf16[8,256,128]{2,1,0:T(8,128)(2,1)S(1)}, bf16[8,256,128]{2,1,0:T(8,128)(2,1)}, u32[]{:S(2)}, u32[]{:S(2)}) collective-permute-start(bf16[8,256,128]{2,1,0:T(8,128)(2,1)S(1)} %constant_dynamic-update-slice_fusion.5.refs_9_.refs_11_), channel_id=1, source_target_pairs={{0,2},{1,3},{2,0},{3,1},{4,6},{5,7},{6,4},{7,5},{8,10},{9,11},{10,... | collective-permute-start | bytes 1572872 | tf_op jit(solution)/shard_map/ppermute | solution.py:342
  182.1 4.7 %collective-permute-start.27 = (bf16[256,128]{1,0:T(8,128)(2,1)S(1)}, bf16[256,128]{1,0:T(8,128)(2,1)S(1)}, u32[]{:S(2)}, u32[]{:S(2)}) collective-permute-start(bf16[256,128]{1,0:T(8,128)(2,1)S(1)} %fusion.7.refs_2_), channel_id=1, source_target_pairs={{0,1},{1,0},{2,3},{3,2},{4,5},{5,4},{6,7},{7,6},{8,9},{9,8},{10,11... | collective-permute-start | bytes 196616 | tf_op jit(solution)/shard_map/ppermute | solution.py:342
  184.1 4.3 %collective-permute-start.28 = (bf16[256,128]{1,0:T(8,128)(2,1)S(1)}, bf16[256,128]{1,0:T(8,128)(2,1)S(1)}, u32[]{:S(2)}, u32[]{:S(2)}) collective-permute-start(bf16[256,128]{1,0:T(8,128)(2,1)S(1)} %fusion.3.refs_3_), channel_id=1, source_target_pairs={{0,1},{1,0},{2,3},{3,2},{4,5},{5,4},{6,7},{7,6},{8,9},{9,8},{10,11... | collective-permute-start | bytes 196616 | tf_op jit(solution)/shard_map/ppermute | solution.py:342
  (4 other events, 5.3 us)
Sparse Core Ops, SparseCore 0:
  126.6 48.0 all-gather.2

commit v7 on v6

--- a/solution.py
+++ b/solution.py
@@ -207,15 +207,11 @@
     )(place, *([unit] * (segs + 1)), *(list(eigs) * segs))
 
 
-def weigh_kernel(slots, n_freq, place, *refs):
-    owns = refs[:slots]
-    mates = refs[slots : 2 * slots]
-    scales = refs[2 * slots : 3 * slots]
-    out = refs[-1]
+def weigh(owns, mates, scales, mine, n_freq, out):
+    slots = len(owns)
     rows, columns = owns[0].shape
     stride = n_freq + 1
     width = scales[0].shape[0]
-    mine = place[0]
     for k in range(slots):
         scale = scales[k][...].astype(jnp.float32).T
         own = owns[k][...].astype(jnp.float32).T
@@ -232,47 +228,33 @@
                     ).astype(jnp.bfloat16)
 
 
-def weigh(owns, mates, units, place, n_freq):
-    slots = len(owns)
-    rows, columns = owns[0].shape
-    width = units[0].shape[0]
-    last = units[0].shape[1] // LANES - 1
-    shape = (slots, n_freq * columns, 2 * rows)
-    return pl.pallas_call(
-        functools.partial(weigh_kernel, slots, n_freq),
-        out_shape=jax.ShapeDtypeStruct(shape, jnp.bfloat16),
-        grid_spec=pltpu.PrefetchScalarGridSpec(
-            num_scalar_prefetch=1,
-            grid=(1,),
-            in_specs=[pl.BlockSpec((rows, columns), lambda i, place: (0, 0))] * (2 * slots)
-            + [pl.BlockSpec((width, LANES), lambda i, place: (0, last))] * slots,
-            out_specs=pl.BlockSpec(shape, lambda i, place: (0, 0, 0)),
-        ),
-        compiler_params=pltpu.CompilerParams(vmem_limit_bytes=24 * 1024 * 1024),
-        cost_estimate=pl.CostEstimate(
-            flops=2 * math.prod(shape), bytes_accessed=3 * math.prod(shape), transcendentals=0
-        ),
-        name="weigh",
-    )(place, *owns, *mates, *units)
-
-
 def chi_kernel(early, late, n_freq, factor, scalars, *refs):
-    weighted = refs[0]
-    rights_a = refs[1:5]
-    rights_b = refs[5 : 5 + 4 * late]
-    out = refs[5 + 4 * late]
+    slots = early + late
+    owns = refs[:slots]
+    mates = refs[slots : 2 * slots]
+    scales = refs[2 * slots : 3 * slots]
+    rights_a = refs[3 * slots : 3 * slots + 4]
+    rights_b = refs[3 * slots + 4 : -2]
+    out, weighted = refs[-2:]
     columns = out.shape[0]
+
+    @pl.when(pl.program_id(0) == 0)
+    def _():
+        weigh(owns, mates, scales, scalars[4], n_freq, weighted)
+
     core = scalars[2]
+    same_y = scalars[1] == lax.rem(pl.program_id(0), 2)
     shift = lax.bitwise_xor(scalars[0], scalars[3] + pl.program_id(0) // 2)
     left, right = [], []
-    for r in range(early + late):
+    for r in range(slots):
         left.append(weighted[lax.bitwise_xor(shift, r)])
         for h in range(2):
             if r < early:
                 pair = [rights_a[2 * h + c][0, r] for c in range(2)]
             else:
-                at = 4 * (r - early) + 2 * h
-                own, mate = rights_b[at][0], rights_b[at + 1][0]
+                own, other, mate, both = [rights_b[8 * (r - early) + 4 * h + q][0] for q in range(4)]
+                own = jnp.where(same_y, own, other)
+                mate = jnp.where(same_y, mate, both)
                 pair = [jnp.where(core == c, own, mate) for c in range(2)]
             right.append(jnp.concatenate(pair, axis=1))
     chi = jnp.dot(
@@ -284,15 +266,17 @@
         out[:, f, :] = chi[f * columns : (f + 1) * columns, :] * factor
 
 
-def make_chi(weighted, right_a, rights_b, scalars, n_freq, factor):
+def make_chi(owns, mates, units, right_a, rights_b, scalars, n_freq, factor):
     members, early, rows, columns = right_a.shape
     tiles = members // 4
     late = len(rights_b)
+    slots = early + late
+    width = units[0].shape[0]
+    last = units[0].shape[1] // LANES - 1
+    flops = 4 * slots * rows * n_freq * columns * tiles * 2 * columns
 
     def near(h, i, scalars):
-        z = lax.bitwise_xor(scalars[0], h * 2 + i // 2)
-        y = lax.bitwise_xor(scalars[1], lax.rem(i, 2))
-        return (y * 4 + z, 0, 0)
+        return (lax.bitwise_xor(scalars[0], h * 2 + i // 2), 0, 0)
 
     return pl.pallas_call(
         functools.partial(chi_kernel, early, late, n_freq, factor),
@@ -300,7 +284,8 @@
         grid_spec=pltpu.PrefetchScalarGridSpec(
             num_scalar_prefetch=1,
             grid=(tiles,),
-            in_specs=[pl.BlockSpec(weighted.shape, lambda i, scalars: (0, 0, 0))]
+            in_specs=[pl.BlockSpec((rows, columns), lambda i, scalars: (0, 0))] * (2 * slots)
+            + [pl.BlockSpec((width, LANES), lambda i, scalars: (0, last))] * slots
             + [
                 pl.BlockSpec(
                     (1, early, rows, columns),
@@ -315,19 +300,20 @@
                 pl.BlockSpec((1, rows, columns), functools.partial(near, h))
                 for r in range(late)
                 for h in range(2)
-                for c in range(2)
+                for q in range(4)
             ],
             out_specs=pl.BlockSpec((columns, n_freq, 2 * columns), lambda i, scalars: (0, 0, i)),
+            scratch_shapes=[pltpu.VMEM((slots, n_freq * columns, 2 * rows), jnp.bfloat16)],
         ),
         compiler_params=pltpu.CompilerParams(vmem_limit_bytes=32 * 1024 * 1024),
         cost_estimate=pl.CostEstimate(
-            flops=2 * weighted.size * tiles * 2 * columns,
+            flops=flops,
             bytes_accessed=2 * (early + late) * members * rows * columns
             + 4 * columns * n_freq * tiles * 2 * columns,
             transcendentals=0,
         ),
         name="chi",
-    )(scalars, weighted, *([right_a] * 4), *[a for pair in rights_b for a in pair * 2])
+    )(scalars, *owns, *mates, *units, *([right_a] * 4), *[a for four in rights_b for a in four * 2])
 
 
 def fast(shape, unit, eigenvectors, part, val_count, cond_count, n_freq, factor):
@@ -368,9 +354,11 @@
 
     place = x[None]
 
-    def coefficients(unit):
+    def coefficients(unit, ready=None):
         keep, away = project(unit, eigs, place, val_count, cond_count)
         sums = keep + send(away, lambda i, j, k, t: (i, j, 1 - k, t))
+        if ready is not None:
+            sums, _ = lax.optimization_barrier((sums, ready))
         total = sums[0, 0] + send(sums[0, 1], lambda i, j, k, t: (i, j, k, 1 - t))
         total = total + send(sums[1, 0], lambda i, j, k, t: (i, 1 - j, k, t))
         total = total + send(sums[1, 1], lambda i, j, k, t: (i, 1 - j, k, 1 - t))
@@ -383,24 +371,27 @@
         return send(own, lambda i, j, k, t: ((2 * t + i % 2) ^ m, j, k, i // 2))
 
     def spread(own):
-        held = jnp.stack([share(own, m) for m in range(nz)])
-        held = jnp.concatenate([held, send(held, lambda i, j, k, t: (i, 1 - j, k, t))])
-        return held, send(held, lambda i, j, k, t: (i, j, 1 - k, t))
+        shares = [share(own, m) for m in range(nz)]
+        shares, paired = lax.optimization_barrier((shares, mate(own)))
+        held = jnp.stack(shares)
+        other = send(held, lambda i, j, k, t: (i, 1 - j, k, t))
+        across_core = lambda i, j, k, t: (i, j, 1 - k, t)
+        return (held, other, send(held, across_core), send(other, across_core)), paired
 
     owns = [coefficients(units[k]) for k in range(2)]
     share_a = share(jnp.stack(owns), 0)
     right_a = lax.all_gather(share_a, ("z", "y", "c"), axis=0)
     mates = [mate(own) for own in owns]
+    owns.append(coefficients(units[2], far))
     units[3], _ = lax.optimization_barrier((units[3], (share_a, mates)))
+    owns.append(coefficients(units[3]))
     rights_b = []
-    for k in range(2, nz):
-        own = coefficients(units[k])
-        rights_b.append(spread(own))
-        owns.append(own)
-        mates.append(mate(own))
-    weighted = weigh(owns, mates, units, place, n_freq)
-    scalars = jnp.stack([z, y, c, 2 * x])
-    return make_chi(weighted, right_a, rights_b, scalars, n_freq, factor)
+    for own in owns[2:]:
+        four, paired = spread(own)
+        rights_b.append(four)
+        mates.append(paired)
+    scalars = jnp.stack([z, y, c, 2 * x, x])
+    return make_chi(owns, mates, units, right_a, rights_b, scalars, n_freq, factor)
 
 
 def plain(shape, unit, eigenvectors, part, val_count, cond_count, n_freq, factor):

time: 208 us -> 223 us (1.072); the launches traced: 207 us -> 219 us
  starting transfers between devices: 55.3 us -> 72.7 us
  other arithmetic: 5.28 us -> 1.99 us
    ppermute x41 -> x43, starting transfers between devices: 50.1 us -> 67.5 us  [send(): lax.ppermute(array, AXES, [(source, number[to]) for source, to in pairs i...]
    ppermute x41 -> x43, waiting for transfers between devices: 74.3 us -> 79.7 us  [send(): lax.ppermute(array, AXES, [(source, number[to]) for source, to in pairs i...]
    all_to_all x1, waiting for transfers between devices: 14.6 us -> 9.14 us  [local(): unit = lax.all_to_all(packed, ('y', 'c', 'x'), 0, 0, tiled=True)]
    unnamed x26 -> x32, local copies, waits for them, and re-layouts: 7.95 us -> 7.11 us
  transfers between devices with their start and end apart: 43 -> 45, of which waited for: 18 -> 20; matrix products, arithmetic and copies ran while one was open for 6% -> 3% of each run, Pallas kernels for 11% -> 9%
where the time goes in v7:
time: 223 us; the launch traced here: 219 us
  waiting for transfers between devices  88.9 us (40%)
  starting transfers between devices  72.7 us (33%)
  Pallas kernels  30.9 us (14%)
  between operations  13.8 us (6%)
  local copies, waits for them, and re-layouts  10.6 us (5%)
    ppermute x43, waiting for transfers between devices, send(): lax.ppermute(array, AXES, [(source, number[to]) for source, to in pairs i...  79.7 us
    ppermute x43, starting transfers between devices, send(): lax.ppermute(array, AXES, [(source, number[to]) for source, to in pairs i...  67.5 us
    pallas_call x4, Pallas kernels, project(): pl.pallas_call(functools.partial(project_kernel, segs, val_count, cond_co...  20.4 us
    all_to_all x1, waiting for transfers between devices, local(): unit = lax.all_to_all(packed, ('y', 'c', 'x'), 0, 0, tiled=True)  9.14 us
    unnamed x32, local copies, waits for them, and re-layouts  7.11 us
    pallas_call x1, Pallas kernels, make_chi(): pl.pallas_call(functools.partial(chi_kernel, early, late, n_freq, factor)...  6.59 us
    all_to_all x1, starting transfers between devices, local(): unit = lax.all_to_all(packed, ('y', 'c', 'x'), 0, 0, tiled=True)  5.17 us
  transfers between devices with their start and end apart: 45, of which 20 were waited for; matrix products, arithmetic and copies ran while one was open for 3% of the time, Pallas kernels for 9%

profile of v7, /device:TPU:0, one launch (start us, length us, event | category | flops | bytes accessed | tf_op | source)
XLA Modules:
  0.0 219.0 jit_solution(9033685289131987379)
XLA Ops:
  6.5 4.0 %pack.1 = bf16[8,16,3968]{2,1,0:T(8,128)(2,1)} custom-call(f32[4]{0:T(128)} %val_energy.1, f32[16]{0:T(128)} %cond_energy.1, s32[64]{0:T(128)} %val_slot.1, s32[64]{0:T(128)} %cond_slot.1, f32[4]{0:T(128)} %frequencies.1, bf16[16,24576]{1,0:T(8,128)(2,1)} %refs_1_.1, bf16[16,24576]{1,0:T(8,128)(2,1)} %refs_1_.1, bf16[4,24576]{1,0:T(4,128)(2,1)} %refs_3_.1, ...), custom_call_target="tpu_custom_call" | custom-call | tf_op jit(solution)/shard_map/pack/pallas_call | solution.py:77
  10.5 5.2 %all-to-all-start = ((bf16[8,16,3968]{2,1,0:T(8,128)(2,1)}), bf16[8,16,3968]{2,1,0:T(8,128)(2,1)}, u32[]{:S(2)}, u32[]{:S(2)}) async-start(bf16[8,16,3968]{2,1,0:T(8,128)(2,1)} %pack.1), calls=%async_computation | async-start | bytes 2031616 | tf_op jit(solution)/shard_map/all_to_all | solution.py:483
  15.8 3.3 %constant_dynamic-slice_fusion = (bf16[3072,128]{1,0:T(8,128)(2,1)}, bf16[3072,128]{1,0:T(8,128)(2,1)}, bf16[3072,128]{1,0:T(8,128)(2,1)S(1)}, bf16[3072,128]{1,0:T(8,128)(2,1)}) fusion(bf16[12288,128]{1,0:T(8,128)(2,1)} %param.14, s32[]{:T(128)S(6)} %select_n.27, s32[]{:T(128)S(6)} %select_n.25, s32[]{:T(128)S(6)} %select_n.24, s32[]{:T(128)S(6)} %select_n.26), kind=kLoop, calls=%fused_computation.36 | loop fusion | bytes 6291472 | tf_op jit(solution)/shard_map/dynamic_slice | solution.py:340
  19.1 1.7 collective-permute-start.2
  21.2 9.1 %all-to-all-done = bf16[8,16,3968]{2,1,0:T(8,128)(2,1)} async-done(((bf16[8,16,3968]{2,1,0:T(8,128)(2,1)}), bf16[8,16,3968]{2,1,0:T(8,128)(2,1)}, u32[]{:S(2)}, u32[]{:S(2)}) %all-to-all-start) | async-done | bytes 1015840 | tf_op jit(solution)/shard_map/all_to_all | solution.py:483
  30.4 2.0 collective-permute-start.7
  32.4 1.6 collective-permute-start.13
  34.0 12.2 %collective-permute-done.2.refs_8_.refs_12_.refs_16_.refs_20_ = bf16[3072,128]{1,0:T(8,128)(2,1)S(1)} collective-permute-done((bf16[3072,128]{1,0:T(8,128)(2,1)}, bf16[3072,128]{1,0:T(8,128)(2,1)S(1)}, u32[]{:S(2)}, u32[]{:S(2)}) %collective-permute-start.2) | collective-permute-done | bytes 786464 | tf_op jit(solution)/shard_map/ppermute | solution.py:328
  46.2 17.3 %collective-permute-done.1.refs_7_.refs_11_.refs_15_.refs_19_ = bf16[3072,128]{1,0:T(8,128)(2,1)S(1)} collective-permute-done((bf16[3072,128]{1,0:T(8,128)(2,1)}, bf16[3072,128]{1,0:T(8,128)(2,1)S(1)}, u32[]{:S(2)}, u32[]{:S(2)}) %collective-permute-start.1) | collective-permute-done | bytes 786464 | tf_op jit(solution)/shard_map/ppermute | solution.py:328
  63.5 5.4 %project.4 = (f32[2,2,256,128]{3,2,1,0:T(8,128)S(1)}, f32[2,2,256,128]{3,2,1,0:T(8,128)S(1)}) custom-call(s32[1]{0:T(128)} %bitcast.4.place, bf16[128,3968]{1,0:T(8,128)(2,1)} %bitcast.5.refs_0_.refs_1_.refs_2_.refs_3_.refs_4_.refs_8_, bf16[128,3968]{1,0:T(8,128)(2,1)} %bitcast.5.refs_0_.refs_1_.refs_2_.refs_3_.refs_4_.refs_8_, ...), custom_call_target="tpu_custom_call" | custom-call | flops 1610612736 | bytes 4161536 | tf_op jit(solution)/shard_map/project/pallas_call | solution.py:187
  69.0 5.5 %project.5 = (f32[2,2,256,128]{3,2,1,0:T(8,128)S(1)}, f32[2,2,256,128]{3,2,1,0:T(8,128)S(1)}) custom-call(s32[1]{0:T(128)} %bitcast.4.place, bf16[128,3968]{1,0:T(8,128)(2,1)} %collective-permute-done.7.refs_0_.refs_1_.refs_2_.refs_3_.refs_4_.refs_9_, bf16[128,3968]{1,0:T(8,128)(2,1)} %collective-permute-done.7.refs_0_.refs_1_.refs_2_.refs_3_.refs_4_.refs_9_, ...), custom_call_target="tpu_custom_call" | custom-call | flops 1610612736 | bytes 4161536 | tf_op jit(solution)/shard_map/project/pallas_call | solution.py:187
  75.0 1.7 collective-permute-start.12
  76.7 1.3 collective-permute-start.14
  78.0 1.5 collective-permute-start.4
  79.9 1.7 collective-permute-start.5
  81.7 2.7 %collective-permute-done.4 = f32[256,128]{1,0:T(8,128)S(1)} collective-permute-done((f32[256,128]{1,0:T(8,128)S(1)}, f32[256,128]{1,0:T(8,128)S(1)}, u32[]{:S(2)}, u32[]{:S(2)}) %collective-permute-start.4) | collective-permute-done | bytes 131104 | tf_op jit(solution)/shard_map/ppermute | solution.py:328
  84.4 1.5 collective-permute-start.9
  86.8 2.8 %collective-permute-start.11 = (f32[256,128]{1,0:T(8,128)S(1)}, f32[256,128]{1,0:T(8,128)S(1)}, u32[]{:S(2)}, u32[]{:S(2)}) collective-permute-start(f32[256,128]{1,0:T(8,128)S(1)} %get-tuple-element.56), channel_id=1, source_target_pairs={{0,5},{1,4},{2,7},{3,6},{4,1},{5,0},{6,3},{7,2},{8,13},{9,12},{10,... | collective-permute-start | bytes 393224 | tf_op jit(solution)/shard_map/ppermute | solution.py:328
  90.2 2.6 %collective-permute-done.11 = f32[256,128]{1,0:T(8,128)S(1)} collective-permute-done((f32[256,128]{1,0:T(8,128)S(1)}, f32[256,128]{1,0:T(8,128)S(1)}, u32[]{:S(2)}, u32[]{:S(2)}) %collective-permute-start.11) | collective-permute-done | bytes 131104 | tf_op jit(solution)/shard_map/ppermute | solution.py:328
  92.8 1.9 collective-permute-done.10
  96.2 1.3 collective-permute-start.16
  97.5 7.7 %collective-permute-done.14 = bf16[128,3968]{1,0:T(8,128)(2,1)} collective-permute-done((bf16[128,3968]{1,0:T(8,128)(2,1)}, bf16[128,3968]{1,0:T(8,128)(2,1)}, u32[]{:S(2)}, u32[]{:S(2)}) %collective-permute-start.14) | collective-permute-done | bytes 1015840 | tf_op jit(solution)/shard_map/ppermute | solution.py:328
  105.2 1.3 broadcast_select_fusion.1.refs_0_.refs_1_.refs_2_.refs_3_.refs_4_.refs_10_
  106.5 4.8 %project.6 = (f32[2,2,256,128]{3,2,1,0:T(8,128)S(1)}, f32[2,2,256,128]{3,2,1,0:T(8,128)S(1)}) custom-call(s32[1]{0:T(128)} %bitcast.4.place, bf16[128,3968]{1,0:T(8,128)(2,1)S(1)} %broadcast_select_fusion.1.refs_0_.refs_1_.refs_2_.refs_3_.refs_4_.refs_10_, bf16[128,3968]{1,0:T(8,128)(2,1)S(1)} %broadcast_select_fusion.1.refs_0_.refs_1_.refs_2_.refs_3_.refs_4_.refs_10_, ...), custom_call_target="tpu_custom_call" | custom-call | flops 1610612736 | bytes 4161536 | tf_op jit(solution)/shard_map/project/pallas_call | solution.py:187
  111.4 7.1 %collective-permute-start.21 = (bf16[256,128]{1,0:T(8,128)(2,1)S(1)}, bf16[256,128]{1,0:T(8,128)(2,1)S(1)}, u32[]{:S(2)}, u32[]{:S(2)}) collective-permute-start(bf16[256,128]{1,0:T(8,128)(2,1)S(1)} %fusion.11.refs_0_), channel_id=1, source_target_pairs={{0,1},{1,0},{2,3},{3,2},{4,5},{5,4},{6,7},{7,6},{8,9},{9,8},{10,11... | collective-permute-start | bytes 196616 | tf_op jit(solution)/shard_map/ppermute | solution.py:328
  118.6 14.6 %collective-permute-done.16 = bf16[128,3968]{1,0:T(8,128)(2,1)S(1)} collective-permute-done((bf16[128,3968]{1,0:T(8,128)(2,1)}, bf16[128,3968]{1,0:T(8,128)(2,1)S(1)}, u32[]{:S(2)}, u32[]{:S(2)}) %collective-permute-start.16) | collective-permute-done | bytes 1015840 | tf_op jit(solution)/shard_map/ppermute | solution.py:328
  133.5 4.8 %project.7 = (f32[2,2,256,128]{3,2,1,0:T(8,128)S(1)}, f32[2,2,256,128]{3,2,1,0:T(8,128)S(1)}) custom-call(s32[1]{0:T(128)} %bitcast.4.place, bf16[128,3968]{1,0:T(8,128)(2,1)S(1)} %broadcast_select_fusion.refs_0_.refs_1_.refs_2_.refs_3_.refs_4_.refs_11_, bf16[128,3968]{1,0:T(8,128)(2,1)S(1)} %broadcast_select_fusion.refs_0_.refs_1_.refs_2_.refs_3_.refs_4_.refs_11_, ...), custom_call_target="tpu_custom_call" | custom-call | flops 1610612736 | bytes 4161536 | tf_op jit(solution)/shard_map/project/pallas_call | solution.py:187
  138.4 14.3 %collective-permute-start.17 = (f32[256,128]{1,0:T(8,128)S(1)}, f32[256,128]{1,0:T(8,128)S(1)}, u32[]{:S(2)}, u32[]{:S(2)}) collective-permute-start(f32[256,128]{1,0:T(8,128)S(1)} %get-tuple-element.52), channel_id=1, source_target_pairs={{0,1},{1,0},{2,3},{3,2},{4,5},{5,4},{6,7},{7,6},{8,9},{9,8},{10,11... | collective-permute-start | bytes 393224 | tf_op jit(solution)/shard_map/ppermute | solution.py:328
  152.7 1.5 collective-permute-start.18
  154.2 2.8 %collective-permute-done.17 = f32[256,128]{1,0:T(8,128)S(1)} collective-permute-done((f32[256,128]{1,0:T(8,128)S(1)}, f32[256,128]{1,0:T(8,128)S(1)}, u32[]{:S(2)}, u32[]{:S(2)}) %collective-permute-start.17) | collective-permute-done | bytes 131104 | tf_op jit(solution)/shard_map/ppermute | solution.py:328
  157.0 2.3 %collective-permute-done.19 = f32[256,128]{1,0:T(8,128)S(1)} collective-permute-done((f32[256,128]{1,0:T(8,128)S(1)}, f32[256,128]{1,0:T(8,128)S(1)}, u32[]{:S(2)}, u32[]{:S(2)}) %collective-permute-start.19) | collective-permute-done | bytes 131104 | tf_op jit(solution)/shard_map/ppermute | solution.py:328
  159.3 1.8 collective-permute-done.18
  161.1 1.3 collective-permute-start.31
  162.4 4.2 %collective-permute-start.30 = (bf16[256,128]{1,0:T(8,128)(2,1)S(1)}, bf16[256,128]{1,0:T(8,128)(2,1)S(1)}, u32[]{:S(2)}, u32[]{:S(2)}) collective-permute-start(bf16[256,128]{1,0:T(8,128)(2,1)S(1)} %fusion.14.refs_2_), channel_id=1, source_target_pairs={{0,24},{1,8},{2,26},{3,10},{4,28},{5,12},{6,30},{7,14},{8,16},{9,0... | collective-permute-start | bytes 196616 | tf_op jit(solution)/shard_map/ppermute | solution.py:328
  166.7 1.3 collective-permute-start.29
  168.9 2.6 %collective-permute-start.26 = (f32[256,128]{1,0:T(8,128)S(1)}, f32[256,128]{1,0:T(8,128)S(1)}, u32[]{:S(2)}, u32[]{:S(2)}) collective-permute-start(f32[256,128]{1,0:T(8,128)S(1)} %get-tuple-element.50), channel_id=1, source_target_pairs={{0,5},{1,4},{2,7},{3,6},{4,1},{5,0},{6,3},{7,2},{8,13},{9,12},{10,... | collective-permute-start | bytes 393224 | tf_op jit(solution)/shard_map/ppermute | solution.py:328
  173.1 2.7 %collective-permute-done.28 = bf16[256,128]{1,0:T(8,128)(2,1)S(1)} collective-permute-done((bf16[256,128]{1,0:T(8,128)(2,1)S(1)}, bf16[256,128]{1,0:T(8,128)(2,1)S(1)}, u32[]{:S(2)}, u32[]{:S(2)}) %collective-permute-start.28) | collective-permute-done | bytes 65568 | tf_op jit(solution)/shard_map/ppermute | solution.py:328
  176.8 1.1 collective-permute-done.25
  177.9 5.6 %collective-permute-start.36 = (bf16[256,128]{1,0:T(8,128)(2,1)S(1)}, bf16[256,128]{1,0:T(8,128)(2,1)S(1)}, u32[]{:S(2)}, u32[]{:S(2)}) collective-permute-start(bf16[256,128]{1,0:T(8,128)(2,1)S(1)} %fusion.3.refs_3_), channel_id=1, source_target_pairs={{0,1},{1,0},{2,3},{3,2},{4,5},{5,4},{6,7},{7,6},{8,9},{9,8},{10,11... | collective-permute-start | bytes 196616 | tf_op jit(solution)/shard_map/ppermute | solution.py:328
  184.1 2.0 collective-permute-start.34
  187.4 1.3 collective-permute-start.37
  188.6 1.5 collective-permute-done.35
  190.6 2.5 %collective-permute-start.40 = (bf16[4,256,128]{2,1,0:T(8,128)(2,1)S(1)}, bf16[4,256,128]{2,1,0:T(8,128)(2,1)S(1)}, u32[]{:S(2)}, u32[]{:S(2)}) collective-permute-start(bf16[4,256,128]{2,1,0:T(8,128)(2,1)S(1)} %pad_maximum_fusion.1.refs_24_.refs_28_), channel_id=1, source_target_pairs={{0,4},{1,5},{2,6},{3,7},{4,0},{5,1},{6,2},{7,3},{8,12},{9,13},{10,... | collective-permute-start | bytes 786440 | tf_op jit(solution)/shard_map/ppermute | solution.py:328
  193.1 2.3 %collective-permute-done.37.refs_17_.refs_21_ = bf16[4,256,128]{2,1,0:T(8,128)(2,1)S(1)} collective-permute-done((bf16[4,256,128]{2,1,0:T(8,128)(2,1)S(1)}, bf16[4,256,128]{2,1,0:T(8,128)(2,1)S(1)}, u32[]{:S(2)}, u32[]{:S(2)}) %collective-permute-start.37) | collective-permute-done | bytes 262176 | tf_op jit(solution)/shard_map/ppermute | solution.py:328
  195.8 2.3 %collective-permute-done.40.refs_25_.refs_29_ = bf16[4,256,128]{2,1,0:T(8,128)(2,1)S(1)} collective-permute-done((bf16[4,256,128]{2,1,0:T(8,128)(2,1)S(1)}, bf16[4,256,128]{2,1,0:T(8,128)(2,1)S(1)}, u32[]{:S(2)}, u32[]{:S(2)}) %collective-permute-start.40) | collective-permute-done | bytes 262176 | tf_op jit(solution)/shard_map/ppermute | solution.py:328
  198.2 1.6 collective-permute-done.42.refs_27_.refs_31_
  199.8 1.6 copy-done.4
  205.6 6.6 %chi.1 = f32[128,4,1024]{2,1,0:T(4,128)} custom-call(s32[5]{0:T(128)S(1)} %stack.62.scalars, bf16[256,128]{1,0:T(8,128)(2,1)S(1)} %fusion.11.refs_0_, bf16[256,128]{1,0:T(8,128)(2,1)S(1)} %fusion.7.refs_1_, bf16[256,128]{1,0:T(8,128)(2,1)S(1)} %fusion.14.refs_2_, bf16[256,128]{1,0:T(8,128)(2,1)S(1)} %copy-done.6, bf16[256,128]{1,0:T(8,128)(2,1)S(1)} %copy-done.8, ...), custom_call_target="tpu_custom_call" | custom-call | flops 2147483648 | bytes 6291456 | tf_op jit(solution)/shard_map/chi/pallas_call | solution.py:281
  (100 shorter events, 15.7 us)
Async XLA Ops:
  10.5 19.9 %all-to-all-start = ((bf16[8,16,3968]{2,1,0:T(8,128)(2,1)}), bf16[8,16,3968]{2,1,0:T(8,128)(2,1)}, u32[]{:S(2)}, u32[]{:S(2)}) async-start(bf16[8,16,3968]{2,1,0:T(8,128)(2,1)} %pack.1), calls=%async_computation | async-start | bytes 2031616 | tf_op jit(solution)/shard_map/all_to_all | solution.py:483
  15.7 184.1 %all-gather.3.cloned.1.call-start = ((), (), s32[]{:S(2)}) async-start(), calls=%async_computation.1 | async-start | bytes 2228224 | tf_op jit(solution)/shard_map/all_gather | solution.py:383
  19.1 27.1 %collective-permute-start.2 = (bf16[3072,128]{1,0:T(8,128)(2,1)}, bf16[3072,128]{1,0:T(8,128)(2,1)S(1)}, u32[]{:S(2)}, u32[]{:S(2)}) collective-permute-start(bf16[3072,128]{1,0:T(8,128)(2,1)} %get-tuple-element.45), channel_id=1, source_target_pairs={{0,6},{1,7},{2,4},{3,5},{4,2},{5,3},{6,0},{7,1},{8,14},{9,15},{10,... | collective-permute-start | bytes 2359304 | tf_op jit(solution)/shard_map/ppermute | solution.py:328
  20.8 25.4 %collective-permute-start = (bf16[3072,128]{1,0:T(8,128)(2,1)}, bf16[3072,128]{1,0:T(8,128)(2,1)S(1)}, u32[]{:S(2)}, u32[]{:S(2)}) collective-permute-start(bf16[3072,128]{1,0:T(8,128)(2,1)} %get-tuple-element.46), channel_id=1, source_target_pairs={{0,2},{1,3},{2,0},{3,1},{4,6},{5,7},{6,4},{7,5},{8,10},{9,11},{10,... | collective-permute-start | bytes 2359304 | tf_op jit(solution)/shard_map/ppermute | solution.py:328
  21.2 42.3 %collective-permute-start.1 = (bf16[3072,128]{1,0:T(8,128)(2,1)}, bf16[3072,128]{1,0:T(8,128)(2,1)S(1)}, u32[]{:S(2)}, u32[]{:S(2)}) collective-permute-start(bf16[3072,128]{1,0:T(8,128)(2,1)} %get-tuple-element.48), channel_id=1, source_target_pairs={{0,4},{1,5},{2,6},{3,7},{4,0},{5,1},{6,2},{7,3},{8,12},{9,13},{10,... | collective-permute-start | bytes 2359304 | tf_op jit(solution)/shard_map/ppermute | solution.py:328
  30.4 38.6 %collective-permute-start.7 = (bf16[128,3968]{1,0:T(8,128)(2,1)}, bf16[128,3968]{1,0:T(8,128)(2,1)}, u32[]{:S(2)}, u32[]{:S(2)}) collective-permute-start(bf16[128,3968]{1,0:T(8,128)(2,1)} %bitcast.5.refs_0_.refs_1_.refs_2_.refs_3_.refs_4_.refs_8_), channel_id=1, source_target_pairs={{0,8},{1,9},{2,10},{3,11},{4,12},{5,13},{6,14},{7,15},{8,0},{9,1},... | collective-permute-start | bytes 3047432 | tf_op jit(solution)/shard_map/ppermute | solution.py:328
  32.4 44.3 %collective-permute-start.13 = (bf16[128,3968]{1,0:T(8,128)(2,1)}, bf16[128,3968]{1,0:T(8,128)(2,1)}, u32[]{:S(2)}, u32[]{:S(2)}) collective-permute-start(bf16[128,3968]{1,0:T(8,128)(2,1)} %bitcast.5.refs_0_.refs_1_.refs_2_.refs_3_.refs_4_.refs_8_), channel_id=1, source_target_pairs={{8,16},{9,17},{10,18},{11,19},{12,20},{13,21},{14,22},{15,23},{16,... | collective-permute-start | bytes 3047432 | tf_op jit(solution)/shard_map/ppermute | solution.py:328
  68.9 6.0 %collective-permute-start.3 = (f32[2,2,256,128]{3,2,1,0:T(8,128)S(1)}, f32[2,2,256,128]{3,2,1,0:T(8,128)S(1)}, u32[]{:S(2)}, u32[]{:S(2)}) collective-permute-start(f32[2,2,256,128]{3,2,1,0:T(8,128)S(1)} %get-tuple-element.26), channel_id=1, source_target_pairs={{0,2},{1,3},{2,0},{3,1},{4,6},{5,7},{6,4},{7,5},{8,10},{9,11},{10,... | collective-permute-start | bytes 1572872 | tf_op jit(solution)/shard_map/ppermute | solution.py:328
  74.4 5.4 %collective-permute-start.8 = (f32[2,2,256,128]{3,2,1,0:T(8,128)S(1)}, f32[2,2,256,128]{3,2,1,0:T(8,128)S(1)}, u32[]{:S(2)}, u32[]{:S(2)}) collective-permute-start(f32[2,2,256,128]{3,2,1,0:T(8,128)S(1)} %get-tuple-element.28), channel_id=1, source_target_pairs={{0,2},{1,3},{2,0},{3,1},{4,6},{5,7},{6,4},{7,5},{8,10},{9,11},{10,... | collective-permute-start | bytes 1572872 | tf_op jit(solution)/shard_map/ppermute | solution.py:328
  75.0 21.2 %collective-permute-start.12 = (bf16[128,3968]{1,0:T(8,128)(2,1)}, bf16[128,3968]{1,0:T(8,128)(2,1)}, u32[]{:S(2)}, u32[]{:S(2)}) collective-permute-start(bf16[128,3968]{1,0:T(8,128)(2,1)} %collective-permute-done.7.refs_0_.refs_1_.refs_2_.refs_3_.refs_4_.refs_9_), channel_id=1, source_target_pairs={{8,16},{9,17},{10,18},{11,19},{12,20},{13,21},{14,22},{15,23},{16,... | collective-permute-start | bytes 3047432 | tf_op jit(solution)/shard_map/ppermute | solution.py:328
  76.7 28.6 %collective-permute-start.14 = (bf16[128,3968]{1,0:T(8,128)(2,1)}, bf16[128,3968]{1,0:T(8,128)(2,1)}, u32[]{:S(2)}, u32[]{:S(2)}) collective-permute-start(bf16[128,3968]{1,0:T(8,128)(2,1)} %collective-permute-done.13), channel_id=1, source_target_pairs={{8,0},{9,1},{10,2},{11,3},{12,4},{13,5},{14,6},{15,7},{16,24},{17,... | collective-permute-start | bytes 3047432 | tf_op jit(solution)/shard_map/ppermute | solution.py:328
  78.0 6.4 %collective-permute-start.4 = (f32[256,128]{1,0:T(8,128)S(1)}, f32[256,128]{1,0:T(8,128)S(1)}, u32[]{:S(2)}, u32[]{:S(2)}) collective-permute-start(f32[256,128]{1,0:T(8,128)S(1)} %get-tuple-element.58), channel_id=1, source_target_pairs={{0,1},{1,0},{2,3},{3,2},{4,5},{5,4},{6,7},{7,6},{8,9},{9,8},{10,11... | collective-permute-start | bytes 393224 | tf_op jit(solution)/shard_map/ppermute | solution.py:328
  79.5 7.3 %collective-permute-start.6 = (f32[256,128]{1,0:T(8,128)S(1)}, f32[256,128]{1,0:T(8,128)S(1)}, u32[]{:S(2)}, u32[]{:S(2)}) collective-permute-start(f32[256,128]{1,0:T(8,128)S(1)} %get-tuple-element.59), channel_id=1, source_target_pairs={{0,5},{1,4},{2,7},{3,6},{4,1},{5,0},{6,3},{7,2},{8,13},{9,12},{10,... | collective-permute-start | bytes 393224 | tf_op jit(solution)/shard_map/ppermute | solution.py:328
  79.9 9.7 %collective-permute-start.5 = (f32[256,128]{1,0:T(8,128)S(1)}, f32[256,128]{1,0:T(8,128)S(1)}, u32[]{:S(2)}, u32[]{:S(2)}) collective-permute-start(f32[256,128]{1,0:T(8,128)S(1)} %get-tuple-element.60), channel_id=1, source_target_pairs={{0,4},{1,5},{2,6},{3,7},{4,0},{5,1},{6,2},{7,3},{8,12},{9,13},{10,... | collective-permute-start | bytes 393224 | tf_op jit(solution)/shard_map/ppermute | solution.py:328
  84.4 5.8 %collective-permute-start.9 = (f32[256,128]{1,0:T(8,128)S(1)}, f32[256,128]{1,0:T(8,128)S(1)}, u32[]{:S(2)}, u32[]{:S(2)}) collective-permute-start(f32[256,128]{1,0:T(8,128)S(1)} %get-tuple-element.55), channel_id=1, source_target_pairs={{0,1},{1,0},{2,3},{3,2},{4,5},{5,4},{6,7},{7,6},{8,9},{9,8},{10,11... | collective-permute-start | bytes 393224 | tf_op jit(solution)/shard_map/ppermute | solution.py:328
  86.8 6.0 %collective-permute-start.11 = (f32[256,128]{1,0:T(8,128)S(1)}, f32[256,128]{1,0:T(8,128)S(1)}, u32[]{:S(2)}, u32[]{:S(2)}) collective-permute-start(f32[256,128]{1,0:T(8,128)S(1)} %get-tuple-element.56), channel_id=1, source_target_pairs={{0,5},{1,4},{2,7},{3,6},{4,1},{5,0},{6,3},{7,2},{8,13},{9,12},{10,... | collective-permute-start | bytes 393224 | tf_op jit(solution)/shard_map/ppermute | solution.py:328
  89.6 5.1 %collective-permute-start.10 = (f32[256,128]{1,0:T(8,128)S(1)}, f32[256,128]{1,0:T(8,128)S(1)}, u32[]{:S(2)}, u32[]{:S(2)}) collective-permute-start(f32[256,128]{1,0:T(8,128)S(1)} %get-tuple-element.57), channel_id=1, source_target_pairs={{0,4},{1,5},{2,6},{3,7},{4,0},{5,1},{6,2},{7,3},{8,12},{9,13},{10,... | collective-permute-start | bytes 393224 | tf_op jit(solution)/shard_map/ppermute | solution.py:328
  94.8 0.7 collective-permute-start.20
  96.2 37.0 %collective-permute-start.16 = (bf16[128,3968]{1,0:T(8,128)(2,1)}, bf16[128,3968]{1,0:T(8,128)(2,1)S(1)}, u32[]{:S(2)}, u32[]{:S(2)}) collective-permute-start(bf16[128,3968]{1,0:T(8,128)(2,1)} %collective-permute-done.12), channel_id=1, source_target_pairs={{8,0},{9,1},{10,2},{11,3},{12,4},{13,5},{14,6},{15,7},{16,24},{17,... | collective-permute-start | bytes 3047432 | tf_op jit(solution)/shard_map/ppermute | solution.py:328
  111.3 7.2 %collective-permute-start.15 = (f32[2,2,256,128]{3,2,1,0:T(8,128)S(1)}, f32[2,2,256,128]{3,2,1,0:T(8,128)S(1)}, u32[]{:S(2)}, u32[]{:S(2)}) collective-permute-start(f32[2,2,256,128]{3,2,1,0:T(8,128)S(1)} %get-tuple-element.30), channel_id=1, source_target_pairs={{0,2},{1,3},{2,0},{3,1},{4,6},{5,7},{6,4},{7,5},{8,10},{9,11},{10,... | collective-permute-start | bytes 1572872 | tf_op jit(solution)/shard_map/ppermute | solution.py:328
  111.4 22.0 %collective-permute-start.21 = (bf16[256,128]{1,0:T(8,128)(2,1)S(1)}, bf16[256,128]{1,0:T(8,128)(2,1)S(1)}, u32[]{:S(2)}, u32[]{:S(2)}) collective-permute-start(bf16[256,128]{1,0:T(8,128)(2,1)S(1)} %fusion.11.refs_0_), channel_id=1, source_target_pairs={{0,1},{1,0},{2,3},{3,2},{4,5},{5,4},{6,7},{7,6},{8,9},{9,8},{10,11... | collective-permute-start | bytes 196616 | tf_op jit(solution)/shard_map/ppermute | solution.py:328
  118.5 15.0 %collective-permute-start.22 = (bf16[256,128]{1,0:T(8,128)(2,1)S(1)}, bf16[256,128]{1,0:T(8,128)(2,1)S(1)}, u32[]{:S(2)}, u32[]{:S(2)}) collective-permute-start(bf16[256,128]{1,0:T(8,128)(2,1)S(1)} %fusion.7.refs_1_), channel_id=1, source_target_pairs={{0,1},{1,0},{2,3},{3,2},{4,5},{5,4},{6,7},{7,6},{8,9},{9,8},{10,11... | collective-permute-start | bytes 196616 | tf_op jit(solution)/shard_map/ppermute | solution.py:328
  138.3 61.5 %copy-start.1 = (bf16[128,3968]{1,0:T(8,128)(2,1)S(1)}, bf16[128,3968]{1,0:T(8,128)(2,1)}, u32[]{:S(2)}) copy-start(bf16[128,3968]{1,0:T(8,128)(2,1)} %copy-done) | copy-start | bytes 3047428
  138.3 61.5 %copy-start.3 = (bf16[128,3968]{1,0:T(8,128)(2,1)S(1)}, bf16[128,3968]{1,0:T(8,128)(2,1)}, u32[]{:S(2)}) copy-start(bf16[128,3968]{1,0:T(8,128)(2,1)} %copy-done.2) | copy-start | bytes 3047428
  138.3 29.7 %collective-permute-start.23 = (f32[2,2,256,128]{3,2,1,0:T(8,128)S(1)}, f32[2,2,256,128]{3,2,1,0:T(8,128)S(1)}, u32[]{:S(2)}, u32[]{:S(2)}) collective-permute-start(f32[2,2,256,128]{3,2,1,0:T(8,128)S(1)} %get-tuple-element.34), channel_id=1, source_target_pairs={{0,2},{1,3},{2,0},{3,1},{4,6},{5,7},{6,4},{7,5},{8,10},{9,11},{10,... | collective-permute-start | bytes 1572872 | tf_op jit(solution)/shard_map/ppermute | solution.py:328
  138.4 18.6 %collective-permute-start.17 = (f32[256,128]{1,0:T(8,128)S(1)}, f32[256,128]{1,0:T(8,128)S(1)}, u32[]{:S(2)}, u32[]{:S(2)}) collective-permute-start(f32[256,128]{1,0:T(8,128)S(1)} %get-tuple-element.52), channel_id=1, source_target_pairs={{0,1},{1,0},{2,3},{3,2},{4,5},{5,4},{6,7},{7,6},{8,9},{9,8},{10,11... | collective-permute-start | bytes 393224 | tf_op jit(solution)/shard_map/ppermute | solution.py:328
  152.7 6.6 %collective-permute-start.19 = (f32[256,128]{1,0:T(8,128)S(1)}, f32[256,128]{1,0:T(8,128)S(1)}, u32[]{:S(2)}, u32[]{:S(2)}) collective-permute-start(f32[256,128]{1,0:T(8,128)S(1)} %get-tuple-element.53), channel_id=1, source_target_pairs={{0,5},{1,4},{2,7},{3,6},{4,1},{5,0},{6,3},{7,2},{8,13},{9,12},{10,... | collective-permute-start | bytes 393224 | tf_op jit(solution)/shard_map/ppermute | solution.py:328
  152.7 8.4 %collective-permute-start.18 = (f32[256,128]{1,0:T(8,128)S(1)}, f32[256,128]{1,0:T(8,128)S(1)}, u32[]{:S(2)}, u32[]{:S(2)}) collective-permute-start(f32[256,128]{1,0:T(8,128)S(1)} %get-tuple-element.54), channel_id=1, source_target_pairs={{0,4},{1,5},{2,6},{3,7},{4,0},{5,1},{6,2},{7,3},{8,12},{9,13},{10,... | collective-permute-start | bytes 393224 | tf_op jit(solution)/shard_map/ppermute | solution.py:328
  161.1 10.4 %collective-permute-start.31 = (bf16[256,128]{1,0:T(8,128)(2,1)S(1)}, bf16[256,128]{1,0:T(8,128)(2,1)S(1)}, u32[]{:S(2)}, u32[]{:S(2)}) collective-permute-start(bf16[256,128]{1,0:T(8,128)(2,1)S(1)} %fusion.14.refs_2_), channel_id=1, source_target_pairs={{0,1},{1,0},{2,3},{3,2},{4,5},{5,4},{6,7},{7,6},{8,9},{9,8},{10,11... | collective-permute-start | bytes 196616 | tf_op jit(solution)/shard_map/ppermute | solution.py:328
  162.4 9.2 %collective-permute-start.30 = (bf16[256,128]{1,0:T(8,128)(2,1)S(1)}, bf16[256,128]{1,0:T(8,128)(2,1)S(1)}, u32[]{:S(2)}, u32[]{:S(2)}) collective-permute-start(bf16[256,128]{1,0:T(8,128)(2,1)S(1)} %fusion.14.refs_2_), channel_id=1, source_target_pairs={{0,24},{1,8},{2,26},{3,10},{4,28},{5,12},{6,30},{7,14},{8,16},{9,0... | collective-permute-start | bytes 196616 | tf_op jit(solution)/shard_map/ppermute | solution.py:328
  166.7 5.8 %collective-permute-start.29 = (bf16[256,128]{1,0:T(8,128)(2,1)S(1)}, bf16[256,128]{1,0:T(8,128)(2,1)S(1)}, u32[]{:S(2)}, u32[]{:S(2)}) collective-permute-start(bf16[256,128]{1,0:T(8,128)(2,1)S(1)} %fusion.14.refs_2_), channel_id=1, source_target_pairs={{0,16},{1,0},{2,18},{3,2},{4,20},{5,4},{6,22},{7,6},{8,24},{9,8},{... | collective-permute-start | bytes 196616 | tf_op jit(solution)/shard_map/ppermute | solution.py:328
  168.0 7.8 %collective-permute-start.24 = (f32[256,128]{1,0:T(8,128)S(1)}, f32[256,128]{1,0:T(8,128)S(1)}, u32[]{:S(2)}, u32[]{:S(2)}) collective-permute-start(f32[256,128]{1,0:T(8,128)S(1)} %get-tuple-element.49), channel_id=1, source_target_pairs={{0,1},{1,0},{2,3},{3,2},{4,5},{5,4},{6,7},{7,6},{8,9},{9,8},{10,11... | collective-permute-start | bytes 393224 | tf_op jit(solution)/shard_map/ppermute | solution.py:328
  168.9 7.9 %collective-permute-start.26 = (f32[256,128]{1,0:T(8,128)S(1)}, f32[256,128]{1,0:T(8,128)S(1)}, u32[]{:S(2)}, u32[]{:S(2)}) collective-permute-start(f32[256,128]{1,0:T(8,128)S(1)} %get-tuple-element.50), channel_id=1, source_target_pairs={{0,5},{1,4},{2,7},{3,6},{4,1},{5,0},{6,3},{7,2},{8,13},{9,12},{10,... | collective-permute-start | bytes 393224 | tf_op jit(solution)/shard_map/ppermute | solution.py:328
  171.5 15.2 %copy-start.11 = (bf16[256,128]{1,0:T(8,128)(2,1)}, bf16[256,128]{1,0:T(8,128)(2,1)S(1)}, u32[]{:S(2)}) copy-start(bf16[256,128]{1,0:T(8,128)(2,1)S(1)} %collective-permute-done.31.refs_6_) | copy-start | bytes 196612
  171.5 6.4 %collective-permute-start.25 = (f32[256,128]{1,0:T(8,128)S(1)}, f32[256,128]{1,0:T(8,128)S(1)}, u32[]{:S(2)}, u32[]{:S(2)}) collective-permute-start(f32[256,128]{1,0:T(8,128)S(1)} %get-tuple-element.51), channel_id=1, source_target_pairs={{0,4},{1,5},{2,6},{3,7},{4,0},{5,1},{6,2},{7,3},{8,12},{9,13},{10,... | collective-permute-start | bytes 393224 | tf_op jit(solution)/shard_map/ppermute | solution.py:328
  171.6 4.3 %collective-permute-start.28 = (bf16[256,128]{1,0:T(8,128)(2,1)S(1)}, bf16[256,128]{1,0:T(8,128)(2,1)S(1)}, u32[]{:S(2)}, u32[]{:S(2)}) collective-permute-start(bf16[256,128]{1,0:T(8,128)(2,1)S(1)} %fusion.14.refs_2_), channel_id=1, source_target_pairs={{0,8},{1,24},{2,10},{3,26},{4,12},{5,28},{6,14},{7,30},{8,0},{9,16... | collective-permute-start | bytes 196616 | tf_op jit(solution)/shard_map/ppermute | solution.py:328
  172.5 3.4 %collective-permute-start.27 = (bf16[256,128]{1,0:T(8,128)(2,1)S(1)}, bf16[256,128]{1,0:T(8,128)(2,1)S(1)}, u32[]{:S(2)}, u32[]{:S(2)}) collective-permute-start(bf16[256,128]{1,0:T(8,128)(2,1)S(1)} %fusion.14.refs_2_), channel_id=1, source_target_pairs={{0,0},{1,16},{2,2},{3,18},{4,4},{5,20},{6,6},{7,22},{8,8},{9,24},{... | collective-permute-start | bytes 196616 | tf_op jit(solution)/shard_map/ppermute | solution.py:328
  177.9 8.8 %collective-permute-start.36 = (bf16[256,128]{1,0:T(8,128)(2,1)S(1)}, bf16[256,128]{1,0:T(8,128)(2,1)S(1)}, u32[]{:S(2)}, u32[]{:S(2)}) collective-permute-start(bf16[256,128]{1,0:T(8,128)(2,1)S(1)} %fusion.3.refs_3_), channel_id=1, source_target_pairs={{0,1},{1,0},{2,3},{3,2},{4,5},{5,4},{6,7},{7,6},{8,9},{9,8},{10,11... | collective-permute-start | bytes 196616 | tf_op jit(solution)/shard_map/ppermute | solution.py:328
  183.6 6.6 %collective-permute-start.35 = (bf16[256,128]{1,0:T(8,128)(2,1)S(1)}, bf16[256,128]{1,0:T(8,128)(2,1)S(1)}, u32[]{:S(2)}, u32[]{:S(2)}) collective-permute-start(bf16[256,128]{1,0:T(8,128)(2,1)S(1)} %fusion.3.refs_3_), channel_id=1, source_target_pairs={{0,24},{1,8},{2,26},{3,10},{4,28},{5,12},{6,30},{7,14},{8,16},{9,0... | collective-permute-start | bytes 196616 | tf_op jit(solution)/shard_map/ppermute | solution.py:328
  184.1 6.1 %collective-permute-start.34 = (bf16[256,128]{1,0:T(8,128)(2,1)S(1)}, bf16[256,128]{1,0:T(8,128)(2,1)S(1)}, u32[]{:S(2)}, u32[]{:S(2)}) collective-permute-start(bf16[256,128]{1,0:T(8,128)(2,1)S(1)} %fusion.3.refs_3_), channel_id=1, source_target_pairs={{0,16},{1,0},{2,18},{3,2},{4,20},{5,4},{6,22},{7,6},{8,24},{9,8},{... | collective-permute-start | bytes 196616 | tf_op jit(solution)/shard_map/ppermute | solution.py:328
  186.0 4.5 %collective-permute-start.33 = (bf16[256,128]{1,0:T(8,128)(2,1)S(1)}, bf16[256,128]{1,0:T(8,128)(2,1)S(1)}, u32[]{:S(2)}, u32[]{:S(2)}) collective-permute-start(bf16[256,128]{1,0:T(8,128)(2,1)S(1)} %fusion.3.refs_3_), channel_id=1, source_target_pairs={{0,8},{1,24},{2,10},{3,26},{4,12},{5,28},{6,14},{7,30},{8,0},{9,16... | collective-permute-start | bytes 196616 | tf_op jit(solution)/shard_map/ppermute | solution.py:328
  186.0 4.5 %collective-permute-start.32 = (bf16[256,128]{1,0:T(8,128)(2,1)S(1)}, bf16[256,128]{1,0:T(8,128)(2,1)S(1)}, u32[]{:S(2)}, u32[]{:S(2)}) collective-permute-start(bf16[256,128]{1,0:T(8,128)(2,1)S(1)} %fusion.3.refs_3_), channel_id=1, source_target_pairs={{0,0},{1,16},{2,2},{3,18},{4,4},{5,20},{6,6},{7,22},{8,8},{9,24},{... | collective-permute-start | bytes 196616 | tf_op jit(solution)/shard_map/ppermute | solution.py:328
  187.4 7.9 %collective-permute-start.37 = (bf16[4,256,128]{2,1,0:T(8,128)(2,1)S(1)}, bf16[4,256,128]{2,1,0:T(8,128)(2,1)S(1)}, u32[]{:S(2)}, u32[]{:S(2)}) collective-permute-start(bf16[4,256,128]{2,1,0:T(8,128)(2,1)S(1)} %pad_maximum_fusion.refs_16_.refs_20_), channel_id=1, source_target_pairs={{0,4},{1,5},{2,6},{3,7},{4,0},{5,1},{6,2},{7,3},{8,12},{9,13},{10,... | collective-permute-start | bytes 786440 | tf_op jit(solution)/shard_map/ppermute | solution.py:328
  190.6 7.5 %collective-permute-start.40 = (bf16[4,256,128]{2,1,0:T(8,128)(2,1)S(1)}, bf16[4,256,128]{2,1,0:T(8,128)(2,1)S(1)}, u32[]{:S(2)}, u32[]{:S(2)}) collective-permute-start(bf16[4,256,128]{2,1,0:T(8,128)(2,1)S(1)} %pad_maximum_fusion.1.refs_24_.refs_28_), channel_id=1, source_target_pairs={{0,4},{1,5},{2,6},{3,7},{4,0},{5,1},{6,2},{7,3},{8,12},{9,13},{10,... | collective-permute-start | bytes 786440 | tf_op jit(solution)/shard_map/ppermute | solution.py:328
  193.1 5.2 %collective-permute-start.38 = (bf16[4,256,128]{2,1,0:T(8,128)(2,1)S(1)}, bf16[4,256,128]{2,1,0:T(8,128)(2,1)S(1)}, u32[]{:S(2)}, u32[]{:S(2)}) collective-permute-start(bf16[4,256,128]{2,1,0:T(8,128)(2,1)S(1)} %pad_maximum_fusion.refs_16_.refs_20_), channel_id=1, source_target_pairs={{0,2},{1,3},{2,0},{3,1},{4,6},{5,7},{6,4},{7,5},{8,10},{9,11},{10,... | collective-permute-start | bytes 786440 | tf_op jit(solution)/shard_map/ppermute | solution.py:328
  195.3 2.9 %collective-permute-start.39 = (bf16[4,256,128]{2,1,0:T(8,128)(2,1)S(1)}, bf16[4,256,128]{2,1,0:T(8,128)(2,1)}, u32[]{:S(2)}, u32[]{:S(2)}) collective-permute-start(bf16[4,256,128]{2,1,0:T(8,128)(2,1)S(1)} %collective-permute-done.37.refs_17_.refs_21_), channel_id=1, source_target_pairs={{0,2},{1,3},{2,0},{3,1},{4,6},{5,7},{6,4},{7,5},{8,10},{9,11},{10,... | collective-permute-start | bytes 786440 | tf_op jit(solution)/shard_map/ppermute | solution.py:328
  195.3 2.9 %collective-permute-start.41 = (bf16[4,256,128]{2,1,0:T(8,128)(2,1)S(1)}, bf16[4,256,128]{2,1,0:T(8,128)(2,1)}, u32[]{:S(2)}, u32[]{:S(2)}) collective-permute-start(bf16[4,256,128]{2,1,0:T(8,128)(2,1)S(1)} %pad_maximum_fusion.1.refs_24_.refs_28_), channel_id=1, source_target_pairs={{0,2},{1,3},{2,0},{3,1},{4,6},{5,7},{6,4},{7,5},{8,10},{9,11},{10,... | collective-permute-start | bytes 786440 | tf_op jit(solution)/shard_map/ppermute | solution.py:328
  198.1 1.7 collective-permute-start.42
  (13 other events, 39.0 us)
Sparse Core Ops, SparseCore 0:
  96.3 54.1 all-gather.2

commit v8 on v7

--- a/solution.py
+++ b/solution.py
@@ -350,7 +350,7 @@
     across = along_z(near, [(1, 2), (2, 1)])
     outward = along_z(middle, [(1, 0), (2, 3)])
     far = along_z(across, [(1, 0), (2, 3)])
-    units = [unit, near, jnp.where(inner, across, outward), jnp.where(inner, middle, far)]
+    units = [unit, near, jnp.where(inner, across, outward)]
 
     place = x[None]
 
@@ -378,18 +378,16 @@
         across_core = lambda i, j, k, t: (i, j, 1 - k, t)
         return (held, other, send(held, across_core), send(other, across_core)), paired
 
-    owns = [coefficients(units[k]) for k in range(2)]
-    share_a = share(jnp.stack(owns), 0)
+    owns = [coefficients(units[0], (across, outward))] + [coefficients(units[k]) for k in (1, 2)]
+    own_a = jnp.stack(owns)
+    share_a, mate_a, far = lax.optimization_barrier((share(own_a, 0), mate(own_a), far))
     right_a = lax.all_gather(share_a, ("z", "y", "c"), axis=0)
-    mates = [mate(own) for own in owns]
-    owns.append(coefficients(units[2], far))
-    units[3], _ = lax.optimization_barrier((units[3], (share_a, mates)))
-    owns.append(coefficients(units[3]))
-    rights_b = []
-    for own in owns[2:]:
-        four, paired = spread(own)
-        rights_b.append(four)
-        mates.append(paired)
+    units.append(jnp.where(inner, middle, far))
+    own_b = coefficients(units[3])
+    four, mate_b = spread(own_b)
+    owns.append(own_b)
+    mates = [mate_a[k] for k in range(3)] + [mate_b]
+    rights_b = [four]
     scalars = jnp.stack([z, y, c, 2 * x, x])
     return make_chi(owns, mates, units, right_a, rights_b, scalars, n_freq, factor)
 

time: 223 us -> 203 us (0.910); the launches traced: 219 us -> 203 us
  starting transfers between devices: 72.7 us -> 45.8 us
  waiting for transfers between devices: 88.9 us -> 98.8 us
  other arithmetic: 1.99 us -> 4.83 us
    ppermute x43 -> x34, starting transfers between devices: 67.5 us -> 40.5 us  [send(): lax.ppermute(array, AXES, [(source, number[to]) for source, to in pairs i...]
    all_gather x1, waiting for transfers between devices: 0.01 us -> 7.34 us  [fast(): right_a = lax.all_gather(share_a, ('z', 'y', 'c'), axis=0)]
    all_to_all x1, waiting for transfers between devices: 9.14 us -> 14.6 us  [local(): unit = lax.all_to_all(packed, ('y', 'c', 'x'), 0, 0, tiled=True)]
    ppermute x43 -> x34, waiting for transfers between devices: 79.7 us -> 76.8 us  [send(): lax.ppermute(array, AXES, [(source, number[to]) for source, to in pairs i...]
    unnamed x32 -> x20, local copies, waits for them, and re-layouts: 7.11 us -> 4.19 us
  transfers between devices with their start and end apart: 45 -> 36, of which waited for: 20 -> 16; matrix products, arithmetic and copies ran while one was open for 3% -> 5% of each run, Pallas kernels for 9% -> 10%
where the time goes in v8:
time: 203 us
  waiting for transfers between devices  98.8 us (49%)
  starting transfers between devices  45.8 us (23%)
  Pallas kernels  31 us (15%)
  between operations  13.7 us (7%)
  local copies, waits for them, and re-layouts  8.58 us (4%)
  other arithmetic  4.83 us (2%)
    ppermute x34, waiting for transfers between devices, send(): lax.ppermute(array, AXES, [(source, number[to]) for source, to in pairs i...  76.8 us
    ppermute x34, starting transfers between devices, send(): lax.ppermute(array, AXES, [(source, number[to]) for source, to in pairs i...  40.5 us
    pallas_call x4, Pallas kernels, project(): pl.pallas_call(functools.partial(project_kernel, segs, val_count, cond_co...  21.1 us
    all_to_all x1, waiting for transfers between devices, local(): unit = lax.all_to_all(packed, ('y', 'c', 'x'), 0, 0, tiled=True)  14.6 us
    all_gather x1, waiting for transfers between devices, fast(): right_a = lax.all_gather(share_a, ('z', 'y', 'c'), axis=0)  7.34 us
    pallas_call x1, Pallas kernels, make_chi(): pl.pallas_call(functools.partial(chi_kernel, early, late, n_freq, factor)...  5.94 us
    all_to_all x1, starting transfers between devices, local(): unit = lax.all_to_all(packed, ('y', 'c', 'x'), 0, 0, tiled=True)  5.17 us
    unnamed x20, local copies, waits for them, and re-layouts  4.19 us
  transfers between devices with their start and end apart: 36, of which 16 were waited for; matrix products, arithmetic and copies ran while one was open for 5% of the time, Pallas kernels for 10%

profile of v8, /device:TPU:0, one launch (start us, length us, event | category | flops | bytes accessed | tf_op | source)
XLA Modules:
  0.0 202.7 jit_solution(2786049816159015704)
XLA Ops:
  6.5 4.0 %pack.1 = bf16[8,16,3968]{2,1,0:T(8,128)(2,1)} custom-call(f32[4]{0:T(128)} %val_energy.1, f32[16]{0:T(128)} %cond_energy.1, s32[64]{0:T(128)} %val_slot.1, s32[64]{0:T(128)} %cond_slot.1, f32[4]{0:T(128)} %frequencies.1, bf16[16,24576]{1,0:T(8,128)(2,1)} %refs_1_.1, bf16[16,24576]{1,0:T(8,128)(2,1)} %refs_1_.1, bf16[4,24576]{1,0:T(4,128)(2,1)} %refs_3_.1, ...), custom_call_target="tpu_custom_call" | custom-call | tf_op jit(solution)/shard_map/pack/pallas_call | solution.py:77
  10.5 5.2 %all-to-all-start = ((bf16[8,16,3968]{2,1,0:T(8,128)(2,1)}), bf16[8,16,3968]{2,1,0:T(8,128)(2,1)}, u32[]{:S(2)}, u32[]{:S(2)}) async-start(bf16[8,16,3968]{2,1,0:T(8,128)(2,1)} %pack.1), calls=%async_computation | async-start | bytes 2031616 | tf_op jit(solution)/shard_map/all_to_all | solution.py:481
  15.8 14.6 %all-to-all-done = bf16[8,16,3968]{2,1,0:T(8,128)(2,1)} async-done(((bf16[8,16,3968]{2,1,0:T(8,128)(2,1)}), bf16[8,16,3968]{2,1,0:T(8,128)(2,1)}, u32[]{:S(2)}, u32[]{:S(2)}) %all-to-all-start) | async-done | bytes 1015840 | tf_op jit(solution)/shard_map/all_to_all | solution.py:481
  30.4 2.0 collective-permute-start.4
  32.4 1.6 collective-permute-start.6
  34.0 3.3 %constant_dynamic-slice_fusion = (bf16[3072,128]{1,0:T(8,128)(2,1)}, bf16[3072,128]{1,0:T(8,128)(2,1)}, bf16[3072,128]{1,0:T(8,128)(2,1)S(1)}, bf16[3072,128]{1,0:T(8,128)(2,1)}) fusion(bf16[12288,128]{1,0:T(8,128)(2,1)} %param.14, s32[]{:T(128)S(6)} %select_n.27, s32[]{:T(128)S(6)} %select_n.25, s32[]{:T(128)S(6)} %select_n.24, s32[]{:T(128)S(6)} %select_n.26), kind=kLoop, calls=%fused_computation.38 | loop fusion | bytes 6291472 | tf_op jit(solution)/shard_map/dynamic_slice | solution.py:340
  37.9 1.3 collective-permute-start.2
  39.1 15.8 %collective-permute-done.4.refs_0_.refs_1_.refs_2_.refs_3_.refs_4_.refs_9_ = bf16[128,3968]{1,0:T(8,128)(2,1)} collective-permute-done((bf16[128,3968]{1,0:T(8,128)(2,1)}, bf16[128,3968]{1,0:T(8,128)(2,1)}, u32[]{:S(2)}, u32[]{:S(2)}) %collective-permute-start.4) | collective-permute-done | bytes 1015840 | tf_op jit(solution)/shard_map/ppermute | solution.py:328
  55.0 1.7 collective-permute-start.5
  56.6 1.3 collective-permute-start.7
  57.9 16.0 %collective-permute-done.2.refs_8_.refs_12_.refs_16_.refs_20_ = bf16[3072,128]{1,0:T(8,128)(2,1)S(1)} collective-permute-done((bf16[3072,128]{1,0:T(8,128)(2,1)}, bf16[3072,128]{1,0:T(8,128)(2,1)S(1)}, u32[]{:S(2)}, u32[]{:S(2)}) %collective-permute-start.2) | collective-permute-done | bytes 786464 | tf_op jit(solution)/shard_map/ppermute | solution.py:328
  73.9 6.1 %project.5 = (f32[2,2,256,128]{3,2,1,0:T(8,128)S(1)}, f32[2,2,256,128]{3,2,1,0:T(8,128)}) custom-call(s32[1]{0:T(128)} %bitcast.4.place, bf16[128,3968]{1,0:T(8,128)(2,1)} %collective-permute-done.4.refs_0_.refs_1_.refs_2_.refs_3_.refs_4_.refs_9_, bf16[128,3968]{1,0:T(8,128)(2,1)} %collective-permute-done.4.refs_0_.refs_1_.refs_2_.refs_3_.refs_4_.refs_9_, ...), custom_call_target="tpu_custom_call" | custom-call | flops 1610612736 | bytes 4161536 | tf_op jit(solution)/shard_map/project/pallas_call | solution.py:187
  81.5 5.4 %project.4 = (f32[2,2,256,128]{3,2,1,0:T(8,128)S(1)}, f32[2,2,256,128]{3,2,1,0:T(8,128)S(1)}) custom-call(s32[1]{0:T(128)} %bitcast.4.place, bf16[128,3968]{1,0:T(8,128)(2,1)} %bitcast.5.refs_0_.refs_1_.refs_2_.refs_3_.refs_4_.refs_8_, bf16[128,3968]{1,0:T(8,128)(2,1)} %bitcast.5.refs_0_.refs_1_.refs_2_.refs_3_.refs_4_.refs_8_, ...), custom_call_target="tpu_custom_call" | custom-call | flops 1610612736 | bytes 4161536 | tf_op jit(solution)/shard_map/project/pallas_call | solution.py:187
  87.0 1.1 add.72
  88.2 1.1 collective-permute-start.14
  89.2 1.5 collective-permute-start.13
  90.7 1.0 collective-permute-start.12
  91.7 1.3 broadcast_select_fusion.1.refs_0_.refs_1_.refs_2_.refs_3_.refs_4_.refs_10_
  93.1 4.8 %project.6 = (f32[2,2,256,128]{3,2,1,0:T(8,128)S(1)}, f32[2,2,256,128]{3,2,1,0:T(8,128)S(1)}) custom-call(s32[1]{0:T(128)} %bitcast.4.place, bf16[128,3968]{1,0:T(8,128)(2,1)S(1)} %broadcast_select_fusion.1.refs_0_.refs_1_.refs_2_.refs_3_.refs_4_.refs_10_, bf16[128,3968]{1,0:T(8,128)(2,1)S(1)} %broadcast_select_fusion.1.refs_0_.refs_1_.refs_2_.refs_3_.refs_4_.refs_10_, ...), custom_call_target="tpu_custom_call" | custom-call | flops 1610612736 | bytes 4161536 | tf_op jit(solution)/shard_map/project/pallas_call | solution.py:187
  98.1 1.1 collective-permute-start.10
  99.2 1.5 collective-permute-start.9
  100.6 1.0 collective-permute-start.8
  101.7 1.3 collective-permute-start.21
  103.1 1.1 collective-permute-start.18
  104.1 1.3 collective-permute-done.10
  105.9 2.3 %collective-permute-done.9 = f32[256,128]{1,0:T(8,128)S(1)} collective-permute-done((f32[256,128]{1,0:T(8,128)S(1)}, f32[256,128]{1,0:T(8,128)S(1)}, u32[]{:S(2)}, u32[]{:S(2)}) %collective-permute-start.9) | collective-permute-done | bytes 131104 | tf_op jit(solution)/shard_map/ppermute | solution.py:328
  108.2 1.1 collective-permute-start.16
  109.3 1.4 collective-permute-done.18
  110.7 2.5 %collective-permute-done.17 = f32[256,128]{1,0:T(8,128)S(1)} collective-permute-done((f32[256,128]{1,0:T(8,128)S(1)}, f32[256,128]{1,0:T(8,128)S(1)}, u32[]{:S(2)}, u32[]{:S(2)}) %collective-permute-start.17) | collective-permute-done | bytes 131104 | tf_op jit(solution)/shard_map/ppermute | solution.py:328
  113.9 1.6 collective-permute-start.19
  115.5 4.8 %collective-permute-start.20 = (bf16[3,256,128]{2,1,0:T(8,128)(2,1)}, bf16[3,256,128]{2,1,0:T(8,128)(2,1)}, u32[]{:S(2)}, u32[]{:S(2)}) collective-permute-start(bf16[3,256,128]{2,1,0:T(8,128)(2,1)} %pad_maximum_fusion.1), channel_id=1, source_target_pairs={{0,1},{1,0},{2,3},{3,2},{4,5},{5,4},{6,7},{7,6},{8,9},{9,8},{10,11... | collective-permute-start | bytes 589832 | tf_op jit(solution)/shard_map/ppermute | solution.py:328
  120.3 5.9 %collective-permute-done.20 = bf16[3,256,128]{2,1,0:T(8,128)(2,1)} collective-permute-done((bf16[3,256,128]{2,1,0:T(8,128)(2,1)}, bf16[3,256,128]{2,1,0:T(8,128)(2,1)}, u32[]{:S(2)}, u32[]{:S(2)}) %collective-permute-start.20) | collective-permute-done | bytes 196640 | tf_op jit(solution)/shard_map/ppermute | solution.py:328
  126.2 7.0 %collective-permute-done.21 = bf16[128,3968]{1,0:T(8,128)(2,1)} collective-permute-done((bf16[128,3968]{1,0:T(8,128)(2,1)}, bf16[128,3968]{1,0:T(8,128)(2,1)}, u32[]{:S(2)}, u32[]{:S(2)}) %collective-permute-start.21) | collective-permute-done | bytes 1015840 | tf_op jit(solution)/shard_map/ppermute | solution.py:328
  133.2 1.3 broadcast_select_fusion.refs_0_.refs_1_.refs_2_.refs_3_.refs_4_.refs_11_
  134.6 4.8 %project.7 = (f32[2,2,256,128]{3,2,1,0:T(8,128)S(1)}, f32[2,2,256,128]{3,2,1,0:T(8,128)S(1)}) custom-call(s32[1]{0:T(128)} %bitcast.4.place, bf16[128,3968]{1,0:T(8,128)(2,1)S(1)} %broadcast_select_fusion.refs_0_.refs_1_.refs_2_.refs_3_.refs_4_.refs_11_, bf16[128,3968]{1,0:T(8,128)(2,1)S(1)} %broadcast_select_fusion.refs_0_.refs_1_.refs_2_.refs_3_.refs_4_.refs_11_, ...), custom_call_target="tpu_custom_call" | custom-call | flops 1610612736 | bytes 4161536 | tf_op jit(solution)/shard_map/project/pallas_call | solution.py:187
  139.4 1.9 collective-permute-done.22
  142.1 2.9 %collective-permute-start.23 = (f32[256,128]{1,0:T(8,128)S(1)}, f32[256,128]{1,0:T(8,128)S(1)}, u32[]{:S(2)}, u32[]{:S(2)}) collective-permute-start(f32[256,128]{1,0:T(8,128)S(1)} %get-tuple-element.43), channel_id=1, source_target_pairs={{0,1},{1,0},{2,3},{3,2},{4,5},{5,4},{6,7},{7,6},{8,9},{9,8},{10,11... | collective-permute-start | bytes 393224 | tf_op jit(solution)/shard_map/ppermute | solution.py:328
  145.0 3.8 %collective-permute-done.25 = f32[256,128]{1,0:T(8,128)S(1)} collective-permute-done((f32[256,128]{1,0:T(8,128)S(1)}, f32[256,128]{1,0:T(8,128)S(1)}, u32[]{:S(2)}, u32[]{:S(2)}) %collective-permute-start.25) | collective-permute-done | bytes 131104 | tf_op jit(solution)/shard_map/ppermute | solution.py:328
  148.8 1.1 collective-permute-done.24
  150.7 0.9 collective-permute-start.27
  151.6 6.0 %collective-permute-start.28 = (bf16[256,128]{1,0:T(8,128)(2,1)S(1)}, bf16[256,128]{1,0:T(8,128)(2,1)S(1)}, u32[]{:S(2)}, u32[]{:S(2)}) collective-permute-start(bf16[256,128]{1,0:T(8,128)(2,1)S(1)} %fusion.3.refs_3_), channel_id=1, source_target_pairs={{0,16},{1,0},{2,18},{3,2},{4,20},{5,4},{6,22},{7,6},{8,24},{9,8},{... | collective-permute-start | bytes 196616 | tf_op jit(solution)/shard_map/ppermute | solution.py:328
  157.6 1.9 collective-permute-start.30
  159.5 4.6 %collective-permute-done.29 = bf16[256,128]{1,0:T(8,128)(2,1)S(1)} collective-permute-done((bf16[256,128]{1,0:T(8,128)(2,1)S(1)}, bf16[256,128]{1,0:T(8,128)(2,1)S(1)}, u32[]{:S(2)}, u32[]{:S(2)}) %collective-permute-start.29) | collective-permute-done | bytes 65568 | tf_op jit(solution)/shard_map/ppermute | solution.py:328
  165.6 12.6 %collective-permute-done.31.refs_17_.refs_21_ = bf16[4,256,128]{2,1,0:T(8,128)(2,1)S(1)} collective-permute-done((bf16[4,256,128]{2,1,0:T(8,128)(2,1)S(1)}, bf16[4,256,128]{2,1,0:T(8,128)(2,1)S(1)}, u32[]{:S(2)}, u32[]{:S(2)}) %collective-permute-start.31) | collective-permute-done | bytes 262176 | tf_op jit(solution)/shard_map/ppermute | solution.py:328
  178.4 0.9 slice_bitcast_fusion.15
  179.8 7.3 %all-gather.3.cloned.1.call-done = bf16[48,256,128]{2,1,0:T(8,128)(2,1)} async-done(((bf16[3,256,128]{2,1,0:T(8,128)(2,1)}), bf16[48,256,128]{2,1,0:T(8,128)(2,1)}) %all-gather.3.cloned.1.call-update) | async-done | bytes 3145744 | tf_op jit(solution)/shard_map/all_gather | solution.py:384
  187.2 1.9 copy-done
  189.9 5.9 %chi.1 = f32[128,4,1024]{2,1,0:T(4,128)} custom-call(s32[5]{0:T(128)S(1)} %stack.50.scalars, bf16[256,128]{1,0:T(8,128)(2,1)S(1)} %fusion.14.refs_0_, bf16[256,128]{1,0:T(8,128)(2,1)S(1)} %fusion.11.refs_1_, bf16[256,128]{1,0:T(8,128)(2,1)S(1)} %fusion.7.refs_2_, bf16[256,128]{1,0:T(8,128)(2,1)S(1)} %fusion.3.refs_3_, ...), custom_call_target="tpu_custom_call" | custom-call | flops 2147483648 | bytes 6291456 | tf_op jit(solution)/shard_map/chi/pallas_call | solution.py:281
  (70 shorter events, 8.4 us)
Async XLA Ops:
  10.5 19.9 %all-to-all-start = ((bf16[8,16,3968]{2,1,0:T(8,128)(2,1)}), bf16[8,16,3968]{2,1,0:T(8,128)(2,1)}, u32[]{:S(2)}, u32[]{:S(2)}) async-start(bf16[8,16,3968]{2,1,0:T(8,128)(2,1)} %pack.1), calls=%async_computation | async-start | bytes 2031616 | tf_op jit(solution)/shard_map/all_to_all | solution.py:481
  15.7 171.5 %all-gather.3.cloned.1.call-start = ((), (), s32[]{:S(2)}) async-start(), calls=%async_computation.1 | async-start | bytes 3342336 | tf_op jit(solution)/shard_map/all_gather | solution.py:384
  30.4 24.6 %collective-permute-start.4 = (bf16[128,3968]{1,0:T(8,128)(2,1)}, bf16[128,3968]{1,0:T(8,128)(2,1)}, u32[]{:S(2)}, u32[]{:S(2)}) collective-permute-start(bf16[128,3968]{1,0:T(8,128)(2,1)} %bitcast.5.refs_0_.refs_1_.refs_2_.refs_3_.refs_4_.refs_8_), channel_id=1, source_target_pairs={{0,8},{1,9},{2,10},{3,11},{4,12},{5,13},{6,14},{7,15},{8,0},{9,1},... | collective-permute-start | bytes 3047432 | tf_op jit(solution)/shard_map/ppermute | solution.py:328
  32.4 24.3 %collective-permute-start.6 = (bf16[128,3968]{1,0:T(8,128)(2,1)}, bf16[128,3968]{1,0:T(8,128)(2,1)}, u32[]{:S(2)}, u32[]{:S(2)}) collective-permute-start(bf16[128,3968]{1,0:T(8,128)(2,1)} %bitcast.5.refs_0_.refs_1_.refs_2_.refs_3_.refs_4_.refs_8_), channel_id=1, source_target_pairs={{8,16},{9,17},{10,18},{11,19},{12,20},{13,21},{14,22},{15,23},{16,... | collective-permute-start | bytes 3047432 | tf_op jit(solution)/shard_map/ppermute | solution.py:328
  37.3 20.6 %collective-permute-start = (bf16[3072,128]{1,0:T(8,128)(2,1)}, bf16[3072,128]{1,0:T(8,128)(2,1)S(1)}, u32[]{:S(2)}, u32[]{:S(2)}) collective-permute-start(bf16[3072,128]{1,0:T(8,128)(2,1)} %get-tuple-element.40), channel_id=1, source_target_pairs={{0,2},{1,3},{2,0},{3,1},{4,6},{5,7},{6,4},{7,5},{8,10},{9,11},{10,... | collective-permute-start | bytes 2359304 | tf_op jit(solution)/shard_map/ppermute | solution.py:328
  37.3 20.7 %collective-permute-start.1 = (bf16[3072,128]{1,0:T(8,128)(2,1)}, bf16[3072,128]{1,0:T(8,128)(2,1)S(1)}, u32[]{:S(2)}, u32[]{:S(2)}) collective-permute-start(bf16[3072,128]{1,0:T(8,128)(2,1)} %get-tuple-element.42), channel_id=1, source_target_pairs={{0,4},{1,5},{2,6},{3,7},{4,0},{5,1},{6,2},{7,3},{8,12},{9,13},{10,... | collective-permute-start | bytes 2359304 | tf_op jit(solution)/shard_map/ppermute | solution.py:328
  37.9 36.0 %collective-permute-start.2 = (bf16[3072,128]{1,0:T(8,128)(2,1)}, bf16[3072,128]{1,0:T(8,128)(2,1)S(1)}, u32[]{:S(2)}, u32[]{:S(2)}) collective-permute-start(bf16[3072,128]{1,0:T(8,128)(2,1)} %get-tuple-element.39), channel_id=1, source_target_pairs={{0,6},{1,7},{2,4},{3,5},{4,2},{5,3},{6,0},{7,1},{8,14},{9,15},{10,... | collective-permute-start | bytes 2359304 | tf_op jit(solution)/shard_map/ppermute | solution.py:328
  55.0 35.7 %collective-permute-start.5 = (bf16[128,3968]{1,0:T(8,128)(2,1)}, bf16[128,3968]{1,0:T(8,128)(2,1)}, u32[]{:S(2)}, u32[]{:S(2)}) collective-permute-start(bf16[128,3968]{1,0:T(8,128)(2,1)} %collective-permute-done.4.refs_0_.refs_1_.refs_2_.refs_3_.refs_4_.refs_9_), channel_id=1, source_target_pairs={{8,16},{9,17},{10,18},{11,19},{12,20},{13,21},{14,22},{15,23},{16,... | collective-permute-start | bytes 3047432 | tf_op jit(solution)/shard_map/ppermute | solution.py:328
  56.6 35.1 %collective-permute-start.7 = (bf16[128,3968]{1,0:T(8,128)(2,1)}, bf16[128,3968]{1,0:T(8,128)(2,1)}, u32[]{:S(2)}, u32[]{:S(2)}) collective-permute-start(bf16[128,3968]{1,0:T(8,128)(2,1)} %collective-permute-done.6), channel_id=1, source_target_pairs={{8,0},{9,1},{10,2},{11,3},{12,4},{13,5},{14,6},{15,7},{16,24},{17,... | collective-permute-start | bytes 3047432 | tf_op jit(solution)/shard_map/ppermute | solution.py:328
  80.1 0.8 copy-start.5
  80.9 6.2 %collective-permute-start.11 = (f32[2,2,256,128]{3,2,1,0:T(8,128)}, f32[2,2,256,128]{3,2,1,0:T(8,128)}, u32[]{:S(2)}, u32[]{:S(2)}) collective-permute-start(f32[2,2,256,128]{3,2,1,0:T(8,128)} %get-tuple-element.26), channel_id=1, source_target_pairs={{0,2},{1,3},{2,0},{3,1},{4,6},{5,7},{6,4},{7,5},{8,10},{9,11},{10,... | collective-permute-start | bytes 1572872 | tf_op jit(solution)/shard_map/ppermute | solution.py:328
  81.5 5.5 %copy-start.6 = (f32[2,2,256,128]{3,2,1,0:T(8,128)S(1)}, f32[2,2,256,128]{3,2,1,0:T(8,128)}, u32[]{:S(2)}) copy-start(f32[2,2,256,128]{3,2,1,0:T(8,128)} %copy-done.5) | copy-start | bytes 1572868
  86.9 11.0 %collective-permute-start.3 = (f32[2,2,256,128]{3,2,1,0:T(8,128)S(1)}, f32[2,2,256,128]{3,2,1,0:T(8,128)S(1)}, u32[]{:S(2)}, u32[]{:S(2)}) collective-permute-start(f32[2,2,256,128]{3,2,1,0:T(8,128)S(1)} %get-tuple-element.23), channel_id=1, source_target_pairs={{0,2},{1,3},{2,0},{3,1},{4,6},{5,7},{6,4},{7,5},{8,10},{9,11},{10,... | collective-permute-start | bytes 1572872 | tf_op jit(solution)/shard_map/ppermute | solution.py:328
  88.2 9.8 %collective-permute-start.14 = (f32[256,128]{1,0:T(8,128)S(1)}, f32[256,128]{1,0:T(8,128)S(1)}, u32[]{:S(2)}, u32[]{:S(2)}) collective-permute-start(f32[256,128]{1,0:T(8,128)S(1)} %get-tuple-element.50), channel_id=1, source_target_pairs={{0,5},{1,4},{2,7},{3,6},{4,1},{5,0},{6,3},{7,2},{8,13},{9,12},{10,... | collective-permute-start | bytes 393224 | tf_op jit(solution)/shard_map/ppermute | solution.py:328
  89.2 8.8 %collective-permute-start.13 = (f32[256,128]{1,0:T(8,128)S(1)}, f32[256,128]{1,0:T(8,128)S(1)}, u32[]{:S(2)}, u32[]{:S(2)}) collective-permute-start(f32[256,128]{1,0:T(8,128)S(1)} %get-tuple-element.51), channel_id=1, source_target_pairs={{0,4},{1,5},{2,6},{3,7},{4,0},{5,1},{6,2},{7,3},{8,12},{9,13},{10,... | collective-permute-start | bytes 393224 | tf_op jit(solution)/shard_map/ppermute | solution.py:328
  90.7 7.3 %collective-permute-start.12 = (f32[256,128]{1,0:T(8,128)S(1)}, f32[256,128]{1,0:T(8,128)S(1)}, u32[]{:S(2)}, u32[]{:S(2)}) collective-permute-start(f32[256,128]{1,0:T(8,128)S(1)} %get-tuple-element.49), channel_id=1, source_target_pairs={{0,1},{1,0},{2,3},{3,2},{4,5},{5,4},{6,7},{7,6},{8,9},{9,8},{10,11... | collective-permute-start | bytes 393224 | tf_op jit(solution)/shard_map/ppermute | solution.py:328
  93.1 4.8 %copy-start.1 = (bf16[128,3968]{1,0:T(8,128)(2,1)}, bf16[128,3968]{1,0:T(8,128)(2,1)S(1)}, u32[]{:S(2)}) copy-start(bf16[128,3968]{1,0:T(8,128)(2,1)S(1)} %broadcast_select_fusion.1.refs_0_.refs_1_.refs_2_.refs_3_.refs_4_.refs_10_) | copy-start | bytes 3047428
  97.9 5.1 %collective-permute-start.15 = (f32[2,2,256,128]{3,2,1,0:T(8,128)S(1)}, f32[2,2,256,128]{3,2,1,0:T(8,128)S(1)}, u32[]{:S(2)}, u32[]{:S(2)}) collective-permute-start(f32[2,2,256,128]{3,2,1,0:T(8,128)S(1)} %get-tuple-element.28), channel_id=1, source_target_pairs={{0,2},{1,3},{2,0},{3,1},{4,6},{5,7},{6,4},{7,5},{8,10},{9,11},{10,... | collective-permute-start | bytes 1572872 | tf_op jit(solution)/shard_map/ppermute | solution.py:328
  98.1 7.3 %collective-permute-start.10 = (f32[256,128]{1,0:T(8,128)S(1)}, f32[256,128]{1,0:T(8,128)S(1)}, u32[]{:S(2)}, u32[]{:S(2)}) collective-permute-start(f32[256,128]{1,0:T(8,128)S(1)} %get-tuple-element.53), channel_id=1, source_target_pairs={{0,5},{1,4},{2,7},{3,6},{4,1},{5,0},{6,3},{7,2},{8,13},{9,12},{10,... | collective-permute-start | bytes 393224 | tf_op jit(solution)/shard_map/ppermute | solution.py:328
  99.2 9.0 %collective-permute-start.9 = (f32[256,128]{1,0:T(8,128)S(1)}, f32[256,128]{1,0:T(8,128)S(1)}, u32[]{:S(2)}, u32[]{:S(2)}) collective-permute-start(f32[256,128]{1,0:T(8,128)S(1)} %get-tuple-element.54), channel_id=1, source_target_pairs={{0,4},{1,5},{2,6},{3,7},{4,0},{5,1},{6,2},{7,3},{8,12},{9,13},{10,... | collective-permute-start | bytes 393224 | tf_op jit(solution)/shard_map/ppermute | solution.py:328
  100.6 8.6 %collective-permute-start.8 = (f32[256,128]{1,0:T(8,128)S(1)}, f32[256,128]{1,0:T(8,128)S(1)}, u32[]{:S(2)}, u32[]{:S(2)}) collective-permute-start(f32[256,128]{1,0:T(8,128)S(1)} %get-tuple-element.52), channel_id=1, source_target_pairs={{0,1},{1,0},{2,3},{3,2},{4,5},{5,4},{6,7},{7,6},{8,9},{9,8},{10,11... | collective-permute-start | bytes 393224 | tf_op jit(solution)/shard_map/ppermute | solution.py:328
  101.7 31.5 %collective-permute-start.21 = (bf16[128,3968]{1,0:T(8,128)(2,1)}, bf16[128,3968]{1,0:T(8,128)(2,1)}, u32[]{:S(2)}, u32[]{:S(2)}) collective-permute-start(bf16[128,3968]{1,0:T(8,128)(2,1)} %collective-permute-done.5), channel_id=1, source_target_pairs={{8,0},{9,1},{10,2},{11,3},{12,4},{13,5},{14,6},{15,7},{16,24},{17,... | collective-permute-start | bytes 3047432 | tf_op jit(solution)/shard_map/ppermute | solution.py:328
  103.1 7.7 %collective-permute-start.18 = (f32[256,128]{1,0:T(8,128)S(1)}, f32[256,128]{1,0:T(8,128)S(1)}, u32[]{:S(2)}, u32[]{:S(2)}) collective-permute-start(f32[256,128]{1,0:T(8,128)S(1)} %get-tuple-element.47), channel_id=1, source_target_pairs={{0,5},{1,4},{2,7},{3,6},{4,1},{5,0},{6,3},{7,2},{8,13},{9,12},{10,... | collective-permute-start | bytes 393224 | tf_op jit(solution)/shard_map/ppermute | solution.py:328
  105.4 7.8 %collective-permute-start.17 = (f32[256,128]{1,0:T(8,128)S(1)}, f32[256,128]{1,0:T(8,128)S(1)}, u32[]{:S(2)}, u32[]{:S(2)}) collective-permute-start(f32[256,128]{1,0:T(8,128)S(1)} %get-tuple-element.48), channel_id=1, source_target_pairs={{0,4},{1,5},{2,6},{3,7},{4,0},{5,1},{6,2},{7,3},{8,12},{9,13},{10,... | collective-permute-start | bytes 393224 | tf_op jit(solution)/shard_map/ppermute | solution.py:328
  108.2 5.0 %collective-permute-start.16 = (f32[256,128]{1,0:T(8,128)S(1)}, f32[256,128]{1,0:T(8,128)S(1)}, u32[]{:S(2)}, u32[]{:S(2)}) collective-permute-start(f32[256,128]{1,0:T(8,128)S(1)} %get-tuple-element.46), channel_id=1, source_target_pairs={{0,1},{1,0},{2,3},{3,2},{4,5},{5,4},{6,7},{7,6},{8,9},{9,8},{10,11... | collective-permute-start | bytes 393224 | tf_op jit(solution)/shard_map/ppermute | solution.py:328
  113.9 6.3 %collective-permute-start.19 = (bf16[3,256,128]{2,1,0:T(8,128)(2,1)}, bf16[3,256,128]{2,1,0:T(8,128)(2,1)S(1)}, u32[]{:S(2)}, u32[]{:S(2)}) collective-permute-start(bf16[3,256,128]{2,1,0:T(8,128)(2,1)} %pad_maximum_fusion.1), channel_id=1, source_target_pairs={{0,0},{1,16},{2,2},{3,18},{4,4},{5,20},{6,6},{7,22},{8,8},{9,24},{... | collective-permute-start | bytes 589832 | tf_op jit(solution)/shard_map/ppermute | solution.py:328
  115.5 10.7 %collective-permute-start.20 = (bf16[3,256,128]{2,1,0:T(8,128)(2,1)}, bf16[3,256,128]{2,1,0:T(8,128)(2,1)}, u32[]{:S(2)}, u32[]{:S(2)}) collective-permute-start(bf16[3,256,128]{2,1,0:T(8,128)(2,1)} %pad_maximum_fusion.1), channel_id=1, source_target_pairs={{0,1},{1,0},{2,3},{3,2},{4,5},{5,4},{6,7},{7,6},{8,9},{9,8},{10,11... | collective-permute-start | bytes 589832 | tf_op jit(solution)/shard_map/ppermute | solution.py:328
  120.3 12.9 %copy-start.9 = (bf16[3,256,128]{2,1,0:T(8,128)(2,1)}, bf16[3,256,128]{2,1,0:T(8,128)(2,1)S(1)}, u32[]{:S(2)}) copy-start(bf16[3,256,128]{2,1,0:T(8,128)(2,1)S(1)} %collective-permute-done.19) | copy-start | bytes 589828
  134.5 4.8 %copy-start.3 = (bf16[128,3968]{1,0:T(8,128)(2,1)}, bf16[128,3968]{1,0:T(8,128)(2,1)S(1)}, u32[]{:S(2)}) copy-start(bf16[128,3968]{1,0:T(8,128)(2,1)S(1)} %broadcast_select_fusion.refs_0_.refs_1_.refs_2_.refs_3_.refs_4_.refs_11_) | copy-start | bytes 3047428
  139.3 47.8 %copy-start.2 = (bf16[128,3968]{1,0:T(8,128)(2,1)S(1)}, bf16[128,3968]{1,0:T(8,128)(2,1)}, u32[]{:S(2)}) copy-start(bf16[128,3968]{1,0:T(8,128)(2,1)} %copy-done.1) | copy-start | bytes 3047428
  139.4 47.8 %copy-start.4 = (bf16[128,3968]{1,0:T(8,128)(2,1)S(1)}, bf16[128,3968]{1,0:T(8,128)(2,1)}, u32[]{:S(2)}) copy-start(bf16[128,3968]{1,0:T(8,128)(2,1)} %copy-done.3) | copy-start | bytes 3047428
  139.4 2.0 collective-permute-start.22
  141.5 7.4 %collective-permute-start.25 = (f32[256,128]{1,0:T(8,128)S(1)}, f32[256,128]{1,0:T(8,128)S(1)}, u32[]{:S(2)}, u32[]{:S(2)}) collective-permute-start(f32[256,128]{1,0:T(8,128)S(1)} %get-tuple-element.44), channel_id=1, source_target_pairs={{0,5},{1,4},{2,7},{3,6},{4,1},{5,0},{6,3},{7,2},{8,13},{9,12},{10,... | collective-permute-start | bytes 393224 | tf_op jit(solution)/shard_map/ppermute | solution.py:328
  141.5 8.4 %collective-permute-start.24 = (f32[256,128]{1,0:T(8,128)S(1)}, f32[256,128]{1,0:T(8,128)S(1)}, u32[]{:S(2)}, u32[]{:S(2)}) collective-permute-start(f32[256,128]{1,0:T(8,128)S(1)} %get-tuple-element.45), channel_id=1, source_target_pairs={{0,4},{1,5},{2,6},{3,7},{4,0},{5,1},{6,2},{7,3},{8,12},{9,13},{10,... | collective-permute-start | bytes 393224 | tf_op jit(solution)/shard_map/ppermute | solution.py:328
  142.1 7.8 %collective-permute-start.23 = (f32[256,128]{1,0:T(8,128)S(1)}, f32[256,128]{1,0:T(8,128)S(1)}, u32[]{:S(2)}, u32[]{:S(2)}) collective-permute-start(f32[256,128]{1,0:T(8,128)S(1)} %get-tuple-element.43), channel_id=1, source_target_pairs={{0,1},{1,0},{2,3},{3,2},{4,5},{5,4},{6,7},{7,6},{8,9},{9,8},{10,11... | collective-permute-start | bytes 393224 | tf_op jit(solution)/shard_map/ppermute | solution.py:328
  150.0 9.5 %collective-permute-start.26 = (bf16[256,128]{1,0:T(8,128)(2,1)S(1)}, bf16[256,128]{1,0:T(8,128)(2,1)S(1)}, u32[]{:S(2)}, u32[]{:S(2)}) collective-permute-start(bf16[256,128]{1,0:T(8,128)(2,1)S(1)} %fusion.3.refs_3_), channel_id=1, source_target_pairs={{0,0},{1,16},{2,2},{3,18},{4,4},{5,20},{6,6},{7,22},{8,8},{9,24},{... | collective-permute-start | bytes 196616 | tf_op jit(solution)/shard_map/ppermute | solution.py:328
  150.7 8.8 %collective-permute-start.27 = (bf16[256,128]{1,0:T(8,128)(2,1)S(1)}, bf16[256,128]{1,0:T(8,128)(2,1)S(1)}, u32[]{:S(2)}, u32[]{:S(2)}) collective-permute-start(bf16[256,128]{1,0:T(8,128)(2,1)S(1)} %fusion.3.refs_3_), channel_id=1, source_target_pairs={{0,8},{1,24},{2,10},{3,26},{4,12},{5,28},{6,14},{7,30},{8,0},{9,16... | collective-permute-start | bytes 196616 | tf_op jit(solution)/shard_map/ppermute | solution.py:328
  151.6 7.9 %collective-permute-start.28 = (bf16[256,128]{1,0:T(8,128)(2,1)S(1)}, bf16[256,128]{1,0:T(8,128)(2,1)S(1)}, u32[]{:S(2)}, u32[]{:S(2)}) collective-permute-start(bf16[256,128]{1,0:T(8,128)(2,1)S(1)} %fusion.3.refs_3_), channel_id=1, source_target_pairs={{0,16},{1,0},{2,18},{3,2},{4,20},{5,4},{6,22},{7,6},{8,24},{9,8},{... | collective-permute-start | bytes 196616 | tf_op jit(solution)/shard_map/ppermute | solution.py:328
  157.6 6.5 %collective-permute-start.29 = (bf16[256,128]{1,0:T(8,128)(2,1)S(1)}, bf16[256,128]{1,0:T(8,128)(2,1)S(1)}, u32[]{:S(2)}, u32[]{:S(2)}) collective-permute-start(bf16[256,128]{1,0:T(8,128)(2,1)S(1)} %fusion.3.refs_3_), channel_id=1, source_target_pairs={{0,24},{1,8},{2,26},{3,10},{4,28},{5,12},{6,30},{7,14},{8,16},{9,0... | collective-permute-start | bytes 196616 | tf_op jit(solution)/shard_map/ppermute | solution.py:328
  157.6 6.5 %collective-permute-start.30 = (bf16[256,128]{1,0:T(8,128)(2,1)S(1)}, bf16[256,128]{1,0:T(8,128)(2,1)S(1)}, u32[]{:S(2)}, u32[]{:S(2)}) collective-permute-start(bf16[256,128]{1,0:T(8,128)(2,1)S(1)} %fusion.3.refs_3_), channel_id=1, source_target_pairs={{0,1},{1,0},{2,3},{3,2},{4,5},{5,4},{6,7},{7,6},{8,9},{9,8},{10,11... | collective-permute-start | bytes 196616 | tf_op jit(solution)/shard_map/ppermute | solution.py:328
  164.1 0.6 copy-start.7
  164.7 13.5 %collective-permute-start.31 = (bf16[4,256,128]{2,1,0:T(8,128)(2,1)S(1)}, bf16[4,256,128]{2,1,0:T(8,128)(2,1)S(1)}, u32[]{:S(2)}, u32[]{:S(2)}) collective-permute-start(bf16[4,256,128]{2,1,0:T(8,128)(2,1)S(1)} %pad_maximum_fusion.refs_16_.refs_20_), channel_id=1, source_target_pairs={{0,4},{1,5},{2,6},{3,7},{4,0},{5,1},{6,2},{7,3},{8,12},{9,13},{10,... | collective-permute-start | bytes 786440 | tf_op jit(solution)/shard_map/ppermute | solution.py:328
  165.6 13.7 %collective-permute-start.32 = (bf16[4,256,128]{2,1,0:T(8,128)(2,1)S(1)}, bf16[4,256,128]{2,1,0:T(8,128)(2,1)S(1)}, u32[]{:S(2)}, u32[]{:S(2)}) collective-permute-start(bf16[4,256,128]{2,1,0:T(8,128)(2,1)S(1)} %pad_maximum_fusion.refs_16_.refs_20_), channel_id=1, source_target_pairs={{0,2},{1,3},{2,0},{3,1},{4,6},{5,7},{6,4},{7,5},{8,10},{9,11},{10,... | collective-permute-start | bytes 786440 | tf_op jit(solution)/shard_map/ppermute | solution.py:328
  178.3 1.6 collective-permute-start.33
  187.2 1.9 copy-start
  189.1 0.8 copy-start.8
Sparse Core Ops, SparseCore 0:
  133.3 53.7 all-gather.2

commit v9 on v8

--- a/solution.py
+++ b/solution.py
@@ -378,12 +378,14 @@
         across_core = lambda i, j, k, t: (i, j, 1 - k, t)
         return (held, other, send(held, across_core), send(other, across_core)), paired
 
-    owns = [coefficients(units[0], (across, outward))] + [coefficients(units[k]) for k in (1, 2)]
+    owns = [coefficients(units[0], (across, outward)), coefficients(units[1])]
+    owns.append(coefficients(units[2], far))
     own_a = jnp.stack(owns)
-    share_a, mate_a, far = lax.optimization_barrier((share(own_a, 0), mate(own_a), far))
+    share_a = share(own_a, 0)
     right_a = lax.all_gather(share_a, ("z", "y", "c"), axis=0)
     units.append(jnp.where(inner, middle, far))
-    own_b = coefficients(units[3])
+    mate_a = mate(own_a)
+    own_b = coefficients(units[3], (share_a, mate_a))
     four, mate_b = spread(own_b)
     owns.append(own_b)
     mates = [mate_a[k] for k in range(3)] + [mate_b]

time: 203 us -> 206 us (1.015); the launches traced: 203 us -> 202 us
  waiting for transfers between devices: 98.8 us -> 89.2 us
  starting transfers between devices: 45.8 us -> 54.1 us
    ppermute x34, starting transfers between devices: 40.5 us -> 48.9 us  [send(): lax.ppermute(array, AXES, [(source, number[to]) for source, to in pairs i...]
    all_gather x1, waiting for transfers between devices: 7.34 us -> 1.34 us  [fast(): right_a = lax.all_gather(share_a, ('z', 'y', 'c'), axis=0)]
    ppermute x34, waiting for transfers between devices: 76.8 us -> 73.2 us  [send(): lax.ppermute(array, AXES, [(source, number[to]) for source, to in pairs i...]
    unnamed x20 -> x28, local copies, waits for them, and re-layouts: 4.19 us -> 5.56 us
  transfers between devices with their start and end apart: 36 -> 36, of which waited for: 16 -> 14; matrix products, arithmetic and copies ran while one was open for 5% -> 4% of each run, Pallas kernels for 10% -> 10%
where the time goes in v9:
time: 206 us; the launch traced here: 202 us
  waiting for transfers between devices  89.2 us (43%)
  starting transfers between devices  54.1 us (26%)
  Pallas kernels  31 us (15%)
  between operations  13.8 us (7%)
  local copies, waits for them, and re-layouts  9.96 us (5%)
  other arithmetic  4.16 us (2%)
    ppermute x34, waiting for transfers between devices, send(): lax.ppermute(array, AXES, [(source, number[to]) for source, to in pairs i...  73.2 us
    ppermute x34, starting transfers between devices, send(): lax.ppermute(array, AXES, [(source, number[to]) for source, to in pairs i...  48.9 us
    pallas_call x4, Pallas kernels, project(): pl.pallas_call(functools.partial(project_kernel, segs, val_count, cond_co...  21.1 us
    all_to_all x1, waiting for transfers between devices, local(): unit = lax.all_to_all(packed, ('y', 'c', 'x'), 0, 0, tiled=True)  14.6 us
    pallas_call x1, Pallas kernels, make_chi(): pl.pallas_call(functools.partial(chi_kernel, early, late, n_freq, factor)...  5.88 us
    unnamed x28, local copies, waits for them, and re-layouts  5.56 us
    all_to_all x1, starting transfers between devices, local(): unit = lax.all_to_all(packed, ('y', 'c', 'x'), 0, 0, tiled=True)  5.17 us
  transfers between devices with their start and end apart: 36, of which 14 were waited for; matrix products, arithmetic and copies ran while one was open for 4% of the time, Pallas kernels for 10%

profile of v9, /device:TPU:0, one launch (start us, length us, event | category | flops | bytes accessed | tf_op | source)
XLA Modules:
  0.0 202.2 jit_solution(10778180083166388083)
XLA Ops:
  6.5 4.0 %pack.1 = bf16[8,16,3968]{2,1,0:T(8,128)(2,1)} custom-call(f32[4]{0:T(128)} %val_energy.1, f32[16]{0:T(128)} %cond_energy.1, s32[64]{0:T(128)} %val_slot.1, s32[64]{0:T(128)} %cond_slot.1, f32[4]{0:T(128)} %frequencies.1, bf16[16,24576]{1,0:T(8,128)(2,1)} %refs_1_.1, bf16[16,24576]{1,0:T(8,128)(2,1)} %refs_1_.1, bf16[4,24576]{1,0:T(4,128)(2,1)} %refs_3_.1, ...), custom_call_target="tpu_custom_call" | custom-call | tf_op jit(solution)/shard_map/pack/pallas_call | solution.py:77
  10.5 5.2 %all-to-all-start = ((bf16[8,16,3968]{2,1,0:T(8,128)(2,1)}), bf16[8,16,3968]{2,1,0:T(8,128)(2,1)}, u32[]{:S(2)}, u32[]{:S(2)}) async-start(bf16[8,16,3968]{2,1,0:T(8,128)(2,1)} %pack.1), calls=%async_computation | async-start | bytes 2031616 | tf_op jit(solution)/shard_map/all_to_all | solution.py:483
  15.8 14.6 %all-to-all-done = bf16[8,16,3968]{2,1,0:T(8,128)(2,1)} async-done(((bf16[8,16,3968]{2,1,0:T(8,128)(2,1)}), bf16[8,16,3968]{2,1,0:T(8,128)(2,1)}, u32[]{:S(2)}, u32[]{:S(2)}) %all-to-all-start) | async-done | bytes 1015840 | tf_op jit(solution)/shard_map/all_to_all | solution.py:483
  30.4 2.0 collective-permute-start.4
  32.4 1.6 collective-permute-start.6
  34.0 3.3 %constant_dynamic-slice_fusion = (bf16[3072,128]{1,0:T(8,128)(2,1)}, bf16[3072,128]{1,0:T(8,128)(2,1)}, bf16[3072,128]{1,0:T(8,128)(2,1)S(1)}, bf16[3072,128]{1,0:T(8,128)(2,1)}) fusion(bf16[12288,128]{1,0:T(8,128)(2,1)} %param.14, s32[]{:T(128)S(6)} %select_n.27, s32[]{:T(128)S(6)} %select_n.25, s32[]{:T(128)S(6)} %select_n.24, s32[]{:T(128)S(6)} %select_n.26), kind=kLoop, calls=%fused_computation.36 | loop fusion | bytes 6291472 | tf_op jit(solution)/shard_map/dynamic_slice | solution.py:340
  37.9 1.3 collective-permute-start.2
  39.1 15.8 %collective-permute-done.4.refs_0_.refs_1_.refs_2_.refs_3_.refs_4_.refs_9_ = bf16[128,3968]{1,0:T(8,128)(2,1)} collective-permute-done((bf16[128,3968]{1,0:T(8,128)(2,1)}, bf16[128,3968]{1,0:T(8,128)(2,1)}, u32[]{:S(2)}, u32[]{:S(2)}) %collective-permute-start.4) | collective-permute-done | bytes 1015840 | tf_op jit(solution)/shard_map/ppermute | solution.py:328
  55.0 1.7 collective-permute-start.5
  56.6 1.3 collective-permute-start.7
  57.9 16.0 %collective-permute-done.2.refs_8_.refs_12_.refs_16_.refs_20_ = bf16[3072,128]{1,0:T(8,128)(2,1)S(1)} collective-permute-done((bf16[3072,128]{1,0:T(8,128)(2,1)}, bf16[3072,128]{1,0:T(8,128)(2,1)S(1)}, u32[]{:S(2)}, u32[]{:S(2)}) %collective-permute-start.2) | collective-permute-done | bytes 786464 | tf_op jit(solution)/shard_map/ppermute | solution.py:328
  73.9 6.1 %project.5 = (f32[2,2,256,128]{3,2,1,0:T(8,128)S(1)}, f32[2,2,256,128]{3,2,1,0:T(8,128)}) custom-call(s32[1]{0:T(128)} %bitcast.4.place, bf16[128,3968]{1,0:T(8,128)(2,1)} %collective-permute-done.4.refs_0_.refs_1_.refs_2_.refs_3_.refs_4_.refs_9_, bf16[128,3968]{1,0:T(8,128)(2,1)} %collective-permute-done.4.refs_0_.refs_1_.refs_2_.refs_3_.refs_4_.refs_9_, ...), custom_call_target="tpu_custom_call" | custom-call | flops 1610612736 | bytes 4161536 | tf_op jit(solution)/shard_map/project/pallas_call | solution.py:187
  81.5 5.4 %project.4 = (f32[2,2,256,128]{3,2,1,0:T(8,128)S(1)}, f32[2,2,256,128]{3,2,1,0:T(8,128)S(1)}) custom-call(s32[1]{0:T(128)} %bitcast.4.place, bf16[128,3968]{1,0:T(8,128)(2,1)} %bitcast.5.refs_0_.refs_1_.refs_2_.refs_3_.refs_4_.refs_8_, bf16[128,3968]{1,0:T(8,128)(2,1)} %bitcast.5.refs_0_.refs_1_.refs_2_.refs_3_.refs_4_.refs_8_, ...), custom_call_target="tpu_custom_call" | custom-call | flops 1610612736 | bytes 4161536 | tf_op jit(solution)/shard_map/project/pallas_call | solution.py:187
  87.0 1.1 add.72
  88.1 1.1 collective-permute-start.14
  89.2 1.5 collective-permute-start.13
  90.7 1.0 collective-permute-start.12
  91.7 1.3 collective-permute-start.16
  93.0 1.3 broadcast_select_fusion.1.refs_0_.refs_1_.refs_2_.refs_3_.refs_4_.refs_10_
  94.3 4.8 %project.6 = (f32[2,2,256,128]{3,2,1,0:T(8,128)S(1)}, f32[2,2,256,128]{3,2,1,0:T(8,128)S(1)}) custom-call(s32[1]{0:T(128)} %bitcast.4.place, bf16[128,3968]{1,0:T(8,128)(2,1)S(1)} %broadcast_select_fusion.1.refs_0_.refs_1_.refs_2_.refs_3_.refs_4_.refs_10_, bf16[128,3968]{1,0:T(8,128)(2,1)S(1)} %broadcast_select_fusion.1.refs_0_.refs_1_.refs_2_.refs_3_.refs_4_.refs_10_, ...), custom_call_target="tpu_custom_call" | custom-call | flops 1610612736 | bytes 4161536 | tf_op jit(solution)/shard_map/project/pallas_call | solution.py:187
  99.4 1.1 collective-permute-start.10
  100.5 1.5 collective-permute-start.9
  101.9 1.0 collective-permute-start.8
  103.0 15.9 %collective-permute-done.16 = bf16[128,3968]{1,0:T(8,128)(2,1)S(1)} collective-permute-done((bf16[128,3968]{1,0:T(8,128)(2,1)}, bf16[128,3968]{1,0:T(8,128)(2,1)S(1)}, u32[]{:S(2)}, u32[]{:S(2)}) %collective-permute-start.16) | collective-permute-done | bytes 1015840 | tf_op jit(solution)/shard_map/ppermute | solution.py:328
  118.9 1.1 collective-permute-start.19
  120.0 1.5 collective-permute-start.18
  121.4 1.0 collective-permute-start.17
  122.5 3.4 %collective-permute-done.19 = f32[256,128]{1,0:T(8,128)S(1)} collective-permute-done((f32[256,128]{1,0:T(8,128)S(1)}, f32[256,128]{1,0:T(8,128)S(1)}, u32[]{:S(2)}, u32[]{:S(2)}) %collective-permute-start.19) | collective-permute-done | bytes 131104 | tf_op jit(solution)/shard_map/ppermute | solution.py:328
  125.9 1.1 collective-permute-done.18
  129.2 1.3 broadcast_select_fusion.refs_0_.refs_1_.refs_2_.refs_3_.refs_4_.refs_11_
  130.5 4.8 %project.7 = (f32[2,2,256,128]{3,2,1,0:T(8,128)S(1)}, f32[2,2,256,128]{3,2,1,0:T(8,128)S(1)}) custom-call(s32[1]{0:T(128)} %bitcast.4.place, bf16[128,3968]{1,0:T(8,128)(2,1)S(1)} %broadcast_select_fusion.refs_0_.refs_1_.refs_2_.refs_3_.refs_4_.refs_11_, bf16[128,3968]{1,0:T(8,128)(2,1)S(1)} %broadcast_select_fusion.refs_0_.refs_1_.refs_2_.refs_3_.refs_4_.refs_11_, ...), custom_call_target="tpu_custom_call" | custom-call | flops 1610612736 | bytes 4161536 | tf_op jit(solution)/shard_map/project/pallas_call | solution.py:187
  135.4 13.5 %collective-permute-start.22 = (bf16[3,256,128]{2,1,0:T(8,128)(2,1)S(1)}, bf16[3,256,128]{2,1,0:T(8,128)(2,1)S(1)}, u32[]{:S(2)}, u32[]{:S(2)}) collective-permute-start(bf16[3,256,128]{2,1,0:T(8,128)(2,1)S(1)} %copy-done.13), channel_id=1, source_target_pairs={{0,1},{1,0},{2,3},{3,2},{4,5},{5,4},{6,7},{7,6},{8,9},{9,8},{10,11... | collective-permute-start | bytes 589832 | tf_op jit(solution)/shard_map/ppermute | solution.py:328
  149.0 5.4 %collective-permute-done.22 = bf16[3,256,128]{2,1,0:T(8,128)(2,1)S(1)} collective-permute-done((bf16[3,256,128]{2,1,0:T(8,128)(2,1)S(1)}, bf16[3,256,128]{2,1,0:T(8,128)(2,1)S(1)}, u32[]{:S(2)}, u32[]{:S(2)}) %collective-permute-start.22) | collective-permute-done | bytes 196640 | tf_op jit(solution)/shard_map/ppermute | solution.py:328
  154.4 1.6 collective-permute-start.25
  156.0 1.7 collective-permute-start.24
  158.0 3.8 %collective-permute-done.25 = f32[256,128]{1,0:T(8,128)S(1)} collective-permute-done((f32[256,128]{1,0:T(8,128)S(1)}, f32[256,128]{1,0:T(8,128)S(1)}, u32[]{:S(2)}, u32[]{:S(2)}) %collective-permute-start.25) | collective-permute-done | bytes 131104 | tf_op jit(solution)/shard_map/ppermute | solution.py:328
  161.8 1.8 collective-permute-done.24
  164.3 4.8 %collective-permute-start.28 = (bf16[256,128]{1,0:T(8,128)(2,1)S(1)}, bf16[256,128]{1,0:T(8,128)(2,1)S(1)}, u32[]{:S(2)}, u32[]{:S(2)}) collective-permute-start(bf16[256,128]{1,0:T(8,128)(2,1)S(1)} %fusion.6.refs_3_), channel_id=1, source_target_pairs={{0,16},{1,0},{2,18},{3,2},{4,20},{5,4},{6,22},{7,6},{8,24},{9,8},{... | collective-permute-start | bytes 196616 | tf_op jit(solution)/shard_map/ppermute | solution.py:328
  169.6 2.0 %collective-permute-start.30 = (bf16[256,128]{1,0:T(8,128)(2,1)S(1)}, bf16[256,128]{1,0:T(8,128)(2,1)S(1)}, u32[]{:S(2)}, u32[]{:S(2)}) collective-permute-start(bf16[256,128]{1,0:T(8,128)(2,1)S(1)} %fusion.6.refs_3_), channel_id=1, source_target_pairs={{0,1},{1,0},{2,3},{3,2},{4,5},{5,4},{6,7},{7,6},{8,9},{9,8},{10,11... | collective-permute-start | bytes 196616 | tf_op jit(solution)/shard_map/ppermute | solution.py:328
  171.6 2.0 collective-permute-done.27
  173.6 3.2 %collective-permute-done.29 = bf16[256,128]{1,0:T(8,128)(2,1)S(1)} collective-permute-done((bf16[256,128]{1,0:T(8,128)(2,1)S(1)}, bf16[256,128]{1,0:T(8,128)(2,1)S(1)}, u32[]{:S(2)}, u32[]{:S(2)}) %collective-permute-start.29) | collective-permute-done | bytes 65568 | tf_op jit(solution)/shard_map/ppermute | solution.py:328
  177.4 2.0 %collective-permute-start.31 = (bf16[4,256,128]{2,1,0:T(8,128)(2,1)S(1)}, bf16[4,256,128]{2,1,0:T(8,128)(2,1)S(1)}, u32[]{:S(2)}, u32[]{:S(2)}) collective-permute-start(bf16[4,256,128]{2,1,0:T(8,128)(2,1)S(1)} %pad_maximum_fusion.refs_16_.refs_20_), channel_id=1, source_target_pairs={{0,4},{1,5},{2,6},{3,7},{4,0},{5,1},{6,2},{7,3},{8,12},{9,13},{10,... | collective-permute-start | bytes 786440 | tf_op jit(solution)/shard_map/ppermute | solution.py:328
  179.5 4.4 %collective-permute-done.31.refs_17_.refs_21_ = bf16[4,256,128]{2,1,0:T(8,128)(2,1)S(1)} collective-permute-done((bf16[4,256,128]{2,1,0:T(8,128)(2,1)S(1)}, bf16[4,256,128]{2,1,0:T(8,128)(2,1)S(1)}, u32[]{:S(2)}, u32[]{:S(2)}) %collective-permute-start.31) | collective-permute-done | bytes 262176 | tf_op jit(solution)/shard_map/ppermute | solution.py:328
  184.0 0.9 slice_bitcast_fusion.13
  185.4 1.3 all-gather.3.cloned.1.call-done
  186.8 1.9 copy-done
  188.7 0.8 copy-done.8
  189.5 5.9 %chi.1 = f32[128,4,1024]{2,1,0:T(4,128)} custom-call(s32[5]{0:T(128)S(1)} %stack.50.scalars, bf16[256,128]{1,0:T(8,128)(2,1)S(1)} %fusion.12.refs_0_, bf16[256,128]{1,0:T(8,128)(2,1)S(1)} %fusion.3.refs_1_, bf16[256,128]{1,0:T(8,128)(2,1)S(1)} %fusion.9.refs_2_, bf16[256,128]{1,0:T(8,128)(2,1)S(1)} %fusion.6.refs_3_, ...), custom_call_target="tpu_custom_call" | custom-call | flops 2147483648 | bytes 6291456 | tf_op jit(solution)/shard_map/chi/pallas_call | solution.py:281
  (78 shorter events, 7.6 us)
Async XLA Ops:
  10.5 19.9 %all-to-all-start = ((bf16[8,16,3968]{2,1,0:T(8,128)(2,1)}), bf16[8,16,3968]{2,1,0:T(8,128)(2,1)}, u32[]{:S(2)}, u32[]{:S(2)}) async-start(bf16[8,16,3968]{2,1,0:T(8,128)(2,1)} %pack.1), calls=%async_computation | async-start | bytes 2031616 | tf_op jit(solution)/shard_map/all_to_all | solution.py:483
  15.7 171.1 %all-gather.3.cloned.1.call-start = ((), (), s32[]{:S(2)}) async-start(), calls=%async_computation.1 | async-start | bytes 3342336 | tf_op jit(solution)/shard_map/all_gather | solution.py:385
  30.4 24.6 %collective-permute-start.4 = (bf16[128,3968]{1,0:T(8,128)(2,1)}, bf16[128,3968]{1,0:T(8,128)(2,1)}, u32[]{:S(2)}, u32[]{:S(2)}) collective-permute-start(bf16[128,3968]{1,0:T(8,128)(2,1)} %bitcast.5.refs_0_.refs_1_.refs_2_.refs_3_.refs_4_.refs_8_), channel_id=1, source_target_pairs={{0,8},{1,9},{2,10},{3,11},{4,12},{5,13},{6,14},{7,15},{8,0},{9,1},... | collective-permute-start | bytes 3047432 | tf_op jit(solution)/shard_map/ppermute | solution.py:328
  32.4 24.3 %collective-permute-start.6 = (bf16[128,3968]{1,0:T(8,128)(2,1)}, bf16[128,3968]{1,0:T(8,128)(2,1)}, u32[]{:S(2)}, u32[]{:S(2)}) collective-permute-start(bf16[128,3968]{1,0:T(8,128)(2,1)} %bitcast.5.refs_0_.refs_1_.refs_2_.refs_3_.refs_4_.refs_8_), channel_id=1, source_target_pairs={{8,16},{9,17},{10,18},{11,19},{12,20},{13,21},{14,22},{15,23},{16,... | collective-permute-start | bytes 3047432 | tf_op jit(solution)/shard_map/ppermute | solution.py:328
  37.3 20.7 %collective-permute-start = (bf16[3072,128]{1,0:T(8,128)(2,1)}, bf16[3072,128]{1,0:T(8,128)(2,1)S(1)}, u32[]{:S(2)}, u32[]{:S(2)}) collective-permute-start(bf16[3072,128]{1,0:T(8,128)(2,1)} %get-tuple-element.38), channel_id=1, source_target_pairs={{0,2},{1,3},{2,0},{3,1},{4,6},{5,7},{6,4},{7,5},{8,10},{9,11},{10,... | collective-permute-start | bytes 2359304 | tf_op jit(solution)/shard_map/ppermute | solution.py:328
  37.3 20.7 %collective-permute-start.1 = (bf16[3072,128]{1,0:T(8,128)(2,1)}, bf16[3072,128]{1,0:T(8,128)(2,1)S(1)}, u32[]{:S(2)}, u32[]{:S(2)}) collective-permute-start(bf16[3072,128]{1,0:T(8,128)(2,1)} %get-tuple-element.40), channel_id=1, source_target_pairs={{0,4},{1,5},{2,6},{3,7},{4,0},{5,1},{6,2},{7,3},{8,12},{9,13},{10,... | collective-permute-start | bytes 2359304 | tf_op jit(solution)/shard_map/ppermute | solution.py:328
  37.9 36.0 %collective-permute-start.2 = (bf16[3072,128]{1,0:T(8,128)(2,1)}, bf16[3072,128]{1,0:T(8,128)(2,1)S(1)}, u32[]{:S(2)}, u32[]{:S(2)}) collective-permute-start(bf16[3072,128]{1,0:T(8,128)(2,1)} %get-tuple-element.37), channel_id=1, source_target_pairs={{0,6},{1,7},{2,4},{3,5},{4,2},{5,3},{6,0},{7,1},{8,14},{9,15},{10,... | collective-permute-start | bytes 2359304 | tf_op jit(solution)/shard_map/ppermute | solution.py:328
  55.0 35.7 %collective-permute-start.5 = (bf16[128,3968]{1,0:T(8,128)(2,1)}, bf16[128,3968]{1,0:T(8,128)(2,1)}, u32[]{:S(2)}, u32[]{:S(2)}) collective-permute-start(bf16[128,3968]{1,0:T(8,128)(2,1)} %collective-permute-done.4.refs_0_.refs_1_.refs_2_.refs_3_.refs_4_.refs_9_), channel_id=1, source_target_pairs={{8,16},{9,17},{10,18},{11,19},{12,20},{13,21},{14,22},{15,23},{16,... | collective-permute-start | bytes 3047432 | tf_op jit(solution)/shard_map/ppermute | solution.py:328
  56.6 35.1 %collective-permute-start.7 = (bf16[128,3968]{1,0:T(8,128)(2,1)}, bf16[128,3968]{1,0:T(8,128)(2,1)}, u32[]{:S(2)}, u32[]{:S(2)}) collective-permute-start(bf16[128,3968]{1,0:T(8,128)(2,1)} %collective-permute-done.6), channel_id=1, source_target_pairs={{8,0},{9,1},{10,2},{11,3},{12,4},{13,5},{14,6},{15,7},{16,24},{17,... | collective-permute-start | bytes 3047432 | tf_op jit(solution)/shard_map/ppermute | solution.py:328
  80.1 0.8 copy-start.5
  80.8 6.2 %collective-permute-start.11 = (f32[2,2,256,128]{3,2,1,0:T(8,128)}, f32[2,2,256,128]{3,2,1,0:T(8,128)}, u32[]{:S(2)}, u32[]{:S(2)}) collective-permute-start(f32[2,2,256,128]{3,2,1,0:T(8,128)} %get-tuple-element.25), channel_id=1, source_target_pairs={{0,2},{1,3},{2,0},{3,1},{4,6},{5,7},{6,4},{7,5},{8,10},{9,11},{10,... | collective-permute-start | bytes 1572872 | tf_op jit(solution)/shard_map/ppermute | solution.py:328
  81.5 5.6 %copy-start.6 = (f32[2,2,256,128]{3,2,1,0:T(8,128)S(1)}, f32[2,2,256,128]{3,2,1,0:T(8,128)}, u32[]{:S(2)}) copy-start(f32[2,2,256,128]{3,2,1,0:T(8,128)} %copy-done.5) | copy-start | bytes 1572868
  86.9 12.2 %collective-permute-start.3 = (f32[2,2,256,128]{3,2,1,0:T(8,128)S(1)}, f32[2,2,256,128]{3,2,1,0:T(8,128)S(1)}, u32[]{:S(2)}, u32[]{:S(2)}) collective-permute-start(f32[2,2,256,128]{3,2,1,0:T(8,128)S(1)} %get-tuple-element.22), channel_id=1, source_target_pairs={{0,2},{1,3},{2,0},{3,1},{4,6},{5,7},{6,4},{7,5},{8,10},{9,11},{10,... | collective-permute-start | bytes 1572872 | tf_op jit(solution)/shard_map/ppermute | solution.py:328
  88.1 11.1 %collective-permute-start.14 = (f32[256,128]{1,0:T(8,128)S(1)}, f32[256,128]{1,0:T(8,128)S(1)}, u32[]{:S(2)}, u32[]{:S(2)}) collective-permute-start(f32[256,128]{1,0:T(8,128)S(1)} %get-tuple-element.48), channel_id=1, source_target_pairs={{0,5},{1,4},{2,7},{3,6},{4,1},{5,0},{6,3},{7,2},{8,13},{9,12},{10,... | collective-permute-start | bytes 393224 | tf_op jit(solution)/shard_map/ppermute | solution.py:328
  89.2 10.1 %collective-permute-start.13 = (f32[256,128]{1,0:T(8,128)S(1)}, f32[256,128]{1,0:T(8,128)S(1)}, u32[]{:S(2)}, u32[]{:S(2)}) collective-permute-start(f32[256,128]{1,0:T(8,128)S(1)} %get-tuple-element.49), channel_id=1, source_target_pairs={{0,4},{1,5},{2,6},{3,7},{4,0},{5,1},{6,2},{7,3},{8,12},{9,13},{10,... | collective-permute-start | bytes 393224 | tf_op jit(solution)/shard_map/ppermute | solution.py:328
  90.7 8.6 %collective-permute-start.12 = (f32[256,128]{1,0:T(8,128)S(1)}, f32[256,128]{1,0:T(8,128)S(1)}, u32[]{:S(2)}, u32[]{:S(2)}) collective-permute-start(f32[256,128]{1,0:T(8,128)S(1)} %get-tuple-element.47), channel_id=1, source_target_pairs={{0,1},{1,0},{2,3},{3,2},{4,5},{5,4},{6,7},{7,6},{8,9},{9,8},{10,11... | collective-permute-start | bytes 393224 | tf_op jit(solution)/shard_map/ppermute | solution.py:328
  91.7 27.2 %collective-permute-start.16 = (bf16[128,3968]{1,0:T(8,128)(2,1)}, bf16[128,3968]{1,0:T(8,128)(2,1)S(1)}, u32[]{:S(2)}, u32[]{:S(2)}) collective-permute-start(bf16[128,3968]{1,0:T(8,128)(2,1)} %collective-permute-done.5), channel_id=1, source_target_pairs={{8,0},{9,1},{10,2},{11,3},{12,4},{13,5},{14,6},{15,7},{16,24},{17,... | collective-permute-start | bytes 3047432 | tf_op jit(solution)/shard_map/ppermute | solution.py:328
  94.3 4.8 %copy-start.1 = (bf16[128,3968]{1,0:T(8,128)(2,1)}, bf16[128,3968]{1,0:T(8,128)(2,1)S(1)}, u32[]{:S(2)}) copy-start(bf16[128,3968]{1,0:T(8,128)(2,1)S(1)} %broadcast_select_fusion.1.refs_0_.refs_1_.refs_2_.refs_3_.refs_4_.refs_10_) | copy-start | bytes 3047428
  99.2 3.8 %collective-permute-start.15 = (f32[2,2,256,128]{3,2,1,0:T(8,128)S(1)}, f32[2,2,256,128]{3,2,1,0:T(8,128)S(1)}, u32[]{:S(2)}, u32[]{:S(2)}) collective-permute-start(f32[2,2,256,128]{3,2,1,0:T(8,128)S(1)} %get-tuple-element.27), channel_id=1, source_target_pairs={{0,2},{1,3},{2,0},{3,1},{4,6},{5,7},{6,4},{7,5},{8,10},{9,11},{10,... | collective-permute-start | bytes 1572872 | tf_op jit(solution)/shard_map/ppermute | solution.py:328
  99.4 22.0 %collective-permute-start.10 = (f32[256,128]{1,0:T(8,128)S(1)}, f32[256,128]{1,0:T(8,128)S(1)}, u32[]{:S(2)}, u32[]{:S(2)}) collective-permute-start(f32[256,128]{1,0:T(8,128)S(1)} %get-tuple-element.51), channel_id=1, source_target_pairs={{0,5},{1,4},{2,7},{3,6},{4,1},{5,0},{6,3},{7,2},{8,13},{9,12},{10,... | collective-permute-start | bytes 393224 | tf_op jit(solution)/shard_map/ppermute | solution.py:328
  100.5 22.0 %collective-permute-start.9 = (f32[256,128]{1,0:T(8,128)S(1)}, f32[256,128]{1,0:T(8,128)S(1)}, u32[]{:S(2)}, u32[]{:S(2)}) collective-permute-start(f32[256,128]{1,0:T(8,128)S(1)} %get-tuple-element.52), channel_id=1, source_target_pairs={{0,4},{1,5},{2,6},{3,7},{4,0},{5,1},{6,2},{7,3},{8,12},{9,13},{10,... | collective-permute-start | bytes 393224 | tf_op jit(solution)/shard_map/ppermute | solution.py:328
  101.9 20.6 %collective-permute-start.8 = (f32[256,128]{1,0:T(8,128)S(1)}, f32[256,128]{1,0:T(8,128)S(1)}, u32[]{:S(2)}, u32[]{:S(2)}) collective-permute-start(f32[256,128]{1,0:T(8,128)S(1)} %get-tuple-element.50), channel_id=1, source_target_pairs={{0,1},{1,0},{2,3},{3,2},{4,5},{5,4},{6,7},{7,6},{8,9},{9,8},{10,11... | collective-permute-start | bytes 393224 | tf_op jit(solution)/shard_map/ppermute | solution.py:328
  118.9 8.1 %copy-start.9 = (bf16[128,3968]{1,0:T(8,128)(2,1)}, bf16[128,3968]{1,0:T(8,128)(2,1)S(1)}, u32[]{:S(2)}) copy-start(bf16[128,3968]{1,0:T(8,128)(2,1)S(1)} %collective-permute-done.16) | copy-start | bytes 3047428
  118.9 7.0 %collective-permute-start.19 = (f32[256,128]{1,0:T(8,128)S(1)}, f32[256,128]{1,0:T(8,128)S(1)}, u32[]{:S(2)}, u32[]{:S(2)}) collective-permute-start(f32[256,128]{1,0:T(8,128)S(1)} %get-tuple-element.45), channel_id=1, source_target_pairs={{0,5},{1,4},{2,7},{3,6},{4,1},{5,0},{6,3},{7,2},{8,13},{9,12},{10,... | collective-permute-start | bytes 393224 | tf_op jit(solution)/shard_map/ppermute | solution.py:328
  120.0 7.0 %collective-permute-start.18 = (f32[256,128]{1,0:T(8,128)S(1)}, f32[256,128]{1,0:T(8,128)S(1)}, u32[]{:S(2)}, u32[]{:S(2)}) collective-permute-start(f32[256,128]{1,0:T(8,128)S(1)} %get-tuple-element.46), channel_id=1, source_target_pairs={{0,4},{1,5},{2,6},{3,7},{4,0},{5,1},{6,2},{7,3},{8,12},{9,13},{10,... | collective-permute-start | bytes 393224 | tf_op jit(solution)/shard_map/ppermute | solution.py:328
  121.4 5.5 %collective-permute-start.17 = (f32[256,128]{1,0:T(8,128)S(1)}, f32[256,128]{1,0:T(8,128)S(1)}, u32[]{:S(2)}, u32[]{:S(2)}) collective-permute-start(f32[256,128]{1,0:T(8,128)S(1)} %get-tuple-element.44), channel_id=1, source_target_pairs={{0,1},{1,0},{2,3},{3,2},{4,5},{5,4},{6,7},{7,6},{8,9},{9,8},{10,11... | collective-permute-start | bytes 393224 | tf_op jit(solution)/shard_map/ppermute | solution.py:328
  127.7 0.7 collective-permute-start.21
  128.4 0.7 copy-start.10
  130.5 4.8 %copy-start.3 = (bf16[128,3968]{1,0:T(8,128)(2,1)}, bf16[128,3968]{1,0:T(8,128)(2,1)S(1)}, u32[]{:S(2)}) copy-start(bf16[128,3968]{1,0:T(8,128)(2,1)S(1)} %broadcast_select_fusion.refs_0_.refs_1_.refs_2_.refs_3_.refs_4_.refs_11_) | copy-start | bytes 3047428
  130.5 4.9 %copy-start.13 = (bf16[3,256,128]{2,1,0:T(8,128)(2,1)S(1)}, bf16[3,256,128]{2,1,0:T(8,128)(2,1)}, u32[]{:S(2)}) copy-start(bf16[3,256,128]{2,1,0:T(8,128)(2,1)} %copy-done.12) | copy-start | bytes 589828
  135.3 51.5 %copy-start.2 = (bf16[128,3968]{1,0:T(8,128)(2,1)S(1)}, bf16[128,3968]{1,0:T(8,128)(2,1)}, u32[]{:S(2)}) copy-start(bf16[128,3968]{1,0:T(8,128)(2,1)} %copy-done.1) | copy-start | bytes 3047428
  135.3 51.5 %copy-start.4 = (bf16[128,3968]{1,0:T(8,128)(2,1)S(1)}, bf16[128,3968]{1,0:T(8,128)(2,1)}, u32[]{:S(2)}) copy-start(bf16[128,3968]{1,0:T(8,128)(2,1)} %copy-done.3) | copy-start | bytes 3047428
  135.3 13.6 %collective-permute-start.20 = (f32[2,2,256,128]{3,2,1,0:T(8,128)S(1)}, f32[2,2,256,128]{3,2,1,0:T(8,128)S(1)}, u32[]{:S(2)}, u32[]{:S(2)}) collective-permute-start(f32[2,2,256,128]{3,2,1,0:T(8,128)S(1)} %get-tuple-element.30), channel_id=1, source_target_pairs={{0,2},{1,3},{2,0},{3,1},{4,6},{5,7},{6,4},{7,5},{8,10},{9,11},{10,... | collective-permute-start | bytes 1572872 | tf_op jit(solution)/shard_map/ppermute | solution.py:328
  135.4 19.0 %collective-permute-start.22 = (bf16[3,256,128]{2,1,0:T(8,128)(2,1)S(1)}, bf16[3,256,128]{2,1,0:T(8,128)(2,1)S(1)}, u32[]{:S(2)}, u32[]{:S(2)}) collective-permute-start(bf16[3,256,128]{2,1,0:T(8,128)(2,1)S(1)} %copy-done.13), channel_id=1, source_target_pairs={{0,1},{1,0},{2,3},{3,2},{4,5},{5,4},{6,7},{7,6},{8,9},{9,8},{10,11... | collective-permute-start | bytes 589832 | tf_op jit(solution)/shard_map/ppermute | solution.py:328
  154.4 9.2 %copy-start.11 = (bf16[3,256,128]{2,1,0:T(8,128)(2,1)}, bf16[3,256,128]{2,1,0:T(8,128)(2,1)S(1)}, u32[]{:S(2)}) copy-start(bf16[3,256,128]{2,1,0:T(8,128)(2,1)S(1)} %collective-permute-done.22) | copy-start | bytes 589828
  154.4 7.4 %collective-permute-start.25 = (f32[256,128]{1,0:T(8,128)S(1)}, f32[256,128]{1,0:T(8,128)S(1)}, u32[]{:S(2)}, u32[]{:S(2)}) collective-permute-start(f32[256,128]{1,0:T(8,128)S(1)} %get-tuple-element.42), channel_id=1, source_target_pairs={{0,5},{1,4},{2,7},{3,6},{4,1},{5,0},{6,3},{7,2},{8,13},{9,12},{10,... | collective-permute-start | bytes 393224 | tf_op jit(solution)/shard_map/ppermute | solution.py:328
  156.0 7.5 %collective-permute-start.24 = (f32[256,128]{1,0:T(8,128)S(1)}, f32[256,128]{1,0:T(8,128)S(1)}, u32[]{:S(2)}, u32[]{:S(2)}) collective-permute-start(f32[256,128]{1,0:T(8,128)S(1)} %get-tuple-element.43), channel_id=1, source_target_pairs={{0,4},{1,5},{2,6},{3,7},{4,0},{5,1},{6,2},{7,3},{8,12},{9,13},{10,... | collective-permute-start | bytes 393224 | tf_op jit(solution)/shard_map/ppermute | solution.py:328
  157.7 5.8 %collective-permute-start.23 = (f32[256,128]{1,0:T(8,128)S(1)}, f32[256,128]{1,0:T(8,128)S(1)}, u32[]{:S(2)}, u32[]{:S(2)}) collective-permute-start(f32[256,128]{1,0:T(8,128)S(1)} %get-tuple-element.41), channel_id=1, source_target_pairs={{0,1},{1,0},{2,3},{3,2},{4,5},{5,4},{6,7},{7,6},{8,9},{9,8},{10,11... | collective-permute-start | bytes 393224 | tf_op jit(solution)/shard_map/ppermute | solution.py:328
  163.6 8.0 %collective-permute-start.26 = (bf16[256,128]{1,0:T(8,128)(2,1)S(1)}, bf16[256,128]{1,0:T(8,128)(2,1)S(1)}, u32[]{:S(2)}, u32[]{:S(2)}) collective-permute-start(bf16[256,128]{1,0:T(8,128)(2,1)S(1)} %fusion.6.refs_3_), channel_id=1, source_target_pairs={{0,0},{1,16},{2,2},{3,18},{4,4},{5,20},{6,6},{7,22},{8,8},{9,24},{... | collective-permute-start | bytes 196616 | tf_op jit(solution)/shard_map/ppermute | solution.py:328
  164.2 9.3 %collective-permute-start.27 = (bf16[256,128]{1,0:T(8,128)(2,1)S(1)}, bf16[256,128]{1,0:T(8,128)(2,1)S(1)}, u32[]{:S(2)}, u32[]{:S(2)}) collective-permute-start(bf16[256,128]{1,0:T(8,128)(2,1)S(1)} %fusion.6.refs_3_), channel_id=1, source_target_pairs={{0,8},{1,24},{2,10},{3,26},{4,12},{5,28},{6,14},{7,30},{8,0},{9,16... | collective-permute-start | bytes 196616 | tf_op jit(solution)/shard_map/ppermute | solution.py:328
  164.3 9.3 %collective-permute-start.28 = (bf16[256,128]{1,0:T(8,128)(2,1)S(1)}, bf16[256,128]{1,0:T(8,128)(2,1)S(1)}, u32[]{:S(2)}, u32[]{:S(2)}) collective-permute-start(bf16[256,128]{1,0:T(8,128)(2,1)S(1)} %fusion.6.refs_3_), channel_id=1, source_target_pairs={{0,16},{1,0},{2,18},{3,2},{4,20},{5,4},{6,22},{7,6},{8,24},{9,8},{... | collective-permute-start | bytes 196616 | tf_op jit(solution)/shard_map/ppermute | solution.py:328
  169.1 7.7 %collective-permute-start.29 = (bf16[256,128]{1,0:T(8,128)(2,1)S(1)}, bf16[256,128]{1,0:T(8,128)(2,1)S(1)}, u32[]{:S(2)}, u32[]{:S(2)}) collective-permute-start(bf16[256,128]{1,0:T(8,128)(2,1)S(1)} %fusion.6.refs_3_), channel_id=1, source_target_pairs={{0,24},{1,8},{2,26},{3,10},{4,28},{5,12},{6,30},{7,14},{8,16},{9,0... | collective-permute-start | bytes 196616 | tf_op jit(solution)/shard_map/ppermute | solution.py:328
  169.6 7.2 %collective-permute-start.30 = (bf16[256,128]{1,0:T(8,128)(2,1)S(1)}, bf16[256,128]{1,0:T(8,128)(2,1)S(1)}, u32[]{:S(2)}, u32[]{:S(2)}) collective-permute-start(bf16[256,128]{1,0:T(8,128)(2,1)S(1)} %fusion.6.refs_3_), channel_id=1, source_target_pairs={{0,1},{1,0},{2,3},{3,2},{4,5},{5,4},{6,7},{7,6},{8,9},{9,8},{10,11... | collective-permute-start | bytes 196616 | tf_op jit(solution)/shard_map/ppermute | solution.py:328
  177.4 6.4 %collective-permute-start.31 = (bf16[4,256,128]{2,1,0:T(8,128)(2,1)S(1)}, bf16[4,256,128]{2,1,0:T(8,128)(2,1)S(1)}, u32[]{:S(2)}, u32[]{:S(2)}) collective-permute-start(bf16[4,256,128]{2,1,0:T(8,128)(2,1)S(1)} %pad_maximum_fusion.refs_16_.refs_20_), channel_id=1, source_target_pairs={{0,4},{1,5},{2,6},{3,7},{4,0},{5,1},{6,2},{7,3},{8,12},{9,13},{10,... | collective-permute-start | bytes 786440 | tf_op jit(solution)/shard_map/ppermute | solution.py:328
  179.5 5.4 %collective-permute-start.32 = (bf16[4,256,128]{2,1,0:T(8,128)(2,1)S(1)}, bf16[4,256,128]{2,1,0:T(8,128)(2,1)S(1)}, u32[]{:S(2)}, u32[]{:S(2)}) collective-permute-start(bf16[4,256,128]{2,1,0:T(8,128)(2,1)S(1)} %pad_maximum_fusion.refs_16_.refs_20_), channel_id=1, source_target_pairs={{0,2},{1,3},{2,0},{3,1},{4,6},{5,7},{6,4},{7,5},{8,10},{9,11},{10,... | collective-permute-start | bytes 786440 | tf_op jit(solution)/shard_map/ppermute | solution.py:328
  183.9 1.5 collective-permute-start.33
  186.8 1.9 copy-start
  188.7 0.8 copy-start.8
  (2 other events, 1.3 us)
Sparse Core Ops, SparseCore 0:
  129.3 57.4 all-gather.2

commit v10 on v8

--- a/solution.py
+++ b/solution.py
@@ -334,14 +334,14 @@
         return send(array, lambda i, j, k, t: (moves[i], j, k, t) if i in moves else None)
 
     here = y * nc + c
-    eigs = []
-    for k in range(ny * nc):
-        at = lax.bitwise_xor(here, k) * part
-        rows = lax.dynamic_slice_in_dim(eigenvectors, at, part, 0)
-        eigs.append(
-            send(rows, functools.partial(lambda q, i, j, k, t: (i, j ^ (q // 2), k ^ (q % 2), t), k))
-            if k
-            else rows
+    eigs = [
+        lax.dynamic_slice_in_dim(eigenvectors, lax.bitwise_xor(here, k) * part, part, 0)
+        for k in range(ny * nc)
+    ]
+    unit, eigs = lax.optimization_barrier((unit, eigs))
+    for q in range(1, ny * nc):
+        eigs[q] = send(
+            eigs[q], functools.partial(lambda q, i, j, k, t: (i, j ^ (q // 2), k ^ (q % 2), t), q)
         )
 
     inner = (z == 1) | (z == 2)
@@ -354,7 +354,7 @@
 
     place = x[None]
 
-    def coefficients(unit, ready=None):
+    def coefficients(unit, ready=None, settled=None):
         keep, away = project(unit, eigs, place, val_count, cond_count)
         sums = keep + send(away, lambda i, j, k, t: (i, j, 1 - k, t))
         if ready is not None:
@@ -362,6 +362,8 @@
         total = sums[0, 0] + send(sums[0, 1], lambda i, j, k, t: (i, j, k, 1 - t))
         total = total + send(sums[1, 0], lambda i, j, k, t: (i, 1 - j, k, t))
         total = total + send(sums[1, 1], lambda i, j, k, t: (i, 1 - j, k, 1 - t))
+        if settled is not None:
+            total, _ = lax.optimization_barrier((total, settled))
         return total.astype(jnp.bfloat16)
 
     def mate(own):
@@ -370,24 +372,21 @@
     def share(own, m):
         return send(own, lambda i, j, k, t: ((2 * t + i % 2) ^ m, j, k, i // 2))
 
-    def spread(own):
-        shares = [share(own, m) for m in range(nz)]
-        shares, paired = lax.optimization_barrier((shares, mate(own)))
-        held = jnp.stack(shares)
-        other = send(held, lambda i, j, k, t: (i, 1 - j, k, t))
-        across_core = lambda i, j, k, t: (i, j, 1 - k, t)
-        return (held, other, send(held, across_core), send(other, across_core)), paired
-
-    owns = [coefficients(units[0], (across, outward))] + [coefficients(units[k]) for k in (1, 2)]
-    own_a = jnp.stack(owns)
-    share_a, mate_a, far = lax.optimization_barrier((share(own_a, 0), mate(own_a), far))
-    right_a = lax.all_gather(share_a, ("z", "y", "c"), axis=0)
+    owns = [coefficients(units[0], (across, outward)), coefficients(units[1])]
+    mate_a = mate(jnp.stack(owns))
+    owns.append(coefficients(units[2], None, (far, mate_a)))
+    right_a = lax.all_gather(share(jnp.stack(owns), 0), ("z", "y", "c"), axis=0)
     units.append(jnp.where(inner, middle, far))
     own_b = coefficients(units[3])
-    four, mate_b = spread(own_b)
+    shares = [share(own_b, m) for m in range(nz)]
+    mate_b = mate(jnp.stack([owns[2], own_b]))
+    shares, mate_b = lax.optimization_barrier((shares, mate_b))
+    held = jnp.stack(shares)
+    other = send(held, lambda i, j, k, t: (i, 1 - j, k, t))
+    across_core = lambda i, j, k, t: (i, j, 1 - k, t)
+    rights_b = [(held, other, send(held, across_core), send(other, across_core))]
     owns.append(own_b)
-    mates = [mate_a[k] for k in range(3)] + [mate_b]
-    rights_b = [four]
+    mates = [mate_a[0], mate_a[1], mate_b[0], mate_b[1]]
     scalars = jnp.stack([z, y, c, 2 * x, x])
     return make_chi(owns, mates, units, right_a, rights_b, scalars, n_freq, factor)
 

time: 203 us -> 207 us (1.020)
  starting transfers between devices: 45.8 us -> 53.2 us
  waiting for transfers between devices: 98.8 us -> 93.3 us
  local copies, waits for them, and re-layouts: 8.58 us -> 10.8 us
    ppermute x34, starting transfers between devices: 40.5 us -> 47.9 us  [send(): lax.ppermute(array, AXES, [(source, number[to]) for source, to in pairs i...]
    all_to_all x1, waiting for transfers between devices: 14.6 us -> 11.3 us  [local(): unit = lax.all_to_all(packed, ('y', 'c', 'x'), 0, 0, tiled=True)]
  transfers between devices with their start and end apart: 36 -> 36, of which waited for: 16 -> 17; matrix products, arithmetic and copies ran while one was open for 5% -> 5% of each run, Pallas kernels for 10% -> 10%
where the time goes in v10:
time: 207 us; the launch traced here: 206 us
  waiting for transfers between devices  93.3 us (45%)
  starting transfers between devices  53.2 us (26%)
  Pallas kernels  31 us (15%)
  between operations  13.8 us (7%)
  local copies, waits for them, and re-layouts  10.8 us (5%)
  other arithmetic  4.18 us (2%)
    ppermute x34, waiting for transfers between devices, send(): lax.ppermute(array, AXES, [(source, number[to]) for source, to in pairs i...  76 us
    ppermute x34, starting transfers between devices, send(): lax.ppermute(array, AXES, [(source, number[to]) for source, to in pairs i...  47.9 us
    pallas_call x4, Pallas kernels, project(): pl.pallas_call(functools.partial(project_kernel, segs, val_count, cond_co...  21.1 us
    all_to_all x1, waiting for transfers between devices, local(): unit = lax.all_to_all(packed, ('y', 'c', 'x'), 0, 0, tiled=True)  11.3 us
    all_gather x1, waiting for transfers between devices, fast(): right_a = lax.all_gather(share(jnp.stack(owns), 0), ('z', 'y', 'c'), axis=0)  6.04 us
    pallas_call x1, Pallas kernels, make_chi(): pl.pallas_call(functools.partial(chi_kernel, early, late, n_freq, factor)...  5.94 us
    all_to_all x1, starting transfers between devices, local(): unit = lax.all_to_all(packed, ('y', 'c', 'x'), 0, 0, tiled=True)  5.17 us
    unnamed x20, local copies, waits for them, and re-layouts  4.89 us
  transfers between devices with their start and end apart: 36, of which 17 were waited for; matrix products, arithmetic and copies ran while one was open for 5% of the time, Pallas kernels for 10%

profile of v10, /device:TPU:0, one launch (start us, length us, event | category | flops | bytes accessed | tf_op | source)
XLA Modules:
  0.0 206.3 jit_solution(6181367087169401829)
XLA Ops:
  6.5 4.0 %pack.1 = bf16[8,16,3968]{2,1,0:T(8,128)(2,1)} custom-call(f32[4]{0:T(128)} %val_energy.1, f32[16]{0:T(128)} %cond_energy.1, s32[64]{0:T(128)} %val_slot.1, s32[64]{0:T(128)} %cond_slot.1, f32[4]{0:T(128)} %frequencies.1, bf16[16,24576]{1,0:T(8,128)(2,1)} %refs_1_.1, bf16[16,24576]{1,0:T(8,128)(2,1)} %refs_1_.1, bf16[4,24576]{1,0:T(4,128)(2,1)} %refs_3_.1, ...), custom_call_target="tpu_custom_call" | custom-call | tf_op jit(solution)/shard_map/pack/pallas_call | solution.py:77
  10.5 5.2 %all-to-all-start = ((bf16[8,16,3968]{2,1,0:T(8,128)(2,1)}), bf16[8,16,3968]{2,1,0:T(8,128)(2,1)}, u32[]{:S(2)}, u32[]{:S(2)}) async-start(bf16[8,16,3968]{2,1,0:T(8,128)(2,1)} %pack.1), calls=%async_computation | async-start | bytes 2031616 | tf_op jit(solution)/shard_map/all_to_all | solution.py:480
  15.8 3.3 %constant_dynamic-slice_fusion = (bf16[3072,128]{1,0:T(8,128)(2,1)}, bf16[3072,128]{1,0:T(8,128)(2,1)}, bf16[3072,128]{1,0:T(8,128)(2,1)S(1)}, bf16[3072,128]{1,0:T(8,128)(2,1)}) fusion(bf16[12288,128]{1,0:T(8,128)(2,1)} %param.14, s32[]{:T(128)S(6)} %select_n.27, s32[]{:T(128)S(6)} %select_n.25, s32[]{:T(128)S(6)} %select_n.24, s32[]{:T(128)S(6)} %select_n.26), kind=kLoop, calls=%fused_computation.40 | loop fusion | bytes 6291472 | tf_op jit(solution)/shard_map/dynamic_slice | solution.py:338
  19.1 11.3 %all-to-all-done = bf16[8,16,3968]{2,1,0:T(8,128)(2,1)} async-done(((bf16[8,16,3968]{2,1,0:T(8,128)(2,1)}), bf16[8,16,3968]{2,1,0:T(8,128)(2,1)}, u32[]{:S(2)}, u32[]{:S(2)}) %all-to-all-start) | async-done | bytes 1015840 | tf_op jit(solution)/shard_map/all_to_all | solution.py:480
  30.4 2.0 collective-permute-start.4
  32.4 1.6 collective-permute-start.6
  34.6 1.3 collective-permute-start.2
  35.9 19.1 %collective-permute-done.4.refs_0_.refs_1_.refs_2_.refs_3_.refs_4_.refs_9_ = bf16[128,3968]{1,0:T(8,128)(2,1)} collective-permute-done((bf16[128,3968]{1,0:T(8,128)(2,1)}, bf16[128,3968]{1,0:T(8,128)(2,1)}, u32[]{:S(2)}, u32[]{:S(2)}) %collective-permute-start.4) | collective-permute-done | bytes 1015840 | tf_op jit(solution)/shard_map/ppermute | solution.py:328
  55.0 1.6 collective-permute-start.5
  56.6 1.3 collective-permute-start.7
  57.9 12.7 %collective-permute-done.2.refs_8_.refs_12_.refs_16_.refs_20_ = bf16[3072,128]{1,0:T(8,128)(2,1)S(1)} collective-permute-done((bf16[3072,128]{1,0:T(8,128)(2,1)}, bf16[3072,128]{1,0:T(8,128)(2,1)S(1)}, u32[]{:S(2)}, u32[]{:S(2)}) %collective-permute-start.2) | collective-permute-done | bytes 786464 | tf_op jit(solution)/shard_map/ppermute | solution.py:328
  70.6 6.1 %project.5 = (f32[2,2,256,128]{3,2,1,0:T(8,128)S(1)}, f32[2,2,256,128]{3,2,1,0:T(8,128)}) custom-call(s32[1]{0:T(128)} %bitcast.4.place, bf16[128,3968]{1,0:T(8,128)(2,1)} %collective-permute-done.4.refs_0_.refs_1_.refs_2_.refs_3_.refs_4_.refs_9_, bf16[128,3968]{1,0:T(8,128)(2,1)} %collective-permute-done.4.refs_0_.refs_1_.refs_2_.refs_3_.refs_4_.refs_9_, ...), custom_call_target="tpu_custom_call" | custom-call | flops 1610612736 | bytes 4161536 | tf_op jit(solution)/shard_map/project/pallas_call | solution.py:187
  78.2 5.4 %project.4 = (f32[2,2,256,128]{3,2,1,0:T(8,128)S(1)}, f32[2,2,256,128]{3,2,1,0:T(8,128)S(1)}) custom-call(s32[1]{0:T(128)} %bitcast.4.place, bf16[128,3968]{1,0:T(8,128)(2,1)} %bitcast.5.refs_0_.refs_1_.refs_2_.refs_3_.refs_4_.refs_8_, bf16[128,3968]{1,0:T(8,128)(2,1)} %bitcast.5.refs_0_.refs_1_.refs_2_.refs_3_.refs_4_.refs_8_, ...), custom_call_target="tpu_custom_call" | custom-call | flops 1610612736 | bytes 4161536 | tf_op jit(solution)/shard_map/project/pallas_call | solution.py:187
  83.8 1.1 add.72
  84.9 1.1 collective-permute-start.14
  86.0 1.5 collective-permute-start.13
  87.4 1.0 collective-permute-start.12
  88.5 1.3 broadcast_select_fusion.1.refs_0_.refs_1_.refs_2_.refs_3_.refs_4_.refs_10_
  89.8 4.8 %project.6 = (f32[2,2,256,128]{3,2,1,0:T(8,128)S(1)}, f32[2,2,256,128]{3,2,1,0:T(8,128)S(1)}) custom-call(s32[1]{0:T(128)} %bitcast.4.place, bf16[128,3968]{1,0:T(8,128)(2,1)S(1)} %broadcast_select_fusion.1.refs_0_.refs_1_.refs_2_.refs_3_.refs_4_.refs_10_, bf16[128,3968]{1,0:T(8,128)(2,1)S(1)} %broadcast_select_fusion.1.refs_0_.refs_1_.refs_2_.refs_3_.refs_4_.refs_10_, ...), custom_call_target="tpu_custom_call" | custom-call | flops 1610612736 | bytes 4161536 | tf_op jit(solution)/shard_map/project/pallas_call | solution.py:187
  94.8 1.3 collective-permute-start.19
  96.2 1.1 collective-permute-start.10
  97.2 1.5 collective-permute-start.9
  98.7 1.0 collective-permute-start.8
  99.8 1.1 collective-permute-start.18
  100.9 2.6 %collective-permute-done.10 = f32[256,128]{1,0:T(8,128)S(1)} collective-permute-done((f32[256,128]{1,0:T(8,128)S(1)}, f32[256,128]{1,0:T(8,128)S(1)}, u32[]{:S(2)}, u32[]{:S(2)}) %collective-permute-start.10) | collective-permute-done | bytes 131104 | tf_op jit(solution)/shard_map/ppermute | solution.py:328
  104.0 2.3 %collective-permute-done.9 = f32[256,128]{1,0:T(8,128)S(1)} collective-permute-done((f32[256,128]{1,0:T(8,128)S(1)}, f32[256,128]{1,0:T(8,128)S(1)}, u32[]{:S(2)}, u32[]{:S(2)}) %collective-permute-start.9) | collective-permute-done | bytes 131104 | tf_op jit(solution)/shard_map/ppermute | solution.py:328
  106.2 1.1 collective-permute-start.16
  107.4 1.0 collective-permute-start.20
  108.8 2.5 %collective-permute-done.17 = f32[256,128]{1,0:T(8,128)S(1)} collective-permute-done((f32[256,128]{1,0:T(8,128)S(1)}, f32[256,128]{1,0:T(8,128)S(1)}, u32[]{:S(2)}, u32[]{:S(2)}) %collective-permute-start.17) | collective-permute-done | bytes 131104 | tf_op jit(solution)/shard_map/ppermute | solution.py:328
  111.2 1.1 collective-permute-done.16
  112.4 1.5 collective-permute-done.20
  113.9 9.1 %collective-permute-done.19 = bf16[128,3968]{1,0:T(8,128)(2,1)} collective-permute-done((bf16[128,3968]{1,0:T(8,128)(2,1)}, bf16[128,3968]{1,0:T(8,128)(2,1)}, u32[]{:S(2)}, u32[]{:S(2)}) %collective-permute-start.19) | collective-permute-done | bytes 1015840 | tf_op jit(solution)/shard_map/ppermute | solution.py:328
  124.4 1.3 broadcast_select_fusion.refs_0_.refs_1_.refs_2_.refs_3_.refs_4_.refs_11_
  125.8 4.8 %project.7 = (f32[2,2,256,128]{3,2,1,0:T(8,128)S(1)}, f32[2,2,256,128]{3,2,1,0:T(8,128)S(1)}) custom-call(s32[1]{0:T(128)} %bitcast.4.place, bf16[128,3968]{1,0:T(8,128)(2,1)S(1)} %broadcast_select_fusion.refs_0_.refs_1_.refs_2_.refs_3_.refs_4_.refs_11_, bf16[128,3968]{1,0:T(8,128)(2,1)S(1)} %broadcast_select_fusion.refs_0_.refs_1_.refs_2_.refs_3_.refs_4_.refs_11_, ...), custom_call_target="tpu_custom_call" | custom-call | flops 1610612736 | bytes 4161536 | tf_op jit(solution)/shard_map/project/pallas_call | solution.py:187
  130.7 1.9 collective-permute-done.21
  132.7 14.0 %collective-permute-start.24 = (f32[256,128]{1,0:T(8,128)S(1)}, f32[256,128]{1,0:T(8,128)S(1)}, u32[]{:S(2)}, u32[]{:S(2)}) collective-permute-start(f32[256,128]{1,0:T(8,128)S(1)} %get-tuple-element.50), channel_id=1, source_target_pairs={{0,5},{1,4},{2,7},{3,6},{4,1},{5,0},{6,3},{7,2},{8,13},{9,12},{10,... | collective-permute-start | bytes 393224 | tf_op jit(solution)/shard_map/ppermute | solution.py:328
  146.7 1.5 collective-permute-start.23
  148.1 2.5 %collective-permute-done.24 = f32[256,128]{1,0:T(8,128)S(1)} collective-permute-done((f32[256,128]{1,0:T(8,128)S(1)}, f32[256,128]{1,0:T(8,128)S(1)}, u32[]{:S(2)}, u32[]{:S(2)}) %collective-permute-start.24) | collective-permute-done | bytes 131104 | tf_op jit(solution)/shard_map/ppermute | solution.py:328
  150.6 2.7 %collective-permute-done.23 = f32[256,128]{1,0:T(8,128)S(1)} collective-permute-done((f32[256,128]{1,0:T(8,128)S(1)}, f32[256,128]{1,0:T(8,128)S(1)}, u32[]{:S(2)}, u32[]{:S(2)}) %collective-permute-start.23) | collective-permute-done | bytes 131104 | tf_op jit(solution)/shard_map/ppermute | solution.py:328
  153.4 1.8 collective-permute-start.29
  156.5 6.6 %collective-permute-start.27 = (bf16[256,128]{1,0:T(8,128)(2,1)S(1)}, bf16[256,128]{1,0:T(8,128)(2,1)S(1)}, u32[]{:S(2)}, u32[]{:S(2)}) collective-permute-start(bf16[256,128]{1,0:T(8,128)(2,1)S(1)} %fusion.3.refs_3_), channel_id=1, source_target_pairs={{0,16},{1,0},{2,18},{3,2},{4,20},{5,4},{6,22},{7,6},{8,24},{9,8},{... | collective-permute-start | bytes 196616 | tf_op jit(solution)/shard_map/ppermute | solution.py:328
  163.2 1.9 collective-permute-done.27
  165.1 4.0 %collective-permute-done.28 = bf16[256,128]{1,0:T(8,128)(2,1)S(1)} collective-permute-done((bf16[256,128]{1,0:T(8,128)(2,1)S(1)}, bf16[256,128]{1,0:T(8,128)(2,1)S(1)}, u32[]{:S(2)}, u32[]{:S(2)}) %collective-permute-start.28) | collective-permute-done | bytes 65568 | tf_op jit(solution)/shard_map/ppermute | solution.py:328
  170.7 11.6 %collective-permute-done.31.refs_17_.refs_21_ = bf16[4,256,128]{2,1,0:T(8,128)(2,1)S(1)} collective-permute-done((bf16[4,256,128]{2,1,0:T(8,128)(2,1)S(1)}, bf16[4,256,128]{2,1,0:T(8,128)(2,1)S(1)}, u32[]{:S(2)}, u32[]{:S(2)}) %collective-permute-start.31) | collective-permute-done | bytes 262176 | tf_op jit(solution)/shard_map/ppermute | solution.py:328
  183.2 1.5 slice_bitcast_fusion.17
  184.7 6.0 %all-gather.3.cloned.1.call-done = bf16[48,256,128]{2,1,0:T(8,128)(2,1)} async-done(((bf16[3,256,128]{2,1,0:T(8,128)(2,1)}), bf16[48,256,128]{2,1,0:T(8,128)(2,1)}) %all-gather.3.cloned.1.call-update) | async-done | bytes 3145744 | tf_op jit(solution)/shard_map/all_gather | solution.py:378
  190.7 1.9 copy-done
  193.5 5.9 %chi.1 = f32[128,4,1024]{2,1,0:T(4,128)} custom-call(s32[5]{0:T(128)S(1)} %stack.62.scalars, bf16[256,128]{1,0:T(8,128)(2,1)S(1)} %fusion.13.refs_0_, bf16[256,128]{1,0:T(8,128)(2,1)S(1)} %fusion.10.refs_1_, bf16[256,128]{1,0:T(8,128)(2,1)S(1)} %fusion.6.refs_2_, bf16[256,128]{1,0:T(8,128)(2,1)S(1)} %fusion.3.refs_3_, ...), custom_call_target="tpu_custom_call" | custom-call | flops 2147483648 | bytes 6291456 | tf_op jit(solution)/shard_map/chi/pallas_call | solution.py:281
  (73 shorter events, 9.7 us)
Async XLA Ops:
  10.5 19.9 %all-to-all-start = ((bf16[8,16,3968]{2,1,0:T(8,128)(2,1)}), bf16[8,16,3968]{2,1,0:T(8,128)(2,1)}, u32[]{:S(2)}, u32[]{:S(2)}) async-start(bf16[8,16,3968]{2,1,0:T(8,128)(2,1)} %pack.1), calls=%async_computation | async-start | bytes 2031616 | tf_op jit(solution)/shard_map/all_to_all | solution.py:480
  15.7 175.1 %all-gather.3.cloned.1.call-start = ((), (), s32[]{:S(2)}) async-start(), calls=%async_computation.1 | async-start | bytes 3342336 | tf_op jit(solution)/shard_map/all_gather | solution.py:378
  30.4 24.6 %collective-permute-start.4 = (bf16[128,3968]{1,0:T(8,128)(2,1)}, bf16[128,3968]{1,0:T(8,128)(2,1)}, u32[]{:S(2)}, u32[]{:S(2)}) collective-permute-start(bf16[128,3968]{1,0:T(8,128)(2,1)} %bitcast.5.refs_0_.refs_1_.refs_2_.refs_3_.refs_4_.refs_8_), channel_id=1, source_target_pairs={{0,8},{1,9},{2,10},{3,11},{4,12},{5,13},{6,14},{7,15},{8,0},{9,1},... | collective-permute-start | bytes 3047432 | tf_op jit(solution)/shard_map/ppermute | solution.py:328
  32.4 24.2 %collective-permute-start.6 = (bf16[128,3968]{1,0:T(8,128)(2,1)}, bf16[128,3968]{1,0:T(8,128)(2,1)}, u32[]{:S(2)}, u32[]{:S(2)}) collective-permute-start(bf16[128,3968]{1,0:T(8,128)(2,1)} %bitcast.5.refs_0_.refs_1_.refs_2_.refs_3_.refs_4_.refs_8_), channel_id=1, source_target_pairs={{8,16},{9,17},{10,18},{11,19},{12,20},{13,21},{14,22},{15,23},{16,... | collective-permute-start | bytes 3047432 | tf_op jit(solution)/shard_map/ppermute | solution.py:328
  34.0 23.9 %collective-permute-start = (bf16[3072,128]{1,0:T(8,128)(2,1)}, bf16[3072,128]{1,0:T(8,128)(2,1)S(1)}, u32[]{:S(2)}, u32[]{:S(2)}) collective-permute-start(bf16[3072,128]{1,0:T(8,128)(2,1)} %get-tuple-element.27), channel_id=1, source_target_pairs={{0,2},{1,3},{2,0},{3,1},{4,6},{5,7},{6,4},{7,5},{8,10},{9,11},{10,... | collective-permute-start | bytes 2359304 | tf_op jit(solution)/shard_map/ppermute | solution.py:328
  34.0 23.9 %collective-permute-start.1 = (bf16[3072,128]{1,0:T(8,128)(2,1)}, bf16[3072,128]{1,0:T(8,128)(2,1)S(1)}, u32[]{:S(2)}, u32[]{:S(2)}) collective-permute-start(bf16[3072,128]{1,0:T(8,128)(2,1)} %get-tuple-element.28), channel_id=1, source_target_pairs={{0,4},{1,5},{2,6},{3,7},{4,0},{5,1},{6,2},{7,3},{8,12},{9,13},{10,... | collective-permute-start | bytes 2359304 | tf_op jit(solution)/shard_map/ppermute | solution.py:328
  34.6 36.0 %collective-permute-start.2 = (bf16[3072,128]{1,0:T(8,128)(2,1)}, bf16[3072,128]{1,0:T(8,128)(2,1)S(1)}, u32[]{:S(2)}, u32[]{:S(2)}) collective-permute-start(bf16[3072,128]{1,0:T(8,128)(2,1)} %get-tuple-element.29), channel_id=1, source_target_pairs={{0,6},{1,7},{2,4},{3,5},{4,2},{5,3},{6,0},{7,1},{8,14},{9,15},{10,... | collective-permute-start | bytes 2359304 | tf_op jit(solution)/shard_map/ppermute | solution.py:328
  55.0 32.5 %collective-permute-start.5 = (bf16[128,3968]{1,0:T(8,128)(2,1)}, bf16[128,3968]{1,0:T(8,128)(2,1)}, u32[]{:S(2)}, u32[]{:S(2)}) collective-permute-start(bf16[128,3968]{1,0:T(8,128)(2,1)} %collective-permute-done.4.refs_0_.refs_1_.refs_2_.refs_3_.refs_4_.refs_9_), channel_id=1, source_target_pairs={{8,16},{9,17},{10,18},{11,19},{12,20},{13,21},{14,22},{15,23},{16,... | collective-permute-start | bytes 3047432 | tf_op jit(solution)/shard_map/ppermute | solution.py:328
  56.6 31.9 %collective-permute-start.7 = (bf16[128,3968]{1,0:T(8,128)(2,1)}, bf16[128,3968]{1,0:T(8,128)(2,1)}, u32[]{:S(2)}, u32[]{:S(2)}) collective-permute-start(bf16[128,3968]{1,0:T(8,128)(2,1)} %collective-permute-done.6), channel_id=1, source_target_pairs={{8,0},{9,1},{10,2},{11,3},{12,4},{13,5},{14,6},{15,7},{16,24},{17,... | collective-permute-start | bytes 3047432 | tf_op jit(solution)/shard_map/ppermute | solution.py:328
  76.8 0.8 copy-start.5
  77.6 6.2 %collective-permute-start.11 = (f32[2,2,256,128]{3,2,1,0:T(8,128)}, f32[2,2,256,128]{3,2,1,0:T(8,128)}, u32[]{:S(2)}, u32[]{:S(2)}) collective-permute-start(f32[2,2,256,128]{3,2,1,0:T(8,128)} %get-tuple-element.34), channel_id=1, source_target_pairs={{0,2},{1,3},{2,0},{3,1},{4,6},{5,7},{6,4},{7,5},{8,10},{9,11},{10,... | collective-permute-start | bytes 1572872 | tf_op jit(solution)/shard_map/ppermute | solution.py:328
  78.2 5.6 %copy-start.6 = (f32[2,2,256,128]{3,2,1,0:T(8,128)S(1)}, f32[2,2,256,128]{3,2,1,0:T(8,128)}, u32[]{:S(2)}) copy-start(f32[2,2,256,128]{3,2,1,0:T(8,128)} %copy-done.5) | copy-start | bytes 1572868
  83.7 11.0 %collective-permute-start.3 = (f32[2,2,256,128]{3,2,1,0:T(8,128)S(1)}, f32[2,2,256,128]{3,2,1,0:T(8,128)S(1)}, u32[]{:S(2)}, u32[]{:S(2)}) collective-permute-start(f32[2,2,256,128]{3,2,1,0:T(8,128)S(1)} %get-tuple-element.31), channel_id=1, source_target_pairs={{0,2},{1,3},{2,0},{3,1},{4,6},{5,7},{6,4},{7,5},{8,10},{9,11},{10,... | collective-permute-start | bytes 1572872 | tf_op jit(solution)/shard_map/ppermute | solution.py:328
  84.9 9.8 %collective-permute-start.14 = (f32[256,128]{1,0:T(8,128)S(1)}, f32[256,128]{1,0:T(8,128)S(1)}, u32[]{:S(2)}, u32[]{:S(2)}) collective-permute-start(f32[256,128]{1,0:T(8,128)S(1)} %get-tuple-element.56), channel_id=1, source_target_pairs={{0,5},{1,4},{2,7},{3,6},{4,1},{5,0},{6,3},{7,2},{8,13},{9,12},{10,... | collective-permute-start | bytes 393224 | tf_op jit(solution)/shard_map/ppermute | solution.py:328
  86.0 8.8 %collective-permute-start.13 = (f32[256,128]{1,0:T(8,128)S(1)}, f32[256,128]{1,0:T(8,128)S(1)}, u32[]{:S(2)}, u32[]{:S(2)}) collective-permute-start(f32[256,128]{1,0:T(8,128)S(1)} %get-tuple-element.57), channel_id=1, source_target_pairs={{0,4},{1,5},{2,6},{3,7},{4,0},{5,1},{6,2},{7,3},{8,12},{9,13},{10,... | collective-permute-start | bytes 393224 | tf_op jit(solution)/shard_map/ppermute | solution.py:328
  87.4 7.3 %collective-permute-start.12 = (f32[256,128]{1,0:T(8,128)S(1)}, f32[256,128]{1,0:T(8,128)S(1)}, u32[]{:S(2)}, u32[]{:S(2)}) collective-permute-start(f32[256,128]{1,0:T(8,128)S(1)} %get-tuple-element.55), channel_id=1, source_target_pairs={{0,1},{1,0},{2,3},{3,2},{4,5},{5,4},{6,7},{7,6},{8,9},{9,8},{10,11... | collective-permute-start | bytes 393224 | tf_op jit(solution)/shard_map/ppermute | solution.py:328
  89.8 4.8 %copy-start.1 = (bf16[128,3968]{1,0:T(8,128)(2,1)}, bf16[128,3968]{1,0:T(8,128)(2,1)S(1)}, u32[]{:S(2)}) copy-start(bf16[128,3968]{1,0:T(8,128)(2,1)S(1)} %broadcast_select_fusion.1.refs_0_.refs_1_.refs_2_.refs_3_.refs_4_.refs_10_) | copy-start | bytes 3047428
  94.6 5.1 %collective-permute-start.15 = (f32[2,2,256,128]{3,2,1,0:T(8,128)S(1)}, f32[2,2,256,128]{3,2,1,0:T(8,128)S(1)}, u32[]{:S(2)}, u32[]{:S(2)}) collective-permute-start(f32[2,2,256,128]{3,2,1,0:T(8,128)S(1)} %get-tuple-element.36), channel_id=1, source_target_pairs={{0,2},{1,3},{2,0},{3,1},{4,6},{5,7},{6,4},{7,5},{8,10},{9,11},{10,... | collective-permute-start | bytes 1572872 | tf_op jit(solution)/shard_map/ppermute | solution.py:328
  94.8 28.2 %collective-permute-start.19 = (bf16[128,3968]{1,0:T(8,128)(2,1)}, bf16[128,3968]{1,0:T(8,128)(2,1)}, u32[]{:S(2)}, u32[]{:S(2)}) collective-permute-start(bf16[128,3968]{1,0:T(8,128)(2,1)} %collective-permute-done.5), channel_id=1, source_target_pairs={{8,0},{9,1},{10,2},{11,3},{12,4},{13,5},{14,6},{15,7},{16,24},{17,... | collective-permute-start | bytes 3047432 | tf_op jit(solution)/shard_map/ppermute | solution.py:328
  96.2 7.3 %collective-permute-start.10 = (f32[256,128]{1,0:T(8,128)S(1)}, f32[256,128]{1,0:T(8,128)S(1)}, u32[]{:S(2)}, u32[]{:S(2)}) collective-permute-start(f32[256,128]{1,0:T(8,128)S(1)} %get-tuple-element.59), channel_id=1, source_target_pairs={{0,5},{1,4},{2,7},{3,6},{4,1},{5,0},{6,3},{7,2},{8,13},{9,12},{10,... | collective-permute-start | bytes 393224 | tf_op jit(solution)/shard_map/ppermute | solution.py:328
  97.2 9.0 %collective-permute-start.9 = (f32[256,128]{1,0:T(8,128)S(1)}, f32[256,128]{1,0:T(8,128)S(1)}, u32[]{:S(2)}, u32[]{:S(2)}) collective-permute-start(f32[256,128]{1,0:T(8,128)S(1)} %get-tuple-element.60), channel_id=1, source_target_pairs={{0,4},{1,5},{2,6},{3,7},{4,0},{5,1},{6,2},{7,3},{8,12},{9,13},{10,... | collective-permute-start | bytes 393224 | tf_op jit(solution)/shard_map/ppermute | solution.py:328
  98.7 8.6 %collective-permute-start.8 = (f32[256,128]{1,0:T(8,128)S(1)}, f32[256,128]{1,0:T(8,128)S(1)}, u32[]{:S(2)}, u32[]{:S(2)}) collective-permute-start(f32[256,128]{1,0:T(8,128)S(1)} %get-tuple-element.58), channel_id=1, source_target_pairs={{0,1},{1,0},{2,3},{3,2},{4,5},{5,4},{6,7},{7,6},{8,9},{9,8},{10,11... | collective-permute-start | bytes 393224 | tf_op jit(solution)/shard_map/ppermute | solution.py:328
  99.8 9.0 %collective-permute-start.18 = (f32[256,128]{1,0:T(8,128)S(1)}, f32[256,128]{1,0:T(8,128)S(1)}, u32[]{:S(2)}, u32[]{:S(2)}) collective-permute-start(f32[256,128]{1,0:T(8,128)S(1)} %get-tuple-element.53), channel_id=1, source_target_pairs={{0,5},{1,4},{2,7},{3,6},{4,1},{5,0},{6,3},{7,2},{8,13},{9,12},{10,... | collective-permute-start | bytes 393224 | tf_op jit(solution)/shard_map/ppermute | solution.py:328
  103.5 7.8 %collective-permute-start.17 = (f32[256,128]{1,0:T(8,128)S(1)}, f32[256,128]{1,0:T(8,128)S(1)}, u32[]{:S(2)}, u32[]{:S(2)}) collective-permute-start(f32[256,128]{1,0:T(8,128)S(1)} %get-tuple-element.54), channel_id=1, source_target_pairs={{0,4},{1,5},{2,6},{3,7},{4,0},{5,1},{6,2},{7,3},{8,12},{9,13},{10,... | collective-permute-start | bytes 393224 | tf_op jit(solution)/shard_map/ppermute | solution.py:328
  106.2 6.1 %collective-permute-start.16 = (f32[256,128]{1,0:T(8,128)S(1)}, f32[256,128]{1,0:T(8,128)S(1)}, u32[]{:S(2)}, u32[]{:S(2)}) collective-permute-start(f32[256,128]{1,0:T(8,128)S(1)} %get-tuple-element.52), channel_id=1, source_target_pairs={{0,1},{1,0},{2,3},{3,2},{4,5},{5,4},{6,7},{7,6},{8,9},{9,8},{10,11... | collective-permute-start | bytes 393224 | tf_op jit(solution)/shard_map/ppermute | solution.py:328
  107.4 6.5 %collective-permute-start.20 = (bf16[2,256,128]{2,1,0:T(8,128)(2,1)S(1)}, bf16[2,256,128]{2,1,0:T(8,128)(2,1)}, u32[]{:S(2)}, u32[]{:S(2)}) collective-permute-start(bf16[2,256,128]{2,1,0:T(8,128)(2,1)S(1)} %pad_maximum_fusion.2), channel_id=1, source_target_pairs={{0,1},{1,0},{2,3},{3,2},{4,5},{5,4},{6,7},{7,6},{8,9},{9,8},{10,11... | collective-permute-start | bytes 393224 | tf_op jit(solution)/shard_map/ppermute | solution.py:328
  123.0 0.7 collective-permute-start.30
  123.7 0.7 copy-start.8
  125.8 4.8 %copy-start.3 = (bf16[128,3968]{1,0:T(8,128)(2,1)}, bf16[128,3968]{1,0:T(8,128)(2,1)S(1)}, u32[]{:S(2)}) copy-start(bf16[128,3968]{1,0:T(8,128)(2,1)S(1)} %broadcast_select_fusion.refs_0_.refs_1_.refs_2_.refs_3_.refs_4_.refs_11_) | copy-start | bytes 3047428
  130.6 60.2 %copy-start.2 = (bf16[128,3968]{1,0:T(8,128)(2,1)S(1)}, bf16[128,3968]{1,0:T(8,128)(2,1)}, u32[]{:S(2)}) copy-start(bf16[128,3968]{1,0:T(8,128)(2,1)} %copy-done.1) | copy-start | bytes 3047428
  130.6 60.1 %copy-start.4 = (bf16[128,3968]{1,0:T(8,128)(2,1)S(1)}, bf16[128,3968]{1,0:T(8,128)(2,1)}, u32[]{:S(2)}) copy-start(bf16[128,3968]{1,0:T(8,128)(2,1)} %copy-done.3) | copy-start | bytes 3047428
  130.6 2.0 collective-permute-start.21
  132.7 17.9 %collective-permute-start.24 = (f32[256,128]{1,0:T(8,128)S(1)}, f32[256,128]{1,0:T(8,128)S(1)}, u32[]{:S(2)}, u32[]{:S(2)}) collective-permute-start(f32[256,128]{1,0:T(8,128)S(1)} %get-tuple-element.50), channel_id=1, source_target_pairs={{0,5},{1,4},{2,7},{3,6},{4,1},{5,0},{6,3},{7,2},{8,13},{9,12},{10,... | collective-permute-start | bytes 393224 | tf_op jit(solution)/shard_map/ppermute | solution.py:328
  146.7 6.7 %collective-permute-start.23 = (f32[256,128]{1,0:T(8,128)S(1)}, f32[256,128]{1,0:T(8,128)S(1)}, u32[]{:S(2)}, u32[]{:S(2)}) collective-permute-start(f32[256,128]{1,0:T(8,128)S(1)} %get-tuple-element.51), channel_id=1, source_target_pairs={{0,4},{1,5},{2,6},{3,7},{4,0},{5,1},{6,2},{7,3},{8,12},{9,13},{10,... | collective-permute-start | bytes 393224 | tf_op jit(solution)/shard_map/ppermute | solution.py:328
  148.1 5.2 %collective-permute-start.22 = (f32[256,128]{1,0:T(8,128)S(1)}, f32[256,128]{1,0:T(8,128)S(1)}, u32[]{:S(2)}, u32[]{:S(2)}) collective-permute-start(f32[256,128]{1,0:T(8,128)S(1)} %get-tuple-element.49), channel_id=1, source_target_pairs={{0,1},{1,0},{2,3},{3,2},{4,5},{5,4},{6,7},{7,6},{8,9},{9,8},{10,11... | collective-permute-start | bytes 393224 | tf_op jit(solution)/shard_map/ppermute | solution.py:328
  153.4 15.7 %collective-permute-start.29 = (bf16[2,256,128]{2,1,0:T(8,128)(2,1)S(1)}, bf16[2,256,128]{2,1,0:T(8,128)(2,1)S(1)}, u32[]{:S(2)}, u32[]{:S(2)}) collective-permute-start(bf16[2,256,128]{2,1,0:T(8,128)(2,1)S(1)} %pad_maximum_fusion.3), channel_id=1, source_target_pairs={{0,1},{1,0},{2,3},{3,2},{4,5},{5,4},{6,7},{7,6},{8,9},{9,8},{10,11... | collective-permute-start | bytes 393224 | tf_op jit(solution)/shard_map/ppermute | solution.py:328
  155.2 8.0 %collective-permute-start.25 = (bf16[256,128]{1,0:T(8,128)(2,1)S(1)}, bf16[256,128]{1,0:T(8,128)(2,1)S(1)}, u32[]{:S(2)}, u32[]{:S(2)}) collective-permute-start(bf16[256,128]{1,0:T(8,128)(2,1)S(1)} %fusion.3.refs_3_), channel_id=1, source_target_pairs={{0,0},{1,16},{2,2},{3,18},{4,4},{5,20},{6,6},{7,22},{8,8},{9,24},{... | collective-permute-start | bytes 196616 | tf_op jit(solution)/shard_map/ppermute | solution.py:328
  155.9 7.3 %collective-permute-start.26 = (bf16[256,128]{1,0:T(8,128)(2,1)S(1)}, bf16[256,128]{1,0:T(8,128)(2,1)S(1)}, u32[]{:S(2)}, u32[]{:S(2)}) collective-permute-start(bf16[256,128]{1,0:T(8,128)(2,1)S(1)} %fusion.3.refs_3_), channel_id=1, source_target_pairs={{0,8},{1,24},{2,10},{3,26},{4,12},{5,28},{6,14},{7,30},{8,0},{9,16... | collective-permute-start | bytes 196616 | tf_op jit(solution)/shard_map/ppermute | solution.py:328
  156.5 8.5 %collective-permute-start.27 = (bf16[256,128]{1,0:T(8,128)(2,1)S(1)}, bf16[256,128]{1,0:T(8,128)(2,1)S(1)}, u32[]{:S(2)}, u32[]{:S(2)}) collective-permute-start(bf16[256,128]{1,0:T(8,128)(2,1)S(1)} %fusion.3.refs_3_), channel_id=1, source_target_pairs={{0,16},{1,0},{2,18},{3,2},{4,20},{5,4},{6,22},{7,6},{8,24},{9,8},{... | collective-permute-start | bytes 196616 | tf_op jit(solution)/shard_map/ppermute | solution.py:328
  163.2 5.9 %collective-permute-start.28 = (bf16[256,128]{1,0:T(8,128)(2,1)S(1)}, bf16[256,128]{1,0:T(8,128)(2,1)S(1)}, u32[]{:S(2)}, u32[]{:S(2)}) collective-permute-start(bf16[256,128]{1,0:T(8,128)(2,1)S(1)} %fusion.3.refs_3_), channel_id=1, source_target_pairs={{0,24},{1,8},{2,26},{3,10},{4,28},{5,12},{6,30},{7,14},{8,16},{9,0... | collective-permute-start | bytes 196616 | tf_op jit(solution)/shard_map/ppermute | solution.py:328
  169.1 0.7 copy-start.9
  169.8 12.5 %collective-permute-start.31 = (bf16[4,256,128]{2,1,0:T(8,128)(2,1)S(1)}, bf16[4,256,128]{2,1,0:T(8,128)(2,1)S(1)}, u32[]{:S(2)}, u32[]{:S(2)}) collective-permute-start(bf16[4,256,128]{2,1,0:T(8,128)(2,1)S(1)} %pad_maximum_fusion.refs_16_.refs_20_), channel_id=1, source_target_pairs={{0,4},{1,5},{2,6},{3,7},{4,0},{5,1},{6,2},{7,3},{8,12},{9,13},{10,... | collective-permute-start | bytes 786440 | tf_op jit(solution)/shard_map/ppermute | solution.py:328
  170.7 14.0 %collective-permute-start.32 = (bf16[4,256,128]{2,1,0:T(8,128)(2,1)S(1)}, bf16[4,256,128]{2,1,0:T(8,128)(2,1)S(1)}, u32[]{:S(2)}, u32[]{:S(2)}) collective-permute-start(bf16[4,256,128]{2,1,0:T(8,128)(2,1)S(1)} %pad_maximum_fusion.refs_16_.refs_20_), channel_id=1, source_target_pairs={{0,2},{1,3},{2,0},{3,1},{4,6},{5,7},{6,4},{7,5},{8,10},{9,11},{10,... | collective-permute-start | bytes 786440 | tf_op jit(solution)/shard_map/ppermute | solution.py:328
  182.3 2.4 %collective-permute-start.33 = (bf16[4,256,128]{2,1,0:T(8,128)(2,1)S(1)}, bf16[4,256,128]{2,1,0:T(8,128)(2,1)S(1)}, u32[]{:S(2)}, u32[]{:S(2)}) collective-permute-start(bf16[4,256,128]{2,1,0:T(8,128)(2,1)S(1)} %collective-permute-done.31.refs_17_.refs_21_), channel_id=1, source_target_pairs={{0,2},{1,3},{2,0},{3,1},{4,6},{5,7},{6,4},{7,5},{8,10},{9,11},{10,... | collective-permute-start | bytes 786440 | tf_op jit(solution)/shard_map/ppermute | solution.py:328
  190.7 1.9 copy-start
  192.6 0.8 copy-start.7
Sparse Core Ops, SparseCore 0:
  124.6 66.1 all-gather.2

commit v11 on v10

--- a/solution.py
+++ b/solution.py
@@ -234,8 +234,8 @@
     mates = refs[slots : 2 * slots]
     scales = refs[2 * slots : 3 * slots]
     rights_a = refs[3 * slots : 3 * slots + 4]
-    rights_b = refs[3 * slots + 4 : -2]
-    out, weighted = refs[-2:]
+    rights_b = refs[3 * slots + 4 : 3 * slots + 12]
+    out, weighted = refs[3 * slots + 12 :]
     columns = out.shape[0]
 
     @pl.when(pl.program_id(0) == 0)
@@ -252,7 +252,7 @@
             if r < early:
                 pair = [rights_a[2 * h + c][0, r] for c in range(2)]
             else:
-                own, other, mate, both = [rights_b[8 * (r - early) + 4 * h + q][0] for q in range(4)]
+                own, other, mate, both = [rights_b[4 * h + q][0, r - early] for q in range(4)]
                 own = jnp.where(same_y, own, other)
                 mate = jnp.where(same_y, mate, both)
                 pair = [jnp.where(core == c, own, mate) for c in range(2)]
@@ -269,14 +269,14 @@
 def make_chi(owns, mates, units, right_a, rights_b, scalars, n_freq, factor):
     members, early, rows, columns = right_a.shape
     tiles = members // 4
-    late = len(rights_b)
+    late = rights_b[0].shape[1]
     slots = early + late
     width = units[0].shape[0]
     last = units[0].shape[1] // LANES - 1
     flops = 4 * slots * rows * n_freq * columns * tiles * 2 * columns
 
     def near(h, i, scalars):
-        return (lax.bitwise_xor(scalars[0], h * 2 + i // 2), 0, 0)
+        return (lax.bitwise_xor(scalars[0], h * 2 + i // 2), 0, 0, 0)
 
     return pl.pallas_call(
         functools.partial(chi_kernel, early, late, n_freq, factor),
@@ -297,8 +297,7 @@
                 for c in range(2)
             ]
             + [
-                pl.BlockSpec((1, rows, columns), functools.partial(near, h))
-                for r in range(late)
+                pl.BlockSpec((1, late, rows, columns), functools.partial(near, h))
                 for h in range(2)
                 for q in range(4)
             ],
@@ -313,7 +312,7 @@
             transcendentals=0,
         ),
         name="chi",
-    )(scalars, *owns, *mates, *units, *([right_a] * 4), *[a for four in rights_b for a in four * 2])
+    )(scalars, *owns, *mates, *units, *([right_a] * 4), *(list(rights_b) * 2))
 
 
 def fast(shape, unit, eigenvectors, part, val_count, cond_count, n_freq, factor):
@@ -373,19 +372,20 @@
         return send(own, lambda i, j, k, t: ((2 * t + i % 2) ^ m, j, k, i // 2))
 
     owns = [coefficients(units[0], (across, outward)), coefficients(units[1])]
-    mate_a = mate(jnp.stack(owns))
-    owns.append(coefficients(units[2], None, (far, mate_a)))
-    right_a = lax.all_gather(share(jnp.stack(owns), 0), ("z", "y", "c"), axis=0)
+    own_a = jnp.stack(owns)
+    share_a = share(own_a, 0)
+    mate_a = mate(own_a)
+    right_a = lax.all_gather(share_a, ("z", "y", "c"), axis=0)
+    owns.append(coefficients(units[2], None, (far, mate_a, share_a)))
     units.append(jnp.where(inner, middle, far))
-    own_b = coefficients(units[3])
+    owns.append(coefficients(units[3], owns[2]))
+    own_b = jnp.stack(owns[2:])
     shares = [share(own_b, m) for m in range(nz)]
-    mate_b = mate(jnp.stack([owns[2], own_b]))
-    shares, mate_b = lax.optimization_barrier((shares, mate_b))
+    shares, mate_b, right_a = lax.optimization_barrier((shares, mate(own_b), right_a))
     held = jnp.stack(shares)
     other = send(held, lambda i, j, k, t: (i, 1 - j, k, t))
     across_core = lambda i, j, k, t: (i, j, 1 - k, t)
-    rights_b = [(held, other, send(held, across_core), send(other, across_core))]
-    owns.append(own_b)
+    rights_b = [held, other, send(held, across_core), send(other, across_core)]
     mates = [mate_a[0], mate_a[1], mate_b[0], mate_b[1]]
     scalars = jnp.stack([z, y, c, 2 * x, x])
     return make_chi(owns, mates, units, right_a, rights_b, scalars, n_freq, factor)

time: 207 us -> 210 us (1.014)
  waiting for transfers between devices: 93.3 us -> 109 us
  starting transfers between devices: 53.2 us -> 43.9 us
  local copies, waits for them, and re-layouts: 10.8 us -> 7.31 us
    ppermute x34, waiting for transfers between devices: 76 us -> 97.6 us  [send(): lax.ppermute(array, AXES, [(source, number[to]) for source, to in pairs i...]
    ppermute x34, starting transfers between devices: 47.9 us -> 38.7 us  [send(): lax.ppermute(array, AXES, [(source, number[to]) for source, to in pairs i...]
    all_gather x1, waiting for transfers between devices: 6.04 us -> 0.01 us  [fast(): right_a = lax.all_gather(share_a, ('z', 'y', 'c'), axis=0)]
    unnamed x20 -> x22, local copies, waits for them, and re-layouts: 4.89 us -> 2.96 us
  transfers between devices with their start and end apart: 36 -> 36, of which waited for: 17 -> 20; matrix products, arithmetic and copies ran while one was open for 5% -> 4% of each run, Pallas kernels for 10% -> 10%
where the time goes in v11:
time: 210 us; the launch traced here: 208 us
  waiting for transfers between devices  109 us (52%)
  starting transfers between devices  43.9 us (21%)
  Pallas kernels  31 us (15%)
  between operations  13.8 us (7%)
  local copies, waits for them, and re-layouts  7.31 us (3%)
  other arithmetic  3.19 us (2%)
    ppermute x34, waiting for transfers between devices, send(): lax.ppermute(array, AXES, [(source, number[to]) for source, to in pairs i...  97.6 us
    ppermute x34, starting transfers between devices, send(): lax.ppermute(array, AXES, [(source, number[to]) for source, to in pairs i...  38.7 us
    pallas_call x4, Pallas kernels, project(): pl.pallas_call(functools.partial(project_kernel, segs, val_count, cond_co...  20.3 us
    all_to_all x1, waiting for transfers between devices, local(): unit = lax.all_to_all(packed, ('y', 'c', 'x'), 0, 0, tiled=True)  11.3 us
    pallas_call x1, Pallas kernels, make_chi(): pl.pallas_call(functools.partial(chi_kernel, early, late, n_freq, factor)...  6.75 us
    all_to_all x1, starting transfers between devices, local(): unit = lax.all_to_all(packed, ('y', 'c', 'x'), 0, 0, tiled=True)  5.17 us
  transfers between devices with their start and end apart: 36, of which 20 were waited for; matrix products, arithmetic and copies ran while one was open for 4% of the time, Pallas kernels for 10%

profile of v11, /device:TPU:0, one launch (start us, length us, event | category | flops | bytes accessed | tf_op | source)
XLA Modules:
  0.0 208.2 jit_solution(13855877262750945731)
XLA Ops:
  6.5 4.0 %pack.1 = bf16[8,16,3968]{2,1,0:T(8,128)(2,1)} custom-call(f32[4]{0:T(128)} %val_energy.1, f32[16]{0:T(128)} %cond_energy.1, s32[64]{0:T(128)} %val_slot.1, s32[64]{0:T(128)} %cond_slot.1, f32[4]{0:T(128)} %frequencies.1, bf16[16,24576]{1,0:T(8,128)(2,1)} %refs_1_.1, bf16[16,24576]{1,0:T(8,128)(2,1)} %refs_1_.1, bf16[4,24576]{1,0:T(4,128)(2,1)} %refs_3_.1, ...), custom_call_target="tpu_custom_call" | custom-call | tf_op jit(solution)/shard_map/pack/pallas_call | solution.py:77
  10.5 5.2 %all-to-all-start = ((bf16[8,16,3968]{2,1,0:T(8,128)(2,1)}), bf16[8,16,3968]{2,1,0:T(8,128)(2,1)}, u32[]{:S(2)}, u32[]{:S(2)}) async-start(bf16[8,16,3968]{2,1,0:T(8,128)(2,1)} %pack.1), calls=%async_computation | async-start | bytes 2031616 | tf_op jit(solution)/shard_map/all_to_all | solution.py:480
  15.8 3.3 %constant_dynamic-slice_fusion = (bf16[3072,128]{1,0:T(8,128)(2,1)}, bf16[3072,128]{1,0:T(8,128)(2,1)}, bf16[3072,128]{1,0:T(8,128)(2,1)S(1)}, bf16[3072,128]{1,0:T(8,128)(2,1)}) fusion(bf16[12288,128]{1,0:T(8,128)(2,1)} %param.14, s32[]{:T(128)S(6)} %select_n.27, s32[]{:T(128)S(6)} %select_n.25, s32[]{:T(128)S(6)} %select_n.24, s32[]{:T(128)S(6)} %select_n.26), kind=kLoop, calls=%fused_computation.38 | loop fusion | bytes 6291472 | tf_op jit(solution)/shard_map/dynamic_slice | solution.py:337
  19.0 11.3 %all-to-all-done = bf16[8,16,3968]{2,1,0:T(8,128)(2,1)} async-done(((bf16[8,16,3968]{2,1,0:T(8,128)(2,1)}), bf16[8,16,3968]{2,1,0:T(8,128)(2,1)}, u32[]{:S(2)}, u32[]{:S(2)}) %all-to-all-start) | async-done | bytes 1015840 | tf_op jit(solution)/shard_map/all_to_all | solution.py:480
  30.4 2.0 collective-permute-start.4
  32.4 1.6 collective-permute-start.6
  34.6 1.3 collective-permute-start.2
  35.9 19.1 %collective-permute-done.4.refs_0_.refs_1_.refs_2_.refs_3_.refs_4_.refs_9_ = bf16[128,3968]{1,0:T(8,128)(2,1)} collective-permute-done((bf16[128,3968]{1,0:T(8,128)(2,1)}, bf16[128,3968]{1,0:T(8,128)(2,1)}, u32[]{:S(2)}, u32[]{:S(2)}) %collective-permute-start.4) | collective-permute-done | bytes 1015840 | tf_op jit(solution)/shard_map/ppermute | solution.py:327
  55.7 1.3 collective-permute-start.7
  57.0 13.6 %collective-permute-done.2.refs_8_.refs_12_.refs_16_.refs_20_ = bf16[3072,128]{1,0:T(8,128)(2,1)S(1)} collective-permute-done((bf16[3072,128]{1,0:T(8,128)(2,1)}, bf16[3072,128]{1,0:T(8,128)(2,1)S(1)}, u32[]{:S(2)}, u32[]{:S(2)}) %collective-permute-start.2) | collective-permute-done | bytes 786464 | tf_op jit(solution)/shard_map/ppermute | solution.py:327
  70.6 5.4 %project.4 = (f32[2,2,256,128]{3,2,1,0:T(8,128)S(1)}, f32[2,2,256,128]{3,2,1,0:T(8,128)S(1)}) custom-call(s32[1]{0:T(128)} %bitcast.4.place, bf16[128,3968]{1,0:T(8,128)(2,1)} %bitcast.5.refs_0_.refs_1_.refs_2_.refs_3_.refs_4_.refs_8_, bf16[128,3968]{1,0:T(8,128)(2,1)} %bitcast.5.refs_0_.refs_1_.refs_2_.refs_3_.refs_4_.refs_8_, ...), custom_call_target="tpu_custom_call" | custom-call | flops 1610612736 | bytes 4161536 | tf_op jit(solution)/shard_map/project/pallas_call | solution.py:187
  76.6 5.4 %project.5 = (f32[2,2,256,128]{3,2,1,0:T(8,128)S(1)}, f32[2,2,256,128]{3,2,1,0:T(8,128)S(1)}) custom-call(s32[1]{0:T(128)} %bitcast.4.place, bf16[128,3968]{1,0:T(8,128)(2,1)} %collective-permute-done.4.refs_0_.refs_1_.refs_2_.refs_3_.refs_4_.refs_9_, bf16[128,3968]{1,0:T(8,128)(2,1)} %collective-permute-done.4.refs_0_.refs_1_.refs_2_.refs_3_.refs_4_.refs_9_, ...), custom_call_target="tpu_custom_call" | custom-call | flops 1610612736 | bytes 4161536 | tf_op jit(solution)/shard_map/project/pallas_call | solution.py:187
  82.2 1.7 collective-permute-done.11
  84.1 1.1 collective-permute-start.14
  85.1 1.5 collective-permute-start.13
  86.6 1.0 collective-permute-start.12
  87.7 1.1 collective-permute-start.10
  88.7 1.5 collective-permute-start.9
  90.2 1.2 collective-permute-done.14
  91.4 1.0 collective-permute-start.8
  92.4 1.9 collective-permute-done.13
  94.3 2.8 %collective-permute-done.10 = f32[256,128]{1,0:T(8,128)S(1)} collective-permute-done((f32[256,128]{1,0:T(8,128)S(1)}, f32[256,128]{1,0:T(8,128)S(1)}, u32[]{:S(2)}, u32[]{:S(2)}) %collective-permute-start.10) | collective-permute-done | bytes 131104 | tf_op jit(solution)/shard_map/ppermute | solution.py:327
  97.1 1.7 collective-permute-done.9
  99.6 1.3 collective-permute-start.19
  101.6 1.3 broadcast_select_fusion.1.refs_0_.refs_1_.refs_2_.refs_3_.refs_4_.refs_10_
  102.9 4.8 %project.6 = (f32[2,2,256,128]{3,2,1,0:T(8,128)S(1)}, f32[2,2,256,128]{3,2,1,0:T(8,128)S(1)}) custom-call(s32[1]{0:T(128)} %bitcast.4.place, bf16[128,3968]{1,0:T(8,128)(2,1)S(1)} %broadcast_select_fusion.1.refs_0_.refs_1_.refs_2_.refs_3_.refs_4_.refs_10_, bf16[128,3968]{1,0:T(8,128)(2,1)S(1)} %broadcast_select_fusion.1.refs_0_.refs_1_.refs_2_.refs_3_.refs_4_.refs_10_, ...), custom_call_target="tpu_custom_call" | custom-call | flops 1610612736 | bytes 4161536 | tf_op jit(solution)/shard_map/project/pallas_call | solution.py:187
  107.8 1.9 collective-permute-done.15
  109.8 23.7 %collective-permute-done.19 = bf16[128,3968]{1,0:T(8,128)(2,1)} collective-permute-done((bf16[128,3968]{1,0:T(8,128)(2,1)}, bf16[128,3968]{1,0:T(8,128)(2,1)}, u32[]{:S(2)}, u32[]{:S(2)}) %collective-permute-start.19) | collective-permute-done | bytes 1015840 | tf_op jit(solution)/shard_map/ppermute | solution.py:327
  133.5 1.3 broadcast_select_fusion.refs_0_.refs_1_.refs_2_.refs_3_.refs_4_.refs_11_
  134.8 4.8 %project.7 = (f32[2,2,256,128]{3,2,1,0:T(8,128)S(1)}, f32[2,2,256,128]{3,2,1,0:T(8,128)S(1)}) custom-call(s32[1]{0:T(128)} %bitcast.4.place, bf16[128,3968]{1,0:T(8,128)(2,1)S(1)} %broadcast_select_fusion.refs_0_.refs_1_.refs_2_.refs_3_.refs_4_.refs_11_, bf16[128,3968]{1,0:T(8,128)(2,1)S(1)} %broadcast_select_fusion.refs_0_.refs_1_.refs_2_.refs_3_.refs_4_.refs_11_, ...), custom_call_target="tpu_custom_call" | custom-call | flops 1610612736 | bytes 4161536 | tf_op jit(solution)/shard_map/project/pallas_call | solution.py:187
  139.7 2.5 %collective-permute-start.18 = (f32[256,128]{1,0:T(8,128)S(1)}, f32[256,128]{1,0:T(8,128)S(1)}, u32[]{:S(2)}, u32[]{:S(2)}) collective-permute-start(f32[256,128]{1,0:T(8,128)S(1)} %get-tuple-element.57), channel_id=1, source_target_pairs={{0,5},{1,4},{2,7},{3,6},{4,1},{5,0},{6,3},{7,2},{8,13},{9,12},{10,... | collective-permute-start | bytes 393224 | tf_op jit(solution)/shard_map/ppermute | solution.py:327
  142.3 1.1 collective-permute-start.17
  143.4 2.0 collective-permute-start.20
  145.4 1.4 collective-permute-done.18
  146.8 2.6 %collective-permute-done.17 = f32[256,128]{1,0:T(8,128)S(1)} collective-permute-done((f32[256,128]{1,0:T(8,128)S(1)}, f32[256,128]{1,0:T(8,128)S(1)}, u32[]{:S(2)}, u32[]{:S(2)}) %collective-permute-start.17) | collective-permute-done | bytes 131104 | tf_op jit(solution)/shard_map/ppermute | solution.py:327
  149.8 1.9 collective-permute-done.20
  151.8 2.8 %collective-permute-start.25 = (f32[256,128]{1,0:T(8,128)S(1)}, f32[256,128]{1,0:T(8,128)S(1)}, u32[]{:S(2)}, u32[]{:S(2)}) collective-permute-start(f32[256,128]{1,0:T(8,128)S(1)} %get-tuple-element.54), channel_id=1, source_target_pairs={{0,5},{1,4},{2,7},{3,6},{4,1},{5,0},{6,3},{7,2},{8,13},{9,12},{10,... | collective-permute-start | bytes 393224 | tf_op jit(solution)/shard_map/ppermute | solution.py:327
  154.6 0.9 collective-permute-start.24
  155.5 3.0 %collective-permute-done.25 = f32[256,128]{1,0:T(8,128)S(1)} collective-permute-done((f32[256,128]{1,0:T(8,128)S(1)}, f32[256,128]{1,0:T(8,128)S(1)}, u32[]{:S(2)}, u32[]{:S(2)}) %collective-permute-start.25) | collective-permute-done | bytes 131104 | tf_op jit(solution)/shard_map/ppermute | solution.py:327
  158.5 2.4 %collective-permute-done.24 = f32[256,128]{1,0:T(8,128)S(1)} collective-permute-done((f32[256,128]{1,0:T(8,128)S(1)}, f32[256,128]{1,0:T(8,128)S(1)}, u32[]{:S(2)}, u32[]{:S(2)}) %collective-permute-start.24) | collective-permute-done | bytes 131104 | tf_op jit(solution)/shard_map/ppermute | solution.py:327
  161.7 7.7 %collective-permute-start.28 = (bf16[2,256,128]{2,1,0:T(8,128)(2,1)S(1)}, bf16[2,256,128]{2,1,0:T(8,128)(2,1)S(1)}, u32[]{:S(2)}, u32[]{:S(2)}) collective-permute-start(bf16[2,256,128]{2,1,0:T(8,128)(2,1)S(1)} %pad_maximum_fusion.2), channel_id=1, source_target_pairs={{0,16},{1,0},{2,18},{3,2},{4,20},{5,4},{6,22},{7,6},{8,24},{9,8},{... | collective-permute-start | bytes 393224 | tf_op jit(solution)/shard_map/ppermute | solution.py:327
  169.4 2.0 collective-permute-start.30
  172.2 6.7 %collective-permute-done.29 = bf16[2,256,128]{2,1,0:T(8,128)(2,1)S(1)} collective-permute-done((bf16[2,256,128]{2,1,0:T(8,128)(2,1)S(1)}, bf16[2,256,128]{2,1,0:T(8,128)(2,1)S(1)}, u32[]{:S(2)}, u32[]{:S(2)}) %collective-permute-start.29) | collective-permute-done | bytes 131104 | tf_op jit(solution)/shard_map/ppermute | solution.py:327
  179.7 1.4 collective-permute-start.31
  181.2 9.8 %collective-permute-done.31.refs_17_.refs_21_ = bf16[4,2,256,128]{3,2,1,0:T(8,128)(2,1)S(1)} collective-permute-done((bf16[4,2,256,128]{3,2,1,0:T(8,128)(2,1)S(1)}, bf16[4,2,256,128]{3,2,1,0:T(8,128)(2,1)S(1)}, u32[]{:S(2)}, u32[]{:S(2)}) %collective-permute-start.31) | collective-permute-done | bytes 524320 | tf_op jit(solution)/shard_map/ppermute | solution.py:327
  192.0 1.0 collective-permute-done.33.refs_19_.refs_23_
  193.0 1.6 copy-done.4
  194.6 6.8 %chi.1 = f32[128,4,1024]{2,1,0:T(4,128)} custom-call(s32[5]{0:T(128)S(1)} %stack.56.scalars, bf16[256,128]{1,0:T(8,128)(2,1)S(1)} %fusion.12.refs_0_, bf16[256,128]{1,0:T(8,128)(2,1)S(1)} %fusion.6.refs_1_, bf16[256,128]{1,0:T(8,128)(2,1)S(1)} %fusion.2.refs_2_, bf16[256,128]{1,0:T(8,128)(2,1)S(1)} %fusion.9.refs_3_, ...), custom_call_target="tpu_custom_call" | custom-call | flops 2147483648 | bytes 6291456 | tf_op jit(solution)/shard_map/chi/pallas_call | solution.py:281
  (74 shorter events, 7.9 us)
Async XLA Ops:
  10.5 19.9 %all-to-all-start = ((bf16[8,16,3968]{2,1,0:T(8,128)(2,1)}), bf16[8,16,3968]{2,1,0:T(8,128)(2,1)}, u32[]{:S(2)}, u32[]{:S(2)}) async-start(bf16[8,16,3968]{2,1,0:T(8,128)(2,1)} %pack.1), calls=%async_computation | async-start | bytes 2031616 | tf_op jit(solution)/shard_map/all_to_all | solution.py:480
  15.7 163.3 %all-gather.3.cloned.1.call-start = ((), (), s32[]{:S(2)}) async-start(), calls=%async_computation.1 | async-start | bytes 2228224 | tf_op jit(solution)/shard_map/all_gather | solution.py:378
  30.4 24.6 %collective-permute-start.4 = (bf16[128,3968]{1,0:T(8,128)(2,1)}, bf16[128,3968]{1,0:T(8,128)(2,1)}, u32[]{:S(2)}, u32[]{:S(2)}) collective-permute-start(bf16[128,3968]{1,0:T(8,128)(2,1)} %bitcast.5.refs_0_.refs_1_.refs_2_.refs_3_.refs_4_.refs_8_), channel_id=1, source_target_pairs={{0,8},{1,9},{2,10},{3,11},{4,12},{5,13},{6,14},{7,15},{8,0},{9,1},... | collective-permute-start | bytes 3047432 | tf_op jit(solution)/shard_map/ppermute | solution.py:327
  32.4 23.3 %collective-permute-start.6 = (bf16[128,3968]{1,0:T(8,128)(2,1)}, bf16[128,3968]{1,0:T(8,128)(2,1)}, u32[]{:S(2)}, u32[]{:S(2)}) collective-permute-start(bf16[128,3968]{1,0:T(8,128)(2,1)} %bitcast.5.refs_0_.refs_1_.refs_2_.refs_3_.refs_4_.refs_8_), channel_id=1, source_target_pairs={{8,16},{9,17},{10,18},{11,19},{12,20},{13,21},{14,22},{15,23},{16,... | collective-permute-start | bytes 3047432 | tf_op jit(solution)/shard_map/ppermute | solution.py:327
  34.0 23.0 %collective-permute-start = (bf16[3072,128]{1,0:T(8,128)(2,1)}, bf16[3072,128]{1,0:T(8,128)(2,1)S(1)}, u32[]{:S(2)}, u32[]{:S(2)}) collective-permute-start(bf16[3072,128]{1,0:T(8,128)(2,1)} %get-tuple-element.29), channel_id=1, source_target_pairs={{0,2},{1,3},{2,0},{3,1},{4,6},{5,7},{6,4},{7,5},{8,10},{9,11},{10,... | collective-permute-start | bytes 2359304 | tf_op jit(solution)/shard_map/ppermute | solution.py:327
  34.0 23.0 %collective-permute-start.1 = (bf16[3072,128]{1,0:T(8,128)(2,1)}, bf16[3072,128]{1,0:T(8,128)(2,1)S(1)}, u32[]{:S(2)}, u32[]{:S(2)}) collective-permute-start(bf16[3072,128]{1,0:T(8,128)(2,1)} %get-tuple-element.30), channel_id=1, source_target_pairs={{0,4},{1,5},{2,6},{3,7},{4,0},{5,1},{6,2},{7,3},{8,12},{9,13},{10,... | collective-permute-start | bytes 2359304 | tf_op jit(solution)/shard_map/ppermute | solution.py:327
  34.6 36.0 %collective-permute-start.2 = (bf16[3072,128]{1,0:T(8,128)(2,1)}, bf16[3072,128]{1,0:T(8,128)(2,1)S(1)}, u32[]{:S(2)}, u32[]{:S(2)}) collective-permute-start(bf16[3072,128]{1,0:T(8,128)(2,1)} %get-tuple-element.31), channel_id=1, source_target_pairs={{0,6},{1,7},{2,4},{3,5},{4,2},{5,3},{6,0},{7,1},{8,14},{9,15},{10,... | collective-permute-start | bytes 2359304 | tf_op jit(solution)/shard_map/ppermute | solution.py:327
  55.0 32.6 %collective-permute-start.5 = (bf16[128,3968]{1,0:T(8,128)(2,1)}, bf16[128,3968]{1,0:T(8,128)(2,1)S(1)}, u32[]{:S(2)}, u32[]{:S(2)}) collective-permute-start(bf16[128,3968]{1,0:T(8,128)(2,1)} %collective-permute-done.4.refs_0_.refs_1_.refs_2_.refs_3_.refs_4_.refs_9_), channel_id=1, source_target_pairs={{8,16},{9,17},{10,18},{11,19},{12,20},{13,21},{14,22},{15,23},{16,... | collective-permute-start | bytes 3047432 | tf_op jit(solution)/shard_map/ppermute | solution.py:327
  55.7 31.9 %collective-permute-start.7 = (bf16[128,3968]{1,0:T(8,128)(2,1)}, bf16[128,3968]{1,0:T(8,128)(2,1)S(1)}, u32[]{:S(2)}, u32[]{:S(2)}) collective-permute-start(bf16[128,3968]{1,0:T(8,128)(2,1)} %collective-permute-done.6), channel_id=1, source_target_pairs={{8,0},{9,1},{10,2},{11,3},{12,4},{13,5},{14,6},{15,7},{16,24},{17,... | collective-permute-start | bytes 3047432 | tf_op jit(solution)/shard_map/ppermute | solution.py:327
  76.0 6.1 %collective-permute-start.3 = (f32[2,2,256,128]{3,2,1,0:T(8,128)S(1)}, f32[2,2,256,128]{3,2,1,0:T(8,128)S(1)}, u32[]{:S(2)}, u32[]{:S(2)}) collective-permute-start(f32[2,2,256,128]{3,2,1,0:T(8,128)S(1)} %get-tuple-element.33), channel_id=1, source_target_pairs={{0,2},{1,3},{2,0},{3,1},{4,6},{5,7},{6,4},{7,5},{8,10},{9,11},{10,... | collective-permute-start | bytes 1572872 | tf_op jit(solution)/shard_map/ppermute | solution.py:327
  82.0 2.0 collective-permute-start.11
  84.1 7.3 %collective-permute-start.14 = (f32[256,128]{1,0:T(8,128)S(1)}, f32[256,128]{1,0:T(8,128)S(1)}, u32[]{:S(2)}, u32[]{:S(2)}) collective-permute-start(f32[256,128]{1,0:T(8,128)S(1)} %get-tuple-element.60), channel_id=1, source_target_pairs={{0,5},{1,4},{2,7},{3,6},{4,1},{5,0},{6,3},{7,2},{8,13},{9,12},{10,... | collective-permute-start | bytes 393224 | tf_op jit(solution)/shard_map/ppermute | solution.py:327
  85.1 9.2 %collective-permute-start.13 = (f32[256,128]{1,0:T(8,128)S(1)}, f32[256,128]{1,0:T(8,128)S(1)}, u32[]{:S(2)}, u32[]{:S(2)}) collective-permute-start(f32[256,128]{1,0:T(8,128)S(1)} %get-tuple-element.61), channel_id=1, source_target_pairs={{0,4},{1,5},{2,6},{3,7},{4,0},{5,1},{6,2},{7,3},{8,12},{9,13},{10,... | collective-permute-start | bytes 393224 | tf_op jit(solution)/shard_map/ppermute | solution.py:327
  86.6 7.7 %collective-permute-start.12 = (f32[256,128]{1,0:T(8,128)S(1)}, f32[256,128]{1,0:T(8,128)S(1)}, u32[]{:S(2)}, u32[]{:S(2)}) collective-permute-start(f32[256,128]{1,0:T(8,128)S(1)} %get-tuple-element.59), channel_id=1, source_target_pairs={{0,1},{1,0},{2,3},{3,2},{4,5},{5,4},{6,7},{7,6},{8,9},{9,8},{10,11... | collective-permute-start | bytes 393224 | tf_op jit(solution)/shard_map/ppermute | solution.py:327
  87.6 11.2 %copy-start.5 = (bf16[128,3968]{1,0:T(8,128)(2,1)}, bf16[128,3968]{1,0:T(8,128)(2,1)S(1)}, u32[]{:S(2)}) copy-start(bf16[128,3968]{1,0:T(8,128)(2,1)S(1)} %collective-permute-done.5) | copy-start | bytes 3047428
  87.6 11.2 %copy-start.6 = (bf16[128,3968]{1,0:T(8,128)(2,1)}, bf16[128,3968]{1,0:T(8,128)(2,1)S(1)}, u32[]{:S(2)}) copy-start(bf16[128,3968]{1,0:T(8,128)(2,1)S(1)} %collective-permute-done.7) | copy-start | bytes 3047428
  87.7 9.4 %collective-permute-start.10 = (f32[256,128]{1,0:T(8,128)S(1)}, f32[256,128]{1,0:T(8,128)S(1)}, u32[]{:S(2)}, u32[]{:S(2)}) collective-permute-start(f32[256,128]{1,0:T(8,128)S(1)} %get-tuple-element.63), channel_id=1, source_target_pairs={{0,5},{1,4},{2,7},{3,6},{4,1},{5,0},{6,3},{7,2},{8,13},{9,12},{10,... | collective-permute-start | bytes 393224 | tf_op jit(solution)/shard_map/ppermute | solution.py:327
  88.7 10.1 %collective-permute-start.9 = (f32[256,128]{1,0:T(8,128)S(1)}, f32[256,128]{1,0:T(8,128)S(1)}, u32[]{:S(2)}, u32[]{:S(2)}) collective-permute-start(f32[256,128]{1,0:T(8,128)S(1)} %get-tuple-element.64), channel_id=1, source_target_pairs={{0,4},{1,5},{2,6},{3,7},{4,0},{5,1},{6,2},{7,3},{8,12},{9,13},{10,... | collective-permute-start | bytes 393224 | tf_op jit(solution)/shard_map/ppermute | solution.py:327
  91.4 7.4 %collective-permute-start.8 = (f32[256,128]{1,0:T(8,128)S(1)}, f32[256,128]{1,0:T(8,128)S(1)}, u32[]{:S(2)}, u32[]{:S(2)}) collective-permute-start(f32[256,128]{1,0:T(8,128)S(1)} %get-tuple-element.62), channel_id=1, source_target_pairs={{0,1},{1,0},{2,3},{3,2},{4,5},{5,4},{6,7},{7,6},{8,9},{9,8},{10,11... | collective-permute-start | bytes 393224 | tf_op jit(solution)/shard_map/ppermute | solution.py:327
  98.9 8.8 %copy-start.8 = (bf16[2,256,128]{2,1,0:T(8,128)(2,1)}, bf16[2,256,128]{2,1,0:T(8,128)(2,1)S(1)}, u32[]{:S(2)}) copy-start(bf16[2,256,128]{2,1,0:T(8,128)(2,1)S(1)} %pad_maximum_fusion.1) | copy-start | bytes 393220
  98.9 2.0 collective-permute-start.21
  99.6 33.9 %collective-permute-start.19 = (bf16[128,3968]{1,0:T(8,128)(2,1)}, bf16[128,3968]{1,0:T(8,128)(2,1)}, u32[]{:S(2)}, u32[]{:S(2)}) collective-permute-start(bf16[128,3968]{1,0:T(8,128)(2,1)} %copy-done.5), channel_id=1, source_target_pairs={{8,0},{9,1},{10,2},{11,3},{12,4},{13,5},{14,6},{15,7},{16,24},{17,... | collective-permute-start | bytes 3047432 | tf_op jit(solution)/shard_map/ppermute | solution.py:327
  100.9 0.7 copy-start.7
  102.9 4.8 %copy-start = (bf16[128,3968]{1,0:T(8,128)(2,1)}, bf16[128,3968]{1,0:T(8,128)(2,1)S(1)}, u32[]{:S(2)}) copy-start(bf16[128,3968]{1,0:T(8,128)(2,1)S(1)} %broadcast_select_fusion.1.refs_0_.refs_1_.refs_2_.refs_3_.refs_4_.refs_10_) | copy-start | bytes 3047428
  107.7 2.0 collective-permute-start.15
  134.8 4.8 %copy-start.2 = (bf16[128,3968]{1,0:T(8,128)(2,1)}, bf16[128,3968]{1,0:T(8,128)(2,1)S(1)}, u32[]{:S(2)}) copy-start(bf16[128,3968]{1,0:T(8,128)(2,1)S(1)} %broadcast_select_fusion.refs_0_.refs_1_.refs_2_.refs_3_.refs_4_.refs_11_) | copy-start | bytes 3047428
  134.8 8.6 %copy-start.9 = (bf16[2,256,128]{2,1,0:T(8,128)(2,1)S(1)}, bf16[2,256,128]{2,1,0:T(8,128)(2,1)}, u32[]{:S(2)}) copy-start(bf16[2,256,128]{2,1,0:T(8,128)(2,1)} %copy-done.8) | copy-start | bytes 393220
  139.6 53.4 %copy-start.1 = (bf16[128,3968]{1,0:T(8,128)(2,1)S(1)}, bf16[128,3968]{1,0:T(8,128)(2,1)}, u32[]{:S(2)}) copy-start(bf16[128,3968]{1,0:T(8,128)(2,1)} %copy-done) | copy-start | bytes 3047428
  139.6 53.4 %copy-start.3 = (bf16[128,3968]{1,0:T(8,128)(2,1)S(1)}, bf16[128,3968]{1,0:T(8,128)(2,1)}, u32[]{:S(2)}) copy-start(bf16[128,3968]{1,0:T(8,128)(2,1)} %copy-done.2) | copy-start | bytes 3047428
  139.6 12.1 %collective-permute-start.22 = (f32[2,2,256,128]{3,2,1,0:T(8,128)S(1)}, f32[2,2,256,128]{3,2,1,0:T(8,128)S(1)}, u32[]{:S(2)}, u32[]{:S(2)}) collective-permute-start(f32[2,2,256,128]{3,2,1,0:T(8,128)S(1)} %get-tuple-element.41), channel_id=1, source_target_pairs={{0,2},{1,3},{2,0},{3,1},{4,6},{5,7},{6,4},{7,5},{8,10},{9,11},{10,... | collective-permute-start | bytes 1572872 | tf_op jit(solution)/shard_map/ppermute | solution.py:327
  139.7 7.1 %collective-permute-start.18 = (f32[256,128]{1,0:T(8,128)S(1)}, f32[256,128]{1,0:T(8,128)S(1)}, u32[]{:S(2)}, u32[]{:S(2)}) collective-permute-start(f32[256,128]{1,0:T(8,128)S(1)} %get-tuple-element.57), channel_id=1, source_target_pairs={{0,5},{1,4},{2,7},{3,6},{4,1},{5,0},{6,3},{7,2},{8,13},{9,12},{10,... | collective-permute-start | bytes 393224 | tf_op jit(solution)/shard_map/ppermute | solution.py:327
  142.3 7.1 %collective-permute-start.17 = (f32[256,128]{1,0:T(8,128)S(1)}, f32[256,128]{1,0:T(8,128)S(1)}, u32[]{:S(2)}, u32[]{:S(2)}) collective-permute-start(f32[256,128]{1,0:T(8,128)S(1)} %get-tuple-element.58), channel_id=1, source_target_pairs={{0,4},{1,5},{2,6},{3,7},{4,0},{5,1},{6,2},{7,3},{8,12},{9,13},{10,... | collective-permute-start | bytes 393224 | tf_op jit(solution)/shard_map/ppermute | solution.py:327
  143.4 6.4 %collective-permute-start.16 = (f32[256,128]{1,0:T(8,128)S(1)}, f32[256,128]{1,0:T(8,128)S(1)}, u32[]{:S(2)}, u32[]{:S(2)}) collective-permute-start(f32[256,128]{1,0:T(8,128)S(1)} %get-tuple-element.56), channel_id=1, source_target_pairs={{0,1},{1,0},{2,3},{3,2},{4,5},{5,4},{6,7},{7,6},{8,9},{9,8},{10,11... | collective-permute-start | bytes 393224 | tf_op jit(solution)/shard_map/ppermute | solution.py:327
  143.4 8.3 %collective-permute-start.20 = (bf16[2,256,128]{2,1,0:T(8,128)(2,1)S(1)}, bf16[2,256,128]{2,1,0:T(8,128)(2,1)S(1)}, u32[]{:S(2)}, u32[]{:S(2)}) collective-permute-start(bf16[2,256,128]{2,1,0:T(8,128)(2,1)S(1)} %copy-done.9), channel_id=1, source_target_pairs={{0,1},{1,0},{2,3},{3,2},{4,5},{5,4},{6,7},{7,6},{8,9},{9,8},{10,11... | collective-permute-start | bytes 393224 | tf_op jit(solution)/shard_map/ppermute | solution.py:327
  151.8 6.7 %collective-permute-start.25 = (f32[256,128]{1,0:T(8,128)S(1)}, f32[256,128]{1,0:T(8,128)S(1)}, u32[]{:S(2)}, u32[]{:S(2)}) collective-permute-start(f32[256,128]{1,0:T(8,128)S(1)} %get-tuple-element.54), channel_id=1, source_target_pairs={{0,5},{1,4},{2,7},{3,6},{4,1},{5,0},{6,3},{7,2},{8,13},{9,12},{10,... | collective-permute-start | bytes 393224 | tf_op jit(solution)/shard_map/ppermute | solution.py:327
  154.6 6.3 %collective-permute-start.24 = (f32[256,128]{1,0:T(8,128)S(1)}, f32[256,128]{1,0:T(8,128)S(1)}, u32[]{:S(2)}, u32[]{:S(2)}) collective-permute-start(f32[256,128]{1,0:T(8,128)S(1)} %get-tuple-element.55), channel_id=1, source_target_pairs={{0,4},{1,5},{2,6},{3,7},{4,0},{5,1},{6,2},{7,3},{8,12},{9,13},{10,... | collective-permute-start | bytes 393224 | tf_op jit(solution)/shard_map/ppermute | solution.py:327
  155.5 5.4 %collective-permute-start.23 = (f32[256,128]{1,0:T(8,128)S(1)}, f32[256,128]{1,0:T(8,128)S(1)}, u32[]{:S(2)}, u32[]{:S(2)}) collective-permute-start(f32[256,128]{1,0:T(8,128)S(1)} %get-tuple-element.53), channel_id=1, source_target_pairs={{0,1},{1,0},{2,3},{3,2},{4,5},{5,4},{6,7},{7,6},{8,9},{9,8},{10,11... | collective-permute-start | bytes 393224 | tf_op jit(solution)/shard_map/ppermute | solution.py:327
  160.9 10.5 %collective-permute-start.26 = (bf16[2,256,128]{2,1,0:T(8,128)(2,1)S(1)}, bf16[2,256,128]{2,1,0:T(8,128)(2,1)S(1)}, u32[]{:S(2)}, u32[]{:S(2)}) collective-permute-start(bf16[2,256,128]{2,1,0:T(8,128)(2,1)S(1)} %pad_maximum_fusion.2), channel_id=1, source_target_pairs={{0,0},{1,16},{2,2},{3,18},{4,4},{5,20},{6,6},{7,22},{8,8},{9,24},{... | collective-permute-start | bytes 393224 | tf_op jit(solution)/shard_map/ppermute | solution.py:327
  161.6 9.8 %collective-permute-start.27 = (bf16[2,256,128]{2,1,0:T(8,128)(2,1)S(1)}, bf16[2,256,128]{2,1,0:T(8,128)(2,1)S(1)}, u32[]{:S(2)}, u32[]{:S(2)}) collective-permute-start(bf16[2,256,128]{2,1,0:T(8,128)(2,1)S(1)} %pad_maximum_fusion.2), channel_id=1, source_target_pairs={{0,8},{1,24},{2,10},{3,26},{4,12},{5,28},{6,14},{7,30},{8,0},{9,16... | collective-permute-start | bytes 393224 | tf_op jit(solution)/shard_map/ppermute | solution.py:327
  161.7 10.6 %collective-permute-start.28 = (bf16[2,256,128]{2,1,0:T(8,128)(2,1)S(1)}, bf16[2,256,128]{2,1,0:T(8,128)(2,1)S(1)}, u32[]{:S(2)}, u32[]{:S(2)}) collective-permute-start(bf16[2,256,128]{2,1,0:T(8,128)(2,1)S(1)} %pad_maximum_fusion.2), channel_id=1, source_target_pairs={{0,16},{1,0},{2,18},{3,2},{4,20},{5,4},{6,22},{7,6},{8,24},{9,8},{... | collective-permute-start | bytes 393224 | tf_op jit(solution)/shard_map/ppermute | solution.py:327
  169.4 9.6 %collective-permute-start.29 = (bf16[2,256,128]{2,1,0:T(8,128)(2,1)S(1)}, bf16[2,256,128]{2,1,0:T(8,128)(2,1)S(1)}, u32[]{:S(2)}, u32[]{:S(2)}) collective-permute-start(bf16[2,256,128]{2,1,0:T(8,128)(2,1)S(1)} %pad_maximum_fusion.2), channel_id=1, source_target_pairs={{0,24},{1,8},{2,26},{3,10},{4,28},{5,12},{6,30},{7,14},{8,16},{9,0... | collective-permute-start | bytes 393224 | tf_op jit(solution)/shard_map/ppermute | solution.py:327
  169.4 9.6 %collective-permute-start.30 = (bf16[2,256,128]{2,1,0:T(8,128)(2,1)S(1)}, bf16[2,256,128]{2,1,0:T(8,128)(2,1)S(1)}, u32[]{:S(2)}, u32[]{:S(2)}) collective-permute-start(bf16[2,256,128]{2,1,0:T(8,128)(2,1)S(1)} %pad_maximum_fusion.2), channel_id=1, source_target_pairs={{0,1},{1,0},{2,3},{3,2},{4,5},{5,4},{6,7},{7,6},{8,9},{9,8},{10,11... | collective-permute-start | bytes 393224 | tf_op jit(solution)/shard_map/ppermute | solution.py:327
  179.0 0.7 copy-start.10
  179.7 11.2 %collective-permute-start.31 = (bf16[4,2,256,128]{3,2,1,0:T(8,128)(2,1)S(1)}, bf16[4,2,256,128]{3,2,1,0:T(8,128)(2,1)S(1)}, u32[]{:S(2)}, u32[]{:S(2)}) collective-permute-start(bf16[4,2,256,128]{3,2,1,0:T(8,128)(2,1)S(1)} %pad_maximum_fusion.refs_16_.refs_20_), channel_id=1, source_target_pairs={{0,4},{1,5},{2,6},{3,7},{4,0},{5,1},{6,2},{7,3},{8,12},{9,13},{10,... | collective-permute-start | bytes 1572872 | tf_op jit(solution)/shard_map/ppermute | solution.py:327
  181.2 10.8 %collective-permute-start.32 = (bf16[4,2,256,128]{3,2,1,0:T(8,128)(2,1)S(1)}, bf16[4,2,256,128]{3,2,1,0:T(8,128)(2,1)}, u32[]{:S(2)}, u32[]{:S(2)}) collective-permute-start(bf16[4,2,256,128]{3,2,1,0:T(8,128)(2,1)S(1)} %pad_maximum_fusion.refs_16_.refs_20_), channel_id=1, source_target_pairs={{0,2},{1,3},{2,0},{3,1},{4,6},{5,7},{6,4},{7,5},{8,10},{9,11},{10,... | collective-permute-start | bytes 1572872 | tf_op jit(solution)/shard_map/ppermute | solution.py:327
  191.0 2.0 collective-permute-start.33
  193.0 1.6 copy-start.4
Sparse Core Ops, SparseCore 0:
  101.7 53.3 all-gather.2

commit v12 on v11

--- a/solution.py
+++ b/solution.py
@@ -371,12 +371,13 @@
     def share(own, m):
         return send(own, lambda i, j, k, t: ((2 * t + i % 2) ^ m, j, k, i // 2))
 
-    owns = [coefficients(units[0], (across, outward)), coefficients(units[1])]
+    units[1], _ = lax.optimization_barrier((units[1], (across, outward)))
+    owns = [coefficients(units[0]), coefficients(units[1])]
     own_a = jnp.stack(owns)
     share_a = share(own_a, 0)
     mate_a = mate(own_a)
     right_a = lax.all_gather(share_a, ("z", "y", "c"), axis=0)
-    owns.append(coefficients(units[2], None, (far, mate_a, share_a)))
+    owns.append(coefficients(units[2], (far, mate_a, share_a)))
     units.append(jnp.where(inner, middle, far))
     owns.append(coefficients(units[3], owns[2]))
     own_b = jnp.stack(owns[2:])

time: 210 us -> 213 us (1.014)
  starting transfers between devices: 43.9 us -> 53.2 us
  waiting for transfers between devices: 109 us -> 104 us
    ppermute x34, starting transfers between devices: 38.7 us -> 48 us  [send(): lax.ppermute(array, AXES, [(source, number[to]) for source, to in pairs i...]
    ppermute x34, waiting for transfers between devices: 97.6 us -> 92.3 us  [send(): lax.ppermute(array, AXES, [(source, number[to]) for source, to in pairs i...]
  transfers between devices with their start and end apart: 36 -> 36, of which waited for: 20 -> 21; matrix products, arithmetic and copies ran while one was open for 4% -> 4% of each run, Pallas kernels for 10% -> 10%
where the time goes in v12:
time: 213 us; the launch traced here: 211 us
  waiting for transfers between devices  104 us (49%)
  starting transfers between devices  53.2 us (25%)
  Pallas kernels  31 us (15%)
  between operations  13.8 us (6%)
  local copies, waits for them, and re-layouts  6.72 us (3%)
  other arithmetic  3.23 us (2%)
    ppermute x34, waiting for transfers between devices, send(): lax.ppermute(array, AXES, [(source, number[to]) for source, to in pairs i...  92.3 us
    ppermute x34, starting transfers between devices, send(): lax.ppermute(array, AXES, [(source, number[to]) for source, to in pairs i...  48 us
    pallas_call x4, Pallas kernels, project(): pl.pallas_call(functools.partial(project_kernel, segs, val_count, cond_co...  20.3 us
    all_to_all x1, waiting for transfers between devices, local(): unit = lax.all_to_all(packed, ('y', 'c', 'x'), 0, 0, tiled=True)  11.2 us
    pallas_call x1, Pallas kernels, make_chi(): pl.pallas_call(functools.partial(chi_kernel, early, late, n_freq, factor)...  6.75 us
    all_to_all x1, starting transfers between devices, local(): unit = lax.all_to_all(packed, ('y', 'c', 'x'), 0, 0, tiled=True)  5.17 us
  transfers between devices with their start and end apart: 36, of which 21 were waited for; matrix products, arithmetic and copies ran while one was open for 4% of the time, Pallas kernels for 10%

profile of v12, /device:TPU:0, one launch (start us, length us, event | category | flops | bytes accessed | tf_op | source)
XLA Modules:
  0.0 211.5 jit_solution(16470745918703215912)
XLA Ops:
  6.5 4.0 %pack.1 = bf16[8,16,3968]{2,1,0:T(8,128)(2,1)} custom-call(f32[4]{0:T(128)} %val_energy.1, f32[16]{0:T(128)} %cond_energy.1, s32[64]{0:T(128)} %val_slot.1, s32[64]{0:T(128)} %cond_slot.1, f32[4]{0:T(128)} %frequencies.1, bf16[16,24576]{1,0:T(8,128)(2,1)} %refs_1_.1, bf16[16,24576]{1,0:T(8,128)(2,1)} %refs_1_.1, bf16[4,24576]{1,0:T(4,128)(2,1)} %refs_3_.1, ...), custom_call_target="tpu_custom_call" | custom-call | tf_op jit(solution)/shard_map/pack/pallas_call | solution.py:77
  10.5 5.2 %all-to-all-start = ((bf16[8,16,3968]{2,1,0:T(8,128)(2,1)}), bf16[8,16,3968]{2,1,0:T(8,128)(2,1)}, u32[]{:S(2)}, u32[]{:S(2)}) async-start(bf16[8,16,3968]{2,1,0:T(8,128)(2,1)} %pack.1), calls=%async_computation | async-start | bytes 2031616 | tf_op jit(solution)/shard_map/all_to_all | solution.py:481
  15.8 3.4 %constant_dynamic-slice_fusion = (bf16[3072,128]{1,0:T(8,128)(2,1)}, bf16[3072,128]{1,0:T(8,128)(2,1)}, bf16[3072,128]{1,0:T(8,128)(2,1)S(1)}, bf16[3072,128]{1,0:T(8,128)(2,1)}) fusion(bf16[12288,128]{1,0:T(8,128)(2,1)} %param.14, s32[]{:T(128)S(6)} %select_n.27, s32[]{:T(128)S(6)} %select_n.25, s32[]{:T(128)S(6)} %select_n.24, s32[]{:T(128)S(6)} %select_n.26), kind=kLoop, calls=%fused_computation.39 | loop fusion | bytes 6291472 | tf_op jit(solution)/shard_map/dynamic_slice | solution.py:337
  19.1 11.2 %all-to-all-done = bf16[8,16,3968]{2,1,0:T(8,128)(2,1)} async-done(((bf16[8,16,3968]{2,1,0:T(8,128)(2,1)}), bf16[8,16,3968]{2,1,0:T(8,128)(2,1)}, u32[]{:S(2)}, u32[]{:S(2)}) %all-to-all-start) | async-done | bytes 1015840 | tf_op jit(solution)/shard_map/all_to_all | solution.py:481
  30.4 2.0 collective-permute-start.7
  32.4 1.6 collective-permute-start.9
  34.6 1.3 collective-permute-start.2
  35.9 19.1 %collective-permute-done.7.refs_0_.refs_1_.refs_2_.refs_3_.refs_4_.refs_9_ = bf16[128,3968]{1,0:T(8,128)(2,1)} collective-permute-done((bf16[128,3968]{1,0:T(8,128)(2,1)}, bf16[128,3968]{1,0:T(8,128)(2,1)}, u32[]{:S(2)}, u32[]{:S(2)}) %collective-permute-start.7) | collective-permute-done | bytes 1015840 | tf_op jit(solution)/shard_map/ppermute | solution.py:327
  55.0 1.6 collective-permute-start.8
  56.6 1.3 collective-permute-start.10
  57.9 12.7 %collective-permute-done.2.refs_8_.refs_12_.refs_16_.refs_20_ = bf16[3072,128]{1,0:T(8,128)(2,1)S(1)} collective-permute-done((bf16[3072,128]{1,0:T(8,128)(2,1)}, bf16[3072,128]{1,0:T(8,128)(2,1)S(1)}, u32[]{:S(2)}, u32[]{:S(2)}) %collective-permute-start.2) | collective-permute-done | bytes 786464 | tf_op jit(solution)/shard_map/ppermute | solution.py:327
  70.7 5.4 %project.4 = (f32[2,2,256,128]{3,2,1,0:T(8,128)S(1)}, f32[2,2,256,128]{3,2,1,0:T(8,128)S(1)}) custom-call(s32[1]{0:T(128)} %bitcast.4.place, bf16[128,3968]{1,0:T(8,128)(2,1)} %bitcast.5.refs_0_.refs_1_.refs_2_.refs_3_.refs_4_.refs_8_, bf16[128,3968]{1,0:T(8,128)(2,1)} %bitcast.5.refs_0_.refs_1_.refs_2_.refs_3_.refs_4_.refs_8_, ...), custom_call_target="tpu_custom_call" | custom-call | flops 1610612736 | bytes 4161536 | tf_op jit(solution)/shard_map/project/pallas_call | solution.py:187
  76.7 6.2 %collective-permute-done.10 = bf16[128,3968]{1,0:T(8,128)(2,1)} collective-permute-done((bf16[128,3968]{1,0:T(8,128)(2,1)}, bf16[128,3968]{1,0:T(8,128)(2,1)}, u32[]{:S(2)}, u32[]{:S(2)}) %collective-permute-start.10) | collective-permute-done | bytes 1015840 | tf_op jit(solution)/shard_map/ppermute | solution.py:327
  82.9 5.4 %project.5 = (f32[2,2,256,128]{3,2,1,0:T(8,128)S(1)}, f32[2,2,256,128]{3,2,1,0:T(8,128)S(1)}) custom-call(s32[1]{0:T(128)} %bitcast.4.place, bf16[128,3968]{1,0:T(8,128)(2,1)} %collective-permute-done.7.refs_0_.refs_1_.refs_2_.refs_3_.refs_4_.refs_9_, bf16[128,3968]{1,0:T(8,128)(2,1)} %collective-permute-done.7.refs_0_.refs_1_.refs_2_.refs_3_.refs_4_.refs_9_, ...), custom_call_target="tpu_custom_call" | custom-call | flops 1610612736 | bytes 4161536 | tf_op jit(solution)/shard_map/project/pallas_call | solution.py:187
  88.5 1.3 collective-permute-start.6
  89.9 1.1 collective-permute-start.5
  91.0 1.1 collective-permute-start.4
  92.2 1.4 collective-permute-start.14
  93.7 1.0 collective-permute-start.13
  94.7 1.1 collective-permute-done.6
  96.6 2.0 collective-permute-done.5
  99.1 2.4 %collective-permute-done.14 = f32[256,128]{1,0:T(8,128)S(1)} collective-permute-done((f32[256,128]{1,0:T(8,128)S(1)}, f32[256,128]{1,0:T(8,128)S(1)}, u32[]{:S(2)}, u32[]{:S(2)}) %collective-permute-start.14) | collective-permute-done | bytes 131104 | tf_op jit(solution)/shard_map/ppermute | solution.py:327
  101.5 2.3 %collective-permute-done.13 = f32[256,128]{1,0:T(8,128)S(1)} collective-permute-done((f32[256,128]{1,0:T(8,128)S(1)}, f32[256,128]{1,0:T(8,128)S(1)}, u32[]{:S(2)}, u32[]{:S(2)}) %collective-permute-start.13) | collective-permute-done | bytes 131104 | tf_op jit(solution)/shard_map/ppermute | solution.py:327
  105.1 1.3 collective-permute-start.16
  107.1 1.3 broadcast_select_fusion.1.refs_0_.refs_1_.refs_2_.refs_3_.refs_4_.refs_10_
  108.5 4.8 %project.6 = (f32[2,2,256,128]{3,2,1,0:T(8,128)S(1)}, f32[2,2,256,128]{3,2,1,0:T(8,128)S(1)}) custom-call(s32[1]{0:T(128)} %bitcast.4.place, bf16[128,3968]{1,0:T(8,128)(2,1)S(1)} %broadcast_select_fusion.1.refs_0_.refs_1_.refs_2_.refs_3_.refs_4_.refs_10_, bf16[128,3968]{1,0:T(8,128)(2,1)S(1)} %broadcast_select_fusion.1.refs_0_.refs_1_.refs_2_.refs_3_.refs_4_.refs_10_, ...), custom_call_target="tpu_custom_call" | custom-call | flops 1610612736 | bytes 4161536 | tf_op jit(solution)/shard_map/project/pallas_call | solution.py:187
  113.3 10.5 %collective-permute-start.17 = (bf16[2,256,128]{2,1,0:T(8,128)(2,1)}, bf16[2,256,128]{2,1,0:T(8,128)(2,1)S(1)}, u32[]{:S(2)}, u32[]{:S(2)}) collective-permute-start(bf16[2,256,128]{2,1,0:T(8,128)(2,1)} %copy-done.6), channel_id=1, source_target_pairs={{0,1},{1,0},{2,3},{3,2},{4,5},{5,4},{6,7},{7,6},{8,9},{9,8},{10,11... | collective-permute-start | bytes 393224 | tf_op jit(solution)/shard_map/ppermute | solution.py:327
  123.9 4.2 %collective-permute-done.17 = bf16[2,256,128]{2,1,0:T(8,128)(2,1)S(1)} collective-permute-done((bf16[2,256,128]{2,1,0:T(8,128)(2,1)}, bf16[2,256,128]{2,1,0:T(8,128)(2,1)S(1)}, u32[]{:S(2)}, u32[]{:S(2)}) %collective-permute-start.17) | collective-permute-done | bytes 131104 | tf_op jit(solution)/shard_map/ppermute | solution.py:327
  128.1 10.3 %collective-permute-done.16 = bf16[128,3968]{1,0:T(8,128)(2,1)} collective-permute-done((bf16[128,3968]{1,0:T(8,128)(2,1)}, bf16[128,3968]{1,0:T(8,128)(2,1)}, u32[]{:S(2)}, u32[]{:S(2)}) %collective-permute-start.16) | collective-permute-done | bytes 1015840 | tf_op jit(solution)/shard_map/ppermute | solution.py:327
  138.4 1.3 broadcast_select_fusion.refs_0_.refs_1_.refs_2_.refs_3_.refs_4_.refs_11_
  139.8 4.8 %project.7 = (f32[2,2,256,128]{3,2,1,0:T(8,128)S(1)}, f32[2,2,256,128]{3,2,1,0:T(8,128)S(1)}) custom-call(s32[1]{0:T(128)} %bitcast.4.place, bf16[128,3968]{1,0:T(8,128)(2,1)S(1)} %broadcast_select_fusion.refs_0_.refs_1_.refs_2_.refs_3_.refs_4_.refs_11_, bf16[128,3968]{1,0:T(8,128)(2,1)S(1)} %broadcast_select_fusion.refs_0_.refs_1_.refs_2_.refs_3_.refs_4_.refs_11_, ...), custom_call_target="tpu_custom_call" | custom-call | flops 1610612736 | bytes 4161536 | tf_op jit(solution)/shard_map/project/pallas_call | solution.py:187
  145.2 1.7 collective-permute-start.20
  146.8 1.4 collective-permute-start.19
  148.2 3.7 %collective-permute-done.21 = f32[256,128]{1,0:T(8,128)S(1)} collective-permute-done((f32[256,128]{1,0:T(8,128)S(1)}, f32[256,128]{1,0:T(8,128)S(1)}, u32[]{:S(2)}, u32[]{:S(2)}) %collective-permute-start.21) | collective-permute-done | bytes 131104 | tf_op jit(solution)/shard_map/ppermute | solution.py:327
  152.0 1.6 collective-permute-done.20
  153.8 1.5 collective-permute-start.25
  155.2 1.4 collective-permute-start.24
  157.3 3.5 %collective-permute-done.25 = f32[256,128]{1,0:T(8,128)S(1)} collective-permute-done((f32[256,128]{1,0:T(8,128)S(1)}, f32[256,128]{1,0:T(8,128)S(1)}, u32[]{:S(2)}, u32[]{:S(2)}) %collective-permute-start.25) | collective-permute-done | bytes 131104 | tf_op jit(solution)/shard_map/ppermute | solution.py:327
  160.8 1.6 collective-permute-done.24
  163.5 1.3 collective-permute-start.27
  164.8 6.3 %collective-permute-start.28 = (bf16[2,256,128]{2,1,0:T(8,128)(2,1)S(1)}, bf16[2,256,128]{2,1,0:T(8,128)(2,1)S(1)}, u32[]{:S(2)}, u32[]{:S(2)}) collective-permute-start(bf16[2,256,128]{2,1,0:T(8,128)(2,1)S(1)} %pad_maximum_fusion.2), channel_id=1, source_target_pairs={{0,16},{1,0},{2,18},{3,2},{4,20},{5,4},{6,22},{7,6},{8,24},{9,8},{... | collective-permute-start | bytes 393224 | tf_op jit(solution)/shard_map/ppermute | solution.py:327
  171.9 2.0 collective-permute-start.30
  174.9 6.7 %collective-permute-done.29 = bf16[2,256,128]{2,1,0:T(8,128)(2,1)S(1)} collective-permute-done((bf16[2,256,128]{2,1,0:T(8,128)(2,1)S(1)}, bf16[2,256,128]{2,1,0:T(8,128)(2,1)S(1)}, u32[]{:S(2)}, u32[]{:S(2)}) %collective-permute-start.29) | collective-permute-done | bytes 131104 | tf_op jit(solution)/shard_map/ppermute | solution.py:327
  181.7 1.2 collective-permute-start.31
  182.9 11.4 %collective-permute-done.31.refs_17_.refs_21_ = bf16[4,2,256,128]{3,2,1,0:T(8,128)(2,1)S(1)} collective-permute-done((bf16[4,2,256,128]{3,2,1,0:T(8,128)(2,1)S(1)}, bf16[4,2,256,128]{3,2,1,0:T(8,128)(2,1)S(1)}, u32[]{:S(2)}, u32[]{:S(2)}) %collective-permute-start.31) | collective-permute-done | bytes 524320 | tf_op jit(solution)/shard_map/ppermute | solution.py:327
  195.2 1.0 collective-permute-done.33.refs_19_.refs_23_
  196.3 1.6 copy-done.4
  197.9 6.8 %chi.1 = f32[128,4,1024]{2,1,0:T(4,128)} custom-call(s32[5]{0:T(128)S(1)} %stack.56.scalars, bf16[256,128]{1,0:T(8,128)(2,1)S(1)} %fusion.7.refs_0_, bf16[256,128]{1,0:T(8,128)(2,1)S(1)} %fusion.3.refs_1_, bf16[256,128]{1,0:T(8,128)(2,1)S(1)} %fusion.13.refs_2_, bf16[256,128]{1,0:T(8,128)(2,1)S(1)} %fusion.10.refs_3_, ...), custom_call_target="tpu_custom_call" | custom-call | flops 2147483648 | bytes 6291456 | tf_op jit(solution)/shard_map/chi/pallas_call | solution.py:281
  (66 shorter events, 10.3 us)
Async XLA Ops:
  10.5 19.9 %all-to-all-start = ((bf16[8,16,3968]{2,1,0:T(8,128)(2,1)}), bf16[8,16,3968]{2,1,0:T(8,128)(2,1)}, u32[]{:S(2)}, u32[]{:S(2)}) async-start(bf16[8,16,3968]{2,1,0:T(8,128)(2,1)} %pack.1), calls=%async_computation | async-start | bytes 2031616 | tf_op jit(solution)/shard_map/all_to_all | solution.py:481
  15.7 165.9 %all-gather.3.cloned.1.call-start = ((), (), s32[]{:S(2)}) async-start(), calls=%async_computation.1 | async-start | bytes 2228224 | tf_op jit(solution)/shard_map/all_gather | solution.py:379
  30.4 24.6 %collective-permute-start.7 = (bf16[128,3968]{1,0:T(8,128)(2,1)}, bf16[128,3968]{1,0:T(8,128)(2,1)}, u32[]{:S(2)}, u32[]{:S(2)}) collective-permute-start(bf16[128,3968]{1,0:T(8,128)(2,1)} %bitcast.5.refs_0_.refs_1_.refs_2_.refs_3_.refs_4_.refs_8_), channel_id=1, source_target_pairs={{0,8},{1,9},{2,10},{3,11},{4,12},{5,13},{6,14},{7,15},{8,0},{9,1},... | collective-permute-start | bytes 3047432 | tf_op jit(solution)/shard_map/ppermute | solution.py:327
  32.4 24.2 %collective-permute-start.9 = (bf16[128,3968]{1,0:T(8,128)(2,1)}, bf16[128,3968]{1,0:T(8,128)(2,1)}, u32[]{:S(2)}, u32[]{:S(2)}) collective-permute-start(bf16[128,3968]{1,0:T(8,128)(2,1)} %bitcast.5.refs_0_.refs_1_.refs_2_.refs_3_.refs_4_.refs_8_), channel_id=1, source_target_pairs={{8,16},{9,17},{10,18},{11,19},{12,20},{13,21},{14,22},{15,23},{16,... | collective-permute-start | bytes 3047432 | tf_op jit(solution)/shard_map/ppermute | solution.py:327
  34.0 23.9 %collective-permute-start = (bf16[3072,128]{1,0:T(8,128)(2,1)}, bf16[3072,128]{1,0:T(8,128)(2,1)S(1)}, u32[]{:S(2)}, u32[]{:S(2)}) collective-permute-start(bf16[3072,128]{1,0:T(8,128)(2,1)} %get-tuple-element.29), channel_id=1, source_target_pairs={{0,2},{1,3},{2,0},{3,1},{4,6},{5,7},{6,4},{7,5},{8,10},{9,11},{10,... | collective-permute-start | bytes 2359304 | tf_op jit(solution)/shard_map/ppermute | solution.py:327
  34.0 23.9 %collective-permute-start.1 = (bf16[3072,128]{1,0:T(8,128)(2,1)}, bf16[3072,128]{1,0:T(8,128)(2,1)S(1)}, u32[]{:S(2)}, u32[]{:S(2)}) collective-permute-start(bf16[3072,128]{1,0:T(8,128)(2,1)} %get-tuple-element.30), channel_id=1, source_target_pairs={{0,4},{1,5},{2,6},{3,7},{4,0},{5,1},{6,2},{7,3},{8,12},{9,13},{10,... | collective-permute-start | bytes 2359304 | tf_op jit(solution)/shard_map/ppermute | solution.py:327
  34.6 36.0 %collective-permute-start.2 = (bf16[3072,128]{1,0:T(8,128)(2,1)}, bf16[3072,128]{1,0:T(8,128)(2,1)S(1)}, u32[]{:S(2)}, u32[]{:S(2)}) collective-permute-start(bf16[3072,128]{1,0:T(8,128)(2,1)} %get-tuple-element.31), channel_id=1, source_target_pairs={{0,6},{1,7},{2,4},{3,5},{4,2},{5,3},{6,0},{7,1},{8,14},{9,15},{10,... | collective-permute-start | bytes 2359304 | tf_op jit(solution)/shard_map/ppermute | solution.py:327
  55.0 21.7 %collective-permute-start.8 = (bf16[128,3968]{1,0:T(8,128)(2,1)}, bf16[128,3968]{1,0:T(8,128)(2,1)}, u32[]{:S(2)}, u32[]{:S(2)}) collective-permute-start(bf16[128,3968]{1,0:T(8,128)(2,1)} %collective-permute-done.7.refs_0_.refs_1_.refs_2_.refs_3_.refs_4_.refs_9_), channel_id=1, source_target_pairs={{8,16},{9,17},{10,18},{11,19},{12,20},{13,21},{14,22},{15,23},{16,... | collective-permute-start | bytes 3047432 | tf_op jit(solution)/shard_map/ppermute | solution.py:327
  56.6 26.3 %collective-permute-start.10 = (bf16[128,3968]{1,0:T(8,128)(2,1)}, bf16[128,3968]{1,0:T(8,128)(2,1)}, u32[]{:S(2)}, u32[]{:S(2)}) collective-permute-start(bf16[128,3968]{1,0:T(8,128)(2,1)} %collective-permute-done.9), channel_id=1, source_target_pairs={{8,0},{9,1},{10,2},{11,3},{12,4},{13,5},{14,6},{15,7},{16,24},{17,... | collective-permute-start | bytes 3047432 | tf_op jit(solution)/shard_map/ppermute | solution.py:327
  76.0 12.4 %collective-permute-start.3 = (f32[2,2,256,128]{3,2,1,0:T(8,128)S(1)}, f32[2,2,256,128]{3,2,1,0:T(8,128)S(1)}, u32[]{:S(2)}, u32[]{:S(2)}) collective-permute-start(f32[2,2,256,128]{3,2,1,0:T(8,128)S(1)} %get-tuple-element.33), channel_id=1, source_target_pairs={{0,2},{1,3},{2,0},{3,1},{4,6},{5,7},{6,4},{7,5},{8,10},{9,11},{10,... | collective-permute-start | bytes 1572872 | tf_op jit(solution)/shard_map/ppermute | solution.py:327
  88.3 3.8 %collective-permute-start.11 = (f32[2,2,256,128]{3,2,1,0:T(8,128)S(1)}, f32[2,2,256,128]{3,2,1,0:T(8,128)S(1)}, u32[]{:S(2)}, u32[]{:S(2)}) collective-permute-start(f32[2,2,256,128]{3,2,1,0:T(8,128)S(1)} %get-tuple-element.36), channel_id=1, source_target_pairs={{0,2},{1,3},{2,0},{3,1},{4,6},{5,7},{6,4},{7,5},{8,10},{9,11},{10,... | collective-permute-start | bytes 1572872 | tf_op jit(solution)/shard_map/ppermute | solution.py:327
  88.5 7.3 %collective-permute-start.6 = (f32[256,128]{1,0:T(8,128)S(1)}, f32[256,128]{1,0:T(8,128)S(1)}, u32[]{:S(2)}, u32[]{:S(2)}) collective-permute-start(f32[256,128]{1,0:T(8,128)S(1)} %get-tuple-element.63), channel_id=1, source_target_pairs={{0,5},{1,4},{2,7},{3,6},{4,1},{5,0},{6,3},{7,2},{8,13},{9,12},{10,... | collective-permute-start | bytes 393224 | tf_op jit(solution)/shard_map/ppermute | solution.py:327
  89.9 8.8 %collective-permute-start.5 = (f32[256,128]{1,0:T(8,128)S(1)}, f32[256,128]{1,0:T(8,128)S(1)}, u32[]{:S(2)}, u32[]{:S(2)}) collective-permute-start(f32[256,128]{1,0:T(8,128)S(1)} %get-tuple-element.64), channel_id=1, source_target_pairs={{0,4},{1,5},{2,6},{3,7},{4,0},{5,1},{6,2},{7,3},{8,12},{9,13},{10,... | collective-permute-start | bytes 393224 | tf_op jit(solution)/shard_map/ppermute | solution.py:327
  91.0 8.1 %collective-permute-start.4 = (f32[256,128]{1,0:T(8,128)S(1)}, f32[256,128]{1,0:T(8,128)S(1)}, u32[]{:S(2)}, u32[]{:S(2)}) collective-permute-start(f32[256,128]{1,0:T(8,128)S(1)} %get-tuple-element.62), channel_id=1, source_target_pairs={{0,1},{1,0},{2,3},{3,2},{4,5},{5,4},{6,7},{7,6},{8,9},{9,8},{10,11... | collective-permute-start | bytes 393224 | tf_op jit(solution)/shard_map/ppermute | solution.py:327
  92.2 9.3 %collective-permute-start.14 = (f32[256,128]{1,0:T(8,128)S(1)}, f32[256,128]{1,0:T(8,128)S(1)}, u32[]{:S(2)}, u32[]{:S(2)}) collective-permute-start(f32[256,128]{1,0:T(8,128)S(1)} %get-tuple-element.60), channel_id=1, source_target_pairs={{0,5},{1,4},{2,7},{3,6},{4,1},{5,0},{6,3},{7,2},{8,13},{9,12},{10,... | collective-permute-start | bytes 393224 | tf_op jit(solution)/shard_map/ppermute | solution.py:327
  93.7 10.2 %collective-permute-start.13 = (f32[256,128]{1,0:T(8,128)S(1)}, f32[256,128]{1,0:T(8,128)S(1)}, u32[]{:S(2)}, u32[]{:S(2)}) collective-permute-start(f32[256,128]{1,0:T(8,128)S(1)} %get-tuple-element.61), channel_id=1, source_target_pairs={{0,4},{1,5},{2,6},{3,7},{4,0},{5,1},{6,2},{7,3},{8,12},{9,13},{10,... | collective-permute-start | bytes 393224 | tf_op jit(solution)/shard_map/ppermute | solution.py:327
  95.8 8.5 %collective-permute-start.12 = (f32[256,128]{1,0:T(8,128)S(1)}, f32[256,128]{1,0:T(8,128)S(1)}, u32[]{:S(2)}, u32[]{:S(2)}) collective-permute-start(f32[256,128]{1,0:T(8,128)S(1)} %get-tuple-element.59), channel_id=1, source_target_pairs={{0,1},{1,0},{2,3},{3,2},{4,5},{5,4},{6,7},{7,6},{8,9},{9,8},{10,11... | collective-permute-start | bytes 393224 | tf_op jit(solution)/shard_map/ppermute | solution.py:327
  104.4 8.8 %copy-start.6 = (bf16[2,256,128]{2,1,0:T(8,128)(2,1)}, bf16[2,256,128]{2,1,0:T(8,128)(2,1)S(1)}, u32[]{:S(2)}) copy-start(bf16[2,256,128]{2,1,0:T(8,128)(2,1)S(1)} %pad_maximum_fusion.1) | copy-start | bytes 393220
  104.4 2.0 collective-permute-start.18
  105.1 33.3 %collective-permute-start.16 = (bf16[128,3968]{1,0:T(8,128)(2,1)}, bf16[128,3968]{1,0:T(8,128)(2,1)}, u32[]{:S(2)}, u32[]{:S(2)}) collective-permute-start(bf16[128,3968]{1,0:T(8,128)(2,1)} %collective-permute-done.8), channel_id=1, source_target_pairs={{8,0},{9,1},{10,2},{11,3},{12,4},{13,5},{14,6},{15,7},{16,24},{17,... | collective-permute-start | bytes 3047432 | tf_op jit(solution)/shard_map/ppermute | solution.py:327
  106.4 0.7 copy-start.5
  108.5 4.8 %copy-start = (bf16[128,3968]{1,0:T(8,128)(2,1)}, bf16[128,3968]{1,0:T(8,128)(2,1)S(1)}, u32[]{:S(2)}) copy-start(bf16[128,3968]{1,0:T(8,128)(2,1)S(1)} %broadcast_select_fusion.1.refs_0_.refs_1_.refs_2_.refs_3_.refs_4_.refs_10_) | copy-start | bytes 3047428
  113.3 10.6 %collective-permute-start.15 = (f32[2,2,256,128]{3,2,1,0:T(8,128)S(1)}, f32[2,2,256,128]{3,2,1,0:T(8,128)S(1)}, u32[]{:S(2)}, u32[]{:S(2)}) collective-permute-start(f32[2,2,256,128]{3,2,1,0:T(8,128)S(1)} %get-tuple-element.38), channel_id=1, source_target_pairs={{0,2},{1,3},{2,0},{3,1},{4,6},{5,7},{6,4},{7,5},{8,10},{9,11},{10,... | collective-permute-start | bytes 1572872 | tf_op jit(solution)/shard_map/ppermute | solution.py:327
  113.3 14.8 %collective-permute-start.17 = (bf16[2,256,128]{2,1,0:T(8,128)(2,1)}, bf16[2,256,128]{2,1,0:T(8,128)(2,1)S(1)}, u32[]{:S(2)}, u32[]{:S(2)}) collective-permute-start(bf16[2,256,128]{2,1,0:T(8,128)(2,1)} %copy-done.6), channel_id=1, source_target_pairs={{0,1},{1,0},{2,3},{3,2},{4,5},{5,4},{6,7},{7,6},{8,9},{9,8},{10,11... | collective-permute-start | bytes 393224 | tf_op jit(solution)/shard_map/ppermute | solution.py:327
  139.8 4.8 %copy-start.2 = (bf16[128,3968]{1,0:T(8,128)(2,1)}, bf16[128,3968]{1,0:T(8,128)(2,1)S(1)}, u32[]{:S(2)}) copy-start(bf16[128,3968]{1,0:T(8,128)(2,1)S(1)} %broadcast_select_fusion.refs_0_.refs_1_.refs_2_.refs_3_.refs_4_.refs_11_) | copy-start | bytes 3047428
  144.6 51.7 %copy-start.1 = (bf16[128,3968]{1,0:T(8,128)(2,1)S(1)}, bf16[128,3968]{1,0:T(8,128)(2,1)}, u32[]{:S(2)}) copy-start(bf16[128,3968]{1,0:T(8,128)(2,1)} %copy-done) | copy-start | bytes 3047428
  144.6 51.7 %copy-start.3 = (bf16[128,3968]{1,0:T(8,128)(2,1)S(1)}, bf16[128,3968]{1,0:T(8,128)(2,1)}, u32[]{:S(2)}) copy-start(bf16[128,3968]{1,0:T(8,128)(2,1)} %copy-done.2) | copy-start | bytes 3047428
  144.6 9.0 %collective-permute-start.22 = (f32[2,2,256,128]{3,2,1,0:T(8,128)S(1)}, f32[2,2,256,128]{3,2,1,0:T(8,128)S(1)}, u32[]{:S(2)}, u32[]{:S(2)}) collective-permute-start(f32[2,2,256,128]{3,2,1,0:T(8,128)S(1)} %get-tuple-element.41), channel_id=1, source_target_pairs={{0,2},{1,3},{2,0},{3,1},{4,6},{5,7},{6,4},{7,5},{8,10},{9,11},{10,... | collective-permute-start | bytes 1572872 | tf_op jit(solution)/shard_map/ppermute | solution.py:327
  144.7 7.3 %collective-permute-start.21 = (f32[256,128]{1,0:T(8,128)S(1)}, f32[256,128]{1,0:T(8,128)S(1)}, u32[]{:S(2)}, u32[]{:S(2)}) collective-permute-start(f32[256,128]{1,0:T(8,128)S(1)} %get-tuple-element.57), channel_id=1, source_target_pairs={{0,5},{1,4},{2,7},{3,6},{4,1},{5,0},{6,3},{7,2},{8,13},{9,12},{10,... | collective-permute-start | bytes 393224 | tf_op jit(solution)/shard_map/ppermute | solution.py:327
  145.2 8.4 %collective-permute-start.20 = (f32[256,128]{1,0:T(8,128)S(1)}, f32[256,128]{1,0:T(8,128)S(1)}, u32[]{:S(2)}, u32[]{:S(2)}) collective-permute-start(f32[256,128]{1,0:T(8,128)S(1)} %get-tuple-element.58), channel_id=1, source_target_pairs={{0,4},{1,5},{2,6},{3,7},{4,0},{5,1},{6,2},{7,3},{8,12},{9,13},{10,... | collective-permute-start | bytes 393224 | tf_op jit(solution)/shard_map/ppermute | solution.py:327
  146.8 6.8 %collective-permute-start.19 = (f32[256,128]{1,0:T(8,128)S(1)}, f32[256,128]{1,0:T(8,128)S(1)}, u32[]{:S(2)}, u32[]{:S(2)}) collective-permute-start(f32[256,128]{1,0:T(8,128)S(1)} %get-tuple-element.56), channel_id=1, source_target_pairs={{0,1},{1,0},{2,3},{3,2},{4,5},{5,4},{6,7},{7,6},{8,9},{9,8},{10,11... | collective-permute-start | bytes 393224 | tf_op jit(solution)/shard_map/ppermute | solution.py:327
  153.8 7.0 %collective-permute-start.25 = (f32[256,128]{1,0:T(8,128)S(1)}, f32[256,128]{1,0:T(8,128)S(1)}, u32[]{:S(2)}, u32[]{:S(2)}) collective-permute-start(f32[256,128]{1,0:T(8,128)S(1)} %get-tuple-element.54), channel_id=1, source_target_pairs={{0,5},{1,4},{2,7},{3,6},{4,1},{5,0},{6,3},{7,2},{8,13},{9,12},{10,... | collective-permute-start | bytes 393224 | tf_op jit(solution)/shard_map/ppermute | solution.py:327
  155.2 7.1 %collective-permute-start.24 = (f32[256,128]{1,0:T(8,128)S(1)}, f32[256,128]{1,0:T(8,128)S(1)}, u32[]{:S(2)}, u32[]{:S(2)}) collective-permute-start(f32[256,128]{1,0:T(8,128)S(1)} %get-tuple-element.55), channel_id=1, source_target_pairs={{0,4},{1,5},{2,6},{3,7},{4,0},{5,1},{6,2},{7,3},{8,12},{9,13},{10,... | collective-permute-start | bytes 393224 | tf_op jit(solution)/shard_map/ppermute | solution.py:327
  156.7 6.1 %collective-permute-start.23 = (f32[256,128]{1,0:T(8,128)S(1)}, f32[256,128]{1,0:T(8,128)S(1)}, u32[]{:S(2)}, u32[]{:S(2)}) collective-permute-start(f32[256,128]{1,0:T(8,128)S(1)} %get-tuple-element.53), channel_id=1, source_target_pairs={{0,1},{1,0},{2,3},{3,2},{4,5},{5,4},{6,7},{7,6},{8,9},{9,8},{10,11... | collective-permute-start | bytes 393224 | tf_op jit(solution)/shard_map/ppermute | solution.py:327
  162.8 11.1 %collective-permute-start.26 = (bf16[2,256,128]{2,1,0:T(8,128)(2,1)S(1)}, bf16[2,256,128]{2,1,0:T(8,128)(2,1)S(1)}, u32[]{:S(2)}, u32[]{:S(2)}) collective-permute-start(bf16[2,256,128]{2,1,0:T(8,128)(2,1)S(1)} %pad_maximum_fusion.2), channel_id=1, source_target_pairs={{0,0},{1,16},{2,2},{3,18},{4,4},{5,20},{6,6},{7,22},{8,8},{9,24},{... | collective-permute-start | bytes 393224 | tf_op jit(solution)/shard_map/ppermute | solution.py:327
  163.5 10.5 %collective-permute-start.27 = (bf16[2,256,128]{2,1,0:T(8,128)(2,1)S(1)}, bf16[2,256,128]{2,1,0:T(8,128)(2,1)S(1)}, u32[]{:S(2)}, u32[]{:S(2)}) collective-permute-start(bf16[2,256,128]{2,1,0:T(8,128)(2,1)S(1)} %pad_maximum_fusion.2), channel_id=1, source_target_pairs={{0,8},{1,24},{2,10},{3,26},{4,12},{5,28},{6,14},{7,30},{8,0},{9,16... | collective-permute-start | bytes 393224 | tf_op jit(solution)/shard_map/ppermute | solution.py:327
  164.8 10.1 %collective-permute-start.28 = (bf16[2,256,128]{2,1,0:T(8,128)(2,1)S(1)}, bf16[2,256,128]{2,1,0:T(8,128)(2,1)S(1)}, u32[]{:S(2)}, u32[]{:S(2)}) collective-permute-start(bf16[2,256,128]{2,1,0:T(8,128)(2,1)S(1)} %pad_maximum_fusion.2), channel_id=1, source_target_pairs={{0,16},{1,0},{2,18},{3,2},{4,20},{5,4},{6,22},{7,6},{8,24},{9,8},{... | collective-permute-start | bytes 393224 | tf_op jit(solution)/shard_map/ppermute | solution.py:327
  171.1 10.6 %collective-permute-start.29 = (bf16[2,256,128]{2,1,0:T(8,128)(2,1)S(1)}, bf16[2,256,128]{2,1,0:T(8,128)(2,1)S(1)}, u32[]{:S(2)}, u32[]{:S(2)}) collective-permute-start(bf16[2,256,128]{2,1,0:T(8,128)(2,1)S(1)} %pad_maximum_fusion.2), channel_id=1, source_target_pairs={{0,24},{1,8},{2,26},{3,10},{4,28},{5,12},{6,30},{7,14},{8,16},{9,0... | collective-permute-start | bytes 393224 | tf_op jit(solution)/shard_map/ppermute | solution.py:327
  171.9 9.7 %collective-permute-start.30 = (bf16[2,256,128]{2,1,0:T(8,128)(2,1)S(1)}, bf16[2,256,128]{2,1,0:T(8,128)(2,1)}, u32[]{:S(2)}, u32[]{:S(2)}) collective-permute-start(bf16[2,256,128]{2,1,0:T(8,128)(2,1)S(1)} %pad_maximum_fusion.2), channel_id=1, source_target_pairs={{0,1},{1,0},{2,3},{3,2},{4,5},{5,4},{6,7},{7,6},{8,9},{9,8},{10,11... | collective-permute-start | bytes 393224 | tf_op jit(solution)/shard_map/ppermute | solution.py:327
  181.7 12.5 %collective-permute-start.31 = (bf16[4,2,256,128]{3,2,1,0:T(8,128)(2,1)S(1)}, bf16[4,2,256,128]{3,2,1,0:T(8,128)(2,1)S(1)}, u32[]{:S(2)}, u32[]{:S(2)}) collective-permute-start(bf16[4,2,256,128]{3,2,1,0:T(8,128)(2,1)S(1)} %pad_maximum_fusion.refs_16_.refs_20_), channel_id=1, source_target_pairs={{0,4},{1,5},{2,6},{3,7},{4,0},{5,1},{6,2},{7,3},{8,12},{9,13},{10,... | collective-permute-start | bytes 1572872 | tf_op jit(solution)/shard_map/ppermute | solution.py:327
  182.9 12.4 %collective-permute-start.32 = (bf16[4,2,256,128]{3,2,1,0:T(8,128)(2,1)S(1)}, bf16[4,2,256,128]{3,2,1,0:T(8,128)(2,1)}, u32[]{:S(2)}, u32[]{:S(2)}) collective-permute-start(bf16[4,2,256,128]{3,2,1,0:T(8,128)(2,1)S(1)} %pad_maximum_fusion.refs_16_.refs_20_), channel_id=1, source_target_pairs={{0,2},{1,3},{2,0},{3,1},{4,6},{5,7},{6,4},{7,5},{8,10},{9,11},{10,... | collective-permute-start | bytes 1572872 | tf_op jit(solution)/shard_map/ppermute | solution.py:327
  194.2 2.0 collective-permute-start.33
  196.3 1.6 copy-start.4
Sparse Core Ops, SparseCore 0:
  107.2 52.8 all-gather.2

commit v13 on v11

--- a/solution.py
+++ b/solution.py
@@ -373,10 +373,10 @@
 
     owns = [coefficients(units[0], (across, outward)), coefficients(units[1])]
     own_a = jnp.stack(owns)
-    share_a = share(own_a, 0)
     mate_a = mate(own_a)
-    right_a = lax.all_gather(share_a, ("z", "y", "c"), axis=0)
-    owns.append(coefficients(units[2], None, (far, mate_a, share_a)))
+    own_a, far = lax.optimization_barrier((own_a, far))
+    right_a = lax.all_gather(share(own_a, 0), ("z", "y", "c"), axis=0)
+    owns.append(coefficients(units[2], mate_a))
     units.append(jnp.where(inner, middle, far))
     owns.append(coefficients(units[3], owns[2]))
     own_b = jnp.stack(owns[2:])

time: 210 us -> 209 us (level)
  waiting for transfers between devices: 109 us -> 104 us
  starting transfers between devices: 43.9 us -> 48.7 us
    ppermute x34, waiting for transfers between devices: 97.6 us -> 92.6 us  [send(): lax.ppermute(array, AXES, [(source, number[to]) for source, to in pairs i...]
    ppermute x34, starting transfers between devices: 38.7 us -> 43.5 us  [send(): lax.ppermute(array, AXES, [(source, number[to]) for source, to in pairs i...]
  transfers between devices with their start and end apart: 36 -> 36, of which waited for: 20 -> 18; matrix products, arithmetic and copies ran while one was open for 4% -> 4% of each run, Pallas kernels for 10% -> 10%
where the time goes in v13:
time: 209 us; the launch traced here: 208 us
  waiting for transfers between devices  104 us (50%)
  starting transfers between devices  48.7 us (23%)
  Pallas kernels  31 us (15%)
  between operations  13.8 us (7%)
  local copies, waits for them, and re-layouts  7.35 us (4%)
  other arithmetic  3.23 us (2%)
    ppermute x34, waiting for transfers between devices, send(): lax.ppermute(array, AXES, [(source, number[to]) for source, to in pairs i...  92.6 us
    ppermute x34, starting transfers between devices, send(): lax.ppermute(array, AXES, [(source, number[to]) for source, to in pairs i...  43.5 us
    pallas_call x4, Pallas kernels, project(): pl.pallas_call(functools.partial(project_kernel, segs, val_count, cond_co...  20.3 us
    all_to_all x1, waiting for transfers between devices, local(): unit = lax.all_to_all(packed, ('y', 'c', 'x'), 0, 0, tiled=True)  11.3 us
    pallas_call x1, Pallas kernels, make_chi(): pl.pallas_call(functools.partial(chi_kernel, early, late, n_freq, factor)...  6.75 us
    all_to_all x1, starting transfers between devices, local(): unit = lax.all_to_all(packed, ('y', 'c', 'x'), 0, 0, tiled=True)  5.17 us
  transfers between devices with their start and end apart: 36, of which 18 were waited for; matrix products, arithmetic and copies ran while one was open for 4% of the time, Pallas kernels for 10%

profile of v13, /device:TPU:0, one launch (start us, length us, event | category | flops | bytes accessed | tf_op | source)
XLA Modules:
  0.0 208.0 jit_solution(12068866418272126261)
XLA Ops:
  6.5 4.0 %pack.1 = bf16[8,16,3968]{2,1,0:T(8,128)(2,1)} custom-call(f32[4]{0:T(128)} %val_energy.1, f32[16]{0:T(128)} %cond_energy.1, s32[64]{0:T(128)} %val_slot.1, s32[64]{0:T(128)} %cond_slot.1, f32[4]{0:T(128)} %frequencies.1, bf16[16,24576]{1,0:T(8,128)(2,1)} %refs_1_.1, bf16[16,24576]{1,0:T(8,128)(2,1)} %refs_1_.1, bf16[4,24576]{1,0:T(4,128)(2,1)} %refs_3_.1, ...), custom_call_target="tpu_custom_call" | custom-call | tf_op jit(solution)/shard_map/pack/pallas_call | solution.py:77
  10.5 5.2 %all-to-all-start = ((bf16[8,16,3968]{2,1,0:T(8,128)(2,1)}), bf16[8,16,3968]{2,1,0:T(8,128)(2,1)}, u32[]{:S(2)}, u32[]{:S(2)}) async-start(bf16[8,16,3968]{2,1,0:T(8,128)(2,1)} %pack.1), calls=%async_computation | async-start | bytes 2031616 | tf_op jit(solution)/shard_map/all_to_all | solution.py:480
  15.8 3.3 %constant_dynamic-slice_fusion = (bf16[3072,128]{1,0:T(8,128)(2,1)}, bf16[3072,128]{1,0:T(8,128)(2,1)}, bf16[3072,128]{1,0:T(8,128)(2,1)S(1)}, bf16[3072,128]{1,0:T(8,128)(2,1)}) fusion(bf16[12288,128]{1,0:T(8,128)(2,1)} %param.14, s32[]{:T(128)S(6)} %select_n.27, s32[]{:T(128)S(6)} %select_n.25, s32[]{:T(128)S(6)} %select_n.24, s32[]{:T(128)S(6)} %select_n.26), kind=kLoop, calls=%fused_computation.38 | loop fusion | bytes 6291472 | tf_op jit(solution)/shard_map/dynamic_slice | solution.py:337
  19.1 11.3 %all-to-all-done = bf16[8,16,3968]{2,1,0:T(8,128)(2,1)} async-done(((bf16[8,16,3968]{2,1,0:T(8,128)(2,1)}), bf16[8,16,3968]{2,1,0:T(8,128)(2,1)}, u32[]{:S(2)}, u32[]{:S(2)}) %all-to-all-start) | async-done | bytes 1015840 | tf_op jit(solution)/shard_map/all_to_all | solution.py:480
  30.4 2.0 collective-permute-start.4
  32.4 1.6 collective-permute-start.6
  34.6 1.3 collective-permute-start.2
  35.9 19.1 %collective-permute-done.4.refs_0_.refs_1_.refs_2_.refs_3_.refs_4_.refs_9_ = bf16[128,3968]{1,0:T(8,128)(2,1)} collective-permute-done((bf16[128,3968]{1,0:T(8,128)(2,1)}, bf16[128,3968]{1,0:T(8,128)(2,1)}, u32[]{:S(2)}, u32[]{:S(2)}) %collective-permute-start.4) | collective-permute-done | bytes 1015840 | tf_op jit(solution)/shard_map/ppermute | solution.py:327
  55.0 1.6 collective-permute-start.5
  56.6 1.3 collective-permute-start.7
  57.9 12.7 %collective-permute-done.2.refs_8_.refs_12_.refs_16_.refs_20_ = bf16[3072,128]{1,0:T(8,128)(2,1)S(1)} collective-permute-done((bf16[3072,128]{1,0:T(8,128)(2,1)}, bf16[3072,128]{1,0:T(8,128)(2,1)S(1)}, u32[]{:S(2)}, u32[]{:S(2)}) %collective-permute-start.2) | collective-permute-done | bytes 786464 | tf_op jit(solution)/shard_map/ppermute | solution.py:327
  70.7 5.4 %project.4 = (f32[2,2,256,128]{3,2,1,0:T(8,128)S(1)}, f32[2,2,256,128]{3,2,1,0:T(8,128)S(1)}) custom-call(s32[1]{0:T(128)} %bitcast.4.place, bf16[128,3968]{1,0:T(8,128)(2,1)} %bitcast.5.refs_0_.refs_1_.refs_2_.refs_3_.refs_4_.refs_8_, bf16[128,3968]{1,0:T(8,128)(2,1)} %bitcast.5.refs_0_.refs_1_.refs_2_.refs_3_.refs_4_.refs_8_, ...), custom_call_target="tpu_custom_call" | custom-call | flops 1610612736 | bytes 4161536 | tf_op jit(solution)/shard_map/project/pallas_call | solution.py:187
  76.6 5.4 %project.5 = (f32[2,2,256,128]{3,2,1,0:T(8,128)S(1)}, f32[2,2,256,128]{3,2,1,0:T(8,128)S(1)}) custom-call(s32[1]{0:T(128)} %bitcast.4.place, bf16[128,3968]{1,0:T(8,128)(2,1)} %collective-permute-done.4.refs_0_.refs_1_.refs_2_.refs_3_.refs_4_.refs_9_, bf16[128,3968]{1,0:T(8,128)(2,1)} %collective-permute-done.4.refs_0_.refs_1_.refs_2_.refs_3_.refs_4_.refs_9_, ...), custom_call_target="tpu_custom_call" | custom-call | flops 1610612736 | bytes 4161536 | tf_op jit(solution)/shard_map/project/pallas_call | solution.py:187
  82.3 1.7 collective-permute-done.11
  84.1 1.3 collective-permute-start.20
  85.4 1.1 collective-permute-start.12
  87.0 2.0 collective-permute-start.14
  89.0 1.0 collective-permute-start.10
  90.1 1.8 collective-permute-done.12
  91.8 1.0 collective-permute-start.8
  92.8 5.1 %collective-permute-done.13 = f32[256,128]{1,0:T(8,128)S(1)} collective-permute-done((f32[256,128]{1,0:T(8,128)S(1)}, f32[256,128]{1,0:T(8,128)S(1)}, u32[]{:S(2)}, u32[]{:S(2)}) %collective-permute-start.13) | collective-permute-done | bytes 131104 | tf_op jit(solution)/shard_map/ppermute | solution.py:327
  98.0 1.5 collective-permute-done.8
  99.5 3.4 %collective-permute-done.9 = f32[256,128]{1,0:T(8,128)S(1)} collective-permute-done((f32[256,128]{1,0:T(8,128)S(1)}, f32[256,128]{1,0:T(8,128)S(1)}, u32[]{:S(2)}, u32[]{:S(2)}) %collective-permute-start.9) | collective-permute-done | bytes 131104 | tf_op jit(solution)/shard_map/ppermute | solution.py:327
  103.0 9.0 %collective-permute-done.20 = bf16[128,3968]{1,0:T(8,128)(2,1)} collective-permute-done((bf16[128,3968]{1,0:T(8,128)(2,1)}, bf16[128,3968]{1,0:T(8,128)(2,1)}, u32[]{:S(2)}, u32[]{:S(2)}) %collective-permute-start.20) | collective-permute-done | bytes 1015840 | tf_op jit(solution)/shard_map/ppermute | solution.py:327
  113.4 1.3 broadcast_select_fusion.1.refs_0_.refs_1_.refs_2_.refs_3_.refs_4_.refs_10_
  114.7 4.8 %project.6 = (f32[2,2,256,128]{3,2,1,0:T(8,128)S(1)}, f32[2,2,256,128]{3,2,1,0:T(8,128)S(1)}) custom-call(s32[1]{0:T(128)} %bitcast.4.place, bf16[128,3968]{1,0:T(8,128)(2,1)S(1)} %broadcast_select_fusion.1.refs_0_.refs_1_.refs_2_.refs_3_.refs_4_.refs_10_, bf16[128,3968]{1,0:T(8,128)(2,1)S(1)} %broadcast_select_fusion.1.refs_0_.refs_1_.refs_2_.refs_3_.refs_4_.refs_10_, ...), custom_call_target="tpu_custom_call" | custom-call | flops 1610612736 | bytes 4161536 | tf_op jit(solution)/shard_map/project/pallas_call | solution.py:187
  119.6 10.9 %collective-permute-start.16 = (bf16[2,256,128]{2,1,0:T(8,128)(2,1)}, bf16[2,256,128]{2,1,0:T(8,128)(2,1)S(1)}, u32[]{:S(2)}, u32[]{:S(2)}) collective-permute-start(bf16[2,256,128]{2,1,0:T(8,128)(2,1)} %copy-done.8), channel_id=1, source_target_pairs={{0,1},{1,0},{2,3},{3,2},{4,5},{5,4},{6,7},{7,6},{8,9},{9,8},{10,11... | collective-permute-start | bytes 393224 | tf_op jit(solution)/shard_map/ppermute | solution.py:327
  130.6 4.2 %collective-permute-done.16 = bf16[2,256,128]{2,1,0:T(8,128)(2,1)S(1)} collective-permute-done((bf16[2,256,128]{2,1,0:T(8,128)(2,1)}, bf16[2,256,128]{2,1,0:T(8,128)(2,1)S(1)}, u32[]{:S(2)}, u32[]{:S(2)}) %collective-permute-start.16) | collective-permute-done | bytes 131104 | tf_op jit(solution)/shard_map/ppermute | solution.py:327
  134.8 1.3 broadcast_select_fusion.refs_0_.refs_1_.refs_2_.refs_3_.refs_4_.refs_11_
  136.1 4.8 %project.7 = (f32[2,2,256,128]{3,2,1,0:T(8,128)S(1)}, f32[2,2,256,128]{3,2,1,0:T(8,128)S(1)}) custom-call(s32[1]{0:T(128)} %bitcast.4.place, bf16[128,3968]{1,0:T(8,128)(2,1)S(1)} %broadcast_select_fusion.refs_0_.refs_1_.refs_2_.refs_3_.refs_4_.refs_11_, bf16[128,3968]{1,0:T(8,128)(2,1)S(1)} %broadcast_select_fusion.refs_0_.refs_1_.refs_2_.refs_3_.refs_4_.refs_11_, ...), custom_call_target="tpu_custom_call" | custom-call | flops 1610612736 | bytes 4161536 | tf_op jit(solution)/shard_map/project/pallas_call | solution.py:187
  141.1 1.8 collective-permute-start.17
  143.4 1.2 collective-permute-start.19
  144.6 2.5 %collective-permute-done.17 = f32[256,128]{1,0:T(8,128)S(1)} collective-permute-done((f32[256,128]{1,0:T(8,128)S(1)}, f32[256,128]{1,0:T(8,128)S(1)}, u32[]{:S(2)}, u32[]{:S(2)}) %collective-permute-start.17) | collective-permute-done | bytes 131104 | tf_op jit(solution)/shard_map/ppermute | solution.py:327
  147.1 6.2 %collective-permute-done.18 = f32[256,128]{1,0:T(8,128)S(1)} collective-permute-done((f32[256,128]{1,0:T(8,128)S(1)}, f32[256,128]{1,0:T(8,128)S(1)}, u32[]{:S(2)}, u32[]{:S(2)}) %collective-permute-start.18) | collective-permute-done | bytes 131104 | tf_op jit(solution)/shard_map/ppermute | solution.py:327
  153.8 3.3 %collective-permute-start.24 = (f32[256,128]{1,0:T(8,128)S(1)}, f32[256,128]{1,0:T(8,128)S(1)}, u32[]{:S(2)}, u32[]{:S(2)}) collective-permute-start(f32[256,128]{1,0:T(8,128)S(1)} %get-tuple-element.58), channel_id=1, source_target_pairs={{0,5},{1,4},{2,7},{3,6},{4,1},{5,0},{6,3},{7,2},{8,13},{9,12},{10,... | collective-permute-start | bytes 393224 | tf_op jit(solution)/shard_map/ppermute | solution.py:327
  157.0 1.5 collective-permute-done.22
  158.5 4.0 %collective-permute-done.23 = f32[256,128]{1,0:T(8,128)S(1)} collective-permute-done((f32[256,128]{1,0:T(8,128)S(1)}, f32[256,128]{1,0:T(8,128)S(1)}, u32[]{:S(2)}, u32[]{:S(2)}) %collective-permute-start.23) | collective-permute-done | bytes 131104 | tf_op jit(solution)/shard_map/ppermute | solution.py:327
  162.6 0.7 collective-permute-start.25
  163.4 5.3 %collective-permute-start.27 = (bf16[2,256,128]{2,1,0:T(8,128)(2,1)S(1)}, bf16[2,256,128]{2,1,0:T(8,128)(2,1)S(1)}, u32[]{:S(2)}, u32[]{:S(2)}) collective-permute-start(bf16[2,256,128]{2,1,0:T(8,128)(2,1)S(1)} %pad_maximum_fusion.2), channel_id=1, source_target_pairs={{0,16},{1,0},{2,18},{3,2},{4,20},{5,4},{6,22},{7,6},{8,24},{9,8},{... | collective-permute-start | bytes 393224 | tf_op jit(solution)/shard_map/ppermute | solution.py:327
  168.6 1.6 collective-permute-start.29
  170.3 2.2 %collective-permute-done.27 = bf16[2,256,128]{2,1,0:T(8,128)(2,1)S(1)} collective-permute-done((bf16[2,256,128]{2,1,0:T(8,128)(2,1)S(1)}, bf16[2,256,128]{2,1,0:T(8,128)(2,1)S(1)}, u32[]{:S(2)}, u32[]{:S(2)}) %collective-permute-start.27) | collective-permute-done | bytes 131104 | tf_op jit(solution)/shard_map/ppermute | solution.py:327
  172.5 4.3 %collective-permute-done.28 = bf16[2,256,128]{2,1,0:T(8,128)(2,1)S(1)} collective-permute-done((bf16[2,256,128]{2,1,0:T(8,128)(2,1)S(1)}, bf16[2,256,128]{2,1,0:T(8,128)(2,1)S(1)}, u32[]{:S(2)}, u32[]{:S(2)}) %collective-permute-start.28) | collective-permute-done | bytes 131104 | tf_op jit(solution)/shard_map/ppermute | solution.py:327
  177.6 1.0 collective-permute-start.31
  178.6 12.2 %collective-permute-done.31.refs_17_.refs_21_ = bf16[4,2,256,128]{3,2,1,0:T(8,128)(2,1)S(1)} collective-permute-done((bf16[4,2,256,128]{3,2,1,0:T(8,128)(2,1)S(1)}, bf16[4,2,256,128]{3,2,1,0:T(8,128)(2,1)S(1)}, u32[]{:S(2)}, u32[]{:S(2)}) %collective-permute-start.31) | collective-permute-done | bytes 524320 | tf_op jit(solution)/shard_map/ppermute | solution.py:327
  190.9 0.9 slice_bitcast_fusion.15
  191.8 1.0 collective-permute-done.33.refs_19_.refs_23_
  192.8 1.6 copy-done.4
  194.4 6.8 %chi.1 = f32[128,4,1024]{2,1,0:T(4,128)} custom-call(s32[5]{0:T(128)S(1)} %stack.56.scalars, bf16[256,128]{1,0:T(8,128)(2,1)S(1)} %fusion.12.refs_0_, bf16[256,128]{1,0:T(8,128)(2,1)S(1)} %fusion.3.refs_1_, bf16[256,128]{1,0:T(8,128)(2,1)S(1)} %fusion.9.refs_2_, bf16[256,128]{1,0:T(8,128)(2,1)S(1)} %fusion.6.refs_3_, ...), custom_call_target="tpu_custom_call" | custom-call | flops 2147483648 | bytes 6291456 | tf_op jit(solution)/shard_map/chi/pallas_call | solution.py:281
  (70 shorter events, 5.8 us)
Async XLA Ops:
  10.5 19.9 %all-to-all-start = ((bf16[8,16,3968]{2,1,0:T(8,128)(2,1)}), bf16[8,16,3968]{2,1,0:T(8,128)(2,1)}, u32[]{:S(2)}, u32[]{:S(2)}) async-start(bf16[8,16,3968]{2,1,0:T(8,128)(2,1)} %pack.1), calls=%async_computation | async-start | bytes 2031616 | tf_op jit(solution)/shard_map/all_to_all | solution.py:480
  15.7 161.2 %all-gather.3.cloned.1.call-start = ((), (), s32[]{:S(2)}) async-start(), calls=%async_computation.1 | async-start | bytes 2228224 | tf_op jit(solution)/shard_map/all_gather | solution.py:378
  30.4 24.6 %collective-permute-start.4 = (bf16[128,3968]{1,0:T(8,128)(2,1)}, bf16[128,3968]{1,0:T(8,128)(2,1)}, u32[]{:S(2)}, u32[]{:S(2)}) collective-permute-start(bf16[128,3968]{1,0:T(8,128)(2,1)} %bitcast.5.refs_0_.refs_1_.refs_2_.refs_3_.refs_4_.refs_8_), channel_id=1, source_target_pairs={{0,8},{1,9},{2,10},{3,11},{4,12},{5,13},{6,14},{7,15},{8,0},{9,1},... | collective-permute-start | bytes 3047432 | tf_op jit(solution)/shard_map/ppermute | solution.py:327
  32.4 24.3 %collective-permute-start.6 = (bf16[128,3968]{1,0:T(8,128)(2,1)}, bf16[128,3968]{1,0:T(8,128)(2,1)}, u32[]{:S(2)}, u32[]{:S(2)}) collective-permute-start(bf16[128,3968]{1,0:T(8,128)(2,1)} %bitcast.5.refs_0_.refs_1_.refs_2_.refs_3_.refs_4_.refs_8_), channel_id=1, source_target_pairs={{8,16},{9,17},{10,18},{11,19},{12,20},{13,21},{14,22},{15,23},{16,... | collective-permute-start | bytes 3047432 | tf_op jit(solution)/shard_map/ppermute | solution.py:327
  34.0 23.9 %collective-permute-start = (bf16[3072,128]{1,0:T(8,128)(2,1)}, bf16[3072,128]{1,0:T(8,128)(2,1)S(1)}, u32[]{:S(2)}, u32[]{:S(2)}) collective-permute-start(bf16[3072,128]{1,0:T(8,128)(2,1)} %get-tuple-element.31), channel_id=1, source_target_pairs={{0,2},{1,3},{2,0},{3,1},{4,6},{5,7},{6,4},{7,5},{8,10},{9,11},{10,... | collective-permute-start | bytes 2359304 | tf_op jit(solution)/shard_map/ppermute | solution.py:327
  34.0 23.9 %collective-permute-start.1 = (bf16[3072,128]{1,0:T(8,128)(2,1)}, bf16[3072,128]{1,0:T(8,128)(2,1)S(1)}, u32[]{:S(2)}, u32[]{:S(2)}) collective-permute-start(bf16[3072,128]{1,0:T(8,128)(2,1)} %get-tuple-element.32), channel_id=1, source_target_pairs={{0,4},{1,5},{2,6},{3,7},{4,0},{5,1},{6,2},{7,3},{8,12},{9,13},{10,... | collective-permute-start | bytes 2359304 | tf_op jit(solution)/shard_map/ppermute | solution.py:327
  34.6 36.0 %collective-permute-start.2 = (bf16[3072,128]{1,0:T(8,128)(2,1)}, bf16[3072,128]{1,0:T(8,128)(2,1)S(1)}, u32[]{:S(2)}, u32[]{:S(2)}) collective-permute-start(bf16[3072,128]{1,0:T(8,128)(2,1)} %get-tuple-element.33), channel_id=1, source_target_pairs={{0,6},{1,7},{2,4},{3,5},{4,2},{5,3},{6,0},{7,1},{8,14},{9,15},{10,... | collective-permute-start | bytes 2359304 | tf_op jit(solution)/shard_map/ppermute | solution.py:327
  55.0 29.1 %collective-permute-start.5 = (bf16[128,3968]{1,0:T(8,128)(2,1)}, bf16[128,3968]{1,0:T(8,128)(2,1)}, u32[]{:S(2)}, u32[]{:S(2)}) collective-permute-start(bf16[128,3968]{1,0:T(8,128)(2,1)} %collective-permute-done.4.refs_0_.refs_1_.refs_2_.refs_3_.refs_4_.refs_9_), channel_id=1, source_target_pairs={{8,16},{9,17},{10,18},{11,19},{12,20},{13,21},{14,22},{15,23},{16,... | collective-permute-start | bytes 3047432 | tf_op jit(solution)/shard_map/ppermute | solution.py:327
  56.6 32.4 %collective-permute-start.7 = (bf16[128,3968]{1,0:T(8,128)(2,1)}, bf16[128,3968]{1,0:T(8,128)(2,1)S(1)}, u32[]{:S(2)}, u32[]{:S(2)}) collective-permute-start(bf16[128,3968]{1,0:T(8,128)(2,1)} %collective-permute-done.6), channel_id=1, source_target_pairs={{8,0},{9,1},{10,2},{11,3},{12,4},{13,5},{14,6},{15,7},{16,24},{17,... | collective-permute-start | bytes 3047432 | tf_op jit(solution)/shard_map/ppermute | solution.py:327
  76.0 6.1 %collective-permute-start.3 = (f32[2,2,256,128]{3,2,1,0:T(8,128)S(1)}, f32[2,2,256,128]{3,2,1,0:T(8,128)S(1)}, u32[]{:S(2)}, u32[]{:S(2)}) collective-permute-start(f32[2,2,256,128]{3,2,1,0:T(8,128)S(1)} %get-tuple-element.35), channel_id=1, source_target_pairs={{0,2},{1,3},{2,0},{3,1},{4,6},{5,7},{6,4},{7,5},{8,10},{9,11},{10,... | collective-permute-start | bytes 1572872 | tf_op jit(solution)/shard_map/ppermute | solution.py:327
  82.0 2.0 collective-permute-start.11
  84.1 27.9 %collective-permute-start.20 = (bf16[128,3968]{1,0:T(8,128)(2,1)}, bf16[128,3968]{1,0:T(8,128)(2,1)}, u32[]{:S(2)}, u32[]{:S(2)}) collective-permute-start(bf16[128,3968]{1,0:T(8,128)(2,1)} %collective-permute-done.5), channel_id=1, source_target_pairs={{8,0},{9,1},{10,2},{11,3},{12,4},{13,5},{14,6},{15,7},{16,24},{17,... | collective-permute-start | bytes 3047432 | tf_op jit(solution)/shard_map/ppermute | solution.py:327
  85.4 6.4 %collective-permute-start.12 = (f32[256,128]{1,0:T(8,128)S(1)}, f32[256,128]{1,0:T(8,128)S(1)}, u32[]{:S(2)}, u32[]{:S(2)}) collective-permute-start(f32[256,128]{1,0:T(8,128)S(1)} %get-tuple-element.63), channel_id=1, source_target_pairs={{0,1},{1,0},{2,3},{3,2},{4,5},{5,4},{6,7},{7,6},{8,9},{9,8},{10,11... | collective-permute-start | bytes 393224 | tf_op jit(solution)/shard_map/ppermute | solution.py:327
  86.5 11.5 %collective-permute-start.13 = (f32[256,128]{1,0:T(8,128)S(1)}, f32[256,128]{1,0:T(8,128)S(1)}, u32[]{:S(2)}, u32[]{:S(2)}) collective-permute-start(f32[256,128]{1,0:T(8,128)S(1)} %get-tuple-element.65), channel_id=1, source_target_pairs={{0,4},{1,5},{2,6},{3,7},{4,0},{5,1},{6,2},{7,3},{8,12},{9,13},{10,... | collective-permute-start | bytes 393224 | tf_op jit(solution)/shard_map/ppermute | solution.py:327
  87.0 10.9 %collective-permute-start.14 = (f32[256,128]{1,0:T(8,128)S(1)}, f32[256,128]{1,0:T(8,128)S(1)}, u32[]{:S(2)}, u32[]{:S(2)}) collective-permute-start(f32[256,128]{1,0:T(8,128)S(1)} %get-tuple-element.64), channel_id=1, source_target_pairs={{0,5},{1,4},{2,7},{3,6},{4,1},{5,0},{6,3},{7,2},{8,13},{9,12},{10,... | collective-permute-start | bytes 393224 | tf_op jit(solution)/shard_map/ppermute | solution.py:327
  89.0 13.9 %copy-start.5 = (bf16[128,3968]{1,0:T(8,128)(2,1)}, bf16[128,3968]{1,0:T(8,128)(2,1)S(1)}, u32[]{:S(2)}) copy-start(bf16[128,3968]{1,0:T(8,128)(2,1)S(1)} %collective-permute-done.7) | copy-start | bytes 3047428
  89.0 8.9 %collective-permute-start.10 = (f32[256,128]{1,0:T(8,128)S(1)}, f32[256,128]{1,0:T(8,128)S(1)}, u32[]{:S(2)}, u32[]{:S(2)}) collective-permute-start(f32[256,128]{1,0:T(8,128)S(1)} %get-tuple-element.67), channel_id=1, source_target_pairs={{0,5},{1,4},{2,7},{3,6},{4,1},{5,0},{6,3},{7,2},{8,13},{9,12},{10,... | collective-permute-start | bytes 393224 | tf_op jit(solution)/shard_map/ppermute | solution.py:327
  91.8 7.7 %collective-permute-start.8 = (f32[256,128]{1,0:T(8,128)S(1)}, f32[256,128]{1,0:T(8,128)S(1)}, u32[]{:S(2)}, u32[]{:S(2)}) collective-permute-start(f32[256,128]{1,0:T(8,128)S(1)} %get-tuple-element.66), channel_id=1, source_target_pairs={{0,1},{1,0},{2,3},{3,2},{4,5},{5,4},{6,7},{7,6},{8,9},{9,8},{10,11... | collective-permute-start | bytes 393224 | tf_op jit(solution)/shard_map/ppermute | solution.py:327
  97.9 5.0 %collective-permute-start.9 = (f32[256,128]{1,0:T(8,128)S(1)}, f32[256,128]{1,0:T(8,128)S(1)}, u32[]{:S(2)}, u32[]{:S(2)}) collective-permute-start(f32[256,128]{1,0:T(8,128)S(1)} %get-tuple-element.68), channel_id=1, source_target_pairs={{0,4},{1,5},{2,6},{3,7},{4,0},{5,1},{6,2},{7,3},{8,12},{9,13},{10,... | collective-permute-start | bytes 393224 | tf_op jit(solution)/shard_map/ppermute | solution.py:327
  103.0 16.6 %copy-start.8 = (bf16[2,256,128]{2,1,0:T(8,128)(2,1)}, bf16[2,256,128]{2,1,0:T(8,128)(2,1)S(1)}, u32[]{:S(2)}) copy-start(bf16[2,256,128]{2,1,0:T(8,128)(2,1)S(1)} %pad_maximum_fusion.1) | copy-start | bytes 393220
  112.0 0.7 collective-permute-start.30
  112.7 0.7 copy-start.6
  114.7 4.8 %copy-start = (bf16[128,3968]{1,0:T(8,128)(2,1)}, bf16[128,3968]{1,0:T(8,128)(2,1)S(1)}, u32[]{:S(2)}) copy-start(bf16[128,3968]{1,0:T(8,128)(2,1)S(1)} %broadcast_select_fusion.1.refs_0_.refs_1_.refs_2_.refs_3_.refs_4_.refs_10_) | copy-start | bytes 3047428
  119.5 11.0 %collective-permute-start.15 = (f32[2,2,256,128]{3,2,1,0:T(8,128)S(1)}, f32[2,2,256,128]{3,2,1,0:T(8,128)S(1)}, u32[]{:S(2)}, u32[]{:S(2)}) collective-permute-start(f32[2,2,256,128]{3,2,1,0:T(8,128)S(1)} %get-tuple-element.40), channel_id=1, source_target_pairs={{0,2},{1,3},{2,0},{3,1},{4,6},{5,7},{6,4},{7,5},{8,10},{9,11},{10,... | collective-permute-start | bytes 1572872 | tf_op jit(solution)/shard_map/ppermute | solution.py:327
  119.6 15.2 %collective-permute-start.16 = (bf16[2,256,128]{2,1,0:T(8,128)(2,1)}, bf16[2,256,128]{2,1,0:T(8,128)(2,1)S(1)}, u32[]{:S(2)}, u32[]{:S(2)}) collective-permute-start(bf16[2,256,128]{2,1,0:T(8,128)(2,1)} %copy-done.8), channel_id=1, source_target_pairs={{0,1},{1,0},{2,3},{3,2},{4,5},{5,4},{6,7},{7,6},{8,9},{9,8},{10,11... | collective-permute-start | bytes 393224 | tf_op jit(solution)/shard_map/ppermute | solution.py:327
  136.1 4.8 %copy-start.2 = (bf16[128,3968]{1,0:T(8,128)(2,1)}, bf16[128,3968]{1,0:T(8,128)(2,1)S(1)}, u32[]{:S(2)}) copy-start(bf16[128,3968]{1,0:T(8,128)(2,1)S(1)} %broadcast_select_fusion.refs_0_.refs_1_.refs_2_.refs_3_.refs_4_.refs_11_) | copy-start | bytes 3047428
  140.9 51.9 %copy-start.1 = (bf16[128,3968]{1,0:T(8,128)(2,1)S(1)}, bf16[128,3968]{1,0:T(8,128)(2,1)}, u32[]{:S(2)}) copy-start(bf16[128,3968]{1,0:T(8,128)(2,1)} %copy-done) | copy-start | bytes 3047428
  140.9 51.9 %copy-start.3 = (bf16[128,3968]{1,0:T(8,128)(2,1)S(1)}, bf16[128,3968]{1,0:T(8,128)(2,1)}, u32[]{:S(2)}) copy-start(bf16[128,3968]{1,0:T(8,128)(2,1)} %copy-done.2) | copy-start | bytes 3047428
  141.0 12.4 %collective-permute-start.21 = (f32[2,2,256,128]{3,2,1,0:T(8,128)S(1)}, f32[2,2,256,128]{3,2,1,0:T(8,128)S(1)}, u32[]{:S(2)}, u32[]{:S(2)}) collective-permute-start(f32[2,2,256,128]{3,2,1,0:T(8,128)S(1)} %get-tuple-element.44), channel_id=1, source_target_pairs={{0,2},{1,3},{2,0},{3,1},{4,6},{5,7},{6,4},{7,5},{8,10},{9,11},{10,... | collective-permute-start | bytes 1572872 | tf_op jit(solution)/shard_map/ppermute | solution.py:327
  141.1 6.1 %collective-permute-start.17 = (f32[256,128]{1,0:T(8,128)S(1)}, f32[256,128]{1,0:T(8,128)S(1)}, u32[]{:S(2)}, u32[]{:S(2)}) collective-permute-start(f32[256,128]{1,0:T(8,128)S(1)} %get-tuple-element.60), channel_id=1, source_target_pairs={{0,1},{1,0},{2,3},{3,2},{4,5},{5,4},{6,7},{7,6},{8,9},{9,8},{10,11... | collective-permute-start | bytes 393224 | tf_op jit(solution)/shard_map/ppermute | solution.py:327
  142.9 10.4 %collective-permute-start.18 = (f32[256,128]{1,0:T(8,128)S(1)}, f32[256,128]{1,0:T(8,128)S(1)}, u32[]{:S(2)}, u32[]{:S(2)}) collective-permute-start(f32[256,128]{1,0:T(8,128)S(1)} %get-tuple-element.62), channel_id=1, source_target_pairs={{0,4},{1,5},{2,6},{3,7},{4,0},{5,1},{6,2},{7,3},{8,12},{9,13},{10,... | collective-permute-start | bytes 393224 | tf_op jit(solution)/shard_map/ppermute | solution.py:327
  143.4 9.9 %collective-permute-start.19 = (f32[256,128]{1,0:T(8,128)S(1)}, f32[256,128]{1,0:T(8,128)S(1)}, u32[]{:S(2)}, u32[]{:S(2)}) collective-permute-start(f32[256,128]{1,0:T(8,128)S(1)} %get-tuple-element.61), channel_id=1, source_target_pairs={{0,5},{1,4},{2,7},{3,6},{4,1},{5,0},{6,3},{7,2},{8,13},{9,12},{10,... | collective-permute-start | bytes 393224 | tf_op jit(solution)/shard_map/ppermute | solution.py:327
  153.5 5.0 %collective-permute-start.22 = (f32[256,128]{1,0:T(8,128)S(1)}, f32[256,128]{1,0:T(8,128)S(1)}, u32[]{:S(2)}, u32[]{:S(2)}) collective-permute-start(f32[256,128]{1,0:T(8,128)S(1)} %get-tuple-element.57), channel_id=1, source_target_pairs={{0,1},{1,0},{2,3},{3,2},{4,5},{5,4},{6,7},{7,6},{8,9},{9,8},{10,11... | collective-permute-start | bytes 393224 | tf_op jit(solution)/shard_map/ppermute | solution.py:327
  153.6 9.0 %collective-permute-start.23 = (f32[256,128]{1,0:T(8,128)S(1)}, f32[256,128]{1,0:T(8,128)S(1)}, u32[]{:S(2)}, u32[]{:S(2)}) collective-permute-start(f32[256,128]{1,0:T(8,128)S(1)} %get-tuple-element.59), channel_id=1, source_target_pairs={{0,4},{1,5},{2,6},{3,7},{4,0},{5,1},{6,2},{7,3},{8,12},{9,13},{10,... | collective-permute-start | bytes 393224 | tf_op jit(solution)/shard_map/ppermute | solution.py:327
  153.8 8.8 %collective-permute-start.24 = (f32[256,128]{1,0:T(8,128)S(1)}, f32[256,128]{1,0:T(8,128)S(1)}, u32[]{:S(2)}, u32[]{:S(2)}) collective-permute-start(f32[256,128]{1,0:T(8,128)S(1)} %get-tuple-element.58), channel_id=1, source_target_pairs={{0,5},{1,4},{2,7},{3,6},{4,1},{5,0},{6,3},{7,2},{8,13},{9,12},{10,... | collective-permute-start | bytes 393224 | tf_op jit(solution)/shard_map/ppermute | solution.py:327
  162.6 7.7 %collective-permute-start.25 = (bf16[2,256,128]{2,1,0:T(8,128)(2,1)S(1)}, bf16[2,256,128]{2,1,0:T(8,128)(2,1)S(1)}, u32[]{:S(2)}, u32[]{:S(2)}) collective-permute-start(bf16[2,256,128]{2,1,0:T(8,128)(2,1)S(1)} %pad_maximum_fusion.2), channel_id=1, source_target_pairs={{0,0},{1,16},{2,2},{3,18},{4,4},{5,20},{6,6},{7,22},{8,8},{9,24},{... | collective-permute-start | bytes 393224 | tf_op jit(solution)/shard_map/ppermute | solution.py:327
  163.3 7.0 %collective-permute-start.26 = (bf16[2,256,128]{2,1,0:T(8,128)(2,1)S(1)}, bf16[2,256,128]{2,1,0:T(8,128)(2,1)S(1)}, u32[]{:S(2)}, u32[]{:S(2)}) collective-permute-start(bf16[2,256,128]{2,1,0:T(8,128)(2,1)S(1)} %pad_maximum_fusion.2), channel_id=1, source_target_pairs={{0,8},{1,24},{2,10},{3,26},{4,12},{5,28},{6,14},{7,30},{8,0},{9,16... | collective-permute-start | bytes 393224 | tf_op jit(solution)/shard_map/ppermute | solution.py:327
  163.4 9.2 %collective-permute-start.27 = (bf16[2,256,128]{2,1,0:T(8,128)(2,1)S(1)}, bf16[2,256,128]{2,1,0:T(8,128)(2,1)S(1)}, u32[]{:S(2)}, u32[]{:S(2)}) collective-permute-start(bf16[2,256,128]{2,1,0:T(8,128)(2,1)S(1)} %pad_maximum_fusion.2), channel_id=1, source_target_pairs={{0,16},{1,0},{2,18},{3,2},{4,20},{5,4},{6,22},{7,6},{8,24},{9,8},{... | collective-permute-start | bytes 393224 | tf_op jit(solution)/shard_map/ppermute | solution.py:327
  168.6 8.2 %collective-permute-start.28 = (bf16[2,256,128]{2,1,0:T(8,128)(2,1)S(1)}, bf16[2,256,128]{2,1,0:T(8,128)(2,1)S(1)}, u32[]{:S(2)}, u32[]{:S(2)}) collective-permute-start(bf16[2,256,128]{2,1,0:T(8,128)(2,1)S(1)} %pad_maximum_fusion.2), channel_id=1, source_target_pairs={{0,24},{1,8},{2,26},{3,10},{4,28},{5,12},{6,30},{7,14},{8,16},{9,0... | collective-permute-start | bytes 393224 | tf_op jit(solution)/shard_map/ppermute | solution.py:327
  168.6 8.2 %collective-permute-start.29 = (bf16[2,256,128]{2,1,0:T(8,128)(2,1)S(1)}, bf16[2,256,128]{2,1,0:T(8,128)(2,1)S(1)}, u32[]{:S(2)}, u32[]{:S(2)}) collective-permute-start(bf16[2,256,128]{2,1,0:T(8,128)(2,1)S(1)} %pad_maximum_fusion.2), channel_id=1, source_target_pairs={{0,1},{1,0},{2,3},{3,2},{4,5},{5,4},{6,7},{7,6},{8,9},{9,8},{10,11... | collective-permute-start | bytes 393224 | tf_op jit(solution)/shard_map/ppermute | solution.py:327
  176.8 0.7 copy-start.7
  177.6 13.2 %collective-permute-start.31 = (bf16[4,2,256,128]{3,2,1,0:T(8,128)(2,1)S(1)}, bf16[4,2,256,128]{3,2,1,0:T(8,128)(2,1)S(1)}, u32[]{:S(2)}, u32[]{:S(2)}) collective-permute-start(bf16[4,2,256,128]{3,2,1,0:T(8,128)(2,1)S(1)} %pad_maximum_fusion.refs_16_.refs_20_), channel_id=1, source_target_pairs={{0,4},{1,5},{2,6},{3,7},{4,0},{5,1},{6,2},{7,3},{8,12},{9,13},{10,... | collective-permute-start | bytes 1572872 | tf_op jit(solution)/shard_map/ppermute | solution.py:327
  178.6 13.2 %collective-permute-start.32 = (bf16[4,2,256,128]{3,2,1,0:T(8,128)(2,1)S(1)}, bf16[4,2,256,128]{3,2,1,0:T(8,128)(2,1)}, u32[]{:S(2)}, u32[]{:S(2)}) collective-permute-start(bf16[4,2,256,128]{3,2,1,0:T(8,128)(2,1)S(1)} %pad_maximum_fusion.refs_16_.refs_20_), channel_id=1, source_target_pairs={{0,2},{1,3},{2,0},{3,1},{4,6},{5,7},{6,4},{7,5},{8,10},{9,11},{10,... | collective-permute-start | bytes 1572872 | tf_op jit(solution)/shard_map/ppermute | solution.py:327
  190.8 2.0 collective-permute-start.33
  192.8 1.6 copy-start.4
Sparse Core Ops, SparseCore 0:
  113.5 54.4 all-gather.2

commit v14 on v13

--- a/solution.py
+++ b/solution.py
@@ -374,11 +374,11 @@
     owns = [coefficients(units[0], (across, outward)), coefficients(units[1])]
     own_a = jnp.stack(owns)
     mate_a = mate(own_a)
-    own_a, far = lax.optimization_barrier((own_a, far))
+    owns.append(coefficients(units[2]))
+    own_a, far, mate_a, owns[2] = lax.optimization_barrier((own_a, far, mate_a, owns[2]))
     right_a = lax.all_gather(share(own_a, 0), ("z", "y", "c"), axis=0)
-    owns.append(coefficients(units[2], mate_a))
     units.append(jnp.where(inner, middle, far))
-    owns.append(coefficients(units[3], owns[2]))
+    owns.append(coefficients(units[3]))
     own_b = jnp.stack(owns[2:])
     shares = [share(own_b, m) for m in range(nz)]
     shares, mate_b, right_a = lax.optimization_barrier((shares, mate(own_b), right_a))

time: 209 us -> 214 us (1.024)
    all_gather x1, waiting for transfers between devices: 0.01 us -> 14.9 us  [fast(): right_a = lax.all_gather(share(own_a, 0), ('z', 'y', 'c'), axis=0)]
    ppermute x34, waiting for transfers between devices: 92.6 us -> 79.8 us  [send(): lax.ppermute(array, AXES, [(source, number[to]) for source, to in pairs i...]
where the time goes in v14:
time: 214 us; the launch traced here: 213 us
  waiting for transfers between devices  106 us (50%)
  starting transfers between devices  50.4 us (24%)
  Pallas kernels  32 us (15%)
  between operations  13.7 us (6%)
  local copies, waits for them, and re-layouts  6.83 us (3%)
  other arithmetic  4.19 us (2%)
    ppermute x34, waiting for transfers between devices, send(): lax.ppermute(array, AXES, [(source, number[to]) for source, to in pairs i...  79.8 us
    ppermute x34, starting transfers between devices, send(): lax.ppermute(array, AXES, [(source, number[to]) for source, to in pairs i...  45.2 us
    pallas_call x4, Pallas kernels, project(): pl.pallas_call(functools.partial(project_kernel, segs, val_count, cond_co...  21.1 us
    all_gather x1, waiting for transfers between devices, fast(): right_a = lax.all_gather(share(own_a, 0), ('z', 'y', 'c'), axis=0)  14.9 us
    all_to_all x1, waiting for transfers between devices, local(): unit = lax.all_to_all(packed, ('y', 'c', 'x'), 0, 0, tiled=True)  11.3 us
    pallas_call x1, Pallas kernels, make_chi(): pl.pallas_call(functools.partial(chi_kernel, early, late, n_freq, factor)...  6.86 us
    all_to_all x1, starting transfers between devices, local(): unit = lax.all_to_all(packed, ('y', 'c', 'x'), 0, 0, tiled=True)  5.17 us
  transfers between devices with their start and end apart: 36, of which 18 were waited for; matrix products, arithmetic and copies ran while one was open for 4% of the time, Pallas kernels for 10%

profile of v14, /device:TPU:0, one launch (start us, length us, event | category | flops | bytes accessed | tf_op | source)
XLA Modules:
  0.0 213.1 jit_solution(3871146700369278905)
XLA Ops:
  6.5 4.0 %pack.1 = bf16[8,16,3968]{2,1,0:T(8,128)(2,1)} custom-call(f32[4]{0:T(128)} %val_energy.1, f32[16]{0:T(128)} %cond_energy.1, s32[64]{0:T(128)} %val_slot.1, s32[64]{0:T(128)} %cond_slot.1, f32[4]{0:T(128)} %frequencies.1, bf16[16,24576]{1,0:T(8,128)(2,1)} %refs_1_.1, bf16[16,24576]{1,0:T(8,128)(2,1)} %refs_1_.1, bf16[4,24576]{1,0:T(4,128)(2,1)} %refs_3_.1, ...), custom_call_target="tpu_custom_call" | custom-call | tf_op jit(solution)/shard_map/pack/pallas_call | solution.py:77
  10.5 5.2 %all-to-all-start = ((bf16[8,16,3968]{2,1,0:T(8,128)(2,1)}), bf16[8,16,3968]{2,1,0:T(8,128)(2,1)}, u32[]{:S(2)}, u32[]{:S(2)}) async-start(bf16[8,16,3968]{2,1,0:T(8,128)(2,1)} %pack.1), calls=%async_computation | async-start | bytes 2031616 | tf_op jit(solution)/shard_map/all_to_all | solution.py:480
  15.8 3.3 %constant_dynamic-slice_fusion = (bf16[3072,128]{1,0:T(8,128)(2,1)}, bf16[3072,128]{1,0:T(8,128)(2,1)}, bf16[3072,128]{1,0:T(8,128)(2,1)S(1)}, bf16[3072,128]{1,0:T(8,128)(2,1)}) fusion(bf16[12288,128]{1,0:T(8,128)(2,1)} %param.14, s32[]{:T(128)S(6)} %select_n.27, s32[]{:T(128)S(6)} %select_n.25, s32[]{:T(128)S(6)} %select_n.24, s32[]{:T(128)S(6)} %select_n.26), kind=kLoop, calls=%fused_computation.40 | loop fusion | bytes 6291472 | tf_op jit(solution)/shard_map/dynamic_slice | solution.py:337
  19.1 11.3 %all-to-all-done = bf16[8,16,3968]{2,1,0:T(8,128)(2,1)} async-done(((bf16[8,16,3968]{2,1,0:T(8,128)(2,1)}), bf16[8,16,3968]{2,1,0:T(8,128)(2,1)}, u32[]{:S(2)}, u32[]{:S(2)}) %all-to-all-start) | async-done | bytes 1015840 | tf_op jit(solution)/shard_map/all_to_all | solution.py:480
  30.4 2.0 collective-permute-start.4
  32.4 1.6 collective-permute-start.6
  34.6 1.3 collective-permute-start.2
  35.8 19.1 %collective-permute-done.4.refs_0_.refs_1_.refs_2_.refs_3_.refs_4_.refs_9_ = bf16[128,3968]{1,0:T(8,128)(2,1)} collective-permute-done((bf16[128,3968]{1,0:T(8,128)(2,1)}, bf16[128,3968]{1,0:T(8,128)(2,1)}, u32[]{:S(2)}, u32[]{:S(2)}) %collective-permute-start.4) | collective-permute-done | bytes 1015840 | tf_op jit(solution)/shard_map/ppermute | solution.py:327
  55.0 1.6 collective-permute-start.5
  56.6 1.3 collective-permute-start.7
  57.9 12.7 %collective-permute-done.2.refs_8_.refs_12_.refs_16_.refs_20_ = bf16[3072,128]{1,0:T(8,128)(2,1)S(1)} collective-permute-done((bf16[3072,128]{1,0:T(8,128)(2,1)}, bf16[3072,128]{1,0:T(8,128)(2,1)S(1)}, u32[]{:S(2)}, u32[]{:S(2)}) %collective-permute-start.2) | collective-permute-done | bytes 786464 | tf_op jit(solution)/shard_map/ppermute | solution.py:327
  70.6 6.1 %project.5 = (f32[2,2,256,128]{3,2,1,0:T(8,128)S(1)}, f32[2,2,256,128]{3,2,1,0:T(8,128)}) custom-call(s32[1]{0:T(128)} %bitcast.4.place, bf16[128,3968]{1,0:T(8,128)(2,1)} %collective-permute-done.4.refs_0_.refs_1_.refs_2_.refs_3_.refs_4_.refs_9_, bf16[128,3968]{1,0:T(8,128)(2,1)} %collective-permute-done.4.refs_0_.refs_1_.refs_2_.refs_3_.refs_4_.refs_9_, ...), custom_call_target="tpu_custom_call" | custom-call | flops 1610612736 | bytes 4161536 | tf_op jit(solution)/shard_map/project/pallas_call | solution.py:187
  78.2 5.4 %project.4 = (f32[2,2,256,128]{3,2,1,0:T(8,128)S(1)}, f32[2,2,256,128]{3,2,1,0:T(8,128)S(1)}) custom-call(s32[1]{0:T(128)} %bitcast.4.place, bf16[128,3968]{1,0:T(8,128)(2,1)} %bitcast.5.refs_0_.refs_1_.refs_2_.refs_3_.refs_4_.refs_8_, bf16[128,3968]{1,0:T(8,128)(2,1)} %bitcast.5.refs_0_.refs_1_.refs_2_.refs_3_.refs_4_.refs_8_, ...), custom_call_target="tpu_custom_call" | custom-call | flops 1610612736 | bytes 4161536 | tf_op jit(solution)/shard_map/project/pallas_call | solution.py:187
  83.7 1.1 add.72
  84.9 1.1 collective-permute-start.14
  85.9 1.5 collective-permute-start.13
  87.4 1.0 collective-permute-start.12
  88.4 1.3 broadcast_select_fusion.1.refs_0_.refs_1_.refs_2_.refs_3_.refs_4_.refs_10_
  89.8 4.8 %project.6 = (f32[2,2,256,128]{3,2,1,0:T(8,128)S(1)}, f32[2,2,256,128]{3,2,1,0:T(8,128)S(1)}) custom-call(s32[1]{0:T(128)} %bitcast.4.place, bf16[128,3968]{1,0:T(8,128)(2,1)S(1)} %broadcast_select_fusion.1.refs_0_.refs_1_.refs_2_.refs_3_.refs_4_.refs_10_, bf16[128,3968]{1,0:T(8,128)(2,1)S(1)} %broadcast_select_fusion.1.refs_0_.refs_1_.refs_2_.refs_3_.refs_4_.refs_10_, ...), custom_call_target="tpu_custom_call" | custom-call | flops 1610612736 | bytes 4161536 | tf_op jit(solution)/shard_map/project/pallas_call | solution.py:187
  94.8 1.3 collective-permute-start.15
  96.1 1.1 collective-permute-start.10
  97.2 1.5 collective-permute-start.9
  98.7 1.0 collective-permute-start.8
  99.8 1.1 collective-permute-start.20
  100.8 2.6 %collective-permute-done.10 = f32[256,128]{1,0:T(8,128)S(1)} collective-permute-done((f32[256,128]{1,0:T(8,128)S(1)}, f32[256,128]{1,0:T(8,128)S(1)}, u32[]{:S(2)}, u32[]{:S(2)}) %collective-permute-start.10) | collective-permute-done | bytes 131104 | tf_op jit(solution)/shard_map/ppermute | solution.py:327
  103.9 2.2 %collective-permute-done.9 = f32[256,128]{1,0:T(8,128)S(1)} collective-permute-done((f32[256,128]{1,0:T(8,128)S(1)}, f32[256,128]{1,0:T(8,128)S(1)}, u32[]{:S(2)}, u32[]{:S(2)}) %collective-permute-start.9) | collective-permute-done | bytes 131104 | tf_op jit(solution)/shard_map/ppermute | solution.py:327
  106.2 1.1 collective-permute-start.18
  108.8 2.5 %collective-permute-done.19 = f32[256,128]{1,0:T(8,128)S(1)} collective-permute-done((f32[256,128]{1,0:T(8,128)S(1)}, f32[256,128]{1,0:T(8,128)S(1)}, u32[]{:S(2)}, u32[]{:S(2)}) %collective-permute-start.19) | collective-permute-done | bytes 131104 | tf_op jit(solution)/shard_map/ppermute | solution.py:327
  111.2 1.1 collective-permute-done.18
  112.4 1.4 collective-permute-done.16
  113.7 9.3 %collective-permute-done.15 = bf16[128,3968]{1,0:T(8,128)(2,1)} collective-permute-done((bf16[128,3968]{1,0:T(8,128)(2,1)}, bf16[128,3968]{1,0:T(8,128)(2,1)}, u32[]{:S(2)}, u32[]{:S(2)}) %collective-permute-start.15) | collective-permute-done | bytes 1015840 | tf_op jit(solution)/shard_map/ppermute | solution.py:327
  123.0 1.3 collective-permute-start.30
  124.4 1.3 broadcast_select_fusion.refs_0_.refs_1_.refs_2_.refs_3_.refs_4_.refs_11_
  125.7 4.8 %project.7 = (f32[2,2,256,128]{3,2,1,0:T(8,128)S(1)}, f32[2,2,256,128]{3,2,1,0:T(8,128)S(1)}) custom-call(s32[1]{0:T(128)} %bitcast.4.place, bf16[128,3968]{1,0:T(8,128)(2,1)S(1)} %broadcast_select_fusion.refs_0_.refs_1_.refs_2_.refs_3_.refs_4_.refs_11_, bf16[128,3968]{1,0:T(8,128)(2,1)S(1)} %broadcast_select_fusion.refs_0_.refs_1_.refs_2_.refs_3_.refs_4_.refs_11_, ...), custom_call_target="tpu_custom_call" | custom-call | flops 1610612736 | bytes 4161536 | tf_op jit(solution)/shard_map/project/pallas_call | solution.py:187
  130.6 1.9 collective-permute-done.21
  132.6 10.6 %collective-permute-start.24 = (f32[256,128]{1,0:T(8,128)S(1)}, f32[256,128]{1,0:T(8,128)S(1)}, u32[]{:S(2)}, u32[]{:S(2)}) collective-permute-start(f32[256,128]{1,0:T(8,128)S(1)} %get-tuple-element.58), channel_id=1, source_target_pairs={{0,5},{1,4},{2,7},{3,6},{4,1},{5,0},{6,3},{7,2},{8,13},{9,12},{10,... | collective-permute-start | bytes 393224 | tf_op jit(solution)/shard_map/ppermute | solution.py:327
  143.2 1.5 collective-permute-start.23
  144.7 2.4 %collective-permute-done.24 = f32[256,128]{1,0:T(8,128)S(1)} collective-permute-done((f32[256,128]{1,0:T(8,128)S(1)}, f32[256,128]{1,0:T(8,128)S(1)}, u32[]{:S(2)}, u32[]{:S(2)}) %collective-permute-start.24) | collective-permute-done | bytes 131104 | tf_op jit(solution)/shard_map/ppermute | solution.py:327
  147.1 2.7 %collective-permute-done.23 = f32[256,128]{1,0:T(8,128)S(1)} collective-permute-done((f32[256,128]{1,0:T(8,128)S(1)}, f32[256,128]{1,0:T(8,128)S(1)}, u32[]{:S(2)}, u32[]{:S(2)}) %collective-permute-start.23) | collective-permute-done | bytes 131104 | tf_op jit(solution)/shard_map/ppermute | solution.py:327
  150.7 6.8 %collective-permute-start.27 = (bf16[2,256,128]{2,1,0:T(8,128)(2,1)S(1)}, bf16[2,256,128]{2,1,0:T(8,128)(2,1)S(1)}, u32[]{:S(2)}, u32[]{:S(2)}) collective-permute-start(bf16[2,256,128]{2,1,0:T(8,128)(2,1)S(1)} %pad_maximum_fusion.2), channel_id=1, source_target_pairs={{0,16},{1,0},{2,18},{3,2},{4,20},{5,4},{6,22},{7,6},{8,24},{9,8},{... | collective-permute-start | bytes 393224 | tf_op jit(solution)/shard_map/ppermute | solution.py:327
  157.8 2.0 collective-permute-start.29
  159.9 1.6 collective-permute-done.27
  161.5 5.2 %collective-permute-done.28 = bf16[2,256,128]{2,1,0:T(8,128)(2,1)S(1)} collective-permute-done((bf16[2,256,128]{2,1,0:T(8,128)(2,1)S(1)}, bf16[2,256,128]{2,1,0:T(8,128)(2,1)S(1)}, u32[]{:S(2)}, u32[]{:S(2)}) %collective-permute-start.28) | collective-permute-done | bytes 131104 | tf_op jit(solution)/shard_map/ppermute | solution.py:327
  166.7 14.9 %all-gather.3.cloned.1.call-done = bf16[32,256,128]{2,1,0:T(8,128)(2,1)} async-done(((bf16[2,256,128]{2,1,0:T(8,128)(2,1)}), bf16[32,256,128]{2,1,0:T(8,128)(2,1)}) %all-gather.3.cloned.1.call-update) | async-done | bytes 2097168 | tf_op jit(solution)/shard_map/all_gather | solution.py:379
  182.3 13.5 %collective-permute-done.31.refs_17_.refs_21_ = bf16[4,2,256,128]{3,2,1,0:T(8,128)(2,1)S(1)} collective-permute-done((bf16[4,2,256,128]{3,2,1,0:T(8,128)(2,1)S(1)}, bf16[4,2,256,128]{3,2,1,0:T(8,128)(2,1)S(1)}, u32[]{:S(2)}, u32[]{:S(2)}) %collective-permute-start.31) | collective-permute-done | bytes 524320 | tf_op jit(solution)/shard_map/ppermute | solution.py:327
  196.8 1.0 collective-permute-done.33.refs_19_.refs_23_
  197.9 1.6 copy-done.4
  199.4 6.9 %chi.1 = f32[128,4,1024]{2,1,0:T(4,128)} custom-call(s32[5]{0:T(128)S(1)} %stack.56.scalars, bf16[256,128]{1,0:T(8,128)(2,1)S(1)} %fusion.14.refs_0_, bf16[256,128]{1,0:T(8,128)(2,1)S(1)} %fusion.11.refs_1_, bf16[256,128]{1,0:T(8,128)(2,1)S(1)} %fusion.7.refs_2_, bf16[256,128]{1,0:T(8,128)(2,1)S(1)} %fusion.3.refs_3_, ...), custom_call_target="tpu_custom_call" | custom-call | flops 2147483648 | bytes 6291456 | tf_op jit(solution)/shard_map/chi/pallas_call | solution.py:281
  (66 shorter events, 7.5 us)
Async XLA Ops:
  10.5 19.9 %all-to-all-start = ((bf16[8,16,3968]{2,1,0:T(8,128)(2,1)}), bf16[8,16,3968]{2,1,0:T(8,128)(2,1)}, u32[]{:S(2)}, u32[]{:S(2)}) async-start(bf16[8,16,3968]{2,1,0:T(8,128)(2,1)} %pack.1), calls=%async_computation | async-start | bytes 2031616 | tf_op jit(solution)/shard_map/all_to_all | solution.py:480
  15.7 165.9 %all-gather.3.cloned.1.call-start = ((), (), s32[]{:S(2)}) async-start(), calls=%async_computation.1 | async-start | bytes 2228224 | tf_op jit(solution)/shard_map/all_gather | solution.py:379
  30.4 24.6 %collective-permute-start.4 = (bf16[128,3968]{1,0:T(8,128)(2,1)}, bf16[128,3968]{1,0:T(8,128)(2,1)}, u32[]{:S(2)}, u32[]{:S(2)}) collective-permute-start(bf16[128,3968]{1,0:T(8,128)(2,1)} %bitcast.5.refs_0_.refs_1_.refs_2_.refs_3_.refs_4_.refs_8_), channel_id=1, source_target_pairs={{0,8},{1,9},{2,10},{3,11},{4,12},{5,13},{6,14},{7,15},{8,0},{9,1},... | collective-permute-start | bytes 3047432 | tf_op jit(solution)/shard_map/ppermute | solution.py:327
  32.4 24.2 %collective-permute-start.6 = (bf16[128,3968]{1,0:T(8,128)(2,1)}, bf16[128,3968]{1,0:T(8,128)(2,1)}, u32[]{:S(2)}, u32[]{:S(2)}) collective-permute-start(bf16[128,3968]{1,0:T(8,128)(2,1)} %bitcast.5.refs_0_.refs_1_.refs_2_.refs_3_.refs_4_.refs_8_), channel_id=1, source_target_pairs={{8,16},{9,17},{10,18},{11,19},{12,20},{13,21},{14,22},{15,23},{16,... | collective-permute-start | bytes 3047432 | tf_op jit(solution)/shard_map/ppermute | solution.py:327
  34.0 23.9 %collective-permute-start = (bf16[3072,128]{1,0:T(8,128)(2,1)}, bf16[3072,128]{1,0:T(8,128)(2,1)S(1)}, u32[]{:S(2)}, u32[]{:S(2)}) collective-permute-start(bf16[3072,128]{1,0:T(8,128)(2,1)} %get-tuple-element.31), channel_id=1, source_target_pairs={{0,2},{1,3},{2,0},{3,1},{4,6},{5,7},{6,4},{7,5},{8,10},{9,11},{10,... | collective-permute-start | bytes 2359304 | tf_op jit(solution)/shard_map/ppermute | solution.py:327
  34.0 23.9 %collective-permute-start.1 = (bf16[3072,128]{1,0:T(8,128)(2,1)}, bf16[3072,128]{1,0:T(8,128)(2,1)S(1)}, u32[]{:S(2)}, u32[]{:S(2)}) collective-permute-start(bf16[3072,128]{1,0:T(8,128)(2,1)} %get-tuple-element.32), channel_id=1, source_target_pairs={{0,4},{1,5},{2,6},{3,7},{4,0},{5,1},{6,2},{7,3},{8,12},{9,13},{10,... | collective-permute-start | bytes 2359304 | tf_op jit(solution)/shard_map/ppermute | solution.py:327
  34.6 36.0 %collective-permute-start.2 = (bf16[3072,128]{1,0:T(8,128)(2,1)}, bf16[3072,128]{1,0:T(8,128)(2,1)S(1)}, u32[]{:S(2)}, u32[]{:S(2)}) collective-permute-start(bf16[3072,128]{1,0:T(8,128)(2,1)} %get-tuple-element.33), channel_id=1, source_target_pairs={{0,6},{1,7},{2,4},{3,5},{4,2},{5,3},{6,0},{7,1},{8,14},{9,15},{10,... | collective-permute-start | bytes 2359304 | tf_op jit(solution)/shard_map/ppermute | solution.py:327
  55.0 32.4 %collective-permute-start.5 = (bf16[128,3968]{1,0:T(8,128)(2,1)}, bf16[128,3968]{1,0:T(8,128)(2,1)}, u32[]{:S(2)}, u32[]{:S(2)}) collective-permute-start(bf16[128,3968]{1,0:T(8,128)(2,1)} %collective-permute-done.4.refs_0_.refs_1_.refs_2_.refs_3_.refs_4_.refs_9_), channel_id=1, source_target_pairs={{8,16},{9,17},{10,18},{11,19},{12,20},{13,21},{14,22},{15,23},{16,... | collective-permute-start | bytes 3047432 | tf_op jit(solution)/shard_map/ppermute | solution.py:327
  56.6 31.9 %collective-permute-start.7 = (bf16[128,3968]{1,0:T(8,128)(2,1)}, bf16[128,3968]{1,0:T(8,128)(2,1)}, u32[]{:S(2)}, u32[]{:S(2)}) collective-permute-start(bf16[128,3968]{1,0:T(8,128)(2,1)} %collective-permute-done.6), channel_id=1, source_target_pairs={{8,0},{9,1},{10,2},{11,3},{12,4},{13,5},{14,6},{15,7},{16,24},{17,... | collective-permute-start | bytes 3047432 | tf_op jit(solution)/shard_map/ppermute | solution.py:327
  76.8 0.8 copy-start.5
  77.6 6.2 %collective-permute-start.11 = (f32[2,2,256,128]{3,2,1,0:T(8,128)}, f32[2,2,256,128]{3,2,1,0:T(8,128)}, u32[]{:S(2)}, u32[]{:S(2)}) collective-permute-start(f32[2,2,256,128]{3,2,1,0:T(8,128)} %get-tuple-element.38), channel_id=1, source_target_pairs={{0,2},{1,3},{2,0},{3,1},{4,6},{5,7},{6,4},{7,5},{8,10},{9,11},{10,... | collective-permute-start | bytes 1572872 | tf_op jit(solution)/shard_map/ppermute | solution.py:327
  78.2 5.6 %copy-start.6 = (f32[2,2,256,128]{3,2,1,0:T(8,128)S(1)}, f32[2,2,256,128]{3,2,1,0:T(8,128)}, u32[]{:S(2)}) copy-start(f32[2,2,256,128]{3,2,1,0:T(8,128)} %copy-done.5) | copy-start | bytes 1572868
  83.6 11.0 %collective-permute-start.3 = (f32[2,2,256,128]{3,2,1,0:T(8,128)S(1)}, f32[2,2,256,128]{3,2,1,0:T(8,128)S(1)}, u32[]{:S(2)}, u32[]{:S(2)}) collective-permute-start(f32[2,2,256,128]{3,2,1,0:T(8,128)S(1)} %get-tuple-element.35), channel_id=1, source_target_pairs={{0,2},{1,3},{2,0},{3,1},{4,6},{5,7},{6,4},{7,5},{8,10},{9,11},{10,... | collective-permute-start | bytes 1572872 | tf_op jit(solution)/shard_map/ppermute | solution.py:327
  84.9 9.8 %collective-permute-start.14 = (f32[256,128]{1,0:T(8,128)S(1)}, f32[256,128]{1,0:T(8,128)S(1)}, u32[]{:S(2)}, u32[]{:S(2)}) collective-permute-start(f32[256,128]{1,0:T(8,128)S(1)} %get-tuple-element.64), channel_id=1, source_target_pairs={{0,5},{1,4},{2,7},{3,6},{4,1},{5,0},{6,3},{7,2},{8,13},{9,12},{10,... | collective-permute-start | bytes 393224 | tf_op jit(solution)/shard_map/ppermute | solution.py:327
  85.9 8.8 %collective-permute-start.13 = (f32[256,128]{1,0:T(8,128)S(1)}, f32[256,128]{1,0:T(8,128)S(1)}, u32[]{:S(2)}, u32[]{:S(2)}) collective-permute-start(f32[256,128]{1,0:T(8,128)S(1)} %get-tuple-element.65), channel_id=1, source_target_pairs={{0,4},{1,5},{2,6},{3,7},{4,0},{5,1},{6,2},{7,3},{8,12},{9,13},{10,... | collective-permute-start | bytes 393224 | tf_op jit(solution)/shard_map/ppermute | solution.py:327
  87.4 7.3 %collective-permute-start.12 = (f32[256,128]{1,0:T(8,128)S(1)}, f32[256,128]{1,0:T(8,128)S(1)}, u32[]{:S(2)}, u32[]{:S(2)}) collective-permute-start(f32[256,128]{1,0:T(8,128)S(1)} %get-tuple-element.63), channel_id=1, source_target_pairs={{0,1},{1,0},{2,3},{3,2},{4,5},{5,4},{6,7},{7,6},{8,9},{9,8},{10,11... | collective-permute-start | bytes 393224 | tf_op jit(solution)/shard_map/ppermute | solution.py:327
  89.8 4.8 %copy-start = (bf16[128,3968]{1,0:T(8,128)(2,1)}, bf16[128,3968]{1,0:T(8,128)(2,1)S(1)}, u32[]{:S(2)}) copy-start(bf16[128,3968]{1,0:T(8,128)(2,1)S(1)} %broadcast_select_fusion.1.refs_0_.refs_1_.refs_2_.refs_3_.refs_4_.refs_10_) | copy-start | bytes 3047428
  94.6 5.1 %collective-permute-start.17 = (f32[2,2,256,128]{3,2,1,0:T(8,128)S(1)}, f32[2,2,256,128]{3,2,1,0:T(8,128)S(1)}, u32[]{:S(2)}, u32[]{:S(2)}) collective-permute-start(f32[2,2,256,128]{3,2,1,0:T(8,128)S(1)} %get-tuple-element.40), channel_id=1, source_target_pairs={{0,2},{1,3},{2,0},{3,1},{4,6},{5,7},{6,4},{7,5},{8,10},{9,11},{10,... | collective-permute-start | bytes 1572872 | tf_op jit(solution)/shard_map/ppermute | solution.py:327
  94.8 28.2 %collective-permute-start.15 = (bf16[128,3968]{1,0:T(8,128)(2,1)}, bf16[128,3968]{1,0:T(8,128)(2,1)}, u32[]{:S(2)}, u32[]{:S(2)}) collective-permute-start(bf16[128,3968]{1,0:T(8,128)(2,1)} %collective-permute-done.5), channel_id=1, source_target_pairs={{8,0},{9,1},{10,2},{11,3},{12,4},{13,5},{14,6},{15,7},{16,24},{17,... | collective-permute-start | bytes 3047432 | tf_op jit(solution)/shard_map/ppermute | solution.py:327
  96.1 7.3 %collective-permute-start.10 = (f32[256,128]{1,0:T(8,128)S(1)}, f32[256,128]{1,0:T(8,128)S(1)}, u32[]{:S(2)}, u32[]{:S(2)}) collective-permute-start(f32[256,128]{1,0:T(8,128)S(1)} %get-tuple-element.67), channel_id=1, source_target_pairs={{0,5},{1,4},{2,7},{3,6},{4,1},{5,0},{6,3},{7,2},{8,13},{9,12},{10,... | collective-permute-start | bytes 393224 | tf_op jit(solution)/shard_map/ppermute | solution.py:327
  97.2 9.0 %collective-permute-start.9 = (f32[256,128]{1,0:T(8,128)S(1)}, f32[256,128]{1,0:T(8,128)S(1)}, u32[]{:S(2)}, u32[]{:S(2)}) collective-permute-start(f32[256,128]{1,0:T(8,128)S(1)} %get-tuple-element.68), channel_id=1, source_target_pairs={{0,4},{1,5},{2,6},{3,7},{4,0},{5,1},{6,2},{7,3},{8,12},{9,13},{10,... | collective-permute-start | bytes 393224 | tf_op jit(solution)/shard_map/ppermute | solution.py:327
  98.7 8.6 %collective-permute-start.8 = (f32[256,128]{1,0:T(8,128)S(1)}, f32[256,128]{1,0:T(8,128)S(1)}, u32[]{:S(2)}, u32[]{:S(2)}) collective-permute-start(f32[256,128]{1,0:T(8,128)S(1)} %get-tuple-element.66), channel_id=1, source_target_pairs={{0,1},{1,0},{2,3},{3,2},{4,5},{5,4},{6,7},{7,6},{8,9},{9,8},{10,11... | collective-permute-start | bytes 393224 | tf_op jit(solution)/shard_map/ppermute | solution.py:327
  99.8 9.0 %collective-permute-start.20 = (f32[256,128]{1,0:T(8,128)S(1)}, f32[256,128]{1,0:T(8,128)S(1)}, u32[]{:S(2)}, u32[]{:S(2)}) collective-permute-start(f32[256,128]{1,0:T(8,128)S(1)} %get-tuple-element.61), channel_id=1, source_target_pairs={{0,5},{1,4},{2,7},{3,6},{4,1},{5,0},{6,3},{7,2},{8,13},{9,12},{10,... | collective-permute-start | bytes 393224 | tf_op jit(solution)/shard_map/ppermute | solution.py:327
  103.4 7.8 %collective-permute-start.19 = (f32[256,128]{1,0:T(8,128)S(1)}, f32[256,128]{1,0:T(8,128)S(1)}, u32[]{:S(2)}, u32[]{:S(2)}) collective-permute-start(f32[256,128]{1,0:T(8,128)S(1)} %get-tuple-element.62), channel_id=1, source_target_pairs={{0,4},{1,5},{2,6},{3,7},{4,0},{5,1},{6,2},{7,3},{8,12},{9,13},{10,... | collective-permute-start | bytes 393224 | tf_op jit(solution)/shard_map/ppermute | solution.py:327
  106.2 6.2 %collective-permute-start.18 = (f32[256,128]{1,0:T(8,128)S(1)}, f32[256,128]{1,0:T(8,128)S(1)}, u32[]{:S(2)}, u32[]{:S(2)}) collective-permute-start(f32[256,128]{1,0:T(8,128)S(1)} %get-tuple-element.60), channel_id=1, source_target_pairs={{0,1},{1,0},{2,3},{3,2},{4,5},{5,4},{6,7},{7,6},{8,9},{9,8},{10,11... | collective-permute-start | bytes 393224 | tf_op jit(solution)/shard_map/ppermute | solution.py:327
  107.4 6.4 %collective-permute-start.16 = (bf16[2,256,128]{2,1,0:T(8,128)(2,1)S(1)}, bf16[2,256,128]{2,1,0:T(8,128)(2,1)S(1)}, u32[]{:S(2)}, u32[]{:S(2)}) collective-permute-start(bf16[2,256,128]{2,1,0:T(8,128)(2,1)S(1)} %pad_maximum_fusion.1), channel_id=1, source_target_pairs={{0,1},{1,0},{2,3},{3,2},{4,5},{5,4},{6,7},{7,6},{8,9},{9,8},{10,11... | collective-permute-start | bytes 393224 | tf_op jit(solution)/shard_map/ppermute | solution.py:327
  123.0 1.3 collective-permute-start.30
  125.7 4.8 %copy-start.2 = (bf16[128,3968]{1,0:T(8,128)(2,1)}, bf16[128,3968]{1,0:T(8,128)(2,1)S(1)}, u32[]{:S(2)}) copy-start(bf16[128,3968]{1,0:T(8,128)(2,1)S(1)} %broadcast_select_fusion.refs_0_.refs_1_.refs_2_.refs_3_.refs_4_.refs_11_) | copy-start | bytes 3047428
  130.5 67.4 %copy-start.1 = (bf16[128,3968]{1,0:T(8,128)(2,1)S(1)}, bf16[128,3968]{1,0:T(8,128)(2,1)}, u32[]{:S(2)}) copy-start(bf16[128,3968]{1,0:T(8,128)(2,1)} %copy-done) | copy-start | bytes 3047428
  130.5 67.3 %copy-start.3 = (bf16[128,3968]{1,0:T(8,128)(2,1)S(1)}, bf16[128,3968]{1,0:T(8,128)(2,1)}, u32[]{:S(2)}) copy-start(bf16[128,3968]{1,0:T(8,128)(2,1)} %copy-done.2) | copy-start | bytes 3047428
  130.5 2.0 collective-permute-start.21
  132.6 14.5 %collective-permute-start.24 = (f32[256,128]{1,0:T(8,128)S(1)}, f32[256,128]{1,0:T(8,128)S(1)}, u32[]{:S(2)}, u32[]{:S(2)}) collective-permute-start(f32[256,128]{1,0:T(8,128)S(1)} %get-tuple-element.58), channel_id=1, source_target_pairs={{0,5},{1,4},{2,7},{3,6},{4,1},{5,0},{6,3},{7,2},{8,13},{9,12},{10,... | collective-permute-start | bytes 393224 | tf_op jit(solution)/shard_map/ppermute | solution.py:327
  143.2 6.6 %collective-permute-start.23 = (f32[256,128]{1,0:T(8,128)S(1)}, f32[256,128]{1,0:T(8,128)S(1)}, u32[]{:S(2)}, u32[]{:S(2)}) collective-permute-start(f32[256,128]{1,0:T(8,128)S(1)} %get-tuple-element.59), channel_id=1, source_target_pairs={{0,4},{1,5},{2,6},{3,7},{4,0},{5,1},{6,2},{7,3},{8,12},{9,13},{10,... | collective-permute-start | bytes 393224 | tf_op jit(solution)/shard_map/ppermute | solution.py:327
  144.7 5.1 %collective-permute-start.22 = (f32[256,128]{1,0:T(8,128)S(1)}, f32[256,128]{1,0:T(8,128)S(1)}, u32[]{:S(2)}, u32[]{:S(2)}) collective-permute-start(f32[256,128]{1,0:T(8,128)S(1)} %get-tuple-element.57), channel_id=1, source_target_pairs={{0,1},{1,0},{2,3},{3,2},{4,5},{5,4},{6,7},{7,6},{8,9},{9,8},{10,11... | collective-permute-start | bytes 393224 | tf_op jit(solution)/shard_map/ppermute | solution.py:327
  149.9 9.9 %collective-permute-start.25 = (bf16[2,256,128]{2,1,0:T(8,128)(2,1)S(1)}, bf16[2,256,128]{2,1,0:T(8,128)(2,1)S(1)}, u32[]{:S(2)}, u32[]{:S(2)}) collective-permute-start(bf16[2,256,128]{2,1,0:T(8,128)(2,1)S(1)} %pad_maximum_fusion.2), channel_id=1, source_target_pairs={{0,0},{1,16},{2,2},{3,18},{4,4},{5,20},{6,6},{7,22},{8,8},{9,24},{... | collective-permute-start | bytes 393224 | tf_op jit(solution)/shard_map/ppermute | solution.py:327
  150.6 9.3 %collective-permute-start.26 = (bf16[2,256,128]{2,1,0:T(8,128)(2,1)S(1)}, bf16[2,256,128]{2,1,0:T(8,128)(2,1)S(1)}, u32[]{:S(2)}, u32[]{:S(2)}) collective-permute-start(bf16[2,256,128]{2,1,0:T(8,128)(2,1)S(1)} %pad_maximum_fusion.2), channel_id=1, source_target_pairs={{0,8},{1,24},{2,10},{3,26},{4,12},{5,28},{6,14},{7,30},{8,0},{9,16... | collective-permute-start | bytes 393224 | tf_op jit(solution)/shard_map/ppermute | solution.py:327
  150.7 10.8 %collective-permute-start.27 = (bf16[2,256,128]{2,1,0:T(8,128)(2,1)S(1)}, bf16[2,256,128]{2,1,0:T(8,128)(2,1)S(1)}, u32[]{:S(2)}, u32[]{:S(2)}) collective-permute-start(bf16[2,256,128]{2,1,0:T(8,128)(2,1)S(1)} %pad_maximum_fusion.2), channel_id=1, source_target_pairs={{0,16},{1,0},{2,18},{3,2},{4,20},{5,4},{6,22},{7,6},{8,24},{9,8},{... | collective-permute-start | bytes 393224 | tf_op jit(solution)/shard_map/ppermute | solution.py:327
  157.5 9.2 %collective-permute-start.28 = (bf16[2,256,128]{2,1,0:T(8,128)(2,1)S(1)}, bf16[2,256,128]{2,1,0:T(8,128)(2,1)S(1)}, u32[]{:S(2)}, u32[]{:S(2)}) collective-permute-start(bf16[2,256,128]{2,1,0:T(8,128)(2,1)S(1)} %pad_maximum_fusion.2), channel_id=1, source_target_pairs={{0,24},{1,8},{2,26},{3,10},{4,28},{5,12},{6,30},{7,14},{8,16},{9,0... | collective-permute-start | bytes 393224 | tf_op jit(solution)/shard_map/ppermute | solution.py:327
  157.8 8.9 %collective-permute-start.29 = (bf16[2,256,128]{2,1,0:T(8,128)(2,1)S(1)}, bf16[2,256,128]{2,1,0:T(8,128)(2,1)}, u32[]{:S(2)}, u32[]{:S(2)}) collective-permute-start(bf16[2,256,128]{2,1,0:T(8,128)(2,1)S(1)} %pad_maximum_fusion.2), channel_id=1, source_target_pairs={{0,1},{1,0},{2,3},{3,2},{4,5},{5,4},{6,7},{7,6},{8,9},{9,8},{10,11... | collective-permute-start | bytes 393224 | tf_op jit(solution)/shard_map/ppermute | solution.py:327
  181.7 14.2 %collective-permute-start.31 = (bf16[4,2,256,128]{3,2,1,0:T(8,128)(2,1)S(1)}, bf16[4,2,256,128]{3,2,1,0:T(8,128)(2,1)S(1)}, u32[]{:S(2)}, u32[]{:S(2)}) collective-permute-start(bf16[4,2,256,128]{3,2,1,0:T(8,128)(2,1)S(1)} %pad_maximum_fusion.refs_16_.refs_20_), channel_id=1, source_target_pairs={{0,4},{1,5},{2,6},{3,7},{4,0},{5,1},{6,2},{7,3},{8,12},{9,13},{10,... | collective-permute-start | bytes 1572872 | tf_op jit(solution)/shard_map/ppermute | solution.py:327
  182.3 14.5 %collective-permute-start.32 = (bf16[4,2,256,128]{3,2,1,0:T(8,128)(2,1)S(1)}, bf16[4,2,256,128]{3,2,1,0:T(8,128)(2,1)}, u32[]{:S(2)}, u32[]{:S(2)}) collective-permute-start(bf16[4,2,256,128]{3,2,1,0:T(8,128)(2,1)S(1)} %pad_maximum_fusion.refs_16_.refs_20_), channel_id=1, source_target_pairs={{0,2},{1,3},{2,0},{3,1},{4,6},{5,7},{6,4},{7,5},{8,10},{9,11},{10,... | collective-permute-start | bytes 1572872 | tf_op jit(solution)/shard_map/ppermute | solution.py:327
  195.8 2.0 collective-permute-start.33
  197.8 1.6 copy-start.4
Sparse Core Ops, SparseCore 0:
  124.5 57.0 all-gather.2

commit v15 on v8

--- a/solution.py
+++ b/solution.py
@@ -334,14 +334,14 @@
         return send(array, lambda i, j, k, t: (moves[i], j, k, t) if i in moves else None)
 
     here = y * nc + c
-    eigs = []
-    for k in range(ny * nc):
-        at = lax.bitwise_xor(here, k) * part
-        rows = lax.dynamic_slice_in_dim(eigenvectors, at, part, 0)
-        eigs.append(
-            send(rows, functools.partial(lambda q, i, j, k, t: (i, j ^ (q // 2), k ^ (q % 2), t), k))
-            if k
-            else rows
+    eigs = [
+        lax.dynamic_slice_in_dim(eigenvectors, lax.bitwise_xor(here, k) * part, part, 0)
+        for k in range(ny * nc)
+    ]
+    unit, eigs = lax.optimization_barrier((unit, eigs))
+    for q in range(1, ny * nc):
+        eigs[q] = send(
+            eigs[q], functools.partial(lambda q, i, j, k, t: (i, j ^ (q // 2), k ^ (q % 2), t), q)
         )
 
     inner = (z == 1) | (z == 2)

time: 203 us -> 200 us (0.985)
  waiting for transfers between devices: 98.8 us -> 95.4 us
    all_to_all x1, waiting for transfers between devices: 14.6 us -> 11.3 us  [local(): unit = lax.all_to_all(packed, ('y', 'c', 'x'), 0, 0, tiled=True)]
  transfers between devices with their start and end apart: 36 -> 36, of which waited for: 16 -> 16; matrix products, arithmetic and copies ran while one was open for 5% -> 5% of each run, Pallas kernels for 10% -> 11%
where the time goes in v15:
time: 200 us; the launch traced here: 199 us
  waiting for transfers between devices  95.4 us (48%)
  starting transfers between devices  45.7 us (23%)
  Pallas kernels  31 us (16%)
  between operations  13.7 us (7%)
  local copies, waits for them, and re-layouts  8.65 us (4%)
  other arithmetic  4.84 us (2%)
    ppermute x34, waiting for transfers between devices, send(): lax.ppermute(array, AXES, [(source, number[to]) for source, to in pairs i...  76.8 us
    ppermute x34, starting transfers between devices, send(): lax.ppermute(array, AXES, [(source, number[to]) for source, to in pairs i...  40.5 us
    pallas_call x4, Pallas kernels, project(): pl.pallas_call(functools.partial(project_kernel, segs, val_count, cond_co...  21.1 us
    all_to_all x1, waiting for transfers between devices, local(): unit = lax.all_to_all(packed, ('y', 'c', 'x'), 0, 0, tiled=True)  11.3 us
    all_gather x1, waiting for transfers between devices, fast(): right_a = lax.all_gather(share_a, ('z', 'y', 'c'), axis=0)  7.27 us
    pallas_call x1, Pallas kernels, make_chi(): pl.pallas_call(functools.partial(chi_kernel, early, late, n_freq, factor)...  5.88 us
    all_to_all x1, starting transfers between devices, local(): unit = lax.all_to_all(packed, ('y', 'c', 'x'), 0, 0, tiled=True)  5.17 us
    unnamed x20, local copies, waits for them, and re-layouts  4.19 us
  transfers between devices with their start and end apart: 36, of which 16 were waited for; matrix products, arithmetic and copies ran while one was open for 5% of the time, Pallas kernels for 11%

profile of v15, /device:TPU:0, one launch (start us, length us, event | category | flops | bytes accessed | tf_op | source)
XLA Modules:
  0.0 199.3 jit_solution(15299519687759075565)
XLA Ops:
  6.5 4.0 %pack.1 = bf16[8,16,3968]{2,1,0:T(8,128)(2,1)} custom-call(f32[4]{0:T(128)} %val_energy.1, f32[16]{0:T(128)} %cond_energy.1, s32[64]{0:T(128)} %val_slot.1, s32[64]{0:T(128)} %cond_slot.1, f32[4]{0:T(128)} %frequencies.1, bf16[16,24576]{1,0:T(8,128)(2,1)} %refs_1_.1, bf16[16,24576]{1,0:T(8,128)(2,1)} %refs_1_.1, bf16[4,24576]{1,0:T(4,128)(2,1)} %refs_3_.1, ...), custom_call_target="tpu_custom_call" | custom-call | tf_op jit(solution)/shard_map/pack/pallas_call | solution.py:77
  10.5 5.2 %all-to-all-start = ((bf16[8,16,3968]{2,1,0:T(8,128)(2,1)}), bf16[8,16,3968]{2,1,0:T(8,128)(2,1)}, u32[]{:S(2)}, u32[]{:S(2)}) async-start(bf16[8,16,3968]{2,1,0:T(8,128)(2,1)} %pack.1), calls=%async_computation | async-start | bytes 2031616 | tf_op jit(solution)/shard_map/all_to_all | solution.py:481
  15.8 3.4 %constant_dynamic-slice_fusion = (bf16[3072,128]{1,0:T(8,128)(2,1)}, bf16[3072,128]{1,0:T(8,128)(2,1)}, bf16[3072,128]{1,0:T(8,128)(2,1)S(1)}, bf16[3072,128]{1,0:T(8,128)(2,1)}) fusion(bf16[12288,128]{1,0:T(8,128)(2,1)} %param.14, s32[]{:T(128)S(6)} %select_n.27, s32[]{:T(128)S(6)} %select_n.25, s32[]{:T(128)S(6)} %select_n.24, s32[]{:T(128)S(6)} %select_n.26), kind=kLoop, calls=%fused_computation.38 | loop fusion | bytes 6291472 | tf_op jit(solution)/shard_map/dynamic_slice | solution.py:338
  19.1 11.3 %all-to-all-done = bf16[8,16,3968]{2,1,0:T(8,128)(2,1)} async-done(((bf16[8,16,3968]{2,1,0:T(8,128)(2,1)}), bf16[8,16,3968]{2,1,0:T(8,128)(2,1)}, u32[]{:S(2)}, u32[]{:S(2)}) %all-to-all-start) | async-done | bytes 1015840 | tf_op jit(solution)/shard_map/all_to_all | solution.py:481
  30.4 2.0 %collective-permute-start.4 = (bf16[128,3968]{1,0:T(8,128)(2,1)}, bf16[128,3968]{1,0:T(8,128)(2,1)}, u32[]{:S(2)}, u32[]{:S(2)}) collective-permute-start(bf16[128,3968]{1,0:T(8,128)(2,1)} %bitcast.5.refs_0_.refs_1_.refs_2_.refs_3_.refs_4_.refs_8_), channel_id=1, source_target_pairs={{0,8},{1,9},{2,10},{3,11},{4,12},{5,13},{6,14},{7,15},{8,0},{9,1},... | collective-permute-start | bytes 3047432 | tf_op jit(solution)/shard_map/ppermute | solution.py:328
  32.4 1.6 collective-permute-start.6
  34.6 1.3 collective-permute-start.2
  35.9 19.1 %collective-permute-done.4.refs_0_.refs_1_.refs_2_.refs_3_.refs_4_.refs_9_ = bf16[128,3968]{1,0:T(8,128)(2,1)} collective-permute-done((bf16[128,3968]{1,0:T(8,128)(2,1)}, bf16[128,3968]{1,0:T(8,128)(2,1)}, u32[]{:S(2)}, u32[]{:S(2)}) %collective-permute-start.4) | collective-permute-done | bytes 1015840 | tf_op jit(solution)/shard_map/ppermute | solution.py:328
  55.0 1.7 collective-permute-start.5
  56.6 1.3 collective-permute-start.7
  57.9 12.7 %collective-permute-done.2.refs_8_.refs_12_.refs_16_.refs_20_ = bf16[3072,128]{1,0:T(8,128)(2,1)S(1)} collective-permute-done((bf16[3072,128]{1,0:T(8,128)(2,1)}, bf16[3072,128]{1,0:T(8,128)(2,1)S(1)}, u32[]{:S(2)}, u32[]{:S(2)}) %collective-permute-start.2) | collective-permute-done | bytes 786464 | tf_op jit(solution)/shard_map/ppermute | solution.py:328
  70.6 6.1 %project.5 = (f32[2,2,256,128]{3,2,1,0:T(8,128)S(1)}, f32[2,2,256,128]{3,2,1,0:T(8,128)}) custom-call(s32[1]{0:T(128)} %bitcast.4.place, bf16[128,3968]{1,0:T(8,128)(2,1)} %collective-permute-done.4.refs_0_.refs_1_.refs_2_.refs_3_.refs_4_.refs_9_, bf16[128,3968]{1,0:T(8,128)(2,1)} %collective-permute-done.4.refs_0_.refs_1_.refs_2_.refs_3_.refs_4_.refs_9_, ...), custom_call_target="tpu_custom_call" | custom-call | flops 1610612736 | bytes 4161536 | tf_op jit(solution)/shard_map/project/pallas_call | solution.py:187
  78.2 5.4 %project.4 = (f32[2,2,256,128]{3,2,1,0:T(8,128)S(1)}, f32[2,2,256,128]{3,2,1,0:T(8,128)S(1)}) custom-call(s32[1]{0:T(128)} %bitcast.4.place, bf16[128,3968]{1,0:T(8,128)(2,1)} %bitcast.5.refs_0_.refs_1_.refs_2_.refs_3_.refs_4_.refs_8_, bf16[128,3968]{1,0:T(8,128)(2,1)} %bitcast.5.refs_0_.refs_1_.refs_2_.refs_3_.refs_4_.refs_8_, ...), custom_call_target="tpu_custom_call" | custom-call | flops 1610612736 | bytes 4161536 | tf_op jit(solution)/shard_map/project/pallas_call | solution.py:187
  83.7 1.1 add.72
  84.9 1.1 collective-permute-start.14
  85.9 1.5 collective-permute-start.13
  87.4 1.0 collective-permute-start.12
  88.4 1.3 broadcast_select_fusion.1.refs_0_.refs_1_.refs_2_.refs_3_.refs_4_.refs_10_
  89.8 4.8 %project.6 = (f32[2,2,256,128]{3,2,1,0:T(8,128)S(1)}, f32[2,2,256,128]{3,2,1,0:T(8,128)S(1)}) custom-call(s32[1]{0:T(128)} %bitcast.4.place, bf16[128,3968]{1,0:T(8,128)(2,1)S(1)} %broadcast_select_fusion.1.refs_0_.refs_1_.refs_2_.refs_3_.refs_4_.refs_10_, bf16[128,3968]{1,0:T(8,128)(2,1)S(1)} %broadcast_select_fusion.1.refs_0_.refs_1_.refs_2_.refs_3_.refs_4_.refs_10_, ...), custom_call_target="tpu_custom_call" | custom-call | flops 1610612736 | bytes 4161536 | tf_op jit(solution)/shard_map/project/pallas_call | solution.py:187
  94.8 1.1 collective-permute-start.10
  95.9 1.5 collective-permute-start.9
  97.3 1.0 collective-permute-start.8
  98.4 1.3 collective-permute-start.21
  99.8 1.1 collective-permute-start.18
  100.9 1.3 collective-permute-done.10
  102.6 2.3 %collective-permute-done.9 = f32[256,128]{1,0:T(8,128)S(1)} collective-permute-done((f32[256,128]{1,0:T(8,128)S(1)}, f32[256,128]{1,0:T(8,128)S(1)}, u32[]{:S(2)}, u32[]{:S(2)}) %collective-permute-start.9) | collective-permute-done | bytes 131104 | tf_op jit(solution)/shard_map/ppermute | solution.py:328
  104.9 1.1 collective-permute-start.16
  106.0 1.4 collective-permute-done.18
  107.4 2.5 %collective-permute-done.17 = f32[256,128]{1,0:T(8,128)S(1)} collective-permute-done((f32[256,128]{1,0:T(8,128)S(1)}, f32[256,128]{1,0:T(8,128)S(1)}, u32[]{:S(2)}, u32[]{:S(2)}) %collective-permute-start.17) | collective-permute-done | bytes 131104 | tf_op jit(solution)/shard_map/ppermute | solution.py:328
  110.6 1.6 collective-permute-start.19
  112.2 4.8 %collective-permute-start.20 = (bf16[3,256,128]{2,1,0:T(8,128)(2,1)}, bf16[3,256,128]{2,1,0:T(8,128)(2,1)}, u32[]{:S(2)}, u32[]{:S(2)}) collective-permute-start(bf16[3,256,128]{2,1,0:T(8,128)(2,1)} %pad_maximum_fusion.1), channel_id=1, source_target_pairs={{0,1},{1,0},{2,3},{3,2},{4,5},{5,4},{6,7},{7,6},{8,9},{9,8},{10,11... | collective-permute-start | bytes 589832 | tf_op jit(solution)/shard_map/ppermute | solution.py:328
  117.0 5.9 %collective-permute-done.20 = bf16[3,256,128]{2,1,0:T(8,128)(2,1)} collective-permute-done((bf16[3,256,128]{2,1,0:T(8,128)(2,1)}, bf16[3,256,128]{2,1,0:T(8,128)(2,1)}, u32[]{:S(2)}, u32[]{:S(2)}) %collective-permute-start.20) | collective-permute-done | bytes 196640 | tf_op jit(solution)/shard_map/ppermute | solution.py:328
  123.0 7.0 %collective-permute-done.21 = bf16[128,3968]{1,0:T(8,128)(2,1)} collective-permute-done((bf16[128,3968]{1,0:T(8,128)(2,1)}, bf16[128,3968]{1,0:T(8,128)(2,1)}, u32[]{:S(2)}, u32[]{:S(2)}) %collective-permute-start.21) | collective-permute-done | bytes 1015840 | tf_op jit(solution)/shard_map/ppermute | solution.py:328
  130.0 1.3 broadcast_select_fusion.refs_0_.refs_1_.refs_2_.refs_3_.refs_4_.refs_11_
  131.3 4.8 %project.7 = (f32[2,2,256,128]{3,2,1,0:T(8,128)S(1)}, f32[2,2,256,128]{3,2,1,0:T(8,128)S(1)}) custom-call(s32[1]{0:T(128)} %bitcast.4.place, bf16[128,3968]{1,0:T(8,128)(2,1)S(1)} %broadcast_select_fusion.refs_0_.refs_1_.refs_2_.refs_3_.refs_4_.refs_11_, bf16[128,3968]{1,0:T(8,128)(2,1)S(1)} %broadcast_select_fusion.refs_0_.refs_1_.refs_2_.refs_3_.refs_4_.refs_11_, ...), custom_call_target="tpu_custom_call" | custom-call | flops 1610612736 | bytes 4161536 | tf_op jit(solution)/shard_map/project/pallas_call | solution.py:187
  136.2 1.9 collective-permute-done.22
  138.9 2.9 %collective-permute-start.23 = (f32[256,128]{1,0:T(8,128)S(1)}, f32[256,128]{1,0:T(8,128)S(1)}, u32[]{:S(2)}, u32[]{:S(2)}) collective-permute-start(f32[256,128]{1,0:T(8,128)S(1)} %get-tuple-element.53), channel_id=1, source_target_pairs={{0,1},{1,0},{2,3},{3,2},{4,5},{5,4},{6,7},{7,6},{8,9},{9,8},{10,11... | collective-permute-start | bytes 393224 | tf_op jit(solution)/shard_map/ppermute | solution.py:328
  141.8 3.8 %collective-permute-done.25 = f32[256,128]{1,0:T(8,128)S(1)} collective-permute-done((f32[256,128]{1,0:T(8,128)S(1)}, f32[256,128]{1,0:T(8,128)S(1)}, u32[]{:S(2)}, u32[]{:S(2)}) %collective-permute-start.25) | collective-permute-done | bytes 131104 | tf_op jit(solution)/shard_map/ppermute | solution.py:328
  145.6 1.1 collective-permute-done.24
  148.3 6.0 %collective-permute-start.28 = (bf16[256,128]{1,0:T(8,128)(2,1)S(1)}, bf16[256,128]{1,0:T(8,128)(2,1)S(1)}, u32[]{:S(2)}, u32[]{:S(2)}) collective-permute-start(bf16[256,128]{1,0:T(8,128)(2,1)S(1)} %fusion.3.refs_3_), channel_id=1, source_target_pairs={{0,16},{1,0},{2,18},{3,2},{4,20},{5,4},{6,22},{7,6},{8,24},{9,8},{... | collective-permute-start | bytes 196616 | tf_op jit(solution)/shard_map/ppermute | solution.py:328
  154.3 1.9 collective-permute-start.30
  156.2 4.6 %collective-permute-done.29 = bf16[256,128]{1,0:T(8,128)(2,1)S(1)} collective-permute-done((bf16[256,128]{1,0:T(8,128)(2,1)S(1)}, bf16[256,128]{1,0:T(8,128)(2,1)S(1)}, u32[]{:S(2)}, u32[]{:S(2)}) %collective-permute-start.29) | collective-permute-done | bytes 65568 | tf_op jit(solution)/shard_map/ppermute | solution.py:328
  162.2 12.7 %collective-permute-done.31.refs_17_.refs_21_ = bf16[4,256,128]{2,1,0:T(8,128)(2,1)S(1)} collective-permute-done((bf16[4,256,128]{2,1,0:T(8,128)(2,1)S(1)}, bf16[4,256,128]{2,1,0:T(8,128)(2,1)S(1)}, u32[]{:S(2)}, u32[]{:S(2)}) %collective-permute-start.31) | collective-permute-done | bytes 262176 | tf_op jit(solution)/shard_map/ppermute | solution.py:328
  175.1 0.9 slice_bitcast_fusion.15
  176.5 7.3 %all-gather.3.cloned.1.call-done = bf16[48,256,128]{2,1,0:T(8,128)(2,1)} async-done(((bf16[3,256,128]{2,1,0:T(8,128)(2,1)}), bf16[48,256,128]{2,1,0:T(8,128)(2,1)}) %all-gather.3.cloned.1.call-update) | async-done | bytes 3145744 | tf_op jit(solution)/shard_map/all_gather | solution.py:384
  183.8 1.9 copy-done
  185.7 0.8 copy-done.8
  186.5 5.9 %chi.1 = f32[128,4,1024]{2,1,0:T(4,128)} custom-call(s32[5]{0:T(128)S(1)} %stack.50.scalars, bf16[256,128]{1,0:T(8,128)(2,1)S(1)} %fusion.14.refs_0_, bf16[256,128]{1,0:T(8,128)(2,1)S(1)} %fusion.11.refs_1_, bf16[256,128]{1,0:T(8,128)(2,1)S(1)} %fusion.7.refs_2_, bf16[256,128]{1,0:T(8,128)(2,1)S(1)} %fusion.3.refs_3_, ...), custom_call_target="tpu_custom_call" | custom-call | flops 2147483648 | bytes 6291456 | tf_op jit(solution)/shard_map/chi/pallas_call | solution.py:281
  (70 shorter events, 8.3 us)
Async XLA Ops:
  10.5 19.9 %all-to-all-start = ((bf16[8,16,3968]{2,1,0:T(8,128)(2,1)}), bf16[8,16,3968]{2,1,0:T(8,128)(2,1)}, u32[]{:S(2)}, u32[]{:S(2)}) async-start(bf16[8,16,3968]{2,1,0:T(8,128)(2,1)} %pack.1), calls=%async_computation | async-start | bytes 2031616 | tf_op jit(solution)/shard_map/all_to_all | solution.py:481
  15.7 168.1 %all-gather.3.cloned.1.call-start = ((), (), s32[]{:S(2)}) async-start(), calls=%async_computation.1 | async-start | bytes 3342336 | tf_op jit(solution)/shard_map/all_gather | solution.py:384
  30.4 24.6 %collective-permute-start.4 = (bf16[128,3968]{1,0:T(8,128)(2,1)}, bf16[128,3968]{1,0:T(8,128)(2,1)}, u32[]{:S(2)}, u32[]{:S(2)}) collective-permute-start(bf16[128,3968]{1,0:T(8,128)(2,1)} %bitcast.5.refs_0_.refs_1_.refs_2_.refs_3_.refs_4_.refs_8_), channel_id=1, source_target_pairs={{0,8},{1,9},{2,10},{3,11},{4,12},{5,13},{6,14},{7,15},{8,0},{9,1},... | collective-permute-start | bytes 3047432 | tf_op jit(solution)/shard_map/ppermute | solution.py:328
  32.4 24.3 %collective-permute-start.6 = (bf16[128,3968]{1,0:T(8,128)(2,1)}, bf16[128,3968]{1,0:T(8,128)(2,1)}, u32[]{:S(2)}, u32[]{:S(2)}) collective-permute-start(bf16[128,3968]{1,0:T(8,128)(2,1)} %bitcast.5.refs_0_.refs_1_.refs_2_.refs_3_.refs_4_.refs_8_), channel_id=1, source_target_pairs={{8,16},{9,17},{10,18},{11,19},{12,20},{13,21},{14,22},{15,23},{16,... | collective-permute-start | bytes 3047432 | tf_op jit(solution)/shard_map/ppermute | solution.py:328
  34.0 23.9 %collective-permute-start = (bf16[3072,128]{1,0:T(8,128)(2,1)}, bf16[3072,128]{1,0:T(8,128)(2,1)S(1)}, u32[]{:S(2)}, u32[]{:S(2)}) collective-permute-start(bf16[3072,128]{1,0:T(8,128)(2,1)} %get-tuple-element.29), channel_id=1, source_target_pairs={{0,2},{1,3},{2,0},{3,1},{4,6},{5,7},{6,4},{7,5},{8,10},{9,11},{10,... | collective-permute-start | bytes 2359304 | tf_op jit(solution)/shard_map/ppermute | solution.py:328
  34.0 23.9 %collective-permute-start.1 = (bf16[3072,128]{1,0:T(8,128)(2,1)}, bf16[3072,128]{1,0:T(8,128)(2,1)S(1)}, u32[]{:S(2)}, u32[]{:S(2)}) collective-permute-start(bf16[3072,128]{1,0:T(8,128)(2,1)} %get-tuple-element.30), channel_id=1, source_target_pairs={{0,4},{1,5},{2,6},{3,7},{4,0},{5,1},{6,2},{7,3},{8,12},{9,13},{10,... | collective-permute-start | bytes 2359304 | tf_op jit(solution)/shard_map/ppermute | solution.py:328
  34.6 36.0 %collective-permute-start.2 = (bf16[3072,128]{1,0:T(8,128)(2,1)}, bf16[3072,128]{1,0:T(8,128)(2,1)S(1)}, u32[]{:S(2)}, u32[]{:S(2)}) collective-permute-start(bf16[3072,128]{1,0:T(8,128)(2,1)} %get-tuple-element.31), channel_id=1, source_target_pairs={{0,6},{1,7},{2,4},{3,5},{4,2},{5,3},{6,0},{7,1},{8,14},{9,15},{10,... | collective-permute-start | bytes 2359304 | tf_op jit(solution)/shard_map/ppermute | solution.py:328
  55.0 32.4 %collective-permute-start.5 = (bf16[128,3968]{1,0:T(8,128)(2,1)}, bf16[128,3968]{1,0:T(8,128)(2,1)}, u32[]{:S(2)}, u32[]{:S(2)}) collective-permute-start(bf16[128,3968]{1,0:T(8,128)(2,1)} %collective-permute-done.4.refs_0_.refs_1_.refs_2_.refs_3_.refs_4_.refs_9_), channel_id=1, source_target_pairs={{8,16},{9,17},{10,18},{11,19},{12,20},{13,21},{14,22},{15,23},{16,... | collective-permute-start | bytes 3047432 | tf_op jit(solution)/shard_map/ppermute | solution.py:328
  56.6 31.8 %collective-permute-start.7 = (bf16[128,3968]{1,0:T(8,128)(2,1)}, bf16[128,3968]{1,0:T(8,128)(2,1)}, u32[]{:S(2)}, u32[]{:S(2)}) collective-permute-start(bf16[128,3968]{1,0:T(8,128)(2,1)} %collective-permute-done.6), channel_id=1, source_target_pairs={{8,0},{9,1},{10,2},{11,3},{12,4},{13,5},{14,6},{15,7},{16,24},{17,... | collective-permute-start | bytes 3047432 | tf_op jit(solution)/shard_map/ppermute | solution.py:328
  76.8 0.8 copy-start.5
  77.6 6.2 %collective-permute-start.11 = (f32[2,2,256,128]{3,2,1,0:T(8,128)}, f32[2,2,256,128]{3,2,1,0:T(8,128)}, u32[]{:S(2)}, u32[]{:S(2)}) collective-permute-start(f32[2,2,256,128]{3,2,1,0:T(8,128)} %get-tuple-element.36), channel_id=1, source_target_pairs={{0,2},{1,3},{2,0},{3,1},{4,6},{5,7},{6,4},{7,5},{8,10},{9,11},{10,... | collective-permute-start | bytes 1572872 | tf_op jit(solution)/shard_map/ppermute | solution.py:328
  78.2 5.5 %copy-start.6 = (f32[2,2,256,128]{3,2,1,0:T(8,128)S(1)}, f32[2,2,256,128]{3,2,1,0:T(8,128)}, u32[]{:S(2)}) copy-start(f32[2,2,256,128]{3,2,1,0:T(8,128)} %copy-done.5) | copy-start | bytes 1572868
  83.6 11.0 %collective-permute-start.3 = (f32[2,2,256,128]{3,2,1,0:T(8,128)S(1)}, f32[2,2,256,128]{3,2,1,0:T(8,128)S(1)}, u32[]{:S(2)}, u32[]{:S(2)}) collective-permute-start(f32[2,2,256,128]{3,2,1,0:T(8,128)S(1)} %get-tuple-element.33), channel_id=1, source_target_pairs={{0,2},{1,3},{2,0},{3,1},{4,6},{5,7},{6,4},{7,5},{8,10},{9,11},{10,... | collective-permute-start | bytes 1572872 | tf_op jit(solution)/shard_map/ppermute | solution.py:328
  84.9 9.8 %collective-permute-start.14 = (f32[256,128]{1,0:T(8,128)S(1)}, f32[256,128]{1,0:T(8,128)S(1)}, u32[]{:S(2)}, u32[]{:S(2)}) collective-permute-start(f32[256,128]{1,0:T(8,128)S(1)} %get-tuple-element.60), channel_id=1, source_target_pairs={{0,5},{1,4},{2,7},{3,6},{4,1},{5,0},{6,3},{7,2},{8,13},{9,12},{10,... | collective-permute-start | bytes 393224 | tf_op jit(solution)/shard_map/ppermute | solution.py:328
  85.9 8.8 %collective-permute-start.13 = (f32[256,128]{1,0:T(8,128)S(1)}, f32[256,128]{1,0:T(8,128)S(1)}, u32[]{:S(2)}, u32[]{:S(2)}) collective-permute-start(f32[256,128]{1,0:T(8,128)S(1)} %get-tuple-element.61), channel_id=1, source_target_pairs={{0,4},{1,5},{2,6},{3,7},{4,0},{5,1},{6,2},{7,3},{8,12},{9,13},{10,... | collective-permute-start | bytes 393224 | tf_op jit(solution)/shard_map/ppermute | solution.py:328
  87.4 7.3 %collective-permute-start.12 = (f32[256,128]{1,0:T(8,128)S(1)}, f32[256,128]{1,0:T(8,128)S(1)}, u32[]{:S(2)}, u32[]{:S(2)}) collective-permute-start(f32[256,128]{1,0:T(8,128)S(1)} %get-tuple-element.59), channel_id=1, source_target_pairs={{0,1},{1,0},{2,3},{3,2},{4,5},{5,4},{6,7},{7,6},{8,9},{9,8},{10,11... | collective-permute-start | bytes 393224 | tf_op jit(solution)/shard_map/ppermute | solution.py:328
  89.8 4.8 %copy-start.1 = (bf16[128,3968]{1,0:T(8,128)(2,1)}, bf16[128,3968]{1,0:T(8,128)(2,1)S(1)}, u32[]{:S(2)}) copy-start(bf16[128,3968]{1,0:T(8,128)(2,1)S(1)} %broadcast_select_fusion.1.refs_0_.refs_1_.refs_2_.refs_3_.refs_4_.refs_10_) | copy-start | bytes 3047428
  94.6 5.1 %collective-permute-start.15 = (f32[2,2,256,128]{3,2,1,0:T(8,128)S(1)}, f32[2,2,256,128]{3,2,1,0:T(8,128)S(1)}, u32[]{:S(2)}, u32[]{:S(2)}) collective-permute-start(f32[2,2,256,128]{3,2,1,0:T(8,128)S(1)} %get-tuple-element.38), channel_id=1, source_target_pairs={{0,2},{1,3},{2,0},{3,1},{4,6},{5,7},{6,4},{7,5},{8,10},{9,11},{10,... | collective-permute-start | bytes 1572872 | tf_op jit(solution)/shard_map/ppermute | solution.py:328
  94.8 7.3 %collective-permute-start.10 = (f32[256,128]{1,0:T(8,128)S(1)}, f32[256,128]{1,0:T(8,128)S(1)}, u32[]{:S(2)}, u32[]{:S(2)}) collective-permute-start(f32[256,128]{1,0:T(8,128)S(1)} %get-tuple-element.63), channel_id=1, source_target_pairs={{0,5},{1,4},{2,7},{3,6},{4,1},{5,0},{6,3},{7,2},{8,13},{9,12},{10,... | collective-permute-start | bytes 393224 | tf_op jit(solution)/shard_map/ppermute | solution.py:328
  95.9 9.0 %collective-permute-start.9 = (f32[256,128]{1,0:T(8,128)S(1)}, f32[256,128]{1,0:T(8,128)S(1)}, u32[]{:S(2)}, u32[]{:S(2)}) collective-permute-start(f32[256,128]{1,0:T(8,128)S(1)} %get-tuple-element.64), channel_id=1, source_target_pairs={{0,4},{1,5},{2,6},{3,7},{4,0},{5,1},{6,2},{7,3},{8,12},{9,13},{10,... | collective-permute-start | bytes 393224 | tf_op jit(solution)/shard_map/ppermute | solution.py:328
  97.3 8.6 %collective-permute-start.8 = (f32[256,128]{1,0:T(8,128)S(1)}, f32[256,128]{1,0:T(8,128)S(1)}, u32[]{:S(2)}, u32[]{:S(2)}) collective-permute-start(f32[256,128]{1,0:T(8,128)S(1)} %get-tuple-element.62), channel_id=1, source_target_pairs={{0,1},{1,0},{2,3},{3,2},{4,5},{5,4},{6,7},{7,6},{8,9},{9,8},{10,11... | collective-permute-start | bytes 393224 | tf_op jit(solution)/shard_map/ppermute | solution.py:328
  98.4 31.6 %collective-permute-start.21 = (bf16[128,3968]{1,0:T(8,128)(2,1)}, bf16[128,3968]{1,0:T(8,128)(2,1)}, u32[]{:S(2)}, u32[]{:S(2)}) collective-permute-start(bf16[128,3968]{1,0:T(8,128)(2,1)} %collective-permute-done.5), channel_id=1, source_target_pairs={{8,0},{9,1},{10,2},{11,3},{12,4},{13,5},{14,6},{15,7},{16,24},{17,... | collective-permute-start | bytes 3047432 | tf_op jit(solution)/shard_map/ppermute | solution.py:328
  99.8 7.6 %collective-permute-start.18 = (f32[256,128]{1,0:T(8,128)S(1)}, f32[256,128]{1,0:T(8,128)S(1)}, u32[]{:S(2)}, u32[]{:S(2)}) collective-permute-start(f32[256,128]{1,0:T(8,128)S(1)} %get-tuple-element.57), channel_id=1, source_target_pairs={{0,5},{1,4},{2,7},{3,6},{4,1},{5,0},{6,3},{7,2},{8,13},{9,12},{10,... | collective-permute-start | bytes 393224 | tf_op jit(solution)/shard_map/ppermute | solution.py:328
  102.1 7.8 %collective-permute-start.17 = (f32[256,128]{1,0:T(8,128)S(1)}, f32[256,128]{1,0:T(8,128)S(1)}, u32[]{:S(2)}, u32[]{:S(2)}) collective-permute-start(f32[256,128]{1,0:T(8,128)S(1)} %get-tuple-element.58), channel_id=1, source_target_pairs={{0,4},{1,5},{2,6},{3,7},{4,0},{5,1},{6,2},{7,3},{8,12},{9,13},{10,... | collective-permute-start | bytes 393224 | tf_op jit(solution)/shard_map/ppermute | solution.py:328
  104.9 5.0 %collective-permute-start.16 = (f32[256,128]{1,0:T(8,128)S(1)}, f32[256,128]{1,0:T(8,128)S(1)}, u32[]{:S(2)}, u32[]{:S(2)}) collective-permute-start(f32[256,128]{1,0:T(8,128)S(1)} %get-tuple-element.56), channel_id=1, source_target_pairs={{0,1},{1,0},{2,3},{3,2},{4,5},{5,4},{6,7},{7,6},{8,9},{9,8},{10,11... | collective-permute-start | bytes 393224 | tf_op jit(solution)/shard_map/ppermute | solution.py:328
  110.6 6.4 %collective-permute-start.19 = (bf16[3,256,128]{2,1,0:T(8,128)(2,1)}, bf16[3,256,128]{2,1,0:T(8,128)(2,1)S(1)}, u32[]{:S(2)}, u32[]{:S(2)}) collective-permute-start(bf16[3,256,128]{2,1,0:T(8,128)(2,1)} %pad_maximum_fusion.1), channel_id=1, source_target_pairs={{0,0},{1,16},{2,2},{3,18},{4,4},{5,20},{6,6},{7,22},{8,8},{9,24},{... | collective-permute-start | bytes 589832 | tf_op jit(solution)/shard_map/ppermute | solution.py:328
  112.2 10.8 %collective-permute-start.20 = (bf16[3,256,128]{2,1,0:T(8,128)(2,1)}, bf16[3,256,128]{2,1,0:T(8,128)(2,1)}, u32[]{:S(2)}, u32[]{:S(2)}) collective-permute-start(bf16[3,256,128]{2,1,0:T(8,128)(2,1)} %pad_maximum_fusion.1), channel_id=1, source_target_pairs={{0,1},{1,0},{2,3},{3,2},{4,5},{5,4},{6,7},{7,6},{8,9},{9,8},{10,11... | collective-permute-start | bytes 589832 | tf_op jit(solution)/shard_map/ppermute | solution.py:328
  117.0 12.9 %copy-start.9 = (bf16[3,256,128]{2,1,0:T(8,128)(2,1)}, bf16[3,256,128]{2,1,0:T(8,128)(2,1)S(1)}, u32[]{:S(2)}) copy-start(bf16[3,256,128]{2,1,0:T(8,128)(2,1)S(1)} %collective-permute-done.19) | copy-start | bytes 589828
  131.3 4.8 %copy-start.3 = (bf16[128,3968]{1,0:T(8,128)(2,1)}, bf16[128,3968]{1,0:T(8,128)(2,1)S(1)}, u32[]{:S(2)}) copy-start(bf16[128,3968]{1,0:T(8,128)(2,1)S(1)} %broadcast_select_fusion.refs_0_.refs_1_.refs_2_.refs_3_.refs_4_.refs_11_) | copy-start | bytes 3047428
  136.1 47.7 %copy-start.2 = (bf16[128,3968]{1,0:T(8,128)(2,1)S(1)}, bf16[128,3968]{1,0:T(8,128)(2,1)}, u32[]{:S(2)}) copy-start(bf16[128,3968]{1,0:T(8,128)(2,1)} %copy-done.1) | copy-start | bytes 3047428
  136.1 47.7 %copy-start.4 = (bf16[128,3968]{1,0:T(8,128)(2,1)S(1)}, bf16[128,3968]{1,0:T(8,128)(2,1)}, u32[]{:S(2)}) copy-start(bf16[128,3968]{1,0:T(8,128)(2,1)} %copy-done.3) | copy-start | bytes 3047428
  136.1 2.0 collective-permute-start.22
  138.2 7.4 %collective-permute-start.25 = (f32[256,128]{1,0:T(8,128)S(1)}, f32[256,128]{1,0:T(8,128)S(1)}, u32[]{:S(2)}, u32[]{:S(2)}) collective-permute-start(f32[256,128]{1,0:T(8,128)S(1)} %get-tuple-element.54), channel_id=1, source_target_pairs={{0,5},{1,4},{2,7},{3,6},{4,1},{5,0},{6,3},{7,2},{8,13},{9,12},{10,... | collective-permute-start | bytes 393224 | tf_op jit(solution)/shard_map/ppermute | solution.py:328
  138.3 8.4 %collective-permute-start.24 = (f32[256,128]{1,0:T(8,128)S(1)}, f32[256,128]{1,0:T(8,128)S(1)}, u32[]{:S(2)}, u32[]{:S(2)}) collective-permute-start(f32[256,128]{1,0:T(8,128)S(1)} %get-tuple-element.55), channel_id=1, source_target_pairs={{0,4},{1,5},{2,6},{3,7},{4,0},{5,1},{6,2},{7,3},{8,12},{9,13},{10,... | collective-permute-start | bytes 393224 | tf_op jit(solution)/shard_map/ppermute | solution.py:328
  138.9 7.8 %collective-permute-start.23 = (f32[256,128]{1,0:T(8,128)S(1)}, f32[256,128]{1,0:T(8,128)S(1)}, u32[]{:S(2)}, u32[]{:S(2)}) collective-permute-start(f32[256,128]{1,0:T(8,128)S(1)} %get-tuple-element.53), channel_id=1, source_target_pairs={{0,1},{1,0},{2,3},{3,2},{4,5},{5,4},{6,7},{7,6},{8,9},{9,8},{10,11... | collective-permute-start | bytes 393224 | tf_op jit(solution)/shard_map/ppermute | solution.py:328
  146.8 9.4 %collective-permute-start.26 = (bf16[256,128]{1,0:T(8,128)(2,1)S(1)}, bf16[256,128]{1,0:T(8,128)(2,1)S(1)}, u32[]{:S(2)}, u32[]{:S(2)}) collective-permute-start(bf16[256,128]{1,0:T(8,128)(2,1)S(1)} %fusion.3.refs_3_), channel_id=1, source_target_pairs={{0,0},{1,16},{2,2},{3,18},{4,4},{5,20},{6,6},{7,22},{8,8},{9,24},{... | collective-permute-start | bytes 196616 | tf_op jit(solution)/shard_map/ppermute | solution.py:328
  147.4 8.7 %collective-permute-start.27 = (bf16[256,128]{1,0:T(8,128)(2,1)S(1)}, bf16[256,128]{1,0:T(8,128)(2,1)S(1)}, u32[]{:S(2)}, u32[]{:S(2)}) collective-permute-start(bf16[256,128]{1,0:T(8,128)(2,1)S(1)} %fusion.3.refs_3_), channel_id=1, source_target_pairs={{0,8},{1,24},{2,10},{3,26},{4,12},{5,28},{6,14},{7,30},{8,0},{9,16... | collective-permute-start | bytes 196616 | tf_op jit(solution)/shard_map/ppermute | solution.py:328
  148.3 7.9 %collective-permute-start.28 = (bf16[256,128]{1,0:T(8,128)(2,1)S(1)}, bf16[256,128]{1,0:T(8,128)(2,1)S(1)}, u32[]{:S(2)}, u32[]{:S(2)}) collective-permute-start(bf16[256,128]{1,0:T(8,128)(2,1)S(1)} %fusion.3.refs_3_), channel_id=1, source_target_pairs={{0,16},{1,0},{2,18},{3,2},{4,20},{5,4},{6,22},{7,6},{8,24},{9,8},{... | collective-permute-start | bytes 196616 | tf_op jit(solution)/shard_map/ppermute | solution.py:328
  154.3 6.5 %collective-permute-start.29 = (bf16[256,128]{1,0:T(8,128)(2,1)S(1)}, bf16[256,128]{1,0:T(8,128)(2,1)S(1)}, u32[]{:S(2)}, u32[]{:S(2)}) collective-permute-start(bf16[256,128]{1,0:T(8,128)(2,1)S(1)} %fusion.3.refs_3_), channel_id=1, source_target_pairs={{0,24},{1,8},{2,26},{3,10},{4,28},{5,12},{6,30},{7,14},{8,16},{9,0... | collective-permute-start | bytes 196616 | tf_op jit(solution)/shard_map/ppermute | solution.py:328
  154.3 6.5 %collective-permute-start.30 = (bf16[256,128]{1,0:T(8,128)(2,1)S(1)}, bf16[256,128]{1,0:T(8,128)(2,1)S(1)}, u32[]{:S(2)}, u32[]{:S(2)}) collective-permute-start(bf16[256,128]{1,0:T(8,128)(2,1)S(1)} %fusion.3.refs_3_), channel_id=1, source_target_pairs={{0,1},{1,0},{2,3},{3,2},{4,5},{5,4},{6,7},{7,6},{8,9},{9,8},{10,11... | collective-permute-start | bytes 196616 | tf_op jit(solution)/shard_map/ppermute | solution.py:328
  160.8 0.6 copy-start.7
  161.4 13.5 %collective-permute-start.31 = (bf16[4,256,128]{2,1,0:T(8,128)(2,1)S(1)}, bf16[4,256,128]{2,1,0:T(8,128)(2,1)S(1)}, u32[]{:S(2)}, u32[]{:S(2)}) collective-permute-start(bf16[4,256,128]{2,1,0:T(8,128)(2,1)S(1)} %pad_maximum_fusion.refs_16_.refs_20_), channel_id=1, source_target_pairs={{0,4},{1,5},{2,6},{3,7},{4,0},{5,1},{6,2},{7,3},{8,12},{9,13},{10,... | collective-permute-start | bytes 786440 | tf_op jit(solution)/shard_map/ppermute | solution.py:328
  162.2 13.7 %collective-permute-start.32 = (bf16[4,256,128]{2,1,0:T(8,128)(2,1)S(1)}, bf16[4,256,128]{2,1,0:T(8,128)(2,1)S(1)}, u32[]{:S(2)}, u32[]{:S(2)}) collective-permute-start(bf16[4,256,128]{2,1,0:T(8,128)(2,1)S(1)} %pad_maximum_fusion.refs_16_.refs_20_), channel_id=1, source_target_pairs={{0,2},{1,3},{2,0},{3,1},{4,6},{5,7},{6,4},{7,5},{8,10},{9,11},{10,... | collective-permute-start | bytes 786440 | tf_op jit(solution)/shard_map/ppermute | solution.py:328
  175.0 1.6 collective-permute-start.33
  183.8 1.9 copy-start
  185.7 0.8 copy-start.8
Sparse Core Ops, SparseCore 0:
  130.1 53.6 all-gather.2
